TPU v7x, 128 devices: a whole 4x4x4 slice. The times are simulated.
128 devices in a mesh: span: 64 (over z, x, y_hi, core), head: 2 (over y_lo).
Axes of the slice: x: 4, y: 4 (y_hi: 2, y_lo: 2; y = y_hi * 2 + y_lo), z: 4, core: 2. Of those that a mesh axis runs over, the one named last changes fastest.
Arguments:
- tokens: bfloat16 [16384, 1536], P(('span', 'head')), may hold values from -6 to 6
- doc_starts: int32 [8], replicated, may hold values from 0 to 16383, as said below
- norm_gain: bfloat16 [2, 1536], P(None, ('span', 'head')), may hold values from 0.5 to 1.5
- in_weight: bfloat16 [2, 1536, 6448], P(None, ('span', 'head')), may hold values from -0.15625 to 0.15625
- conv_weight: bfloat16 [2, 4, 3328], P(None, None, ('span', 'head')), may hold values from -3 to 3
- conv_bias: bfloat16 [2, 3328], P(None, ('span', 'head')), may hold values from -1.5 to 1.5
- step_bias: float32 [2, 48], P(None, 'head')
- decay_log: float32 [2, 48], P(None, 'head')
- skip_gain: float32 [2, 48], P(None, 'head'), may hold values from 0.5 to 1.5
- gate_gain: bfloat16 [2, 3072], P(None, ('span', 'head')), may hold values from 0.5 to 1.5
- out_weight: bfloat16 [2, 3072, 1536], P(None, ('span', 'head')), may hold values from -0.109375 to 0.109375
- cotangent: bfloat16 [16384, 1536], P(('span', 'head')), may hold values from -6 to 6
Outputs:
- output: bfloat16 [16384, 1536], P(('span', 'head'))
- tokens_grad: float32 [16384, 1536], P(('span', 'head'))
- norm_gain_grad: float32 [2, 1536], P(None, ('span', 'head'))
- in_weight_grad: float32 [2, 1536, 6448], P(None, ('span', 'head'))
- conv_weight_grad: float32 [2, 4, 3328], P(None, None, ('span', 'head'))
- conv_bias_grad: float32 [2, 3328], P(None, ('span', 'head'))
- step_bias_grad: float32 [2, 48], P(None, 'head')
- decay_log_grad: float32 [2, 48], P(None, 'head')
- skip_gain_grad: float32 [2, 48], P(None, 'head')
- gate_gain_grad: float32 [2, 3072], P(None, ('span', 'head'))
- out_weight_grad: float32 [2, 3072, 1536], P(None, ('span', 'head'))
Inputs may be any that keep to these rules, and one draw needn't show every extreme that they name: `doc_starts`: strictly increasing; the first is 0.
All inputs are finite; a program needn't handle non-finite values.
Results may differ from a plain program's by a relative error of at most 0.03.
Values may be sent and summed in bfloat16 or wider, within the bound.
No kernel may reach another device: no remote copies, remote signals or barrier semaphores. Data moves between devices by JAX's collectives and lax.ppermute only.
A program may use at most 896 MiB of HBM per device.

v0:
```python
from functools import partial

import jax
import jax.numpy as jnp
from jax import lax
from jax.sharding import PartitionSpec as P

DI = 3072
H = 48
HP = 64
N = 128
CONV = 4
LAYERS = 2


epsilon = 1e-05


def for_sending(shard):

    def short(part):
        return part.astype(jnp.bfloat16) if part.dtype == jnp.float32 else part

    return jax.tree.map(short, shard)


def partner_2(value, axis, distance):
    mask = 2**distance
    pairs = [(source, source ^ mask) for source in range(lax.axis_size(axis))]
    return lax.ppermute(value, axis, pairs)


def shifted_2(block, axis, distance):
    devices = range(lax.axis_size(axis))
    route = [(i - distance, i) for i in devices if i - distance in devices]
    return lax.ppermute(block, axis, route)


def in_blocks(shard, dim, count):
    dims = shard.shape
    blocks = shard.reshape(*dims[:dim], count, dims[dim] // count, *dims[dim + 1 :])
    return jnp.moveaxis(blocks, dim, 0)


def summed_on_arrival(shard, axis, dim):
    count = lax.axis_size(axis)
    blocks = lax.all_to_all(in_blocks(shard, dim, count), axis, 0, 0, tiled=True)
    return jnp.sum(blocks.astype(jnp.float32), axis=0)


def sent_together(arrays, axis, split_dim, concat_dim, along):
    ends, at = ([], 0)
    for a in arrays[:-1]:
        at += a.shape[along]
        ends.append(at)
    both = jnp.concatenate(arrays, axis=along)
    return tuple(
        jnp.split(
            lax.all_to_all(both, axis, split_axis=split_dim, concat_axis=concat_dim, tiled=True),
            ends,
            axis=along,
        )
    )


def in_order(blocks, dim):
    blocks = jnp.moveaxis(blocks, 0, dim)
    dims = blocks.shape
    return blocks.reshape(*dims[:dim], dims[dim] * dims[dim + 1], *dims[dim + 2 :])


def gather_together(arrays, axis, dims):
    line = jnp.concatenate([a.reshape(-1) for a in arrays])
    lines, at, outs = (lax.all_gather(line, axis), 0, [])
    for a, dim in zip(arrays, dims):
        blocks = lines[:, at : at + a.size].reshape(-1, *a.shape)
        outs.append(in_order(blocks, dim))
        at += a.size
    return tuple(outs)


def copy_for_each(shard, axis):
    count = lax.axis_size(axis)
    return lax.all_to_all(
        jnp.broadcast_to(shard[None], (count, *shard.shape)), axis, 0, 0, tiled=True
    )


def taken_together(shard, axis):
    return copy_for_each(shard, axis).sum(axis=0)


def rms_gain(hidden, gain):
    mean_square = jnp.mean(hidden * hidden, axis=-1, keepdims=True)
    return hidden * lax.rsqrt(mean_square + epsilon) * gain


def gated_norm(mixed_in, gate_part, gain):
    gated = mixed_in * jax.nn.silu(gate_part)
    mean_square = jnp.mean(gated * gated, axis=-1, keepdims=True)
    return gated * lax.rsqrt(mean_square + epsilon) * gain


def segment_ids(doc_starts, positions):
    return jnp.sum((doc_starts[None, :] <= positions[:, None]).astype(jnp.int32), axis=1) - 1


def conv_apply(segment_ext, extended, weight, bias):
    span_len = extended.shape[0] - (CONV - 1)
    segment = segment_ext[CONV - 1 :]
    summed = jnp.zeros((span_len, extended.shape[1]), jnp.float32) + bias[None, :]
    for offset in range(CONV):
        first_row = CONV - 1 - offset
        shifted = extended[first_row : first_row + span_len]
        same_doc = (segment_ext[first_row : first_row + span_len] == segment).astype(jnp.float32)
        summed = summed + weight[offset][None, :] * shifted * same_doc[:, None]
    return jax.nn.silu(summed)


def span_factors(step_raw, step_bias, decay_log, segment, seg_before):
    step_size = jax.nn.softplus(step_raw + step_bias[None, :])
    running = jnp.cumsum(-jnp.exp(decay_log)[None, :] * step_size, axis=0)
    run_heads = running.T
    length = segment.shape[0]
    order = jnp.arange(length)
    intra_mask = (order[None, :] <= order[:, None]) & (segment[None, :] == segment[:, None])
    mask_float = intra_mask.astype(jnp.float32)
    spread = run_heads[:, :, None] - run_heads[:, None, :]
    decay_matrix = (
        jnp.exp(jnp.where(intra_mask[None], spread, 0.0))
        * mask_float[None]
        * step_size.T[:, None, :]
    )
    inflow = jnp.exp(running) * (segment == seg_before).astype(jnp.float32)[:, None]
    weights = (
        jnp.exp(running[-1][None, :] - running)
        * step_size
        * (segment == segment[-1]).astype(jnp.float32)[:, None]
    )
    span_decay = jnp.exp(running[-1]) * (segment[-1] == seg_before).astype(jnp.float32)
    return (decay_matrix, inflow, weights, span_decay)


def chain_combine(first_part, second_part):
    return (
        first_part[0] * second_part[0],
        second_part[0][:, None, None] * first_part[1] + second_part[1],
    )


def pick_pair(flag, left, right):
    return (jnp.where(flag, left[0], right[0]), jnp.where(flag, left[1], right[1]))


def span_prefix(element, identity, backward):
    span_count = lax.axis_size("span")
    bit_count = span_count.bit_length() - 1
    span_index = lax.axis_index("span")
    prefix = identity
    total = element
    for bit in range(bit_count):
        if backward:
            partner = partner_2((for_sending(total[0]), for_sending(total[1])), "span", bit)
        else:
            partner = partner_2((for_sending(total[0]), for_sending(total[1])), "span", bit)
        upper = span_index >> bit & 1 == 1
        partner_first = jnp.logical_not(upper) if backward else upper
        prefix = pick_pair(partner_first, chain_combine(partner, prefix), prefix)
        total = pick_pair(
            partner_first, chain_combine(partner, total), chain_combine(total, partner)
        )
    return prefix


def head_forward(x_heads, bc_heads, step_heads, conv_full, bias_full, head_params, doc_starts):
    step_bias, decay_log, skip_gain = head_params
    span_len, local_width = x_heads.shape
    head_local = step_bias.shape[0]
    group_index = lax.axis_index("head")
    conv_x = lax.dynamic_slice_in_dim(conv_full, group_index * local_width, local_width, 1)
    conv_here = jnp.concatenate([conv_x, conv_full[:, DI:]], axis=1).astype(jnp.float32)
    bias_x = lax.dynamic_slice_in_dim(bias_full, group_index * local_width, local_width, 0)
    bias_here = jnp.concatenate([bias_x, bias_full[DI:]], axis=0).astype(jnp.float32)
    joined = jnp.concatenate([x_heads, bc_heads], axis=1)
    edge_rows = shifted_2(joined[span_len - (CONV - 1) :], "span", 1)
    extended = jnp.concatenate([edge_rows, joined], axis=0).astype(jnp.float32)
    positions = (
        lax.axis_index("span") * span_len
        + jnp.arange(span_len + CONV - 1, dtype=jnp.int32)
        - (CONV - 1)
    )
    segment_ext = segment_ids(doc_starts, positions)
    segment = segment_ext[CONV - 1 :]
    seg_before = segment_ext[CONV - 2]
    conv_out, conv_back = jax.vjp(partial(conv_apply, segment_ext), extended, conv_here, bias_here)
    x_full = conv_out[:, :local_width]
    x_wide = x_full.reshape(span_len, head_local, HP)
    x_split = x_full.astype(jnp.bfloat16).reshape(span_len, head_local, HP)
    b_low = conv_out[:, local_width : local_width + N].astype(jnp.bfloat16)
    c_low = conv_out[:, local_width + N :].astype(jnp.bfloat16)
    c_wide = c_low.astype(jnp.float32)
    factors, factor_back = jax.vjp(
        partial(span_factors, segment=segment, seg_before=seg_before),
        step_heads.astype(jnp.float32),
        step_bias,
        decay_log,
    )
    decay_matrix, inflow, weights, span_decay = factors
    gram_matrix = lax.dot_general(
        c_low, b_low, (((1,), (1,)), ((), ())), preferred_element_type=jnp.float32
    )
    mixing = (gram_matrix[None] * decay_matrix).astype(jnp.bfloat16)
    within = jnp.einsum("hts,shp->thp", mixing, x_split, preferred_element_type=jnp.float32)
    weighted = (weights[:, :, None] * x_wide).astype(jnp.bfloat16)
    own_state = jnp.einsum("shp,sn->hpn", weighted, b_low, preferred_element_type=jnp.float32)
    identity = (jnp.ones_like(span_decay), jnp.zeros_like(own_state))
    prefix = span_prefix((span_decay, own_state), identity, False)
    carried_in = prefix[1]
    reading = jnp.einsum("hpn,tn->thp", carried_in, c_wide)
    mixed_out = within + inflow[:, :, None] * reading + skip_gain[None, :, None] * x_wide
    mixed_low = mixed_out.reshape(span_len, local_width).astype(jnp.bfloat16)
    stash = dict(
        conv_back=conv_back,
        factor_back=factor_back,
        x_wide=x_wide,
        x_split=x_split,
        b_low=b_low,
        c_low=c_low,
        c_wide=c_wide,
        gram_matrix=gram_matrix,
        decay_matrix=decay_matrix,
        mixing=mixing,
        inflow=inflow,
        weights=weights,
        span_decay=span_decay,
        weighted=weighted,
        carried_in=carried_in,
        reading=reading,
        skip_gain=skip_gain,
        identity=identity,
    )
    return (mixed_low, stash)


def head_backward(grad_heads, stash):
    span_len, head_local, head_size = grad_heads.shape
    local_width = head_local * head_size
    grad_wide = grad_heads.astype(jnp.float32)
    x_wide = stash["x_wide"]
    inflow = stash["inflow"]
    carried_in = stash["carried_in"]
    b_low = stash["b_low"]
    c_low = stash["c_low"]
    skip_grad = jnp.sum(grad_wide * x_wide, axis=(0, 2))
    x_grad = stash["skip_gain"][None, :, None] * grad_wide
    inflow_grad = jnp.sum(grad_wide * stash["reading"], axis=2)
    scaled = inflow[:, :, None] * grad_wide
    carried_grad = jnp.einsum("thp,tn->hpn", scaled, stash["c_wide"])
    c_grad = jnp.einsum("thp,hpn->tn", scaled, carried_in)
    mixing_grad = jnp.einsum(
        "thp,shp->hts", grad_heads, stash["x_split"], preferred_element_type=jnp.float32
    )
    x_grad = x_grad + jnp.einsum(
        "hts,thp->shp", stash["mixing"], grad_heads, preferred_element_type=jnp.float32
    )
    decay_grad = mixing_grad * stash["gram_matrix"][None]
    gram_grad = jnp.sum(mixing_grad * stash["decay_matrix"], axis=0).astype(jnp.bfloat16)
    c_grad = c_grad + jnp.dot(gram_grad, b_low, preferred_element_type=jnp.float32)
    b_grad = lax.dot_general(
        gram_grad, c_low, (((0,), (0,)), ((), ())), preferred_element_type=jnp.float32
    )
    later_sum = span_prefix((stash["span_decay"], carried_grad), stash["identity"], True)
    end_grad = later_sum[1]
    span_decay_grad = jnp.sum(end_grad * carried_in, axis=(1, 2))
    weighted_grad = jnp.einsum("hpn,sn->shp", end_grad, b_low.astype(jnp.float32))
    b_grad = b_grad + jnp.einsum("hpn,shp->sn", end_grad, stash["weighted"].astype(jnp.float32))
    x_grad = x_grad + stash["weights"][:, :, None] * weighted_grad
    weights_grad = jnp.sum(weighted_grad * x_wide, axis=2)
    step_grad, bias_grad, log_grad = stash["factor_back"](
        (decay_grad, inflow_grad, weights_grad, span_decay_grad)
    )
    conv_grad = jnp.concatenate([x_grad.reshape(span_len, local_width), b_grad, c_grad], axis=1)
    ext_grad, conv_weight_part, conv_bias_part = stash["conv_back"](conv_grad)
    returned = shifted_2(ext_grad[: CONV - 1], "span", -1)
    own_grad = ext_grad[CONV - 1 :]
    own_grad = jnp.concatenate(
        [own_grad[: span_len - (CONV - 1)], own_grad[span_len - (CONV - 1) :] + returned], axis=0
    )
    x_back = own_grad[:, :local_width].astype(jnp.bfloat16).reshape(span_len, 1, local_width)
    step_back = step_grad.astype(jnp.bfloat16).reshape(span_len, 1, head_local)
    x_tok, step_tok = (
        lax.all_to_all(x_back, "head", split_axis=0, concat_axis=1, tiled=True),
        lax.all_to_all(step_back, "head", split_axis=0, concat_axis=1, tiled=True),
    )
    bc_tok = summed_on_arrival(own_grad[:, local_width:].astype(jnp.bfloat16), "head", 0)
    group_index = lax.axis_index("head")
    weight_full = jnp.zeros((CONV, DI + 2 * N), jnp.float32)
    weight_full = lax.dynamic_update_slice_in_dim(
        weight_full, conv_weight_part[:, :local_width], group_index * local_width, 1
    )
    weight_full = weight_full.at[:, DI:].set(conv_weight_part[:, local_width:])
    bias_grad_full = jnp.zeros((DI + 2 * N,), jnp.float32)
    bias_grad_full = lax.dynamic_update_slice_in_dim(
        bias_grad_full, conv_bias_part[:local_width], group_index * local_width, 0
    )
    bias_grad_full = bias_grad_full.at[DI:].set(conv_bias_part[local_width:])
    return (x_tok, step_tok, bc_tok, weight_full, bias_grad_full, (bias_grad, log_grad, skip_grad))


def layer_forward(hidden, params, head_params, doc_starts):
    gain_full, in_full, conv_full, bias_full, gate_full, out_full = params
    tok_rows = hidden.shape[0]
    groups = lax.axis_size("head")
    local_width = DI // groups
    head_local = H // groups
    normed, norm_back = jax.vjp(rms_gain, hidden, gain_full.astype(jnp.float32))
    normed_low = normed.astype(jnp.bfloat16)
    project = jnp.dot(normed_low, in_full, preferred_element_type=jnp.float32)
    gate_part = project[:, :DI]
    x_send = project[:, DI : 2 * DI].astype(jnp.bfloat16).reshape(tok_rows, groups, local_width)
    bc_send = project[:, 2 * DI : 2 * DI + 2 * N].astype(jnp.bfloat16)
    step_send = (
        project[:, 2 * DI + 2 * N :].astype(jnp.bfloat16).reshape(tok_rows, groups, head_local)
    )
    copies = jnp.broadcast_to(bc_send[:, None, :], (tok_rows, groups, 2 * N))
    x_heads, step_heads, copies = sent_together((x_send, step_send, copies), "head", 1, 0, 2)
    bc_heads = copies[:, 0, :]
    span_len = tok_rows * groups
    mixed_low, head_stash = head_forward(
        x_heads.reshape(span_len, local_width),
        bc_heads,
        step_heads.reshape(span_len, head_local),
        conv_full,
        bias_full,
        head_params,
        doc_starts,
    )
    mixed_back = lax.all_to_all(
        mixed_low.reshape(span_len, 1, local_width), "head", split_axis=0, concat_axis=1, tiled=True
    )
    gate_normed, gate_back = jax.vjp(
        gated_norm,
        mixed_back.reshape(tok_rows, DI).astype(jnp.float32),
        gate_part,
        gate_full.astype(jnp.float32),
    )
    gate_low = gate_normed.astype(jnp.bfloat16)
    branch = jnp.dot(gate_low, out_full, preferred_element_type=jnp.float32)
    return (hidden + branch, (norm_back, normed_low, gate_back, gate_low, head_stash))


def layer_backward(grad, params, stash):
    gain_full, in_full, conv_full, bias_full, gate_full, out_full = params
    norm_back, normed_low, gate_back, gate_low, head_stash = stash
    tok_rows = grad.shape[0]
    groups = lax.axis_size("head")
    local_width = DI // groups
    branch_low = grad.astype(jnp.bfloat16)
    out_grad = lax.dot_general(
        gate_low, branch_low, (((0,), (0,)), ((), ())), preferred_element_type=jnp.float32
    )
    gate_normed_grad = lax.dot_general(
        branch_low, out_full, (((1,), (1,)), ((), ())), preferred_element_type=jnp.float32
    )
    mixed_grad, gate_part_grad, gate_gain_grad = gate_back(gate_normed_grad)
    grad_send = mixed_grad.astype(jnp.bfloat16).reshape(tok_rows, groups, local_width)
    grad_heads = lax.all_to_all(grad_send, "head", split_axis=1, concat_axis=0, tiled=True)
    x_tok, step_tok, bc_tok, conv_weight_grad, conv_bias_grad, head_grads = head_backward(
        grad_heads.reshape(tok_rows * groups, H // groups, HP), head_stash
    )
    project_grad = jnp.concatenate(
        [
            gate_part_grad.astype(jnp.bfloat16),
            x_tok.reshape(tok_rows, DI),
            bc_tok.astype(jnp.bfloat16),
            step_tok.reshape(tok_rows, H),
        ],
        axis=1,
    )
    in_grad = lax.dot_general(
        normed_low, project_grad, (((0,), (0,)), ((), ())), preferred_element_type=jnp.float32
    )
    normed_grad = lax.dot_general(
        project_grad, in_full, (((1,), (1,)), ((), ())), preferred_element_type=jnp.float32
    )
    hidden_grad, norm_gain_grad = norm_back(normed_grad)
    partials = (norm_gain_grad, in_grad, conv_weight_grad, conv_bias_grad, gate_gain_grad, out_grad)
    return (grad + hidden_grad, partials, head_grads)


def gather_params(weight_args, layer_index):
    return gather_together(
        (
            weight_args[0][layer_index],
            weight_args[1][layer_index],
            weight_args[2][layer_index],
            weight_args[3][layer_index],
            weight_args[4][layer_index],
            weight_args[5][layer_index],
        ),
        ("span", "head"),
        (0, 0, 1, 0, 0, 0),
    )


def per_device(
    tokens,
    doc_starts,
    norm_gain,
    in_weight,
    conv_weight,
    conv_bias,
    step_bias,
    decay_log,
    skip_gain,
    gate_gain,
    out_weight,
    cotangent,
):
    weight_args = (norm_gain, in_weight, conv_weight, conv_bias, gate_gain, out_weight)
    hidden = tokens.astype(jnp.float32)
    layer_inputs = []
    layer_saved = []
    for layer_index in range(LAYERS):
        params = gather_params(weight_args, layer_index)
        head_params = (step_bias[layer_index], decay_log[layer_index], skip_gain[layer_index])
        layer_inputs.append(hidden)
        hidden, stash = layer_forward(hidden, params, head_params, doc_starts)
        layer_saved.append((params, stash))
    output = hidden.astype(jnp.bfloat16)
    grad = cotangent.astype(jnp.float32)
    shares_list = [None] * LAYERS
    heads_list = [None] * LAYERS
    for layer_index in reversed(range(LAYERS)):
        head_params = (step_bias[layer_index], decay_log[layer_index], skip_gain[layer_index])
        params, stash = layer_saved[layer_index]
        grad, partials, head_grads = layer_backward(grad, params, stash)
        shares_list[layer_index] = partials
        heads_list[layer_index] = head_grads
    stacked = tuple((jnp.stack([member[slot] for member in shares_list]) for slot in range(6)))
    stacked = (
        lax.psum_scatter(stacked[0], ("span", "head"), scatter_dimension=1, tiled=True),
        lax.psum_scatter(stacked[1], ("span", "head"), scatter_dimension=1, tiled=True),
        lax.psum_scatter(stacked[2], ("span", "head"), scatter_dimension=2, tiled=True),
        lax.psum_scatter(stacked[3], ("span", "head"), scatter_dimension=1, tiled=True),
        lax.psum_scatter(stacked[4], ("span", "head"), scatter_dimension=1, tiled=True),
        lax.psum_scatter(stacked[5], ("span", "head"), scatter_dimension=1, tiled=True),
    )
    bias_stack = jnp.stack([member[0] for member in heads_list])
    log_stack = jnp.stack([member[1] for member in heads_list])
    skip_stack = jnp.stack([member[2] for member in heads_list])
    bias_total, log_total, skip_total = (
        taken_together(bias_stack, "span"),
        taken_together(log_stack, "span"),
        taken_together(skip_stack, "span"),
    )
    return (
        output,
        grad,
        stacked[0],
        stacked[1],
        stacked[2],
        stacked[3],
        bias_total,
        log_total,
        skip_total,
        stacked[4],
        stacked[5],
    )


def solution(mesh):
    return jax.shard_map(
        per_device,
        mesh=mesh,
        in_specs=(
            P(("span", "head"), None),
            P(),
            P(None, ("span", "head")),
            P(None, ("span", "head"), None),
            P(None, None, ("span", "head")),
            P(None, ("span", "head")),
            P(None, "head"),
            P(None, "head"),
            P(None, "head"),
            P(None, ("span", "head")),
            P(None, ("span", "head"), None),
            P(("span", "head"), None),
        ),
        out_specs=(
            P(("span", "head"), None),
            P(("span", "head"), None),
            P(None, ("span", "head")),
            P(None, ("span", "head"), None),
            P(None, None, ("span", "head")),
            P(None, ("span", "head")),
            P(None, "head"),
            P(None, "head"),
            P(None, "head"),
            P(None, ("span", "head")),
            P(None, ("span", "head"), None),
        ),
        check_vma=False,
    )
```

profile of v0, /device:TPU:1, one launch (start us, length us, event | category | flops | bytes accessed | tf_op | source)
XLA Modules:
  0.0 2776.5 jit_solution(7735604282996892046)
XLA Ops:
  16.6 9.7 broadcast.421.clone
  33.2 9.7 broadcast.421.clone.1
  51.3 383.3 %all-reduce.37.cloned.1.call-done = (bf16[14643968]{0:T(1024)(128)(2,1)}, bf16[14643968]{0:T(1024)(128)(2,1)}) async-done(((bf16[14643968]{0:T(1024)(128)(2,1)}, bf16[14643968]{0:T(1024)(128)(2,1)}), (bf16[14643968]{0:T(1024)(128)(2,1)}, bf16[14643968]{0:T(1024)(128)(2,1)})) %all-reduce.37.cloned.1.call-update) | async-done | bytes 58575888
  434.6 70.3 %reshape.899 = bf16[128,114406]{1,0:T(8,128)(2,1)} reshape(bf16[14643968]{0:T(1024)(128)(2,1)} %get-tuple-element.133) | data formatting | bytes 58575872 | tf_op jit(solution)/shard_map/all_gather | solution.py:74
  506.6 18.4 slice.503
  525.1 29.8 %reshape_reshape.12 = bf16[1536,6448]{1,0:T(8,128)(2,1)} reshape(bf16[128,77376]{1,0:T(8,128)(2,1)} %slice.503) | data formatting | bytes 39616512 | tf_op jit(solution)/shard_map/reshape;reshape | solution.py:69
  554.9 13.8 fusion.249
  574.0 70.1 %reshape.900 = bf16[128,114406]{1,0:T(8,128)(2,1)} reshape(bf16[14643968]{0:T(1024)(128)(2,1)} %get-tuple-element.134) | data formatting | bytes 58575872 | tf_op jit(solution)/shard_map/all_gather | solution.py:74
  677.0 9.6 collective-permute-done.2
  715.9 10.2 slice.521
  726.1 18.5 slice.528
  775.3 14.1 reshape_reshape.13
  790.9 29.7 %reshape_reshape.14 = bf16[1536,6448]{1,0:T(8,128)(2,1)} reshape(bf16[128,77376]{1,0:T(8,128)(2,1)} %slice.528) | data formatting | bytes 39616512 | tf_op jit(solution)/shard_map/reshape;reshape | solution.py:69
  830.6 14.0 fusion.251
  957.1 10.3 slice.546
  970.4 14.1 reshape_reshape.15
  1006.3 9.7 all_to_all.169
  1039.4 11.2 collective-permute-done.25
  1191.0 11.1 multiply_reduce_fusion.20
  1213.9 12.9 all_to_all.170
  1243.7 11.3 collective-permute-done.32
  1255.8 23.2 convolution_bitcast_fusion
  1376.2 16.5 convolution_bitcast_fusion.1
  1392.6 51.5 %pad_maximum_fusion = f32[2,1536,6448]{1,2,0:T(8,128)} fusion(f32[1,1536,6448]{1,2,0:T(8,128)} %convolution_bitcast_fusion, f32[1,1536,6448]{1,2,0:T(8,128)} %convolution_bitcast_fusion.1), kind=kLoop, calls=%fused_computation | loop fusion | flops 19808256 | bytes 158466048 | tf_op jit(solution)/shard_map/stack | solution.py:440
  1444.2 114.0 %copy.584 = f32[2,1536,6448]{2,0,1:T(2,128)} copy(f32[2,1536,6448]{1,2,0:T(8,128)} %pad_maximum_fusion) | data formatting | bytes 158466048 | tf_op jit(solution)/shard_map/stack | solution.py:440
  1572.0 21.5 pad_maximum_fusion.1
  1615.1 10.2 all-to-all-start.14
  1641.2 9.6 all-to-all-done.13
  1668.0 11.3 fusion.52
  1679.3 64.8 %all-reduce.27 = (f32[2,1536]{1,0:T(2,128)S(1)}, f32[2,3328]{1,0:T(2,128)S(1)}, f32[2,3072]{1,0:T(2,128)S(1)}) all-reduce(f32[2,1536]{1,0:T(2,128)S(1)} %pad_maximum_fusion.17, f32[2,3328]{1,0:T(2,128)} %pad_maximum_fusion.15, f32[2,3072]{1,0:T(2,128)} %pad_maximum_fusion.16), channel_id=4, replica_groups=mesh['span'=64,'head'=2] {'span','head'}, use_global_device_ids=true, to_apply=%region_37.39.clone | all-reduce | flops 15872 | bytes 126976
  1748.5 322.2 %all-reduce.33.cloned.1.call-done = f32[2,1536,6448]{2,0,1:T(2,128)} async-done(((f32[2,1536,6448]{2,0,1:T(2,128)}), f32[2,1536,6448]{2,0,1:T(2,128)}) %all-reduce.33.cloned.1.call-update) | async-done | bytes 79233040
  2072.7 697.1 %reduce-scatter.6.cloned.1.call-done = f32[2,24,1536]{2,1,0:T(8,128)} async-done(((f32[2,3072,1536]{2,1,0:T(8,128)}), f32[2,24,1536]{2,1,0:T(8,128)}) %reduce-scatter.6.cloned.1.call-update) | async-done | bytes 294928 | tf_op jit(solution)/shard_map/reduce_scatter | solution.py:447
  (984 shorter events, 633.6 us)
Async XLA Ops:
  7.2 427.4 %all-reduce.37.cloned.1.call-start = ((), (), s32[]{:S(2)}) async-start(), calls=%async_computation.19 | async-start | bytes 117153792
  570.2 77.1 %all-to-all-start = ((bf16[128,2,1816]{0,2,1:T(8,128)(2,1)}), bf16[128,2,1816]{0,2,1:T(8,128)(2,1)S(1)}, u32[]{:S(2)}, u32[]{:S(2)}) async-start(bf16[128,2,1816]{0,2,1:T(8,128)(2,1)} %pad_maximum_fusion.6), calls=%async_computation | async-start | bytes 1859584 | tf_op jit(solution)/shard_map/all_to_all | solution.py:59
  649.5 12.0 collective-permute-start
  673.0 13.6 collective-permute-start.7
  689.6 10.3 collective-permute-start.8
  702.6 10.6 collective-permute-start.9
  714.3 32.9 %collective-permute-start.10 = (bf16[24,64,128]{2,1,0:T(8,128)(2,1)}, bf16[24,64,128]{2,1,0:T(8,128)(2,1)}, u32[]{:S(2)}, u32[]{:S(2)}) collective-permute-start(bf16[24,64,128]{2,1,0:T(8,128)(2,1)} %fusion.209), channel_id=1, source_target_pairs={{0,32},{2,34},{4,36},{6,38},{8,40},{10,42},{12,44},{14,46},{16,48}... | collective-permute-start | bytes 1179656 | tf_op jit(solution)/shard_map/ppermute | solution.py:30
  770.4 50.2 %all-to-all-start.1 = ((bf16[2,2,98304]{2,1,0:T(2,128)(2,1)}), bf16[2,2,98304]{2,1,0:T(2,128)(2,1)S(1)}, u32[]{:S(2)}, u32[]{:S(2)}) async-start(bf16[2,2,98304]{2,1,0:T(2,128)(2,1)} %reshape.941), calls=%async_computation.1 | async-start | bytes 1572864 | tf_op jit(solution)/shard_map/all_to_all | solution.py:338
  845.8 11.4 all-to-all-start.2
  860.2 14.6 collective-permute-start.12
  883.1 13.0 collective-permute-start.19
  896.5 10.8 collective-permute-start.20
  908.1 10.2 collective-permute-start.21
  927.3 10.8 collective-permute-start.23
  952.6 32.0 %all-to-all-start.3 = ((bf16[2,2,98304]{2,1,0:T(2,128)(2,1)}), bf16[2,2,98304]{2,1,0:T(2,128)(2,1)}, u32[]{:S(2)}, u32[]{:S(2)}) async-start(bf16[2,2,98304]{2,1,0:T(2,128)(2,1)} %reshape.943), calls=%async_computation.3 | async-start | bytes 1572864 | tf_op jit(solution)/shard_map/all_to_all | solution.py:338
  1038.6 11.9 collective-permute-start.25
  1064.7 10.1 collective-permute-start.27
  1125.2 21.6 collective-permute-start.30
  1142.9 11.3 all-to-all-start.7
  1154.2 13.8 all-to-all-start.6
  1168.0 15.7 all-to-all-start.5
  1242.6 12.4 collective-permute-start.32
  1255.5 23.6 collective-permute-start.33
  1279.7 10.7 collective-permute-start.34
  1334.7 14.1 collective-permute-start.37
  1360.2 14.0 all-to-all-start.9
  1363.7 302.9 %all-reduce.35.cloned.1.call-start = ((), (), s32[]{:S(2)}) async-start(), calls=%async_computation.18 | async-start | bytes 212992
  1364.5 706.3 %all-reduce.33.cloned.1.call-start = ((), (), s32[]{:S(2)}) async-start(), calls=%async_computation.17 | async-start | bytes 160432128
  1558.3 1211.5 %reduce-scatter.6.cloned.1.call-start = ((), (), s32[]{:S(2)}) async-start(), calls=%async_computation.16 | async-start | bytes 38043648 | tf_op jit(solution)/shard_map/reduce_scatter | solution.py:447
  1615.1 19.7 all-to-all-start.14
  1636.2 14.6 all-to-all-start.13
  1651.5 14.5 all-to-all-start.12
  (288 other events, 8570.5 us)
Sparse Core Ops, SparseCore 0:
  48.0 386.6 all-reduce.36
  1369.9 138.2 all-reduce.34
  1558.3 512.3 all-reduce.32
  2073.6 696.1 reduce-scatter.5
where the time goes:
time: 2790 us; the launch traced here: 2780 us
  waiting for transfers between devices  1590 us (57%)
  local copies, waits for them, and re-layouts  574 us (21%)
  other arithmetic  201 us (7%)
  matrix products  167 us (6%)
  starting transfers between devices  142 us (5%)
  blocking collectives  87.5 us (3%)
    unnamed x7, waiting for transfers between devices  706 us
    reduce_scatter x1, waiting for transfers between devices, per_device(): lax.psum_scatter(stacked[5], ('span', 'head'), scatter_dimension=1, tiled...  697 us
    all_gather x2, local copies, waits for them, and re-layouts, gather_together(): lines, at, outs = (lax.all_gather(line, axis), 0, [])  140 us
    ppermute x34, waiting for transfers between devices, partner_2(): return lax.ppermute(value, axis, pairs)  129 us
    another operation x5, local copies, waits for them, and re-layouts, per_device(): jnp.stack([member[slot] for member in shares_list])  114 us
    another operation x4, local copies, waits for them, and re-layouts, in_order(): blocks.reshape(*dims[:dim], dims[dim] * dims[dim + 1], *dims[dim + 2:])  87.8 us
    unnamed x557, local copies, waits for them, and re-layouts  77.4 us
    another operation x6, other arithmetic, per_device(): jnp.stack([member[slot] for member in shares_list])  75 us
  transfers between devices with their start and end apart: 55, of which 35 were waited for; matrix products, arithmetic and copies ran while one was open for 19% of the time, Pallas kernels for 0%

commit v1 on v0

v1 whole, which is shorter than its diff:
```python
import functools

import jax
import jax.numpy as jnp
from jax import lax
from jax.experimental import pallas as pl
from jax.experimental.pallas import tpu as pltpu
from jax.sharding import Mesh, PartitionSpec as P

D = 1536
DI = 3072
H = 48
HP = 64
N = 128
CONV = 4
LAYERS = 2
CH = DI + 2 * N
EPS = 1e-05

AX = ("z", "x", "yh", "c", "yl")
ZX = ("z", "x")
LINE = ("yh", "c", "yl")
Y = ("yh", "yl")
NQ = 16
NG = 8
TOK = 128
GT = TOK * NG
SPAN = 256
NS = GT // SPAN
HL = H // NG
W = HL * HP
CA = W + 2 * N + 128

bf = jnp.bfloat16
f32 = jnp.float32
HI = lax.Precision.HIGHEST


def mm(a, b, ca=1, cb=0):
    return lax.dot_general(a, b, (((ca,), (cb,)), ((), ())), preferred_element_type=f32)


def mm_hi(a, b):
    return jnp.dot(a, b, precision=HI, preferred_element_type=f32)


def a2a(a, axes):
    return lax.all_to_all(a, axes, 0, 0, tiled=True)


def core_swap(a):
    return lax.ppermute(a, "c", [(0, 1), (1, 0)])


def line_gather(own):
    n = own.shape[1]
    line = a2a(jnp.broadcast_to(own[None], (4,) + own.shape), Y)
    both = lax.all_gather(line, "c", axis=0)
    both = both.reshape(2, 2, 2, TOK, n)
    return both.transpose(1, 0, 2, 3, 4).reshape(GT, n)


def line_reduce(part):
    n = part.shape[1]
    core = lax.axis_index("c")
    blocks = part.reshape(2, 2, 2, TOK, n)
    mine = lax.dynamic_index_in_dim(blocks, core, 1, keepdims=False)
    other = lax.dynamic_index_in_dim(blocks, 1 - core, 1, keepdims=False)
    got = core_swap(other.astype(bf))
    chip = (mine + got.astype(f32)).astype(bf).reshape(4, TOK, n)
    return jnp.sum(a2a(chip, Y).astype(f32), axis=0)


def small_reduce(parts):
    m = parts.shape[0]
    sent = parts.reshape(m, NG, TOK).transpose(1, 0, 2)
    return jnp.sum(a2a(sent, LINE), axis=0)


def small_gather(own):
    m = own.shape[0]
    got = a2a(jnp.broadcast_to(own[None], (NG,) + own.shape), LINE)
    return got.transpose(1, 0, 2).reshape(m, GT)


def group_gather(block):
    return lax.all_gather(block, ZX, axis=0, tiled=True)


def group_gather_now(block):
    r, n = block.shape
    return a2a(jnp.broadcast_to(block[None], (NQ, r, n)), ZX).reshape(NQ * r, n)


def group_reduce(full):
    r = full.shape[0] // NQ
    return jnp.sum(a2a(full.reshape(NQ, r, full.shape[1]), ZX).astype(f32), axis=0)


def heads_out(cols, width):
    r = cols.shape[0]
    return cols.reshape(r, 2, 2, 2, width).transpose(2, 3, 1, 0, 4).reshape(NG, r, width)


def heads_in(blocks):
    _, r, width = blocks.shape
    return blocks.reshape(2, 2, 2, r, width).transpose(3, 2, 0, 1, 4).reshape(r, NG * width)


def line_of(group):
    yl, yh, c = group // 4, (group // 2) % 2, group % 2
    return yh * 4 + c * 2 + yl


TO_HEADS = [(s, (s % NQ) * NG + line_of(s // NQ)) for s in range(NQ * NG)]
TO_OWNER = [(b, a) for a, b in TO_HEADS]


def in_blocks(weight, gain, extra):
    folded = (weight.astype(f32) * gain.astype(f32)[:, None]).astype(bf)
    z = heads_out(folded[:, :DI], W)
    x = heads_out(folded[:, DI : 2 * DI], W)
    bc = jnp.broadcast_to(folded[None, :, 2 * DI : 2 * DI + 2 * N], (NG, 12, 2 * N))
    step = heads_out(folded[:, 2 * DI + 2 * N :], HL)
    extra = jnp.broadcast_to(extra[None], (NG,) + extra.shape)
    step = jnp.concatenate([step, extra], axis=2)
    step = jnp.pad(step, ((0, 0), (0, 0), (0, 128 - step.shape[2])))
    return jnp.concatenate([x, bc, step, z], axis=2)


SCAN_ROWS = HL * HP // NQ


def scan_kernel(reverse, q_ref, got_ref, out_ref):
    row = q_ref[0] * SCAN_ROWS + lax.broadcasted_iota(jnp.int32, (SCAN_ROWS, N), 0)
    lane = lax.broadcasted_iota(jnp.int32, (SCAN_ROWS, N), 1)
    head = jnp.zeros((SCAN_ROWS, N), jnp.int32)
    for k in range(1, HL):
        head = head + (row >= k * HP).astype(jnp.int32)
    chosen = (lane == head) | (lane == head + HL) | (lane == head + 2 * HL)
    carry = jnp.zeros((SCAN_ROWS, N), f32)
    pad = jnp.zeros((32 - SCAN_ROWS, N), f32)
    for j in range(NQ - 1, -1, -1) if reverse else range(NQ):
        out_ref[j] = jnp.concatenate([carry, pad], axis=0).astype(bf)
        block = got_ref[j].astype(f32)
        decay = jnp.sum(
            jnp.where(chosen, block[SCAN_ROWS : SCAN_ROWS + 1], 0.0), axis=1, keepdims=True
        )
        carry = decay * carry + block[:SCAN_ROWS]


def exclusive_scan(total_decay, total_state, reverse):
    q = lax.axis_index(ZX)
    rows = SCAN_ROWS
    hi = total_decay.astype(bf)
    rest = total_decay - hi.astype(f32)
    mid = rest.astype(bf)
    low = (rest - mid.astype(f32)).astype(bf)
    tail = jnp.pad(jnp.concatenate([hi, mid, low])[None], ((0, 7), (0, N - 3 * HL)))
    sent = jnp.concatenate(
        [total_state.astype(bf).reshape(NQ, rows, N), jnp.broadcast_to(tail[None], (NQ, 8, N))],
        axis=1,
    )
    got = a2a(sent, ZX)
    outs = pl.pallas_call(
        functools.partial(scan_kernel, reverse),
        out_shape=jax.ShapeDtypeStruct((NQ, 32, N), bf),
        in_specs=[
            pl.BlockSpec(memory_space=pltpu.SMEM),
            pl.BlockSpec(memory_space=pltpu.VMEM),
        ],
        out_specs=pl.BlockSpec(memory_space=pltpu.VMEM),
        name="group_scan",
    )(q.reshape(1).astype(jnp.int32), got)
    back = a2a(outs, ZX)[:, :rows]
    return back.reshape(HL * HP, N).astype(f32)


def silu_parts(v):
    s = jax.nn.sigmoid(v)
    return v * s, s * (1.0 + v * (1.0 - s))


def per_device(
    tokens,
    doc_starts,
    norm_gain,
    in_weight,
    conv_weight,
    conv_bias,
    step_bias,
    decay_log,
    skip_gain,
    gate_gain,
    out_weight,
    cotangent,
):
    q = lax.axis_index(ZX)
    yh, core, yl = lax.axis_index("yh"), lax.axis_index("c"), lax.axis_index("yl")
    sub = yh * 2 + core
    group = yl * 4 + sub

    a_blocks, z_blocks = [], []
    own_ch = CH // (NQ * NG)
    conv_own = jnp.concatenate([conv_weight, conv_bias[:, None]], axis=1).reshape(-1, own_ch)
    conv_own = jnp.pad(conv_own, ((0, 12 - conv_own.shape[0]), (0, 0)))
    sent = [in_blocks(in_weight[l], norm_gain[l], conv_own if l == 0 else conv_own[:, :0]) for l in range(LAYERS)]
    got = a2a(jnp.stack(sent, axis=1), LINE)
    for l in range(LAYERS):
        block = got[:, l].reshape(NG * 12, CA + W)
        a_blocks.append(block[:, :CA])
        z_blocks.append(block[:, CA:])
    folded_out = (out_weight.astype(f32) * gate_gain.astype(f32)[:, :, None]).astype(bf)
    out_blocks = lax.ppermute(folded_out, AX, TO_HEADS)
    w_a, w_z, w_o = [None] * 2, [None] * 2, [None] * 2
    w_a[0] = group_gather_now(a_blocks[0])
    conv_all = w_a[0][:, W + 2 * N + HL : W + 2 * N + HL + own_ch].reshape(NQ * NG, 12, own_ch)
    conv_all = conv_all[:, : LAYERS * (CONV + 1)].transpose(1, 0, 2)
    conv_all = conv_all.reshape(LAYERS, CONV + 1, CH).astype(f32)
    conv_x = lax.dynamic_slice_in_dim(conv_all, group * W, W, 2)
    conv_here = jnp.concatenate([conv_x, conv_all[:, :, DI:]], axis=2)
    w_z[0] = group_gather(z_blocks[0])
    w_o[0] = group_gather(out_blocks[0])
    w_a[1] = group_gather(a_blocks[1])
    w_z[1] = group_gather(z_blocks[1])
    w_o[1] = group_gather(out_blocks[1])

    pos = q * GT + jnp.arange(-(CONV - 1), GT + CONV - 1, dtype=jnp.int32)
    seg_ext = jnp.sum((doc_starts[None, :] <= pos[:, None]).astype(jnp.int32), axis=1) - 1
    seg = seg_ext[CONV - 1 : CONV - 1 + GT]
    seg_spans = seg.reshape(NS, SPAN)
    seg_before = seg_ext[CONV - 2 : CONV - 2 + GT : SPAN]
    same_back = [
        (seg_ext[CONV - 1 - k : CONV - 1 - k + GT] == seg).astype(f32)[:, None] for k in range(CONV)
    ]
    same_fwd = [
        (seg_ext[CONV - 1 + k : CONV - 1 + k + GT] == seg).astype(f32)[:, None] for k in range(CONV)
    ]
    order = jnp.arange(SPAN)
    tri = (order[None, :] <= order[:, None]).astype(f32)
    mask = (order[None, :] <= order[:, None])[None] & (
        seg_spans[:, None, :] == seg_spans[:, :, None]
    )
    in_mask = (seg_spans == seg_before[:, None]).astype(f32)[:, :, None]
    end_mask = (seg_spans == seg_spans[:, -1:]).astype(f32)[:, :, None]
    span_mask = in_mask[:, -1]
    head_of = (jnp.arange(W)[:, None] // HP == jnp.arange(HL)[None]).astype(f32)

    def expand(a):
        return mm_hi(a.reshape(-1, HL), head_of.T)

    def by_head(a):
        return mm_hi(a, head_of).reshape(NS, SPAN, HL)

    def heads(a):
        return a.reshape(NS, SPAN, HL, HP)

    def pick_heads(a):
        return lax.dynamic_slice_in_dim(a, sub * HL, HL, 0)

    h = tokens.astype(f32)
    saved = []
    grad_full = line_gather(cotangent)

    for l in range(LAYERS):
        bias_h, log_h, skip_h = (pick_heads(p[l]) for p in (step_bias, decay_log, skip_gain))
        r_in = lax.rsqrt(jnp.mean(h * h, axis=-1, keepdims=True) + EPS)
        normed = line_gather((h * r_in).astype(bf))
        proj = mm(normed, w_a[l])
        u = proj[:, : W + 2 * N].astype(bf)
        step_in = proj[:, W + 2 * N : W + 2 * N + HL].astype(bf).astype(f32)
        step_in = step_in.reshape(NS, SPAN, HL) + bias_h
        edge = lax.ppermute(u[GT - (CONV - 1) :], ZX, [(i, i + 1) for i in range(NQ - 1)])
        z = mm(normed, w_z[l])
        ext = jnp.concatenate([edge, u], axis=0).astype(f32)
        cw = conv_here[l]
        pre = jnp.broadcast_to(cw[CONV][None], (GT, W + 2 * N))
        for k in range(CONV):
            pre = pre + cw[k][None] * ext[CONV - 1 - k : CONV - 1 - k + GT] * same_back[k]
        v = pre * jax.nn.sigmoid(pre)
        xc = v[:, :W]
        b_low = v[:, W : W + N].astype(bf).reshape(NS, SPAN, N)
        c_low = v[:, W + N :].astype(bf).reshape(NS, SPAN, N)
        step = jax.nn.softplus(step_in)
        rate = -jnp.exp(log_h)
        run = jnp.einsum("ts,ksh->kth", tri, rate * step, precision=HI)
        run_t = run.transpose(0, 2, 1)
        spread = run_t[:, :, :, None] - run_t[:, :, None, :]
        decay = jnp.where(mask[:, None], jnp.exp(jnp.where(mask[:, None], spread, 0.0)), 0.0)
        inflow = jnp.exp(run) * in_mask
        w_end = jnp.exp(run[:, -1:] - run) * end_mask
        span_decay = jnp.exp(run[:, -1]) * span_mask
        gram = jnp.einsum("ktn,ksn->kts", c_low, b_low, preferred_element_type=f32)
        mixing = (gram[:, None] * decay).astype(bf)
        step_x = expand(step)
        xs = (step_x * xc).astype(bf)
        weights_x = expand(w_end * step)
        weighted = (weights_x * xc).astype(bf)
        own = jnp.einsum("kshp,ksn->khpn", heads(weighted), b_low, preferred_element_type=f32)
        total = own[0]
        total_decay = span_decay[0]
        for k in range(1, NS):
            total = span_decay[k][:, None, None] * total + own[k]
            total_decay = total_decay * span_decay[k]
        carried = exclusive_scan(total_decay, total.reshape(HL * HP, N), False)
        within = jnp.einsum("khts,kshp->kthp", mixing, heads(xs), preferred_element_type=f32)
        carry = carried.reshape(HL, HP, N)
        carries = []
        for k in range(NS):
            carries.append(carry)
            carry = span_decay[k][:, None, None] * carry + own[k]
        carried_in = jnp.stack(carries)
        carried_low = carried_in.astype(bf)
        reading = jnp.einsum("khpn,ktn->kthp", carried_low, c_low, preferred_element_type=f32)
        inflow_x = expand(inflow)
        y0 = within.reshape(GT, W) + inflow_x * reading.reshape(GT, W)
        skip_x = jnp.repeat(skip_h, HP)[None]
        mixed = (y0 + skip_x * xc).astype(bf).astype(f32)
        silu_z, dsilu_z = silu_parts(z)
        gated = mixed * silu_z
        gated_low = gated.astype(bf)
        square = jnp.sum(gated * gated, axis=1)
        part = mm(gated_low, w_o[l])
        if l == LAYERS - 1:
            d_q = mm(grad_full, w_o[l], 1, 1)
            sums = small_reduce(jnp.stack([square, jnp.sum(d_q * gated, axis=1)]))
            r_gate = lax.rsqrt(sums[0] / DI + EPS)
            kappa = r_gate * r_gate * r_gate * sums[1] / DI
            gate_scales = small_gather(jnp.stack([r_gate, kappa]))
        else:
            d_q = None
            gate_scales = None
            r_gate = lax.rsqrt(small_reduce(square[None])[0] / DI + EPS)
        branch = line_reduce(part) * r_gate[:, None]
        saved.append(
            dict(
                h=h, r_in=r_in, normed=normed, ext=ext, pre=pre, v=v, b_low=b_low, c_low=c_low,
                step_in=step_in, step=step, rate=rate, decay=decay, inflow_x=inflow_x, w_end=w_end,
                span_decay=span_decay, gram=gram, mixing=mixing, step_x=step_x, xs=xs,
                weights_x=weights_x, weighted=weighted, carried_in=carried_in,
                carried_low=carried_low, y0=y0, skip_x=skip_x, mixed=mixed, silu_z=silu_z,
                dsilu_z=dsilu_z, gated=gated, r_gate=r_gate, branch=branch, d_q=d_q,
                gate_scales=gate_scales,
            )
        )
        h = h + branch
    output = h.astype(bf)

    grad = cotangent.astype(f32)
    in_grads, gain_grads, out_grads, gate_grads = ([None] * LAYERS for _ in range(4))
    conv_grads, head_grads = [None] * LAYERS, [None] * LAYERS
    for l in reversed(range(LAYERS)):
        s = saved[l]
        if l == LAYERS - 1:
            d_q, gate_scales = s["d_q"], s["gate_scales"]
        else:
            grad_low = grad.astype(bf)
            dot = jnp.sum(grad_low.astype(f32) * s["branch"], axis=1)
            kappa = s["r_gate"] * s["r_gate"] * dot / DI
            gate_scales = small_gather(jnp.stack([s["r_gate"], kappa]))
            grad_full = line_gather(grad_low)
            d_q = mm(grad_full, w_o[l], 1, 1)
        r_full, k_full = gate_scales[0][:, None], gate_scales[1][:, None]
        gated = s["gated"]
        out_part = mm((gated * r_full).astype(bf), grad_full, 0, 0)
        out_sum = group_reduce(out_part.astype(bf))
        d_gated = r_full * d_q - gated * k_full
        dy = (d_gated * s["silu_z"]).astype(bf)
        dz = (d_gated * s["mixed"] * s["dsilu_z"]).astype(bf)
        z_part = mm(s["normed"], dz, 0, 0)
        z_sum = group_reduce(z_part.astype(bf))
        dyf = dy.astype(f32)
        xc = s["v"][:, :W]
        b_low, c_low = s["b_low"], s["c_low"]
        dyh = heads(dy)
        scaled = (s["inflow_x"] * dyf).astype(bf)
        dcarr = jnp.einsum("kthp,ktn->khpn", heads(scaled), c_low, preferred_element_type=f32)
        sd = s["span_decay"]
        total = dcarr[NS - 1]
        total_decay = sd[NS - 1]
        for k in range(NS - 2, -1, -1):
            total = dcarr[k] + sd[k][:, None, None] * total
            total_decay = total_decay * sd[k]
        later = exclusive_scan(total_decay, total.reshape(HL * HP, N), True)
        d_mix = jnp.einsum("kthp,kshp->khts", dyh, heads(s["xs"]), preferred_element_type=f32)
        d_gram = jnp.sum(d_mix * s["decay"], axis=1).astype(bf)
        d_xs = jnp.einsum(
            "khts,kthp->kshp", s["mixing"], dyh, preferred_element_type=f32
        ).reshape(GT, W)
        d_c = jnp.einsum("kts,ksn->ktn", d_gram, b_low, preferred_element_type=f32)
        d_c = d_c + jnp.einsum(
            "kthp,khpn->ktn", heads(scaled), s["carried_low"], preferred_element_type=f32
        )
        d_b = jnp.einsum("kts,ktn->ksn", d_gram, c_low, preferred_element_type=f32)
        end = later.reshape(HL, HP, N)
        ends = [None] * NS
        for k in range(NS - 1, -1, -1):
            ends[k] = end
            end = dcarr[k] + sd[k][:, None, None] * end
        d_end = jnp.stack(ends)
        d_end_low = d_end.astype(bf)
        d_span = jnp.sum(d_end * s["carried_in"], axis=(2, 3))
        d_weighted = jnp.einsum(
            "khpn,ksn->kshp", d_end_low, b_low, preferred_element_type=f32
        ).reshape(GT, W)
        d_b = d_b + jnp.einsum(
            "khpn,kshp->ksn", d_end_low, heads(s["weighted"]), preferred_element_type=f32
        )
        d_xc = s["skip_x"] * dyf + s["step_x"] * d_xs + s["weights_x"] * d_weighted
        skip_sum = by_head(dyf * xc)
        skip_grad = jnp.sum(skip_sum, axis=(0, 1))
        row_sum = by_head(dyf * s["y0"])
        col_sum = by_head(s["xs"].astype(f32) * d_xs)
        d_step = by_head(xc * d_xs)
        d_w = by_head(d_weighted * xc)
        step, w_end, rate = s["step"], s["w_end"], s["rate"]
        d_step = d_step + d_w * w_end
        d_ww = d_w * w_end * step
        d_run = row_sum - col_sum - d_ww
        d_last = jnp.sum(d_ww, axis=1) + d_span * sd
        d_a = jnp.einsum("ts,kth->ksh", tri, d_run, precision=HI) + d_last[:, None, :]
        d_step = d_step + rate * d_a
        log_grad = rate * jnp.sum(step * d_a, axis=(0, 1))
        d_raw = d_step * jax.nn.sigmoid(s["step_in"])
        bias_grad = jnp.sum(d_raw, axis=(0, 1))
        dv = jnp.concatenate([d_xc, d_b.reshape(GT, N), d_c.reshape(GT, N)], axis=1)
        pre = s["pre"]
        sig = jax.nn.sigmoid(pre)
        d_pre = dv * (sig * (1.0 + pre * (1.0 - sig)))
        edge = lax.ppermute(d_pre[: CONV - 1], ZX, [(i + 1, i) for i in range(NQ - 1)])
        d_ext = jnp.concatenate([d_pre, edge], axis=0)
        cw = conv_here[l]
        du = jnp.zeros_like(d_pre)
        taps = []
        for k in range(CONV):
            du = du + cw[k][None] * d_ext[k : k + GT] * same_fwd[k]
            past = s["ext"][CONV - 1 - k : CONV - 1 - k + GT]
            taps.append(jnp.sum(d_pre * past * same_back[k], axis=0))
        taps.append(jnp.sum(d_pre, axis=0))
        taps = jnp.stack(taps)
        conv_full = jnp.zeros((CONV + 1, CH), f32)
        conv_full = lax.dynamic_update_slice_in_dim(conv_full, taps[:, :W], group * W, 1)
        conv_grads[l] = conv_full.at[:, DI:].set(taps[:, W:])
        head_full = jnp.zeros((3, H), f32)
        head_grads[l] = lax.dynamic_update_slice_in_dim(
            head_full, jnp.stack([bias_grad, log_grad, skip_grad]), group * HL, 1
        )
        da = jnp.concatenate(
            [du.astype(bf), jnp.pad(d_raw.reshape(GT, HL), ((0, 0), (0, 128 - HL))).astype(bf)],
            axis=1,
        )
        d_norm = line_reduce(mm(da, w_a[l], 1, 1) + mm(dz, w_z[l], 1, 1))
        a_part = mm(s["normed"], da, 0, 0)
        a_sum = group_reduce(a_part.astype(bf))
        hidden, r_in = s["h"], s["r_in"]
        inner = jnp.mean(hidden * d_norm, axis=1, keepdims=True)
        grad = grad + r_in * d_norm - hidden * (r_in * r_in * r_in) * inner
        both = jnp.concatenate([a_sum, z_sum], axis=1).reshape(NG, 12, CA + W)
        both = a2a(both, LINE)
        g_in = jnp.concatenate(
            [
                heads_in(both[:, :, CA:]),
                heads_in(both[:, :, :W]),
                jnp.sum(both[:, :, W : W + 2 * N], axis=0),
                heads_in(both[:, :, W + 2 * N : W + 2 * N + HL]),
            ],
            axis=1,
        )
        in_grads[l] = g_in * norm_gain[l].astype(f32)[:, None]
        gain_grads[l] = jnp.sum(g_in * in_weight[l].astype(f32), axis=1)
        g_out = lax.ppermute(out_sum, AX, TO_OWNER)
        out_grads[l] = g_out * gate_gain[l].astype(f32)[:, None]
        gate_grads[l] = jnp.sum(g_out * out_weight[l].astype(f32), axis=1)

    conv_sent = jnp.stack(conv_grads).reshape(LAYERS, CONV + 1, NQ * NG, CH // (NQ * NG))
    conv_sent = conv_sent.transpose(2, 0, 1, 3).reshape(NQ * NG, -1)
    head_sent = jnp.stack(head_grads).reshape(LAYERS, 3, 2, H // 2).transpose(2, 0, 1, 3)
    head_sent = jnp.tile(head_sent.reshape(2, -1), (NQ * NG // 2, 1))
    small = jnp.concatenate([conv_sent, head_sent], axis=1)
    small = jnp.sum(a2a(small, AX), axis=0)
    n_conv = conv_sent.shape[1]
    conv_grad = small[:n_conv].reshape(LAYERS, CONV + 1, -1)
    head_grad = small[n_conv:].reshape(LAYERS, 3, -1)
    return (
        output,
        grad,
        jnp.stack(gain_grads),
        jnp.stack(in_grads),
        conv_grad[:, :CONV],
        conv_grad[:, CONV],
        head_grad[:, 0],
        head_grad[:, 1],
        head_grad[:, 2],
        jnp.stack(gate_grads),
        jnp.stack(out_grads),
    )


def solution(mesh):
    fine = Mesh(mesh.devices.reshape(4, 4, 2, 2, 2), AX)
    tok, last, mid, heads = P(AX, None), P(None, AX), P(None, AX, None), P(None, "yl")
    conv = P(None, None, AX)
    return jax.shard_map(
        per_device,
        mesh=fine,
        in_specs=(tok, P(), last, mid, conv, last, heads, heads, heads, last, mid, tok),
        out_specs=(tok, tok, last, mid, conv, last, heads, heads, heads, last, mid),
        check_vma=False,
    )
```

time: 2790 us -> 1040 us (0.37)
  waiting for transfers between devices: 1590 us -> 297 us
  local copies, waits for them, and re-layouts: 574 us -> 186 us
  other arithmetic: 201 us -> 110 us
  starting transfers between devices: 142 us -> 198 us
  blocking collectives: 87.5 us -> 35 us
    unnamed x7 -> x9, waiting for transfers between devices: 706 us -> 0.74 us
    reduce_scatter x1 -> x0, waiting for transfers between devices: 697 us -> none  [per_device(): lax.psum_scatter(stacked[5], ('span', 'head'), scatter_dimension=1, tiled...]
    another operation x25 -> x27, local copies, waits for them, and re-layouts: 206 us -> 2.18 us  [the longest x4 0.95 us: per_device(): head_sent = jnp.tile(head_sent.reshape(2, -1), (NQ * NG // 2, 1))]
    all_to_all x13 -> x29, waiting for transfers between devices: 43.6 us -> 228 us  [a2a(): return lax.all_to_all(a, axes, 0, 0, tiled=True)]
    all_gather x2 -> x0, local copies, waits for them, and re-layouts: 140 us -> none  [gather_together(): lines, at, outs = (lax.all_gather(line, axis), 0, [])]
    ppermute x38 -> x11, waiting for transfers between devices: 139 us -> 13.2 us  [the longest x2 10.5 us: per_device(): g_out = lax.ppermute(out_sum, AX, TO_OWNER)]
    all_to_all x13 -> x29, starting transfers between devices: 58.1 us -> 168 us  [a2a(): return lax.all_to_all(a, axes, 0, 0, tiled=True)]
    another operation x25 -> x15, other arithmetic: 95.7 us -> 8.76 us  [the longest x6 75 us: per_device(): jnp.stack([member[slot] for member in shares_list])]
  transfers between devices with their start and end apart: 55 -> 49, of which waited for: 35 -> 27; matrix products, arithmetic and copies ran while one was open for 19% -> 42% of each run, Pallas kernels for 0% -> 1%
where the time goes in v1:
time: 1040 us; the launch traced here: 1030 us
  waiting for transfers between devices  297 us (29%)
  starting transfers between devices  198 us (19%)
  local copies, waits for them, and re-layouts  186 us (18%)
  matrix products  178 us (17%)
  other arithmetic  110 us (11%)
  blocking collectives  35 us (3%)
  between operations  18.1 us (2%)
    all_to_all x29, waiting for transfers between devices, a2a(): return lax.all_to_all(a, axes, 0, 0, tiled=True)  228 us
    all_to_all x29, starting transfers between devices, a2a(): return lax.all_to_all(a, axes, 0, 0, tiled=True)  168 us
    dot_general x18, matrix products, mm(): lax.dot_general(a, b, (((ca,), (cb,)), ((), ())), preferred_element_type=...  85.9 us
    all_gather x5, waiting for transfers between devices, group_gather(): return lax.all_gather(block, ZX, axis=0, tiled=True)  46.3 us
    dot_general x16, matrix products, mm_hi(): return jnp.dot(a, b, precision=HI, preferred_element_type=f32)  40.6 us
    unnamed x547, local copies, waits for them, and re-layouts  39.9 us
    all_to_all x2, blocking collectives, a2a(): return lax.all_to_all(a, axes, 0, 0, tiled=True)  35 us
  transfers between devices with their start and end apart: 49, of which 27 were waited for; matrix products, arithmetic and copies ran while one was open for 42% of the time, Pallas kernels for 1%

profile of v1, /device:TPU:1, one launch (start us, length us, event | category | flops | bytes accessed | tf_op | source)
XLA Modules:
  0.0 1028.4 jit_solution(11997166820211810787)
XLA Ops:
  17.6 19.3 %all-to-all-done = bf16[4,128,1536]{2,1,0:T(8,128)(2,1)S(1)} async-done(((bf16[4,128,1536]{2,1,0:T(8,128)(2,1)}), bf16[4,128,1536]{2,1,0:T(8,128)(2,1)S(1)}, u32[]{:S(2)}, u32[]{:S(2)}) %all-to-all-start) | async-done | bytes 1572896 | tf_op jit(solution)/shard_map/all_to_all | solution.py:48
  40.2 12.7 %all_to_all.159 = bf16[8,2,12,1152]{3,1,2,0:T(2,128)(2,1)S(1)} all-to-all(bf16[8,2,12,1152]{3,1,2,0:T(2,128)(2,1)S(1)} %copy.982), channel_id=1, replica_groups=mesh['z'=4,'x'=4,'yh'=2,'c'=2,'yl'=2] {'yh','c','yl'}, dimensions={0} | all-to-all | bytes 884736 | tf_op jit(solution)/shard_map/all_to_all | solution.py:48
  70.7 14.9 %all-to-all-done.11 = bf16[4,128,1536]{2,1,0:T(8,128)(2,1)S(1)} async-done(((bf16[4,128,1536]{2,1,0:T(8,128)(2,1)}), bf16[4,128,1536]{2,1,0:T(8,128)(2,1)S(1)}, u32[]{:S(2)}, u32[]{:S(2)}) %all-to-all-start.11) | async-done | bytes 1572896 | tf_op jit(solution)/shard_map/all_to_all | solution.py:48
  87.5 9.3 all-to-all-start.2
  102.6 29.4 %all-to-all-done.2 = bf16[16,96,768]{2,1,0:T(8,128)(2,1)} async-done(((bf16[16,96,768]{2,1,0:T(8,128)(2,1)}), bf16[16,96,768]{2,1,0:T(8,128)(2,1)}, u32[]{:S(2)}, u32[]{:S(2)}) %all-to-all-start.2) | async-done | bytes 2359328 | tf_op jit(solution)/shard_map/all_to_all | solution.py:48
  186.2 6.8 all-to-all-start.4
  210.7 8.3 multiply_reduce_fusion.11
  228.9 9.7 all-to-all-start.6
  247.8 18.8 %all-to-all-done.5 = bf16[4,128,1536]{2,1,0:T(8,128)(2,1)S(1)} async-done(((bf16[4,128,1536]{2,1,0:T(8,128)(2,1)}), bf16[4,128,1536]{2,1,0:T(8,128)(2,1)S(1)}, u32[]{:S(2)}, u32[]{:S(2)}) %all-to-all-start.5) | async-done | bytes 1572896 | tf_op jit(solution)/shard_map/all_to_all | solution.py:48
  268.4 22.3 %all_to_all.160 = bf16[4,128,1536]{2,1,0:T(8,128)(2,1)} all-to-all(bf16[4,128,1536]{2,1,0:T(8,128)(2,1)S(1)} %broadcast_in_dim.87), channel_id=1, replica_groups=mesh['z'=4,'x'=4,'yh'=2,'c'=2,'yl'=2] {'yh','yl'}, dimensions={0} | all-to-all | bytes 3145728 | tf_op jit(solution)/shard_map/all_to_all | solution.py:48
  301.8 8.9 all-gather.26.cloned.1.call-done
  313.0 46.2 %all-gather.18.cloned.1.call-done = bf16[1536,768]{1,0:T(8,128)(2,1)} async-done(((bf16[96,768]{1,0:T(8,128)(2,1)}), bf16[1536,768]{1,0:T(8,128)(2,1)}) %all-gather.18.cloned.1.call-update) | async-done | bytes 2359312 | tf_op jit(solution)/shard_map/all_gather | solution.py:87
  411.7 6.8 all-to-all-start.9
  435.4 7.8 multiply_reduce_fusion.10
  443.9 7.2 all-to-all-start.12
  504.1 7.1 all-to-all-start.14
  588.8 15.7 %all-to-all-done.10 = bf16[4,128,1536]{2,1,0:T(8,128)(2,1)} async-done(((bf16[4,128,1536]{2,1,0:T(8,128)(2,1)}), bf16[4,128,1536]{2,1,0:T(8,128)(2,1)}, u32[]{:S(2)}, u32[]{:S(2)}) %all-to-all-start.10) | async-done | bytes 1572896 | tf_op jit(solution)/shard_map/all_to_all | solution.py:48
  613.8 13.7 %all-to-all-done.16 = bf16[4,128,1536]{2,1,0:T(8,128)(2,1)} async-done(((bf16[4,128,1536]{2,1,0:T(8,128)(2,1)}), bf16[4,128,1536]{2,1,0:T(8,128)(2,1)}, u32[]{:S(2)}, u32[]{:S(2)}) %all-to-all-start.16) | async-done | bytes 1572896 | tf_op jit(solution)/shard_map/all_to_all | solution.py:48
  638.1 10.3 %all-to-all-done.26 = bf16[16,96,384]{2,1,0:T(8,128)(2,1)} async-done(((bf16[16,96,384]{2,1,0:T(8,128)(2,1)}), bf16[16,96,384]{2,1,0:T(8,128)(2,1)}, u32[]{:S(2)}, u32[]{:S(2)}) %all-to-all-start.26) | async-done | bytes 1179680 | tf_op jit(solution)/shard_map/all_to_all | solution.py:48
  661.5 9.5 all-to-all-done.18
  683.4 22.1 %all-to-all-done.25 = bf16[16,96,768]{2,1,0:T(8,128)(2,1)} async-done(((bf16[16,96,768]{2,1,0:T(8,128)(2,1)}), bf16[16,96,768]{2,1,0:T(8,128)(2,1)}, u32[]{:S(2)}, u32[]{:S(2)}) %all-to-all-start.25) | async-done | bytes 2359328 | tf_op jit(solution)/shard_map/all_to_all | solution.py:48
  705.6 7.6 all-to-all-start.30
  721.5 7.8 all-to-all-done.30
  729.3 7.5 all-to-all-start.27
  748.3 6.6 all-to-all-start.17
  852.4 6.9 multiply_reduce_fusion.2
  873.7 7.6 all-to-all-start.28
  885.3 7.2 all-to-all-done.28
  907.6 9.3 all-to-all-done.29
  929.4 8.6 all-to-all-done.23
  966.6 10.5 %collective-permute-done.9 = f32[24,1536]{1,0:T(8,128)S(1)} collective-permute-done((f32[24,1536]{1,0:T(8,128)S(1)}, f32[24,1536]{1,0:T(8,128)S(1)}, u32[]{:S(2)}, u32[]{:S(2)}) %collective-permute-start.9) | collective-permute-done | bytes 147488 | tf_op jit(solution)/shard_map/ppermute | solution.py:471
  1003.6 16.4 %all-to-all-done.21 = bf16[4,128,1536]{2,1,0:T(8,128)(2,1)S(1)} async-done(((bf16[4,128,1536]{2,1,0:T(8,128)(2,1)}), bf16[4,128,1536]{2,1,0:T(8,128)(2,1)S(1)}, u32[]{:S(2)}, u32[]{:S(2)}) %all-to-all-start.21) | async-done | bytes 1572896 | tf_op jit(solution)/shard_map/all_to_all | solution.py:48
  (1073 shorter events, 607.3 us)
Async XLA Ops:
  11.9 24.9 %all-to-all-start = ((bf16[4,128,1536]{2,1,0:T(8,128)(2,1)}), bf16[4,128,1536]{2,1,0:T(8,128)(2,1)S(1)}, u32[]{:S(2)}, u32[]{:S(2)}) async-start(bf16[4,128,1536]{2,1,0:T(8,128)(2,1)} %broadcast_in_dim.74), calls=%async_computation | async-start | bytes 3145728 | tf_op jit(solution)/shard_map/all_to_all | solution.py:48
  17.1 117.7 %all-gather.22.cloned.1.call-start = ((), (), s32[]{:S(2)}) async-start(), calls=%async_computation.34 | async-start | bytes 4718592 | tf_op jit(solution)/shard_map/all_gather | solution.py:58
  38.0 172.7 %all-gather.16.cloned.1.call-start = ((), (), s32[]{:S(2)}) async-start(), calls=%async_computation.31 | async-start | bytes 1253376 | tf_op jit(solution)/shard_map/all_gather | solution.py:87
  57.6 28.0 %all-to-all-start.11 = ((bf16[4,128,1536]{2,1,0:T(8,128)(2,1)}), bf16[4,128,1536]{2,1,0:T(8,128)(2,1)S(1)}, u32[]{:S(2)}, u32[]{:S(2)}) async-start(bf16[4,128,1536]{2,1,0:T(8,128)(2,1)} %broadcast_in_dim.93), calls=%async_computation.11 | async-start | bytes 3145728 | tf_op jit(solution)/shard_map/all_to_all | solution.py:48
  61.3 157.7 %all-gather.24.cloned.1.call-start = ((), (), s32[]{:S(2)}) async-start(), calls=%async_computation.35 | async-start | bytes 1253376 | tf_op jit(solution)/shard_map/all_gather | solution.py:87
  87.5 44.5 %all-to-all-start.2 = ((bf16[16,96,768]{2,1,0:T(8,128)(2,1)}), bf16[16,96,768]{2,1,0:T(8,128)(2,1)}, u32[]{:S(2)}, u32[]{:S(2)}) async-start(bf16[16,96,768]{2,1,0:T(8,128)(2,1)} %broadcast_in_dim.79), calls=%async_computation.2 | async-start | bytes 4718592 | tf_op jit(solution)/shard_map/all_to_all | solution.py:48
  96.9 197.5 %all-gather.30.cloned.1.call-start = ((), (), s32[]{:S(2)}) async-start(), calls=%async_computation.38 | async-start | bytes 4718592 | tf_op jit(solution)/shard_map/all_gather | solution.py:58
  186.2 15.9 %all-to-all-start.4 = ((bf16[16,32,128]{2,1,0:T(8,128)(2,1)}), bf16[16,32,128]{2,1,0:T(8,128)(2,1)}, u32[]{:S(2)}, u32[]{:S(2)}) async-start(bf16[16,32,128]{2,1,0:T(8,128)(2,1)} %group_scan.4), calls=%async_computation.4 | async-start | bytes 262144 | tf_op jit(solution)/shard_map/all_to_all | solution.py:48
  243.1 23.6 %all-to-all-start.5 = ((bf16[4,128,1536]{2,1,0:T(8,128)(2,1)}), bf16[4,128,1536]{2,1,0:T(8,128)(2,1)S(1)}, u32[]{:S(2)}, u32[]{:S(2)}) async-start(bf16[4,128,1536]{2,1,0:T(8,128)(2,1)} %bitcast.50), calls=%async_computation.5 | async-start | bytes 3145728 | tf_op jit(solution)/shard_map/all_to_all | solution.py:48
  246.6 50.0 %all-gather.28.cloned.1.call-start = ((), (), s32[]{:S(2)}) async-start(), calls=%async_computation.37 | async-start | bytes 1253376 | tf_op jit(solution)/shard_map/all_gather | solution.py:87
  247.2 63.5 %all-gather.26.cloned.1.call-start = ((), (), s32[]{:S(2)}) async-start(), calls=%async_computation.36 | async-start | bytes 4718592 | tf_op jit(solution)/shard_map/all_gather | solution.py:58
  290.8 68.4 %all-gather.18.cloned.1.call-start = ((), (), s32[]{:S(2)}) async-start(), calls=%async_computation.32 | async-start | bytes 2506752 | tf_op jit(solution)/shard_map/all_gather | solution.py:87
  292.5 142.9 %all-gather.20.cloned.1.call-start = ((), (), s32[]{:S(2)}) async-start(), calls=%async_computation.33 | async-start | bytes 1253376 | tf_op jit(solution)/shard_map/all_gather | solution.py:87
  411.7 15.9 %all-to-all-start.9 = ((bf16[16,32,128]{2,1,0:T(8,128)(2,1)}), bf16[16,32,128]{2,1,0:T(8,128)(2,1)}, u32[]{:S(2)}, u32[]{:S(2)}) async-start(bf16[16,32,128]{2,1,0:T(8,128)(2,1)} %group_scan.5), calls=%async_computation.9 | async-start | bytes 262144 | tf_op jit(solution)/shard_map/all_to_all | solution.py:48
  466.0 111.3 %collective-permute-start.4 = (bf16[2,2,128,1536]{3,2,1,0:T(8,128)(2,1)}, bf16[2,2,128,1536]{3,2,1,0:T(8,128)(2,1)}, u32[]{:S(2)}, u32[]{:S(2)}) collective-permute-start(bf16[2,2,128,1536]{3,2,1,0:T(8,128)(2,1)} %fusion.51), channel_id=1, source_target_pairs={{0,2},{2,0},{1,3},{3,1},{4,6},{6,4},{5,7},{7,5},{8,10},{10,8},{9,1... | collective-permute-start | bytes 4718600 | tf_op jit(solution)/shard_map/ppermute | solution.py:52
  580.4 24.0 %all-to-all-start.10 = ((bf16[4,128,1536]{2,1,0:T(8,128)(2,1)}), bf16[4,128,1536]{2,1,0:T(8,128)(2,1)}, u32[]{:S(2)}, u32[]{:S(2)}) async-start(bf16[4,128,1536]{2,1,0:T(8,128)(2,1)} %bitcast.647), calls=%async_computation.10 | async-start | bytes 3145728 | tf_op jit(solution)/shard_map/all_to_all | solution.py:48
  604.4 23.1 %all-to-all-start.16 = ((bf16[4,128,1536]{2,1,0:T(8,128)(2,1)}), bf16[4,128,1536]{2,1,0:T(8,128)(2,1)}, u32[]{:S(2)}, u32[]{:S(2)}) async-start(bf16[4,128,1536]{2,1,0:T(8,128)(2,1)} %bitcast.648), calls=%async_computation.16 | async-start | bytes 3145728 | tf_op jit(solution)/shard_map/all_to_all | solution.py:48
  627.5 20.8 %all-to-all-start.26 = ((bf16[16,96,384]{2,1,0:T(8,128)(2,1)}), bf16[16,96,384]{2,1,0:T(8,128)(2,1)}, u32[]{:S(2)}, u32[]{:S(2)}) async-start(bf16[16,96,384]{2,1,0:T(8,128)(2,1)} %bitcast.694), calls=%async_computation.26 | async-start | bytes 2359296 | tf_op jit(solution)/shard_map/all_to_all | solution.py:48
  650.6 20.3 %all-to-all-start.18 = ((bf16[4,128,1536]{2,1,0:T(8,128)(2,1)}), bf16[4,128,1536]{2,1,0:T(8,128)(2,1)}, u32[]{:S(2)}, u32[]{:S(2)}) async-start(bf16[4,128,1536]{2,1,0:T(8,128)(2,1)} %broadcast_in_dim.98), calls=%async_computation.18 | async-start | bytes 3145728 | tf_op jit(solution)/shard_map/all_to_all | solution.py:48
  671.0 34.6 %all-to-all-start.25 = ((bf16[16,96,768]{2,1,0:T(8,128)(2,1)}), bf16[16,96,768]{2,1,0:T(8,128)(2,1)}, u32[]{:S(2)}, u32[]{:S(2)}) async-start(bf16[16,96,768]{2,1,0:T(8,128)(2,1)} %bitcast.676), calls=%async_computation.25 | async-start | bytes 4718592 | tf_op jit(solution)/shard_map/all_to_all | solution.py:48
  677.5 83.4 %all-gather.32.cloned.1.call-start = ((), (), s32[]{:S(2)}) async-start(), calls=%async_computation.39 | async-start | bytes 4718592 | tf_op jit(solution)/shard_map/all_gather | solution.py:58
  705.6 23.8 %all-to-all-start.30 = ((bf16[16,24,1536]{2,1,0:T(8,128)(2,1)}), bf16[16,24,1536]{2,1,0:T(8,128)(2,1)}, u32[]{:S(2)}, u32[]{:S(2)}) async-start(bf16[16,24,1536]{2,1,0:T(8,128)(2,1)} %bitcast.693), calls=%async_computation.30 | async-start | bytes 2359296 | tf_op jit(solution)/shard_map/all_to_all | solution.py:48
  729.3 17.7 %all-to-all-start.27 = ((f32[8,12,1152]{2,1,0:T(8,128)}), f32[8,12,1152]{2,1,0:T(8,128)S(1)}, u32[]{:S(2)}, u32[]{:S(2)}) async-start(f32[8,12,1152]{2,1,0:T(8,128)} %reshape.1209), calls=%async_computation.27 | async-start | bytes 1179648 | tf_op jit(solution)/shard_map/all_to_all | solution.py:48
  739.6 227.0 %collective-permute-start.10 = (f32[24,1536]{1,0:T(8,128)}, f32[24,1536]{1,0:T(8,128)}, u32[]{:S(2)}, u32[]{:S(2)}) collective-permute-start(f32[24,1536]{1,0:T(8,128)} %convert_reduce_fusion.6), channel_id=1, source_target_pairs={{0,0},{8,1},{16,2},{24,3},{32,4},{40,5},{48,6},{56,7},{64,8},{72,9... | collective-permute-start | bytes 442376 | tf_op jit(solution)/shard_map/ppermute | solution.py:471
  873.7 18.7 %all-to-all-start.28 = ((f32[128,1,404]{2,1,0:T(1,128)}), f32[128,1,404]{2,1,0:T(1,128)S(1)}, u32[]{:S(2)}, u32[]{:S(2)}) async-start(f32[128,1,404]{2,1,0:T(1,128)} %copy.1113), calls=%async_computation.28 | async-start | bytes 524288 | tf_op jit(solution)/shard_map/all_to_all | solution.py:48
  893.1 23.8 %all-to-all-start.29 = ((bf16[16,24,1536]{2,1,0:T(8,128)(2,1)}), bf16[16,24,1536]{2,1,0:T(8,128)(2,1)}, u32[]{:S(2)}, u32[]{:S(2)}) async-start(bf16[16,24,1536]{2,1,0:T(8,128)(2,1)} %bitcast.655), calls=%async_computation.29 | async-start | bytes 2359296 | tf_op jit(solution)/shard_map/all_to_all | solution.py:48
  901.2 20.1 %collective-permute-start.7 = (f32[3,640]{1,0:T(4,128)}, f32[3,640]{1,0:T(4,128)S(1)}, u32[]{:S(2)}, u32[]{:S(2)}) collective-permute-start(f32[3,640]{1,0:T(4,128)} %slice.769), channel_id=1, source_target_pairs={{8,0},{16,8},{24,16},{32,24},{40,32},{48,40},{56,48},{64,56},{72,6... | collective-permute-start | bytes 23048 | tf_op jit(solution)/shard_map/ppermute | solution.py:430
  916.9 21.1 %all-to-all-start.23 = ((bf16[16,96,384]{2,1,0:T(8,128)(2,1)}), bf16[16,96,384]{2,1,0:T(8,128)(2,1)}, u32[]{:S(2)}, u32[]{:S(2)}) async-start(bf16[16,96,384]{2,1,0:T(8,128)(2,1)} %bitcast.695), calls=%async_computation.23 | async-start | bytes 2359296 | tf_op jit(solution)/shard_map/all_to_all | solution.py:48
  938.0 41.5 %all-to-all-start.22 = ((bf16[16,96,768]{2,1,0:T(8,128)(2,1)}), bf16[16,96,768]{2,1,0:T(8,128)(2,1)S(1)}, u32[]{:S(2)}, u32[]{:S(2)}) async-start(bf16[16,96,768]{2,1,0:T(8,128)(2,1)} %bitcast.675), calls=%async_computation.22 | async-start | bytes 4718592 | tf_op jit(solution)/shard_map/all_to_all | solution.py:48
  953.3 33.2 %collective-permute-start.8 = (bf16[2,2,128,1536]{3,2,1,0:T(8,128)(2,1)}, bf16[2,2,128,1536]{3,2,1,0:T(8,128)(2,1)}, u32[]{:S(2)}, u32[]{:S(2)}) collective-permute-start(bf16[2,2,128,1536]{3,2,1,0:T(8,128)(2,1)} %fusion.53), channel_id=1, source_target_pairs={{0,2},{2,0},{1,3},{3,1},{4,6},{6,4},{5,7},{7,5},{8,10},{10,8},{9,1... | collective-permute-start | bytes 4718600 | tf_op jit(solution)/shard_map/ppermute | solution.py:52
  960.1 17.0 %collective-permute-start.9 = (f32[24,1536]{1,0:T(8,128)S(1)}, f32[24,1536]{1,0:T(8,128)S(1)}, u32[]{:S(2)}, u32[]{:S(2)}) collective-permute-start(f32[24,1536]{1,0:T(8,128)S(1)} %convert_reduce_fusion.7), channel_id=1, source_target_pairs={{0,0},{8,1},{16,2},{24,3},{32,4},{40,5},{48,6},{56,7},{64,8},{72,9... | collective-permute-start | bytes 442376 | tf_op jit(solution)/shard_map/ppermute | solution.py:471
  996.6 23.4 %all-to-all-start.21 = ((bf16[4,128,1536]{2,1,0:T(8,128)(2,1)}), bf16[4,128,1536]{2,1,0:T(8,128)(2,1)S(1)}, u32[]{:S(2)}, u32[]{:S(2)}) async-start(bf16[4,128,1536]{2,1,0:T(8,128)(2,1)} %bitcast.155), calls=%async_computation.21 | async-start | bytes 3145728 | tf_op jit(solution)/shard_map/all_to_all | solution.py:48
  (285 other events, 2564.4 us)
Sparse Core Ops, SparseCore 0:
  38.1 16.7 all-gather.21
  57.1 45.1 all-gather.15
  104.5 54.0 all-gather.23
  160.1 15.9 all-gather.29
  249.3 44.4 all-gather.27
  295.3 15.3 all-gather.25
  313.4 45.7 all-gather.17
  361.3 42.5 all-gather.19
  680.0 17.9 all-gather.31

commit v2 on v1

v2 whole, which is shorter than its diff:
```python
import functools

import jax
import jax.numpy as jnp
from jax import lax
from jax.experimental import pallas as pl
from jax.experimental.pallas import tpu as pltpu
from jax.sharding import Mesh, PartitionSpec as P

D = 1536
DI = 3072
H = 48
HP = 64
N = 128
CONV = 4
LAYERS = 2
CH = DI + 2 * N
EPS = 1e-05

AX = ("z", "x", "yh", "c", "yl")
ZX = ("z", "x")
LINE = ("yh", "c", "yl")
Y = ("yh", "yl")
NQ = 16
NG = 8
TOK = 128
GT = TOK * NG
SPAN = 256
NS = GT // SPAN
HL = H // NG
W = HL * HP
CC = W + 2 * N
CA = CC + 128

bf = jnp.bfloat16
f32 = jnp.float32
HI = lax.Precision.HIGHEST


SMEM = pl.BlockSpec(memory_space=pltpu.SMEM)


def struct(shape, dtype=f32):
    return jax.ShapeDtypeStruct(shape, dtype)


def mm(a, b, ca=1, cb=0):
    return lax.dot_general(a, b, (((ca,), (cb,)), ((), ())), preferred_element_type=f32)


def a2a(a, axes):
    return lax.all_to_all(a, axes, 0, 0, tiled=True)


def core_swap(a):
    return lax.ppermute(a, "c", [(0, 1), (1, 0)])


def line_index():
    return lax.axis_index("yh") * 2 + lax.axis_index("yl")


def along_line(a, distance):
    return lax.ppermute(a, Y, [(i, (i + distance) % 4) for i in range(4)])


def place_kernel(extra, pos_ref, *refs):
    blocks, outs = refs[:NG], refs[NG:]
    step = pl.program_id(0)
    for i, block in enumerate(blocks):

        @pl.when(step == i)
        def _(block=block):
            outs[0][...] = block[:TOK]
            if extra:
                outs[1][...] = block[TOK:]


def line_gather(own):
    rows, n = own.shape
    extra = rows - TOK
    y, core = line_index(), lax.axis_index("c")
    blocks, places = [], []

    def place(distance, c):
        at = (y - distance) % 4
        return (at // 2) * 4 + c * 2 + at % 2

    for d in (0, 1, 3, 2):
        got = along_line(own, d) if d else own
        blocks += [got, core_swap(got)]
        places += [place(d, core), place(d, 1 - core)]
    shapes = [struct((GT, n), own.dtype)]
    if extra:
        shapes.append(struct((NG * extra, n), own.dtype))
    outs = pl.pallas_call(
        functools.partial(place_kernel, extra),
        out_shape=shapes,
        grid_spec=pltpu.PrefetchScalarGridSpec(
            num_scalar_prefetch=1,
            grid=(NG,),
            in_specs=[pl.BlockSpec((rows, n), lambda i, pos: (0, 0))] * NG,
            out_specs=[pl.BlockSpec((TOK, n), lambda i, pos: (pos[i], 0))]
            + [pl.BlockSpec((extra, n), lambda i, pos: (pos[i], 0))] * (extra > 0),
        ),
        compiler_params=pltpu.CompilerParams(vmem_limit_bytes=60 * 1024 * 1024),
        name="place_tokens",
    )(jnp.stack(places).astype(jnp.int32), *blocks)
    return outs if extra else outs[0]


def line_reduce(part):
    n = part.shape[1]
    core, y = lax.axis_index("c"), line_index()
    blocks = part.reshape(2, 2, 2, TOK, n)
    mine = lax.dynamic_index_in_dim(blocks, core, 1, keepdims=False)
    other = lax.dynamic_index_in_dim(blocks, 1 - core, 1, keepdims=False)
    got = core_swap(other.astype(bf))
    chip = (mine.astype(f32) + got.astype(f32)).reshape(4, TOK, n)
    total = lax.dynamic_index_in_dim(chip, y, 0, keepdims=False)
    chip = chip.astype(bf)
    for d in (1, 3, 2):
        sent = lax.dynamic_index_in_dim(chip, (y + d) % 4, 0, keepdims=False)
        total = total + along_line(sent, d).astype(f32)
    return total


def small_reduce(parts):
    m = parts.shape[0]
    sent = parts.reshape(m, NG, TOK).transpose(1, 0, 2)
    return jnp.sum(a2a(sent, LINE), axis=0)


def small_sum(parts):
    return jnp.sum(a2a(jnp.broadcast_to(parts[None], (NG,) + parts.shape), LINE), axis=0)


def rounded(a):
    return lax.reduce_precision(a, exponent_bits=8, mantissa_bits=7)


def three_parts(a):
    hi = rounded(a)
    mid = rounded(a - hi)
    return [hi.astype(bf), mid.astype(bf), (a - hi - mid).astype(bf)]


def group_gather(block):
    return lax.all_gather(block, ZX, axis=0, tiled=True)


def group_gather_now(block):
    r, n = block.shape
    return a2a(jnp.broadcast_to(block[None], (NQ, r, n)), ZX).reshape(NQ * r, n)


def tie(*arrays):
    return lax.optimization_barrier(arrays)


def group_reduce(full):
    r = full.shape[0] // NQ
    return jnp.sum(a2a(full.reshape(NQ, r, full.shape[1]), ZX).astype(f32), axis=0)


def heads_out(cols, width):
    r = cols.shape[0]
    return cols.reshape(r, 2, 2, 2, width).transpose(2, 3, 1, 0, 4).reshape(NG, r, width)


def heads_in(blocks):
    _, r, width = blocks.shape
    return blocks.reshape(2, 2, 2, r, width).transpose(3, 2, 0, 1, 4).reshape(r, NG * width)


def line_of(group):
    yl, yh, c = group // 4, (group // 2) % 2, group % 2
    return yh * 4 + c * 2 + yl


TO_HEADS = [(s, (s % NQ) * NG + line_of(s // NQ)) for s in range(NQ * NG)]
TO_OWNER = [(b, a) for a, b in TO_HEADS]


def in_blocks(weight, gain, extra):
    folded = (weight.astype(f32) * gain.astype(f32)[:, None]).astype(bf)
    z = heads_out(folded[:, :DI], W)
    x = heads_out(folded[:, DI : 2 * DI], W)
    bc = jnp.broadcast_to(folded[None, :, 2 * DI : 2 * DI + 2 * N], (NG, 12, 2 * N))
    step = heads_out(folded[:, 2 * DI + 2 * N :], HL)
    extra = jnp.broadcast_to(extra[None], (NG,) + extra.shape)
    step = jnp.concatenate([step, extra], axis=2)
    step = jnp.pad(step, ((0, 0), (0, 0), (0, 128 - step.shape[2])))
    return jnp.concatenate([x, bc, step, z], axis=2)


SCAN_ROWS = HL * HP // NQ


def scan_kernel(reverse, q_ref, got_ref, out_ref):
    row = q_ref[0] * SCAN_ROWS + lax.broadcasted_iota(jnp.int32, (SCAN_ROWS, N), 0)
    lane = lax.broadcasted_iota(jnp.int32, (SCAN_ROWS, N), 1)
    head = jnp.zeros((SCAN_ROWS, N), jnp.int32)
    for k in range(1, HL):
        head = head + (row >= k * HP).astype(jnp.int32)
    chosen = (lane == head) | (lane == head + HL) | (lane == head + 2 * HL)
    carry = jnp.zeros((SCAN_ROWS, N), f32)
    pad = jnp.zeros((32 - SCAN_ROWS, N), f32)
    for j in range(NQ - 1, -1, -1) if reverse else range(NQ):
        out_ref[j] = jnp.concatenate([carry, pad], axis=0).astype(bf)
        block = got_ref[j].astype(f32)
        decay = jnp.sum(
            jnp.where(chosen, block[SCAN_ROWS : SCAN_ROWS + 1], 0.0), axis=1, keepdims=True
        )
        carry = decay * carry + block[:SCAN_ROWS]


def exclusive_scan(sent, reverse):
    q = lax.axis_index(ZX)
    got = a2a(sent, ZX)
    outs = pl.pallas_call(
        functools.partial(scan_kernel, reverse),
        out_shape=jax.ShapeDtypeStruct((NQ, 32, N), bf),
        in_specs=[
            pl.BlockSpec(memory_space=pltpu.SMEM),
            pl.BlockSpec(memory_space=pltpu.VMEM),
        ],
        out_specs=pl.BlockSpec(memory_space=pltpu.VMEM),
        name="group_scan",
    )(q.reshape(1).astype(jnp.int32), got)
    return a2a(outs, ZX)


PAIRS = HL // 2
LAST = NS - 1


def dot(a, b, ca, cb, precision=None):
    return lax.dot_general(
        a, b, (((ca,), (cb,)), ((), ())), preferred_element_type=f32, precision=precision
    )


def by_lanes(cols):
    lane = lax.broadcasted_iota(jnp.int32, (cols.shape[0], 128), 1)
    return jnp.concatenate(
        [
            jnp.where(lane < HP, cols[:, 2 * p : 2 * p + 1], cols[:, 2 * p + 1 : 2 * p + 2])
            for p in range(PAIRS)
        ],
        axis=1,
    )


def by_rows(row, states):
    return jnp.concatenate(
        [row[:, h : h + 1] * states[h * HP : (h + 1) * HP] for h in range(HL)], axis=0
    )


def head_sums(wide):
    column = lax.broadcasted_iota(jnp.int32, (W, 128), 0)
    lane = lax.broadcasted_iota(jnp.int32, (W, 128), 1)
    chosen = ((column >= lane * HP) & (column < lane * HP + HP)).astype(f32)
    return dot(wide, chosen, 1, 0, HI)


def token_sums(wide):
    return dot(jnp.ones((8, wide.shape[1]), f32), wide, 1, 1, HI)


def write_states(sent_ref, states, decay):
    lane = lax.broadcasted_iota(jnp.int32, (8, 128), 1)
    decay = jnp.where(lane < HL, jnp.broadcast_to(decay, (8, 128)), 0.0)
    hi = decay.astype(bf).astype(f32)
    mid = (decay - hi).astype(bf).astype(f32)
    low = decay - hi - mid
    tail = hi + pltpu.roll(mid, HL, 1) + pltpu.roll(low, 2 * HL, 1)
    for j in range(NQ):
        block = states[j * SCAN_ROWS : (j + 1) * SCAN_ROWS]
        sent_ref[j] = jnp.concatenate([block, tail], axis=0).astype(bf)


def read_states(back_ref):
    return jnp.concatenate([back_ref[j].astype(f32)[:SCAN_ROWS] for j in range(NQ)], axis=0)


def span_masks(segc_ref, segr_ref):
    row = lax.broadcasted_iota(jnp.int32, (SPAN, SPAN), 0)
    col = lax.broadcasted_iota(jnp.int32, (SPAN, SPAN), 1)
    return (col <= row) & (segc_ref[...] == segr_ref[0])


def head_decay(mask, run, run_t, h):
    return jnp.exp(jnp.where(mask, run[:, h : h + 1] - run_t[h : h + 1], -1e30))


def end_weights(run, segc_ref, seg_end):
    return jnp.exp(run[SPAN - 1 :] - run) * (segc_ref[...] == seg_end).astype(f32)


def inflow_of(run, segc_ref, seg_before):
    return jnp.exp(run) * (segc_ref[...] == seg_before).astype(f32)


def mix_kernel(
    seg_ref, v_ref, raw_ref, bias_ref, rate_ref, segc_ref, segr_ref,
    within_ref, local_ref, step_ref, run_ref, before_ref, decay_ref, sent_ref, acc_ref, dec_ref,
):
    k = pl.program_id(0)

    @pl.when(k == 0)
    def _():
        acc_ref[...] = jnp.zeros_like(acc_ref)
        dec_ref[...] = jnp.ones_like(dec_ref)

    lane = lax.broadcasted_iota(jnp.int32, (SPAN, 128), 1)
    raw = raw_ref[...].astype(f32) + bias_ref[...]
    step = jnp.where(lane < HL, jax.nn.softplus(raw), 0.0)
    row = lax.broadcasted_iota(jnp.int32, (SPAN, SPAN), 0)
    col = lax.broadcasted_iota(jnp.int32, (SPAN, SPAN), 1)
    run = dot((col <= row).astype(f32), rate_ref[...] * step, 1, 0, HI)
    step_ref[...] = step
    run_ref[...] = run
    run_t = run.T
    mask = span_masks(segc_ref, segr_ref)
    xc = v_ref[:, :W]
    b_low = v_ref[:, W : W + N].astype(bf)
    c_low = v_ref[:, W + N :].astype(bf)
    gram = dot(c_low, b_low, 1, 1)
    xs = (by_lanes(step) * xc).astype(bf)
    half = lane < HP
    for p in range(PAIRS):
        cols = slice(p * 128, (p + 1) * 128)
        out = [
            dot((gram * head_decay(mask, run, run_t, h)).astype(bf), xs[:, cols], 1, 0)
            for h in (2 * p, 2 * p + 1)
        ]
        within_ref[:, cols] = jnp.where(half, out[0], out[1])
    w_end = end_weights(run, segc_ref, seg_ref[1, k])
    weighted = (by_lanes(w_end * step) * xc).astype(bf)
    own = dot(weighted, b_low, 0, 0)
    local_ref[0] = acc_ref[...]
    before_ref[0] = dec_ref[...]
    inside = (seg_ref[1, k] == seg_ref[0, k]).astype(f32)
    decay = jnp.exp(run[SPAN - 1 :]) * inside
    decay_ref[0] = decay
    acc = by_rows(decay, acc_ref[...]) + own
    acc_ref[...] = acc
    dec = dec_ref[...] * decay
    dec_ref[...] = dec

    @pl.when(k == LAST)
    def _():
        write_states(sent_ref, acc, dec)


def silu_both(v):
    s = 1.0 / (1.0 + jnp.exp(-v))
    return v * s, s * (1.0 + v * (1.0 - s))


def gate_kernel(
    last, seg_ref, back_ref, local_ref, before_ref, run_ref, v_ref, within_ref, z_ref, segc_ref,
    skip_ref, wo_ref, *rest,
):
    if last:
        grad_ref, y0_ref, part_ref, sums_ref, carry_ref = rest
    else:
        y0_ref, part_ref, sums_ref, carry_ref = rest
    k = pl.program_id(0)

    @pl.when(k == 0)
    def _():
        carry_ref[...] = read_states(back_ref)

    carried = (by_rows(before_ref[0], carry_ref[...]) + local_ref[0]).astype(bf)
    xc = v_ref[:, :W]
    c_low = v_ref[:, W + N :].astype(bf)
    reading = dot(c_low, carried, 1, 1)
    y0 = within_ref[...] + by_lanes(inflow_of(run_ref[...], segc_ref, seg_ref[0, k])) * reading
    y0_ref[...] = y0
    mixed = (y0 + skip_ref[...] * xc).astype(bf).astype(f32)
    gated = mixed * silu_both(z_ref[...])[0]
    part_ref[...] = dot(gated.astype(bf), wo_ref[...], 1, 0).astype(bf)
    sums = token_sums(gated * gated)
    if last:
        d_q = dot(grad_ref[...], wo_ref[...], 1, 1)
        row = lax.broadcasted_iota(jnp.int32, (8, SPAN), 0)
        sums = jnp.where(row < 1, sums, token_sums(gated * d_q))
    sums_ref[...] = sums


def gate_back_kernel(
    seg_ref, grad_ref, wo_ref, scale_ref, v_ref, y0_ref, z_ref, run_ref, segc_ref, skip_ref,
    decay_ref, dy_ref, dz_ref, gr_ref, local_ref, after_ref, sent_ref, acc_ref, dec_ref,
):
    i = pl.program_id(0)
    k = LAST - i

    @pl.when(i == 0)
    def _():
        acc_ref[...] = jnp.zeros_like(acc_ref)
        dec_ref[...] = jnp.ones_like(dec_ref)

    scales = scale_ref[...].T
    r, kappa = scales[:, 0:1], scales[:, 1:2]
    d_q = dot(grad_ref[...], wo_ref[...], 1, 1)
    mixed = (y0_ref[...] + skip_ref[...] * v_ref[:, :W]).astype(bf).astype(f32)
    silu, d_silu = silu_both(z_ref[...])
    gated = mixed * silu
    gr_ref[...] = (r * gated).astype(bf)
    d_gated = r * d_q - kappa * gated
    dy = (d_gated * silu).astype(bf)
    dy_ref[...] = dy
    dz_ref[...] = (d_gated * mixed * d_silu).astype(bf)
    inflow = by_lanes(inflow_of(run_ref[...], segc_ref, seg_ref[0, k]))
    scaled = (inflow * dy.astype(f32)).astype(bf)
    d_carried = dot(scaled, v_ref[:, W + N :].astype(bf), 0, 0)
    local_ref[0] = acc_ref[...]
    after_ref[0] = dec_ref[...]
    decay = decay_ref[0]
    acc = by_rows(decay, acc_ref[...]) + d_carried
    acc_ref[...] = acc
    dec = dec_ref[...] * decay
    dec_ref[...] = dec

    @pl.when(i == LAST)
    def _():
        write_states(sent_ref, acc, dec)


def mix_back_kernel(v_ref, step_ref, run_ref, segc_ref, segr_ref, dy_ref, dxs_ref, dbc_ref):
    lane = lax.broadcasted_iota(jnp.int32, (SPAN, 128), 1)
    half = lane < HP
    run = run_ref[...]
    run_t = run.T
    mask = span_masks(segc_ref, segr_ref)
    xs = (by_lanes(step_ref[...]) * v_ref[:, :W]).astype(bf)
    b_low = v_ref[:, W : W + N].astype(bf)
    c_low = v_ref[:, W + N :].astype(bf)
    gram = dot(c_low, b_low, 1, 1)
    d_gram = jnp.zeros((SPAN, SPAN), f32)
    zero = jnp.zeros((SPAN, 128), bf)
    for p in range(PAIRS):
        cols = slice(p * 128, (p + 1) * 128)
        dy = dy_ref[:, cols]
        out = []
        for i, h in enumerate((2 * p, 2 * p + 1)):
            decay = head_decay(mask, run, run_t, h)
            mixing = (gram * decay).astype(bf)
            dy_one = jnp.where(half, dy, zero) if i == 0 else jnp.where(half, zero, dy)
            d_gram = d_gram + dot(dy_one, xs[:, cols], 1, 1) * decay
            out.append(dot(mixing, dy, 0, 0))
        dxs_ref[:, cols] = jnp.where(half, out[0], out[1])
    d_gram = d_gram.astype(bf)
    dbc_ref[:, :N] = dot(d_gram, c_low, 0, 0)
    dbc_ref[:, N:] = dot(d_gram, b_low, 1, 0)


def end_kernel(
    seg_ref, later_ref, back_ref, local_ref, before_ref, dlocal_ref, after_ref, decay_ref, v_ref,
    pre_ref, raw_ref, bias_ref, rate_ref, step_ref, run_ref, segc_ref, skip_ref, dy_ref, dxs_ref,
    dbc_ref, y0_ref, dpre_ref, draw_ref, sums_ref, later_s, carry_s,
):
    k = pl.program_id(0)

    @pl.when(k == 0)
    def _():
        later_s[...] = read_states(later_ref)
        carry_s[...] = read_states(back_ref)
        sums_ref[...] = jnp.zeros_like(sums_ref)

    d_end = by_rows(after_ref[0], later_s[...]) + dlocal_ref[0]
    carried = by_rows(before_ref[0], carry_s[...]) + local_ref[0]
    d_end_low = d_end.astype(bf)
    run, step, rate = run_ref[...], step_ref[...], rate_ref[...]
    xc = v_ref[:, :W]
    b_low = v_ref[:, W : W + N].astype(bf)
    dy = dy_ref[...].astype(f32)
    dxs = dxs_ref[...]
    step_x = by_lanes(step)
    xs = (step_x * xc).astype(bf).astype(f32)
    w_end = end_weights(run, segc_ref, seg_ref[1, k])
    weights_x = by_lanes(w_end * step)
    weighted = (weights_x * xc).astype(bf)
    scaled = (by_lanes(inflow_of(run, segc_ref, seg_ref[0, k])) * dy).astype(bf)
    d_weighted = dot(b_low, d_end_low, 1, 1)
    d_b = dbc_ref[:, :N] + dot(weighted, d_end_low, 1, 0)
    d_c = dbc_ref[:, N:] + dot(scaled, carried.astype(bf), 1, 0)
    d_xc = skip_ref[...] * dy + step_x * dxs + weights_x * d_weighted
    dv = jnp.concatenate([d_xc, d_b, d_c], axis=1)
    dpre_ref[...] = dv * silu_both(pre_ref[...])[1]
    skip_sum = head_sums(dy * xc)
    d_run = head_sums(dy * y0_ref[...] - xs * dxs)
    d_step = head_sums(xc * dxs)
    d_w = head_sums(d_weighted * xc)
    product = d_end * carried
    ones = jnp.ones((8, N), f32)
    lane8 = lax.broadcasted_iota(jnp.int32, (8, 128), 1)
    d_span = jnp.zeros((8, 128), f32)
    for h in range(HL):
        rows = dot(ones, product[h * HP : (h + 1) * HP], 1, 1, HI)
        d_span = d_span + jnp.where(lane8 == h, jnp.sum(rows, axis=1, keepdims=True), 0.0)
    d_step = d_step + d_w * w_end
    d_ww = d_w * w_end * step
    d_run = d_run - d_ww
    d_last = jnp.sum(d_ww, axis=0, keepdims=True) + d_span[:1] * decay_ref[0]
    row = lax.broadcasted_iota(jnp.int32, (SPAN, SPAN), 0)
    col = lax.broadcasted_iota(jnp.int32, (SPAN, SPAN), 1)
    d_a = dot((col >= row).astype(f32), d_run, 1, 0, HI) + d_last
    d_step = d_step + rate * d_a
    raw = raw_ref[...].astype(f32) + bias_ref[...]
    lane = lax.broadcasted_iota(jnp.int32, (SPAN, 128), 1)
    d_raw = jnp.where(lane < HL, d_step / (1.0 + jnp.exp(-raw)), 0.0)
    draw_ref[...] = d_raw.astype(bf)
    sums = jnp.concatenate(
        [
            jnp.sum(d_raw, axis=0, keepdims=True),
            rate * jnp.sum(step * d_a, axis=0, keepdims=True),
            jnp.sum(skip_sum, axis=0, keepdims=True),
            jnp.zeros((5, 128), f32),
        ],
        axis=0,
    )
    sums_ref[...] = sums_ref[...] + sums


def tok_block(n, reverse=False):
    return pl.BlockSpec((SPAN, n), lambda k: (LAST - k if reverse else k, 0))


def span_block(rows, n, reverse=False):
    return pl.BlockSpec((1, rows, n), lambda k: (LAST - k if reverse else k, 0, 0))


def whole(*shape):
    return pl.BlockSpec(shape, lambda k: (0,) * len(shape))


STATE = struct((NS, W, N))
ROW = struct((NS, 1, 128))
SENT = struct((NQ, 32, N), bf)
STATE_SCRATCH = pltpu.VMEM((W, N), f32)


def call(kernel, name, ins, outs, shapes, scratch, args, us):
    return pl.pallas_call(
        kernel,
        grid=(NS,),
        in_specs=ins,
        out_specs=outs,
        out_shape=shapes,
        scratch_shapes=scratch,
        compiler_params=pltpu.CompilerParams(
            dimension_semantics=("arbitrary",), vmem_limit_bytes=60 * 1024 * 1024
        ),
        cost_estimate=pl.CostEstimate(
            flops=int(us * 8e8), bytes_accessed=int(us * 3e6), transcendentals=0
        ),
        name=name,
    )(*args)


def span_mix(seg, v, raw, bias, rate, segc, segr):
    return call(
        mix_kernel,
        "span_mix",
        [SMEM, tok_block(CC), tok_block(128), whole(1, 128), whole(1, 128), tok_block(1),
         span_block(1, SPAN)],
        [tok_block(W), span_block(W, N), tok_block(128), tok_block(128), span_block(1, 128),
         span_block(1, 128), whole(NQ, 32, N)],
        [struct((GT, W)), STATE, struct((GT, 128)), struct((GT, 128)), ROW, ROW, SENT],
        [STATE_SCRATCH, pltpu.VMEM((1, 128), f32)],
        (seg, v, raw, bias, rate, segc, segr),
        12,
    )


def span_gate(seg, back, local, before, run, v, within, z, segc, skip, wo, grad):
    last = grad is not None
    ins = [SMEM, whole(NQ, 32, N), span_block(W, N), span_block(1, 128), tok_block(128),
           tok_block(CC), tok_block(W), tok_block(W), tok_block(1), whole(1, W), whole(W, D)]
    args = (seg, back, local, before, run, v, within, z, segc, skip, wo)
    return call(
        functools.partial(gate_kernel, last),
        "span_gate",
        ins + [tok_block(D)] if last else ins,
        [tok_block(W), tok_block(D), pl.BlockSpec((8, SPAN), lambda k: (0, k))],
        [struct((GT, W)), struct((GT, D), bf), struct((8, GT))],
        [STATE_SCRATCH],
        args + (grad,) if last else args,
        10,
    )


def span_gate_back(seg, grad, wo, scales, v, y0, z, run, segc, skip, decay):
    return call(
        gate_back_kernel,
        "span_gate_back",
        [SMEM, tok_block(D, True), whole(W, D), pl.BlockSpec((8, SPAN), lambda k: (0, LAST - k)),
         tok_block(CC, True), tok_block(W, True), tok_block(W, True), tok_block(128, True),
         tok_block(1, True), whole(1, W), span_block(1, 128, True)],
        [tok_block(W, True), tok_block(W, True), tok_block(W, True), span_block(W, N, True),
         span_block(1, 128, True), whole(NQ, 32, N)],
        [struct((GT, W), bf), struct((GT, W), bf), struct((GT, W), bf), STATE, ROW, SENT],
        [STATE_SCRATCH, pltpu.VMEM((1, 128), f32)],
        (seg, grad, wo, scales, v, y0, z, run, segc, skip, decay),
        12,
    )


def span_mix_back(v, step, run, segc, segr, dy):
    return call(
        mix_back_kernel,
        "span_mix_back",
        [tok_block(CC), tok_block(128), tok_block(128), tok_block(1), span_block(1, SPAN),
         tok_block(W)],
        [tok_block(W), tok_block(2 * N)],
        [struct((GT, W)), struct((GT, 2 * N))],
        [],
        (v, step, run, segc, segr, dy),
        14,
    )


def span_end(seg, later, back, local, before, dlocal, after, decay, v, pre, raw, bias, rate, step,
             run, segc, skip, dy, dxs, dbc, y0):
    return call(
        end_kernel,
        "span_end",
        [SMEM, whole(NQ, 32, N), whole(NQ, 32, N), span_block(W, N), span_block(1, 128),
         span_block(W, N), span_block(1, 128), span_block(1, 128), tok_block(CC), tok_block(CC),
         tok_block(128), whole(1, 128), whole(1, 128), tok_block(128), tok_block(128),
         tok_block(1), whole(1, W), tok_block(W), tok_block(W), tok_block(2 * N), tok_block(W)],
        [tok_block(CC), tok_block(128), whole(8, 128)],
        [struct((GT, CC)), struct((GT, 128), bf), struct((8, 128))],
        [STATE_SCRATCH, STATE_SCRATCH],
        (seg, later, back, local, before, dlocal, after, decay, v, pre, raw, bias, rate, step, run,
         segc, skip, dy, dxs, dbc, y0),
        16,
    )


SMALL = CC + HL


def small_block(conv_grads, head_grads):
    own_ch = CH // (NQ * NG)
    conv = jnp.stack(conv_grads).reshape(LAYERS * (CONV + 1), NQ * NG, own_ch)
    conv = jnp.pad(conv.transpose(1, 0, 2), ((0, 0), (0, 12 - LAYERS * (CONV + 1)), (0, 0)))
    head = jnp.stack(head_grads, axis=1)
    high = rounded(head)
    head = jnp.concatenate([high, head - high], axis=1)
    head = jnp.tile(head, (NQ * NG // 2, 1, 1))
    head = jnp.pad(head, ((0, 0), (0, 12 - 2 * LAYERS), (0, 0)))
    block = jnp.concatenate([conv, head], axis=2).reshape(D, own_ch + 3 * H // 2)
    return jnp.pad(block.astype(bf), ((0, 0), (SMALL, CA - SMALL - block.shape[1])))


def per_device(
    tokens,
    doc_starts,
    norm_gain,
    in_weight,
    conv_weight,
    conv_bias,
    step_bias,
    decay_log,
    skip_gain,
    gate_gain,
    out_weight,
    cotangent,
):
    q = lax.axis_index(ZX)
    yh, core, yl = lax.axis_index("yh"), lax.axis_index("c"), lax.axis_index("yl")
    sub = yh * 2 + core
    group = yl * 4 + sub

    own_ch = CH // (NQ * NG)
    conv_own = jnp.concatenate([conv_weight, conv_bias[:, None]], axis=1).reshape(-1, own_ch)
    conv_own = jnp.pad(conv_own, ((0, 12 - conv_own.shape[0]), (0, 0)))
    sent = [in_blocks(in_weight[l], norm_gain[l], conv_own if l == 0 else conv_own[:, :0]) for l in range(LAYERS)]
    got = a2a(jnp.stack(sent, axis=1), LINE)
    got, tokens, out_weight = tie(got, tokens, out_weight)
    in_0 = got[:, 0].reshape(NG * 12, CA + W)
    in_1 = got[:, 1].reshape(NG * 12, CA + W)
    folded_out = (out_weight.astype(f32) * gate_gain.astype(f32)[:, :, None]).astype(bf)
    out_blocks = lax.ppermute(folded_out, AX, TO_HEADS)
    w_a0 = group_gather_now(in_0[:, :CA])
    conv_all = w_a0[:, W + 2 * N + HL : W + 2 * N + HL + own_ch].reshape(NQ * NG, 12, own_ch)
    conv_all = conv_all[:, : LAYERS * (CONV + 1)].transpose(1, 0, 2)
    conv_all = conv_all.reshape(LAYERS, CONV + 1, CH).astype(f32)
    conv_x = lax.dynamic_slice_in_dim(conv_all, group * W, W, 2)
    conv_here = jnp.concatenate([conv_x, conv_all[:, :, DI:]], axis=2)
    w_z0 = group_gather_now(in_0[:, CA:])
    w_o = [group_gather(out_blocks[l]) for l in range(LAYERS)]
    w_in1 = group_gather(in_1)

    pos = q * GT + jnp.arange(-(CONV - 1), GT + CONV - 1, dtype=jnp.int32)
    seg_ext = jnp.sum((doc_starts[None, :] <= pos[:, None]).astype(jnp.int32), axis=1) - 1
    seg = seg_ext[CONV - 1 : CONV - 1 + GT]
    seg_spans = seg.reshape(NS, SPAN)
    seg_before = seg_ext[CONV - 2 : CONV - 2 + GT : SPAN]
    seg_ends = jnp.stack([seg_before, seg_spans[:, -1]])
    seg_col, seg_row = seg[:, None], seg_spans[:, None, :]
    same_back = [
        (seg_ext[CONV - 1 - k : CONV - 1 - k + GT] == seg).astype(f32)[:, None] for k in range(CONV)
    ]
    same_fwd = [
        (seg_ext[CONV - 1 + k : CONV - 1 + k + GT] == seg).astype(f32)[:, None] for k in range(CONV)
    ]

    def pick_heads(a):
        own = lax.dynamic_slice_in_dim(a, sub * HL, HL, 0)
        return jnp.pad(own, (0, 128 - HL))[None]

    h = tokens.astype(f32)
    saved = []
    cot_late, w_a0 = tie(cotangent, w_a0)
    grad_full = line_gather(cot_late)

    for l in range(LAYERS):
        bias_h = pick_heads(step_bias[l])
        rate = jnp.where(jnp.arange(128)[None] < HL, -jnp.exp(pick_heads(decay_log[l])), 0.0)
        skip_x = jnp.repeat(lax.dynamic_slice_in_dim(skip_gain[l], sub * HL, HL, 0), HP)[None]
        r_in = lax.rsqrt(jnp.mean(h * h, axis=-1, keepdims=True) + EPS)
        normed = line_gather((h * r_in).astype(bf))
        proj = mm(normed, w_a0 if l == 0 else w_in1)
        u = proj[:, :CC].astype(bf)
        raw = proj[:, CC:CA].astype(bf)
        edge = lax.ppermute(u[GT - (CONV - 1) :], ZX, [(i, i + 1) for i in range(NQ - 1)])
        z = mm(normed, w_z0) if l == 0 else proj[:, CA:]
        ext = jnp.concatenate([edge, u], axis=0).astype(f32)
        cw = conv_here[l]
        pre = jnp.broadcast_to(cw[CONV][None], (GT, W + 2 * N))
        for k in range(CONV):
            pre = pre + cw[k][None] * ext[CONV - 1 - k : CONV - 1 - k + GT] * same_back[k]
        v = pre * jax.nn.sigmoid(pre)
        within, local, step, run, before, decay, sent = span_mix(
            seg_ends, v, raw, bias_h, rate, seg_col, seg_row
        )
        if l == 0:
            sent, w_z0 = tie(sent, w_z0)
        back = exclusive_scan(sent, False)
        if l == 0:
            back, grad_full, w_o[0] = tie(back, grad_full, w_o[0])
        y0, part, sums = span_gate(
            seg_ends, back, local, before, run, v, within, z, seg_col, skip_x, w_o[l],
            grad_full if l == LAYERS - 1 else None,
        )
        total = line_reduce(part)
        if l == LAYERS - 1:
            sums = small_sum(sums[:2])
            r_all = lax.rsqrt(sums[0] / DI + EPS)
            gate_scales = jnp.stack([r_all, r_all * r_all * r_all * sums[1] / DI])
            r_gate = lax.dynamic_slice_in_dim(r_all, (line_index() // 2 * 4 + core * 2 + yl) * TOK, TOK, 0)
        else:
            gate_scales = None
            total, square, w_in1, w_o[1] = tie(total, small_reduce(sums[:1])[0], w_in1, w_o[1])
            r_gate = lax.rsqrt(square / DI + EPS)
        branch = total * r_gate[:, None]
        saved.append(
            dict(
                h=h, r_in=r_in, normed=normed, ext=ext, pre=pre, v=v, z=z, raw=raw, bias_h=bias_h,
                rate=rate, skip_x=skip_x, step=step, run=run, before=before, decay=decay,
                local=local, back=back, y0=y0, r_gate=r_gate, branch=branch,
                gate_scales=gate_scales,
            )
        )
        h = h + branch
    output = h.astype(bf)

    grad = cotangent.astype(f32)
    in_grads, gain_grads, out_grads, gate_grads = ([None] * LAYERS for _ in range(4))
    conv_grads, head_grads = [None] * LAYERS, [None] * LAYERS
    in_sums, out_sums = [None] * LAYERS, [None] * LAYERS
    for l in reversed(range(LAYERS)):
        s = saved[l]
        if l == LAYERS - 1:
            gate_scales = s["gate_scales"]
        else:
            grad_low = grad.astype(bf)
            inner = jnp.sum(grad_low.astype(f32) * s["branch"], axis=1)
            kappa = s["r_gate"] * s["r_gate"] * inner / DI
            extra = jnp.concatenate(three_parts(s["r_gate"]) + three_parts(kappa))
            extra = jnp.pad(extra[None], ((0, 15), (0, D - 6 * TOK)))
            grad_full, extra = line_gather(jnp.concatenate([grad_low, extra], axis=0))
            extra = extra.reshape(NG, 16, D)[:, 0, : 6 * TOK].reshape(NG, 2, 3, TOK).astype(f32)
            gate_scales = jnp.sum(extra, axis=2).transpose(1, 0, 2).reshape(2, GT)
            grad_full, in_sums[1] = tie(grad_full, in_sums[1])
        scales = jnp.pad(gate_scales, ((0, 6), (0, 0)))
        dy, dz, gr, dlocal, after, sent = span_gate_back(
            seg_ends, grad_full, w_o[l], scales, s["v"], s["y0"], s["z"], s["run"], seg_col,
            s["skip_x"], s["decay"],
        )
        later = exclusive_scan(sent, True)
        later, dz, gr = tie(later, dz, gr)
        if l == LAYERS - 1:
            later, output = tie(later, output)
        else:
            z_sum = group_reduce(mm(s["normed"], dz, 0, 0).astype(bf))
        out_sum = group_reduce(mm(gr, grad_full, 0, 0).astype(bf))
        dxs, dbc = span_mix_back(s["v"], s["step"], s["run"], seg_col, seg_row, dy)
        d_pre, d_raw, head_sum = span_end(
            seg_ends, later, s["back"], s["local"], s["before"], dlocal, after, s["decay"], s["v"],
            s["pre"], s["raw"], s["bias_h"], s["rate"], s["step"], s["run"], seg_col, s["skip_x"],
            dy, dxs, dbc, s["y0"],
        )
        if l == LAYERS - 1:
            d_pre, out_sum = tie(d_pre, out_sum)
        edge = lax.ppermute(d_pre[: CONV - 1], ZX, [(i + 1, i) for i in range(NQ - 1)])
        d_ext = jnp.concatenate([d_pre, edge], axis=0)
        cw = conv_here[l]
        du = jnp.zeros_like(d_pre)
        taps = []
        for k in range(CONV):
            du = du + cw[k][None] * d_ext[k : k + GT] * same_fwd[k]
            past = s["ext"][CONV - 1 - k : CONV - 1 - k + GT]
            taps.append(jnp.sum(d_pre * past * same_back[k], axis=0))
        taps.append(jnp.sum(d_pre, axis=0))
        taps = jnp.stack(taps)
        conv_full = jnp.zeros((CONV + 1, CH), f32)
        conv_full = lax.dynamic_update_slice_in_dim(conv_full, taps[:, :W], group * W, 1)
        conv_grads[l] = conv_full.at[:, DI:].set(taps[:, W:])
        head_full = lax.dynamic_update_slice_in_dim(
            jnp.zeros((3, H), f32), head_sum[:3, :HL], group * HL, 1
        )
        head_grads[l] = head_full.reshape(3, 2, H // 2).transpose(1, 0, 2).reshape(2, 3 * H // 2)
        da = jnp.concatenate([du.astype(bf), d_raw], axis=1)
        if l == 0:
            small = small_block(conv_grads, head_grads)
            a_part = mm(s["normed"], da, 0, 0) + small.astype(f32)
            in_sum = jnp.concatenate([group_reduce(a_part.astype(bf)), z_sum], axis=1)
            d_norm = line_reduce(mm(da, w_a0, 1, 1) + mm(dz, w_z0, 1, 1))
        else:
            da = jnp.concatenate([da, dz], axis=1)
            d_norm = line_reduce(mm(da, w_in1, 1, 1))
            in_sum = group_reduce(mm(s["normed"], da, 0, 0).astype(bf))
        hidden, r_in = s["h"], s["r_in"]
        inner = jnp.mean(hidden * d_norm, axis=1, keepdims=True)
        grad = grad + r_in * d_norm - hidden * (r_in * r_in * r_in) * inner
        in_sums[l], out_sums[l] = in_sum, out_sum

    for l in reversed(range(LAYERS)):
        both = in_sums[l].reshape(NG, 12, CA + W)
        both = a2a(both, LINE)
        if l == 0:
            small = jnp.sum(both[:, :, SMALL:CA], axis=0)
        g_in = jnp.concatenate(
            [
                heads_in(both[:, :, CA:]),
                heads_in(both[:, :, :W]),
                jnp.sum(both[:, :, W : W + 2 * N], axis=0),
                heads_in(both[:, :, W + 2 * N : W + 2 * N + HL]),
            ],
            axis=1,
        )
        in_grads[l] = g_in * norm_gain[l].astype(f32)[:, None]
        gain_grads[l] = jnp.sum(g_in * in_weight[l].astype(f32), axis=1)
        g_out = lax.ppermute(out_sums[l], AX, TO_OWNER)
        out_grads[l] = g_out * gate_gain[l].astype(f32)[:, None]
        gate_grads[l] = jnp.sum(g_out * out_weight[l].astype(f32), axis=1)

    conv_grad = small[: LAYERS * (CONV + 1), :own_ch].reshape(LAYERS, CONV + 1, own_ch)
    head_grad = small[:LAYERS] + small[LAYERS : 2 * LAYERS]
    head_grad = head_grad[:, own_ch : own_ch + 3 * H // 2].reshape(LAYERS, 3, H // 2)
    return (
        output,
        grad,
        jnp.stack(gain_grads),
        jnp.stack(in_grads),
        conv_grad[:, :CONV],
        conv_grad[:, CONV],
        head_grad[:, 0],
        head_grad[:, 1],
        head_grad[:, 2],
        jnp.stack(gate_grads),
        jnp.stack(out_grads),
    )


def solution(mesh):
    fine = Mesh(mesh.devices.reshape(4, 4, 2, 2, 2), AX)
    tok, last, mid, heads = P(AX, None), P(None, AX), P(None, AX, None), P(None, "yl")
    conv = P(None, None, AX)
    return jax.shard_map(
        per_device,
        mesh=fine,
        in_specs=(tok, P(), last, mid, conv, last, heads, heads, heads, last, mid, tok),
        out_specs=(tok, tok, last, mid, conv, last, heads, heads, heads, last, mid),
        check_vma=False,
    )
```

time: 1040 us -> 750 us (0.72)
  waiting for transfers between devices: 297 us -> 154 us
  matrix products: 178 us -> 49.8 us
  Pallas kernels: 6.79 us -> 132 us
  local copies, waits for them, and re-layouts: 186 us -> 86 us
  other arithmetic: 110 us -> 71.9 us
  blocking collectives: 35 us -> 24.2 us
    all_to_all x29 -> x18, waiting for transfers between devices: 228 us -> 74.7 us  [a2a(): return lax.all_to_all(a, axes, 0, 0, tiled=True)]
    pallas_call x0 -> x14, Pallas kernels: none -> 125 us  [the longest x10 101 us: call(): pl.pallas_call(kernel, grid=(NS,), in_specs=ins, out_specs=outs, out_shap...]
    dot_general x44 -> x0, matrix products: 91.7 us -> none  [the longest x16 40.6 us: mm_hi(): return jnp.dot(a, b, precision=HI, preferred_element_type=f32)]
    ppermute x2 -> x26, waiting for transfers between devices: 10.5 us -> 69.1 us  [the longest x24 69.1 us: along_line(): return lax.ppermute(a, Y, [(i, (i + distance) % 4) for i in range(4)])]
    all_to_all x29 -> x18, starting transfers between devices: 168 us -> 113 us  [a2a(): return lax.all_to_all(a, axes, 0, 0, tiled=True)]
    all_gather x5 -> x3, waiting for transfers between devices: 46.3 us -> 0.01 us  [group_gather(): return lax.all_gather(block, ZX, axis=0, tiled=True)]
    reshape x34 -> x8, local copies, waits for them, and re-layouts: 51.8 us -> 5.66 us  [the longest x2 2.74 us: per_device(): both = in_sums[l].reshape(NG, 12, CA + W)]
    dot_general x18 -> x11, matrix products: 85.9 us -> 49.8 us  [mm(): lax.dot_general(a, b, (((ca,), (cb,)), ((), ())), preferred_element_type=...]
  transfers between devices with their start and end apart: 49 -> 72, of which waited for: 27 -> 35; matrix products, arithmetic and copies ran while one was open for 42% -> 19% of each run, Pallas kernels for 1% -> 11%
where the time goes in v2:
time: 750 us; the launch traced here: 739 us
  starting transfers between devices  205 us (27%)
  waiting for transfers between devices  154 us (21%)
  Pallas kernels  132 us (18%)
  local copies, waits for them, and re-layouts  86 us (11%)
  other arithmetic  71.9 us (10%)
  matrix products  49.8 us (7%)
  blocking collectives  24.2 us (3%)
  between operations  16.4 us (2%)
    all_to_all x18, starting transfers between devices, a2a(): return lax.all_to_all(a, axes, 0, 0, tiled=True)  113 us
    pallas_call x10, Pallas kernels, call(): pl.pallas_call(kernel, grid=(NS,), in_specs=ins, out_specs=outs, out_shap...  101 us
    all_to_all x18, waiting for transfers between devices, a2a(): return lax.all_to_all(a, axes, 0, 0, tiled=True)  74.7 us
    ppermute x24, waiting for transfers between devices, along_line(): return lax.ppermute(a, Y, [(i, (i + distance) % 4) for i in range(4)])  69.1 us
    dot_general x11, matrix products, mm(): lax.dot_general(a, b, (((ca,), (cb,)), ((), ())), preferred_element_type=...  49.8 us
    ppermute x20, starting transfers between devices, core_swap(): return lax.ppermute(a, 'c', [(0, 1), (1, 0)])  34 us
    ppermute x24, starting transfers between devices, along_line(): return lax.ppermute(a, Y, [(i, (i + distance) % 4) for i in range(4)])  31.2 us
    unnamed x262, local copies, waits for them, and re-layouts  28.8 us
  transfers between devices with their start and end apart: 72, of which 35 were waited for; matrix products, arithmetic and copies ran while one was open for 19% of the time, Pallas kernels for 11%

profile of v2, /device:TPU:1, one launch (start us, length us, event | category | flops | bytes accessed | tf_op | source)
XLA Modules:
  0.0 738.5 jit_solution(12058492674153060003)
XLA Ops:
  19.2 8.6 %all-to-all-done = bf16[8,2,12,1152]{3,1,2,0:T(2,128)(2,1)S(1)} async-done(((bf16[8,2,12,1152]{3,1,2,0:T(2,128)(2,1)}), bf16[8,2,12,1152]{3,1,2,0:T(2,128)(2,1)S(1)}, u32[]{:S(2)}, u32[]{:S(2)}) %all-to-all-start) | async-done | bytes 442400 | tf_op jit(solution)/shard_map/all_to_all | solution.py:52
  41.1 12.0 %all-to-all-start.1 = ((bf16[16,96,768]{2,1,0:T(8,128)(2,1)}), bf16[16,96,768]{2,1,0:T(8,128)(2,1)S(1)}, u32[]{:S(2)}, u32[]{:S(2)}) async-start(bf16[16,96,768]{2,1,0:T(8,128)(2,1)} %broadcast_in_dim.43), calls=%async_computation.1 | async-start | bytes 4718592 | tf_op jit(solution)/shard_map/all_to_all | solution.py:52
  88.7 6.7 all-to-all-start.2
  120.1 8.6 %span_mix.2 = (f32[1024,384]{1,0:T(8,128)}, f32[4,384,128]{2,1,0:T(8,128)}, f32[1024,128]{1,0:T(8,128)}, f32[1024,128]{1,0:T(8,128)}, f32[4,1,128]{2,1,0:T(1,128...) custom-call(s32[2,4]{1,0:T(2,128)} %pad_add_fusion.seg_ref, f32[1024,640]{1,0:T(8,128)} %get-tuple-element.282.v_ref, ...), custom_call_target="tpu_custom_call" | custom-call | flops 9600000000 | bytes 36000000 | tf_op jit(solution)/shard_map/span_mix/pallas_call | solution.py:548
  128.7 7.4 %all-to-all-start.3 = ((bf16[16,32,128]{2,1,0:T(8,128)(2,1)}), bf16[16,32,128]{2,1,0:T(8,128)(2,1)S(1)}, u32[]{:S(2)}, u32[]{:S(2)}) async-start(bf16[16,32,128]{2,1,0:T(8,128)(2,1)} %get-tuple-element.109), calls=%async_computation.3 | async-start | bytes 262144 | tf_op jit(solution)/shard_map/all_to_all | solution.py:52
  167.0 8.6 %span_gate.2 = (f32[1024,384]{1,0:T(8,128)}, bf16[1024,1536]{1,0:T(8,128)(2,1)}, f32[8,1024]{1,0:T(8,128)}) custom-call(s32[2,4]{1,0:T(2,128)} %pad_add_fusion.seg_ref, bf16[16,32,128]{2,1,0:T(8,128)(2,1)} %copy-done.60, f32[4,384,128]{2,1,0:T(8,128)} %get-tuple-element.114.local_ref, f32[4,1,128]{2,1,0:T(1,128)} %get-tuple-element.115.before_ref, ...), custom_call_target="tpu_custom_call" | custom-call | flops 8000000000 | bytes 30000000 | tf_op jit(solution)/shard_map/span_gate/pallas_call | solution.py:548
  194.5 12.3 %all-to-all-done.5 = f32[8,1,128]{2,1,0:T(1,128)} async-done(((f32[8,1,128]{2,1,0:T(1,128)}), f32[8,1,128]{2,1,0:T(1,128)}, u32[]{:S(2)}, u32[]{:S(2)}) %all-to-all-start.5) | async-done | bytes 4128 | tf_op jit(solution)/shard_map/all_to_all | solution.py:52
  218.0 7.6 %collective-permute-done.25.refs_6_ = bf16[128,1536]{1,0:T(8,128)(2,1)S(1)} collective-permute-done((bf16[128,1536]{1,0:T(8,128)(2,1)S(1)}, bf16[128,1536]{1,0:T(8,128)(2,1)S(1)}, u32[]{:S(2)}, u32[]{:S(2)}) %collective-permute-start.25) | collective-permute-done | bytes 393248 | tf_op jit(solution)/shard_map/ppermute | solution.py:64
  244.1 9.3 %fusion.93 = (bf16[1024,1152]{1,0:T(8,128)(2,1)S(1)}, f32[1024,1152]{1,0:T(8,128)}) fusion(bf16[1024,1536]{1,0:T(8,128)(2,1)} %place_tokens.6, bf16[1536,1152]{1,0:T(8,128)(2,1)} %all-gather.6.cloned.1.call-done), kind=kOutput, calls=%fused_computation.281 | convolution fusion | flops 3625058304 | bytes 13762560 | tf_op jit(solution)/shard_map/dot_general | solution.py:48
  262.8 8.6 %span_mix.3 = (f32[1024,384]{1,0:T(8,128)}, f32[4,384,128]{2,1,0:T(8,128)}, f32[1024,128]{1,0:T(8,128)}, f32[1024,128]{1,0:T(8,128)}, f32[4,1,128]{2,1,0:T(1,128...) custom-call(s32[2,4]{1,0:T(2,128)} %pad_add_fusion.seg_ref, f32[1024,640]{1,0:T(8,128)} %get-tuple-element.278.v_ref, ...), custom_call_target="tpu_custom_call" | custom-call | flops 9600000000 | bytes 36000000 | tf_op jit(solution)/shard_map/span_mix/pallas_call | solution.py:548
  271.3 13.2 %all_to_all.100.got_ref = bf16[16,32,128]{2,1,0:T(8,128)(2,1)} all-to-all(bf16[16,32,128]{2,1,0:T(8,128)(2,1)} %get-tuple-element.125), channel_id=1, replica_groups=mesh['z'=4,'x'=4,'yh'=2,'c'=2,'yl'=2] {'z','x'}, dimensions={0} | all-to-all | bytes 262144 | tf_op jit(solution)/shard_map/all_to_all | solution.py:52
  297.3 11.8 %span_gate.3 = (f32[1024,384]{1,0:T(8,128)}, bf16[1024,1536]{1,0:T(8,128)(2,1)}, f32[8,1024]{1,0:T(8,128)}) custom-call(s32[2,4]{1,0:T(2,128)} %pad_add_fusion.seg_ref, bf16[16,32,128]{2,1,0:T(8,128)(2,1)} %copy-done.61, f32[4,384,128]{2,1,0:T(8,128)} %get-tuple-element.126.local_ref, f32[4,1,128]{2,1,0:T(1,128)} %get-tuple-element.127.before_ref, ...), custom_call_target="tpu_custom_call" | custom-call | flops 8000000000 | bytes 30000000 | tf_op jit(solution)/shard_map/span_gate/pallas_call | solution.py:548
  310.5 7.7 %all-to-all-start.8 = ((f32[8,2,1024]{2,1,0:T(2,128)}), f32[8,2,1024]{2,1,0:T(2,128)S(1)}, u32[]{:S(2)}, u32[]{:S(2)}) async-start(f32[8,2,1024]{2,1,0:T(2,128)} %broadcast_in_dim.55), calls=%async_computation.8 | async-start | bytes 131072 | tf_op jit(solution)/shard_map/all_to_all | solution.py:52
  323.7 8.5 %span_gate_back.2 = (bf16[1024,384]{1,0:T(8,128)(2,1)}, bf16[1024,384]{1,0:T(8,128)(2,1)}, bf16[1024,384]{1,0:T(8,128)(2,1)}, f32[4,384,128]{2,1,0:T(8,128)}, f3...) custom-call(s32[2,4]{1,0:T(2,128)} %pad_add_fusion.seg_ref, bf16[1024,1536]{1,0:T(8,128)(2,1)} %place_tokens.5.rest_0_.grad_ref, ...), custom_call_target="tpu_custom_call" | custom-call | flops 9600000000 | bytes 36000000 | tf_op jit(solution)/shard_map/span_gate_back/pallas_call | solution.py:548
  332.2 11.0 %all_to_all.101.got_ref = bf16[16,32,128]{2,1,0:T(8,128)(2,1)} all-to-all(bf16[16,32,128]{2,1,0:T(8,128)(2,1)} %get-tuple-element.133), channel_id=1, replica_groups=mesh['z'=4,'x'=4,'yh'=2,'c'=2,'yl'=2] {'z','x'}, dimensions={0} | all-to-all | bytes 262144 | tf_op jit(solution)/shard_map/all_to_all | solution.py:52
  348.4 6.8 all-to-all-done.10.later_ref
  370.6 8.0 %span_mix_back.2 = (f32[1024,384]{1,0:T(8,128)}, f32[1024,256]{1,0:T(8,128)}) custom-call(f32[1024,640]{1,0:T(8,128)} %get-tuple-element.278.v_ref, f32[1024,128]{1,0:T(8,128)} %get-tuple-element.142.step_ref, f32[1024,128]{1,0:T(8,128)} %get-tuple-element.128.run_ref, s32[1024,1]{1,0:T(8,128)} %copy.307.segc_ref, s32[4,1,256]{2,1,0:T(1,128)} %bitcast.353, ...), custom_call_target="tpu_custom_call" | custom-call | flops 11200000000 | bytes 42000000 | tf_op jit(solution)/shard_map/span_mix_back/pallas_call | solution.py:548
  389.7 15.1 %span_end.2 = (f32[1024,640]{1,0:T(8,128)}, bf16[1024,128]{1,0:T(8,128)(2,1)}, f32[8,128]{1,0:T(8,128)}) custom-call(s32[2,4]{1,0:T(2,128)} %pad_add_fusion.seg_ref, bf16[16,32,128]{2,1,0:T(8,128)(2,1)} %copy-done.62, bf16[16,32,128]{2,1,0:T(8,128)(2,1)} %copy-done.61, f32[4,384,128]{2,1,0:T(8,128)} %get-tuple-element.126.local_ref, ...), custom_call_target="tpu_custom_call" | custom-call | flops 12800000000 | bytes 48000000 | tf_op jit(solution)/shard_map/span_end/pallas_call | solution.py:548
  426.6 8.5 %all-to-all-start.12 = ((bf16[16,96,1152]{2,1,0:T(8,128)(2,1)}), bf16[16,96,1152]{2,1,0:T(8,128)(2,1)}, u32[]{:S(2)}, u32[]{:S(2)}) async-start(bf16[16,96,1152]{2,1,0:T(8,128)(2,1)} %bitcast.70), calls=%async_computation.12 | async-start | bytes 7077888 | tf_op jit(solution)/shard_map/all_to_all | solution.py:52
  450.0 9.9 %collective-permute-done.36 = bf16[128,1536]{1,0:T(8,128)(2,1)} collective-permute-done((bf16[128,1536]{1,0:T(8,128)(2,1)}, bf16[128,1536]{1,0:T(8,128)(2,1)}, u32[]{:S(2)}, u32[]{:S(2)}) %collective-permute-start.36) | collective-permute-done | bytes 393248 | tf_op jit(solution)/shard_map/ppermute | solution.py:64
  512.9 8.5 %span_gate_back.3 = (bf16[1024,384]{1,0:T(8,128)(2,1)}, bf16[1024,384]{1,0:T(8,128)(2,1)}, bf16[1024,384]{1,0:T(8,128)(2,1)}, f32[4,384,128]{2,1,0:T(8,128)}, f3...) custom-call(s32[2,4]{1,0:T(2,128)} %pad_add_fusion.seg_ref, bf16[1024,1536]{1,0:T(8,128)(2,1)} %get-tuple-element.152.grad_ref, ...), custom_call_target="tpu_custom_call" | custom-call | flops 9600000000 | bytes 36000000 | tf_op jit(solution)/shard_map/span_gate_back/pallas_call | solution.py:548
  521.4 6.6 all-to-all-start.13
  542.8 8.0 %span_mix_back.3 = (f32[1024,384]{1,0:T(8,128)}, f32[1024,256]{1,0:T(8,128)}) custom-call(f32[1024,640]{1,0:T(8,128)} %get-tuple-element.282.v_ref, f32[1024,128]{1,0:T(8,128)} %get-tuple-element.162.step_ref, f32[1024,128]{1,0:T(8,128)} %get-tuple-element.116.run_ref, s32[1024,1]{1,0:T(8,128)} %copy.307.segc_ref, s32[4,1,256]{2,1,0:T(1,128)} %bitcast.354, ...), custom_call_target="tpu_custom_call" | custom-call | flops 11200000000 | bytes 42000000 | tf_op jit(solution)/shard_map/span_mix_back/pallas_call | solution.py:548
  555.8 15.3 %span_end.3 = (f32[1024,640]{1,0:T(8,128)}, bf16[1024,128]{1,0:T(8,128)(2,1)}, f32[8,128]{1,0:T(8,128)}) custom-call(s32[2,4]{1,0:T(2,128)} %pad_add_fusion.seg_ref, bf16[16,32,128]{2,1,0:T(8,128)(2,1)} %copy-done.63, bf16[16,32,128]{2,1,0:T(8,128)(2,1)} %copy-done.60, f32[4,384,128]{2,1,0:T(8,128)} %get-tuple-element.114.local_ref, ...), custom_call_target="tpu_custom_call" | custom-call | flops 12800000000 | bytes 48000000 | tf_op jit(solution)/shard_map/span_end/pallas_call | solution.py:548
  571.1 9.2 %multiply_reduce_fusion = (bf16[640]{0:T(1024)(128)(2,1)S(1)}, bf16[640]{0:T(1024)(128)(2,1)S(1)}, bf16[640]{0:T(1024)(128)(2,1)S(1)}, bf16[640]{0:T(1024)(128)(...) fusion(f32[1024,640]{1,0:T(8,128)} %get-tuple-element.148, ...), kind=kLoop, calls=%fused_computation.34 | loop fusion | flops 15722240 | bytes 26239488 | tf_op jit(solution)/shard_map/reduce_sum | solution.py:820
  608.6 8.0 %all-to-all-start.19 = ((bf16[16,24,1536]{2,1,0:T(8,128)(2,1)}), bf16[16,24,1536]{2,1,0:T(8,128)(2,1)S(1)}, u32[]{:S(2)}, u32[]{:S(2)}) async-start(bf16[16,24,1536]{2,1,0:T(8,128)(2,1)} %bitcast.329), calls=%async_computation.19 | async-start | bytes 2359296 | tf_op jit(solution)/shard_map/all_to_all | solution.py:52
  624.2 10.6 %all-to-all-done.19 = bf16[16,24,1536]{2,1,0:T(8,128)(2,1)S(1)} async-done(((bf16[16,24,1536]{2,1,0:T(8,128)(2,1)}), bf16[16,24,1536]{2,1,0:T(8,128)(2,1)S(1)}, u32[]{:S(2)}, u32[]{:S(2)}) %all-to-all-start.19) | async-done | bytes 1179680 | tf_op jit(solution)/shard_map/all_to_all | solution.py:52
  647.2 9.3 %all-to-all-done.16 = bf16[16,96,384]{2,1,0:T(8,128)(2,1)S(1)} async-done(((bf16[16,96,384]{2,1,0:T(8,128)(2,1)}), bf16[16,96,384]{2,1,0:T(8,128)(2,1)S(1)}, u32[]{:S(2)}, u32[]{:S(2)}) %all-to-all-start.16) | async-done | bytes 1179680 | tf_op jit(solution)/shard_map/all_to_all | solution.py:52
  656.5 9.8 %all-to-all-start.15 = ((bf16[16,96,768]{2,1,0:T(8,128)(2,1)}), bf16[16,96,768]{2,1,0:T(8,128)(2,1)}, u32[]{:S(2)}, u32[]{:S(2)}) async-start(bf16[16,96,768]{2,1,0:T(8,128)(2,1)} %bitcast.318), calls=%async_computation.15 | async-start | bytes 4718592 | tf_op jit(solution)/shard_map/all_to_all | solution.py:52
  680.8 8.4 %collective-permute-done.48 = bf16[128,1536]{1,0:T(8,128)(2,1)S(1)} collective-permute-done((bf16[128,1536]{1,0:T(8,128)(2,1)S(1)}, bf16[128,1536]{1,0:T(8,128)(2,1)S(1)}, u32[]{:S(2)}, u32[]{:S(2)}) %collective-permute-start.48) | collective-permute-done | bytes 393248 | tf_op jit(solution)/shard_map/ppermute | solution.py:64
  690.6 11.1 %all-to-all-done.15 = bf16[16,96,768]{2,1,0:T(8,128)(2,1)} async-done(((bf16[16,96,768]{2,1,0:T(8,128)(2,1)}), bf16[16,96,768]{2,1,0:T(8,128)(2,1)}, u32[]{:S(2)}, u32[]{:S(2)}) %all-to-all-start.15) | async-done | bytes 2359328 | tf_op jit(solution)/shard_map/all_to_all | solution.py:52
  715.1 7.6 %all-to-all-done.17 = f32[8,12,1152]{2,1,0:T(8,128)} async-done(((f32[8,12,1152]{2,1,0:T(8,128)}), f32[8,12,1152]{2,1,0:T(8,128)}, u32[]{:S(2)}, u32[]{:S(2)}) %all-to-all-start.17) | async-done | bytes 442400 | tf_op jit(solution)/shard_map/all_to_all | solution.py:52
  (651 shorter events, 419.5 us)
Async XLA Ops:
  19.2 147.1 %all-gather.8.cloned.1.call-start = ((), (), s32[]{:S(2)}) async-start(), calls=%async_computation.21 | async-start | bytes 1253376 | tf_op jit(solution)/shard_map/all_gather | solution.py:149
  41.1 45.7 %all-to-all-start.1 = ((bf16[16,96,768]{2,1,0:T(8,128)(2,1)}), bf16[16,96,768]{2,1,0:T(8,128)(2,1)S(1)}, u32[]{:S(2)}, u32[]{:S(2)}) async-start(bf16[16,96,768]{2,1,0:T(8,128)(2,1)} %broadcast_in_dim.43), calls=%async_computation.1 | async-start | bytes 4718592 | tf_op jit(solution)/shard_map/all_to_all | solution.py:52
  53.1 157.3 %all-gather.10.cloned.1.call-start = ((), (), s32[]{:S(2)}) async-start(), calls=%async_computation.22 | async-start | bytes 1253376 | tf_op jit(solution)/shard_map/all_gather | solution.py:149
  53.8 156.6 %all-gather.6.cloned.1.call-start = ((), (), s32[]{:S(2)}) async-start(), calls=%async_computation.20 | async-start | bytes 3760128 | tf_op jit(solution)/shard_map/all_gather | solution.py:149
  55.0 18.9 %collective-permute-start.3 = (bf16[128,1536]{1,0:T(8,128)(2,1)S(1)}, bf16[128,1536]{1,0:T(8,128)(2,1)}, u32[]{:S(2)}, u32[]{:S(2)}) collective-permute-start(bf16[128,1536]{1,0:T(8,128)(2,1)S(1)} %fusion.22.refs_0_), channel_id=1, source_target_pairs={{0,5},{1,0},{4,1},{5,4},{2,7},{3,2},{6,3},{7,6},{8,13},{9,8},{12,9... | collective-permute-start | bytes 1179656 | tf_op jit(solution)/shard_map/ppermute | solution.py:64
  57.4 18.7 %collective-permute-start.1 = (bf16[128,1536]{1,0:T(8,128)(2,1)S(1)}, bf16[128,1536]{1,0:T(8,128)(2,1)}, u32[]{:S(2)}, u32[]{:S(2)}) collective-permute-start(bf16[128,1536]{1,0:T(8,128)(2,1)S(1)} %fusion.22.refs_0_), channel_id=1, source_target_pairs={{0,1},{1,4},{4,5},{5,0},{2,3},{3,6},{6,7},{7,2},{8,9},{9,12},{12,1... | collective-permute-start | bytes 1179656 | tf_op jit(solution)/shard_map/ppermute | solution.py:64
  58.8 22.1 %collective-permute-start = (bf16[128,1536]{1,0:T(8,128)(2,1)S(1)}, bf16[128,1536]{1,0:T(8,128)(2,1)}, u32[]{:S(2)}, u32[]{:S(2)}) collective-permute-start(bf16[128,1536]{1,0:T(8,128)(2,1)S(1)} %fusion.22.refs_0_), channel_id=1, source_target_pairs={{0,2},{2,0},{1,3},{3,1},{4,6},{6,4},{5,7},{7,5},{8,10},{10,8},{9,1... | collective-permute-start | bytes 1179656 | tf_op jit(solution)/shard_map/ppermute | solution.py:56
  88.7 40.1 %all-to-all-start.2 = ((bf16[16,96,384]{2,1,0:T(8,128)(2,1)}), bf16[16,96,384]{2,1,0:T(8,128)(2,1)S(1)}, u32[]{:S(2)}, u32[]{:S(2)}) async-start(bf16[16,96,384]{2,1,0:T(8,128)(2,1)} %broadcast_in_dim.49), calls=%async_computation.2 | async-start | bytes 2359296 | tf_op jit(solution)/shard_map/all_to_all | solution.py:52
  97.2 52.7 %collective-permute-start.13 = (bf16[128,1536]{1,0:T(8,128)(2,1)}, bf16[128,1536]{1,0:T(8,128)(2,1)}, u32[]{:S(2)}, u32[]{:S(2)}) collective-permute-start(bf16[128,1536]{1,0:T(8,128)(2,1)} %refs_0_), channel_id=1, source_target_pairs={{0,4},{1,5},{4,0},{5,1},{2,6},{3,7},{6,2},{7,3},{8,12},{9,13},{12,... | collective-permute-start | bytes 1179656 | tf_op jit(solution)/shard_map/ppermute | solution.py:64
  97.9 55.4 %collective-permute-start.11 = (bf16[128,1536]{1,0:T(8,128)(2,1)}, bf16[128,1536]{1,0:T(8,128)(2,1)}, u32[]{:S(2)}, u32[]{:S(2)}) collective-permute-start(bf16[128,1536]{1,0:T(8,128)(2,1)} %refs_0_), channel_id=1, source_target_pairs={{0,5},{1,0},{4,1},{5,4},{2,7},{3,2},{6,3},{7,6},{8,13},{9,8},{12,9... | collective-permute-start | bytes 1179656 | tf_op jit(solution)/shard_map/ppermute | solution.py:64
  101.1 52.3 %collective-permute-start.9 = (bf16[128,1536]{1,0:T(8,128)(2,1)}, bf16[128,1536]{1,0:T(8,128)(2,1)}, u32[]{:S(2)}, u32[]{:S(2)}) collective-permute-start(bf16[128,1536]{1,0:T(8,128)(2,1)} %refs_0_), channel_id=1, source_target_pairs={{0,1},{1,4},{4,5},{5,0},{2,3},{3,6},{6,7},{7,2},{8,9},{9,12},{12,1... | collective-permute-start | bytes 1179656 | tf_op jit(solution)/shard_map/ppermute | solution.py:64
  137.5 21.2 %collective-permute-start.8 = (bf16[128,1536]{1,0:T(8,128)(2,1)}, bf16[128,1536]{1,0:T(8,128)(2,1)S(1)}, u32[]{:S(2)}, u32[]{:S(2)}) collective-permute-start(bf16[128,1536]{1,0:T(8,128)(2,1)} %refs_0_), channel_id=1, source_target_pairs={{0,2},{2,0},{1,3},{3,1},{4,6},{6,4},{5,7},{7,5},{8,10},{10,8},{9,1... | collective-permute-start | bytes 1179656 | tf_op jit(solution)/shard_map/ppermute | solution.py:56
  145.4 20.9 %all-to-all-start.4 = ((bf16[16,32,128]{2,1,0:T(8,128)(2,1)}), bf16[16,32,128]{2,1,0:T(8,128)(2,1)S(1)}, u32[]{:S(2)}, u32[]{:S(2)}) async-start(bf16[16,32,128]{2,1,0:T(8,128)(2,1)} %group_scan.4), calls=%async_computation.4 | async-start | bytes 262144 | tf_op jit(solution)/shard_map/all_to_all | solution.py:52
  184.3 23.8 %collective-permute-start.17 = (bf16[128,1536]{1,0:T(8,128)(2,1)}, bf16[128,1536]{1,0:T(8,128)(2,1)}, u32[]{:S(2)}, u32[]{:S(2)}) collective-permute-start(bf16[128,1536]{1,0:T(8,128)(2,1)} %get-tuple-element.293), channel_id=1, source_target_pairs={{0,1},{1,4},{4,5},{5,0},{2,3},{3,6},{6,7},{7,2},{8,9},{9,12},{12,1... | collective-permute-start | bytes 1179656 | tf_op jit(solution)/shard_map/ppermute | solution.py:64
  185.3 22.8 %collective-permute-start.19 = (bf16[128,1536]{1,0:T(8,128)(2,1)}, bf16[128,1536]{1,0:T(8,128)(2,1)}, u32[]{:S(2)}, u32[]{:S(2)}) collective-permute-start(bf16[128,1536]{1,0:T(8,128)(2,1)} %get-tuple-element.294), channel_id=1, source_target_pairs={{0,4},{1,5},{4,0},{5,1},{2,6},{3,7},{6,2},{7,3},{8,12},{9,13},{12,... | collective-permute-start | bytes 1179656 | tf_op jit(solution)/shard_map/ppermute | solution.py:64
  188.5 19.6 %collective-permute-start.18 = (bf16[128,1536]{1,0:T(8,128)(2,1)}, bf16[128,1536]{1,0:T(8,128)(2,1)}, u32[]{:S(2)}, u32[]{:S(2)}) collective-permute-start(bf16[128,1536]{1,0:T(8,128)(2,1)} %get-tuple-element.295), channel_id=1, source_target_pairs={{0,5},{1,0},{4,1},{5,4},{2,7},{3,2},{6,3},{7,6},{8,13},{9,8},{12,9... | collective-permute-start | bytes 1179656 | tf_op jit(solution)/shard_map/ppermute | solution.py:64
  214.7 18.8 %collective-permute-start.23 = (bf16[128,1536]{1,0:T(8,128)(2,1)S(1)}, bf16[128,1536]{1,0:T(8,128)(2,1)S(1)}, u32[]{:S(2)}, u32[]{:S(2)}) collective-permute-start(bf16[128,1536]{1,0:T(8,128)(2,1)S(1)} %multiply_convert_fusion.refs_0_), channel_id=1, source_target_pairs={{0,5},{1,0},{4,1},{5,4},{2,7},{3,2},{6,3},{7,6},{8,13},{9,8},{12,9... | collective-permute-start | bytes 1179656 | tf_op jit(solution)/shard_map/ppermute | solution.py:64
  216.2 20.3 %collective-permute-start.20 = (bf16[128,1536]{1,0:T(8,128)(2,1)S(1)}, bf16[128,1536]{1,0:T(8,128)(2,1)S(1)}, u32[]{:S(2)}, u32[]{:S(2)}) collective-permute-start(bf16[128,1536]{1,0:T(8,128)(2,1)S(1)} %multiply_convert_fusion.refs_0_), channel_id=1, source_target_pairs={{0,2},{2,0},{1,3},{3,1},{4,6},{6,4},{5,7},{7,5},{8,10},{10,8},{9,1... | collective-permute-start | bytes 1179656 | tf_op jit(solution)/shard_map/ppermute | solution.py:56
  320.9 42.6 %collective-permute-start.28 = (bf16[2,2,128,1536]{3,2,1,0:T(8,128)(2,1)}, bf16[2,2,128,1536]{3,2,1,0:T(8,128)(2,1)S(1)}, u32[]{:S(2)}, u32[]{:S(2)}) collective-permute-start(bf16[2,2,128,1536]{3,2,1,0:T(8,128)(2,1)} %dynamic-slice_bitcast_fusion), channel_id=1, source_target_pairs={{0,2},{2,0},{1,3},{3,1},{4,6},{6,4},{5,7},{7,5},{8,10},{10,8},{9,1... | collective-permute-start | bytes 4718600 | tf_op jit(solution)/shard_map/ppermute | solution.py:56
  359.8 19.5 %all-to-all-start.11 = ((bf16[16,24,1536]{2,1,0:T(8,128)(2,1)}), bf16[16,24,1536]{2,1,0:T(8,128)(2,1)S(1)}, u32[]{:S(2)}, u32[]{:S(2)}) async-start(bf16[16,24,1536]{2,1,0:T(8,128)(2,1)} %bitcast.330), calls=%async_computation.11 | async-start | bytes 2359296 | tf_op jit(solution)/shard_map/all_to_all | solution.py:52
  426.6 83.7 %all-to-all-start.12 = ((bf16[16,96,1152]{2,1,0:T(8,128)(2,1)}), bf16[16,96,1152]{2,1,0:T(8,128)(2,1)}, u32[]{:S(2)}, u32[]{:S(2)}) async-start(bf16[16,96,1152]{2,1,0:T(8,128)(2,1)} %bitcast.70), calls=%async_computation.12 | async-start | bytes 7077888 | tf_op jit(solution)/shard_map/all_to_all | solution.py:52
  441.2 18.7 %collective-permute-start.36 = (bf16[128,1536]{1,0:T(8,128)(2,1)}, bf16[128,1536]{1,0:T(8,128)(2,1)}, u32[]{:S(2)}, u32[]{:S(2)}) collective-permute-start(bf16[128,1536]{1,0:T(8,128)(2,1)} %get-tuple-element.288), channel_id=1, source_target_pairs={{0,4},{1,5},{4,0},{5,1},{2,6},{3,7},{6,2},{7,3},{8,12},{9,13},{12,... | collective-permute-start | bytes 1179656 | tf_op jit(solution)/shard_map/ppermute | solution.py:64
  476.4 21.9 %collective-permute-start.40 = (bf16[144,1536]{1,0:T(8,128)(2,1)S(1)}, bf16[144,1536]{1,0:T(8,128)(2,1)S(1)}, u32[]{:S(2)}, u32[]{:S(2)}) collective-permute-start(bf16[144,1536]{1,0:T(8,128)(2,1)S(1)} %fusion.38.refs_0_), channel_id=1, source_target_pairs={{0,5},{1,0},{4,1},{5,4},{2,7},{3,2},{6,3},{7,6},{8,13},{9,8},{12,9... | collective-permute-start | bytes 1327112 | tf_op jit(solution)/shard_map/ppermute | solution.py:64
  479.2 20.4 %collective-permute-start.38 = (bf16[144,1536]{1,0:T(8,128)(2,1)S(1)}, bf16[144,1536]{1,0:T(8,128)(2,1)S(1)}, u32[]{:S(2)}, u32[]{:S(2)}) collective-permute-start(bf16[144,1536]{1,0:T(8,128)(2,1)S(1)} %fusion.38.refs_0_), channel_id=1, source_target_pairs={{0,1},{1,4},{4,5},{5,0},{2,3},{3,6},{6,7},{7,2},{8,9},{9,12},{12,1... | collective-permute-start | bytes 1327112 | tf_op jit(solution)/shard_map/ppermute | solution.py:64
  479.2 20.9 %collective-permute-start.37 = (bf16[144,1536]{1,0:T(8,128)(2,1)S(1)}, bf16[144,1536]{1,0:T(8,128)(2,1)S(1)}, u32[]{:S(2)}, u32[]{:S(2)}) collective-permute-start(bf16[144,1536]{1,0:T(8,128)(2,1)S(1)} %fusion.38.refs_0_), channel_id=1, source_target_pairs={{0,2},{2,0},{1,3},{3,1},{4,6},{6,4},{5,7},{7,5},{8,10},{10,8},{9,1... | collective-permute-start | bytes 1327112 | tf_op jit(solution)/shard_map/ppermute | solution.py:56
  529.0 146.9 %collective-permute-start.50 = (f32[24,1536]{1,0:T(8,128)}, f32[24,1536]{1,0:T(8,128)}, u32[]{:S(2)}, u32[]{:S(2)}) collective-permute-start(f32[24,1536]{1,0:T(8,128)} %convert_reduce_fusion.4), channel_id=1, source_target_pairs={{0,0},{8,1},{16,2},{24,3},{32,4},{40,5},{48,6},{56,7},{64,8},{72,9... | collective-permute-start | bytes 442376 | tf_op jit(solution)/shard_map/ppermute | solution.py:861
  551.7 56.9 %all-to-all-start.18 = ((f32[8,12,1152]{2,1,0:T(8,128)}), f32[8,12,1152]{2,1,0:T(8,128)S(1)}, u32[]{:S(2)}, u32[]{:S(2)}) async-start(f32[8,12,1152]{2,1,0:T(8,128)} %reshape.587), calls=%async_computation.18 | async-start | bytes 1179648 | tf_op jit(solution)/shard_map/all_to_all | solution.py:52
  608.6 58.6 %collective-permute-start.45 = (bf16[2,2,128,1536]{3,2,1,0:T(8,128)(2,1)}, bf16[2,2,128,1536]{3,2,1,0:T(8,128)(2,1)}, u32[]{:S(2)}, u32[]{:S(2)}) collective-permute-start(bf16[2,2,128,1536]{3,2,1,0:T(8,128)(2,1)} %fusion.15), channel_id=1, source_target_pairs={{0,2},{2,0},{1,3},{3,1},{4,6},{6,4},{5,7},{7,5},{8,10},{10,8},{9,1... | collective-permute-start | bytes 4718600 | tf_op jit(solution)/shard_map/ppermute | solution.py:56
  608.6 26.2 %all-to-all-start.19 = ((bf16[16,24,1536]{2,1,0:T(8,128)(2,1)}), bf16[16,24,1536]{2,1,0:T(8,128)(2,1)S(1)}, u32[]{:S(2)}, u32[]{:S(2)}) async-start(bf16[16,24,1536]{2,1,0:T(8,128)(2,1)} %bitcast.329), calls=%async_computation.19 | async-start | bytes 2359296 | tf_op jit(solution)/shard_map/all_to_all | solution.py:52
  634.8 21.7 %all-to-all-start.16 = ((bf16[16,96,384]{2,1,0:T(8,128)(2,1)}), bf16[16,96,384]{2,1,0:T(8,128)(2,1)S(1)}, u32[]{:S(2)}, u32[]{:S(2)}) async-start(bf16[16,96,384]{2,1,0:T(8,128)(2,1)} %bitcast.328), calls=%async_computation.16 | async-start | bytes 2359296 | tf_op jit(solution)/shard_map/all_to_all | solution.py:52
  641.1 34.8 %collective-permute-start.49 = (f32[24,1536]{1,0:T(8,128)}, f32[24,1536]{1,0:T(8,128)}, u32[]{:S(2)}, u32[]{:S(2)}) collective-permute-start(f32[24,1536]{1,0:T(8,128)} %convert_reduce_fusion.2), channel_id=1, source_target_pairs={{0,0},{8,1},{16,2},{24,3},{32,4},{40,5},{48,6},{56,7},{64,8},{72,9... | collective-permute-start | bytes 442376 | tf_op jit(solution)/shard_map/ppermute | solution.py:861
  656.5 45.1 %all-to-all-start.15 = ((bf16[16,96,768]{2,1,0:T(8,128)(2,1)}), bf16[16,96,768]{2,1,0:T(8,128)(2,1)}, u32[]{:S(2)}, u32[]{:S(2)}) async-start(bf16[16,96,768]{2,1,0:T(8,128)(2,1)} %bitcast.318), calls=%async_computation.15 | async-start | bytes 4718592 | tf_op jit(solution)/shard_map/all_to_all | solution.py:52
  (166 other events, 1506.6 us)
Sparse Core Ops, SparseCore 0:
  36.9 70.0 all-gather.7
  109.1 47.3 all-gather.9
  158.7 49.8 all-gather.5

commit v3 on v2

--- a/solution.py
+++ b/solution.py
@@ -64,21 +64,52 @@
     return lax.ppermute(a, Y, [(i, (i + distance) % 4) for i in range(4)])
 
 
-def place_kernel(extra, pos_ref, *refs):
-    blocks, outs = refs[:NG], refs[NG:]
-    step = pl.program_id(0)
+def fill_places(pos_ref, blocks, x_ref):
     for i, block in enumerate(blocks):
-
-        @pl.when(step == i)
-        def _(block=block):
-            outs[0][...] = block[:TOK]
-            if extra:
-                outs[1][...] = block[TOK:]
-
-
-def line_gather(own):
-    rows, n = own.shape
-    extra = rows - TOK
+        at = pl.multiple_of(pos_ref[i] * TOK, TOK)
+        x_ref[pl.ds(at, TOK)] = block[:TOK]
+
+
+def place_kernel(pos_ref, *refs):
+    blocks, (out_ref, extra_ref, x_ref) = refs[:NG], refs[NG:]
+    k = pl.program_id(0)
+
+    @pl.when(k == 0)
+    def _():
+        fill_places(pos_ref, blocks, x_ref)
+        for i, block in enumerate(blocks):
+            extra_ref[pl.ds(pl.multiple_of(pos_ref[i] * 16, 16), 16)] = block[TOK:]
+
+    out_ref[...] = x_ref[pl.ds(pl.multiple_of(k * SPAN, SPAN), SPAN)]
+
+
+def place_plain_kernel(pos_ref, *refs):
+    blocks, (out_ref, x_ref) = refs[:NG], refs[NG:]
+    k = pl.program_id(0)
+
+    @pl.when(k == 0)
+    def _():
+        fill_places(pos_ref, blocks, x_ref)
+
+    out_ref[...] = x_ref[pl.ds(pl.multiple_of(k * SPAN, SPAN), SPAN)]
+
+
+def place_project_kernel(pos_ref, *refs):
+    blocks, (w_ref, out_ref, u_ref, raw_ref, x_ref) = refs[:NG], refs[NG:]
+    k = pl.program_id(0)
+
+    @pl.when(k == 0)
+    def _():
+        fill_places(pos_ref, blocks, x_ref)
+
+    x = x_ref[pl.ds(pl.multiple_of(k * SPAN, SPAN), SPAN)]
+    out_ref[...] = x
+    project = jnp.dot(x, w_ref[...], preferred_element_type=f32).astype(bf)
+    u_ref[...] = project[:, :CC]
+    raw_ref[...] = project[:, CC:]
+
+
+def line_blocks(own, first=None):
     y, core = line_index(), lax.axis_index("c")
     blocks, places = [], []
 
@@ -88,61 +119,175 @@
 
     for d in (0, 1, 3, 2):
         got = along_line(own, d) if d else own
+        if d and first is not None:
+            got = wait_for(got, first)
         blocks += [got, core_swap(got)]
         places += [place(d, core), place(d, 1 - core)]
-    shapes = [struct((GT, n), own.dtype)]
-    if extra:
-        shapes.append(struct((NG * extra, n), own.dtype))
-    outs = pl.pallas_call(
-        functools.partial(place_kernel, extra),
+    return jnp.stack(places).astype(jnp.int32), blocks
+
+
+X_SCRATCH = pltpu.VMEM((GT, D), bf)
+
+
+def place_tokens(places, blocks):
+    return call(
+        place_plain_kernel,
+        "place_tokens",
+        [SMEM] + [whole(TOK, D)] * NG,
+        tok_block(D),
+        struct((GT, D), bf),
+        [X_SCRATCH],
+        (places, *blocks),
+        4,
+    )
+
+
+def line_gather_more(own, first):
+    places, blocks = line_blocks(own, first)
+    return call(
+        place_kernel,
+        "place_gradient",
+        [SMEM] + [whole(TOK + 16, D)] * NG,
+        [tok_block(D), whole(NG * 16, D)],
+        [struct((GT, D), bf), struct((NG * 16, D), bf)],
+        [X_SCRATCH],
+        (places, *blocks),
+        4,
+    )
+
+
+def line_project(own, weight):
+    return place_project(*line_blocks(own), weight)
+
+
+def place_project(places, blocks, weight):
+    return call(
+        place_project_kernel,
+        "place_project",
+        [SMEM] + [whole(TOK, D)] * NG + [whole(D, CA)],
+        [tok_block(D), tok_block(CC), tok_block(128)],
+        [struct((GT, D), bf), struct((GT, CC), bf), struct((GT, 128), bf)],
+        [X_SCRATCH],
+        (places, *blocks, weight),
+        9,
+    )
+
+
+def chip_kernel(y_ref, mine_ref, got_ref, own_ref, *sent_refs):
+    def rows(distance):
+        at = pl.multiple_of((y_ref[0] + distance) % 4 * TOK, TOK)
+        return mine_ref[pl.ds(at, TOK)].astype(f32) + got_ref[pl.ds(at, TOK)].astype(f32)
+
+    own_ref[...] = rows(0)
+    for distance, ref in zip((1, 3, 2), sent_refs):
+        ref[...] = rows(distance).astype(bf)
+
+
+def line_parts(other, mine, first=None):
+    got = core_swap(other)
+    if first is not None:
+        got = wait_for(got, first)
+    own, *sent = pl.pallas_call(
+        chip_kernel,
+        out_shape=[struct((TOK, D))] + [struct((TOK, D), bf)] * 3,
+        in_specs=[SMEM] + [pl.BlockSpec(memory_space=pltpu.VMEM)] * 2,
+        out_specs=[pl.BlockSpec(memory_space=pltpu.VMEM)] * 4,
+        compiler_params=pltpu.CompilerParams(vmem_limit_bytes=60 * 1024 * 1024),
+        name="chip_sum",
+    )(line_index().reshape(1).astype(jnp.int32), mine, got)
+    return [own] + [along_line(block, d) for block, d in zip(sent, (1, 3, 2))]
+
+
+def span_order():
+    core = lax.axis_index("c")
+    return jnp.stack([1 - core, 3 - core, core, 2 + core]).astype(jnp.int32)
+
+
+def write_half(other_ref, mine_ref, value):
+    i = pl.program_id(0)
+
+    @pl.when(i < 2)
+    def _():
+        other_ref[...] = value
+
+    @pl.when(i >= 2)
+    def _():
+        mine_ref[...] = value
+
+
+def parts_sum(refs):
+    total = refs[0][...]
+    for ref in refs[1:]:
+        total = total + ref[...].astype(f32)
+    return total
+
+
+def inverse_rms(a):
+    return lax.rsqrt(jnp.mean(a * a, axis=1, keepdims=True) + EPS)
+
+
+def advance_kernel(p0, p1, p2, p3, square_ref, h_ref, out_ref, branch_ref, normed_ref, scale_ref):
+    square = jnp.sum(square_ref[...], axis=0, keepdims=True)
+    r_gate = jnp.broadcast_to(lax.rsqrt(square / DI + EPS), (8, TOK))
+    scale_ref[...] = r_gate
+    branch = parts_sum((p0, p1, p2, p3)) * r_gate.T[:, 0:1]
+    h = h_ref[...] + branch
+    out_ref[...] = h
+    branch_ref[...] = branch
+    normed_ref[...] = (h * inverse_rms(h)).astype(bf)
+
+
+def in_parts(row):
+    hi = row.astype(bf).astype(f32)
+    mid = (row - hi).astype(bf).astype(f32)
+    return [hi, mid, row - hi - mid]
+
+
+def retreat_kernel(extra, p0, p1, p2, p3, h_ref, grad_ref, *refs):
+    h = h_ref[...]
+    r_in = inverse_rms(h)
+    d_norm = parts_sum((p0, p1, p2, p3))
+    inner = jnp.mean(h * d_norm, axis=1, keepdims=True)
+    grad = grad_ref[...].astype(f32) + r_in * d_norm - h * (r_in * r_in * r_in * inner)
+    if not extra:
+        refs[0][...] = grad
+        return
+    branch_ref, scale_ref, out_ref, sent_ref = refs
+    out_ref[...] = grad
+    low = grad.astype(bf)
+    r_gate = scale_ref[...]
+    column = jnp.sum(low.astype(f32) * branch_ref[...], axis=1, keepdims=True)
+    row = jnp.broadcast_to(column, (TOK, 128)).T[:8]
+    kappa = r_gate * r_gate * row / DI
+    rows = in_parts(r_gate) + in_parts(kappa)
+    rows = jnp.concatenate(rows + [jnp.zeros((8, D - 6 * TOK), f32)], axis=1)
+    sent_ref[:TOK] = low
+    sent_ref[TOK:] = jnp.concatenate([rows, jnp.zeros((8, D), f32)], axis=0).astype(bf)
+
+
+def plain_call(kernel, name, shapes, args):
+    return pl.pallas_call(
+        kernel,
         out_shape=shapes,
-        grid_spec=pltpu.PrefetchScalarGridSpec(
-            num_scalar_prefetch=1,
-            grid=(NG,),
-            in_specs=[pl.BlockSpec((rows, n), lambda i, pos: (0, 0))] * NG,
-            out_specs=[pl.BlockSpec((TOK, n), lambda i, pos: (pos[i], 0))]
-            + [pl.BlockSpec((extra, n), lambda i, pos: (pos[i], 0))] * (extra > 0),
+        compiler_params=pltpu.CompilerParams(vmem_limit_bytes=60 * 1024 * 1024),
+        cost_estimate=pl.CostEstimate(
+            flops=int(2e8), bytes_accessed=int(1e6), transcendentals=0
         ),
-        compiler_params=pltpu.CompilerParams(vmem_limit_bytes=60 * 1024 * 1024),
-        name="place_tokens",
-    )(jnp.stack(places).astype(jnp.int32), *blocks)
-    return outs if extra else outs[0]
-
-
-def line_reduce(part):
-    n = part.shape[1]
-    core, y = lax.axis_index("c"), line_index()
-    blocks = part.reshape(2, 2, 2, TOK, n)
-    mine = lax.dynamic_index_in_dim(blocks, core, 1, keepdims=False)
-    other = lax.dynamic_index_in_dim(blocks, 1 - core, 1, keepdims=False)
-    got = core_swap(other.astype(bf))
-    chip = (mine.astype(f32) + got.astype(f32)).reshape(4, TOK, n)
-    total = lax.dynamic_index_in_dim(chip, y, 0, keepdims=False)
-    chip = chip.astype(bf)
-    for d in (1, 3, 2):
-        sent = lax.dynamic_index_in_dim(chip, (y + d) % 4, 0, keepdims=False)
-        total = total + along_line(sent, d).astype(f32)
-    return total
-
-
-def small_reduce(parts):
-    m = parts.shape[0]
-    sent = parts.reshape(m, NG, TOK).transpose(1, 0, 2)
-    return jnp.sum(a2a(sent, LINE), axis=0)
-
-
-def small_sum(parts):
-    return jnp.sum(a2a(jnp.broadcast_to(parts[None], (NG,) + parts.shape), LINE), axis=0)
+        name=name,
+    )(*args)
+
+
+def to_owners(row):
+    return a2a(row.reshape(NG, TOK), LINE)
+
+
+def to_line(rows):
+    m = rows.shape[0]
+    return a2a(jnp.broadcast_to(rows[None], (NG,) + rows.shape), LINE).reshape(NG * m, GT)
 
 
 def rounded(a):
     return lax.reduce_precision(a, exponent_bits=8, mantissa_bits=7)
-
-
-def three_parts(a):
-    hi = rounded(a)
-    mid = rounded(a - hi)
-    return [hi.astype(bf), mid.astype(bf), (a - hi - mid).astype(bf)]
 
 
 def group_gather(block):
@@ -154,8 +299,8 @@
     return a2a(jnp.broadcast_to(block[None], (NQ, r, n)), ZX).reshape(NQ * r, n)
 
 
-def tie(*arrays):
-    return lax.optimization_barrier(arrays)
+def wait_for(value, *others):
+    return lax.optimization_barrier((value, others))[0]
 
 
 def group_reduce(full):
@@ -215,9 +360,11 @@
         carry = decay * carry + block[:SCAN_ROWS]
 
 
-def exclusive_scan(sent, reverse):
+def exclusive_scan(sent, reverse, first, second):
     q = lax.axis_index(ZX)
     got = a2a(sent, ZX)
+    if first is not None:
+        got = wait_for(got, first)
     outs = pl.pallas_call(
         functools.partial(scan_kernel, reverse),
         out_shape=jax.ShapeDtypeStruct((NQ, 32, N), bf),
@@ -228,7 +375,7 @@
         out_specs=pl.BlockSpec(memory_space=pltpu.VMEM),
         name="group_scan",
     )(q.reshape(1).astype(jnp.int32), got)
-    return a2a(outs, ZX)
+    return wait_for(a2a(outs, ZX), second)
 
 
 PAIRS = HL // 2
@@ -258,15 +405,33 @@
     )
 
 
+def two_parts(a):
+    hi = a.astype(bf)
+    return hi, (a - hi.astype(f32)).astype(bf)
+
+
 def head_sums(wide):
     column = lax.broadcasted_iota(jnp.int32, (W, 128), 0)
     lane = lax.broadcasted_iota(jnp.int32, (W, 128), 1)
-    chosen = ((column >= lane * HP) & (column < lane * HP + HP)).astype(f32)
-    return dot(wide, chosen, 1, 0, HI)
+    chosen = ((column >= lane * HP) & (column < lane * HP + HP)).astype(f32).astype(bf)
+    hi, low = two_parts(wide)
+    return dot(hi, chosen, 1, 0) + dot(low, chosen, 1, 0)
 
 
 def token_sums(wide):
-    return dot(jnp.ones((8, wide.shape[1]), f32), wide, 1, 1, HI)
+    ones = jnp.ones((8, wide.shape[1]), bf)
+    hi, low = two_parts(wide)
+    return dot(ones, hi, 1, 1) + dot(ones, low, 1, 1)
+
+
+def running_sums(chosen, a):
+    hi = a.astype(bf).astype(f32)
+    mid = (a - hi).astype(bf).astype(f32)
+    packed = hi + pltpu.roll(mid, 8, 1) + pltpu.roll(a - hi - mid, 16, 1)
+    out = dot(chosen.astype(f32).astype(bf), packed.astype(bf), 1, 0)
+    total = out + pltpu.roll(out, 128 - 8, 1) + pltpu.roll(out, 128 - 16, 1)
+    lane = lax.broadcasted_iota(jnp.int32, (SPAN, 128), 1)
+    return jnp.where(lane < HL, total, 0.0)
 
 
 def write_states(sent_ref, states, decay):
@@ -303,9 +468,18 @@
     return jnp.exp(run) * (segc_ref[...] == seg_before).astype(f32)
 
 
+def past_rows(k, u_ref, past_ref, edge_ref):
+    past = jnp.where(k == 0, edge_ref[...].astype(f32), past_ref[...].astype(f32))
+    return jnp.concatenate([past, u_ref[...].astype(f32)], axis=0)
+
+
+def back_by(rows, distance):
+    return (pltpu.roll(rows, distance, 0) if distance else rows)[16:]
+
+
 def mix_kernel(
-    seg_ref, v_ref, raw_ref, bias_ref, rate_ref, segc_ref, segr_ref,
-    within_ref, local_ref, step_ref, run_ref, before_ref, decay_ref, sent_ref, acc_ref, dec_ref,
+    seg_ref, u_ref, past_ref, edge_ref, same_ref, conv_ref, raw_ref, bias_ref, rate_ref, segc_ref,
+    segr_ref, v_ref, pre_ref, within_ref, local_ref, step_ref, run_ref, before_ref, decay_ref, sent_ref, acc_ref, dec_ref,
 ):
     k = pl.program_id(0)
 
@@ -314,19 +488,26 @@
         acc_ref[...] = jnp.zeros_like(acc_ref)
         dec_ref[...] = jnp.ones_like(dec_ref)
 
+    rows = past_rows(k, u_ref, past_ref, edge_ref)
+    pre = jnp.broadcast_to(conv_ref[CONV : CONV + 1], (SPAN, CC))
+    for i in range(CONV):
+        pre = pre + conv_ref[i : i + 1] * back_by(rows, i) * same_ref[:, i : i + 1]
+    pre_ref[...] = pre
+    v = silu_both(pre)[0]
+    v_ref[...] = v
     lane = lax.broadcasted_iota(jnp.int32, (SPAN, 128), 1)
     raw = raw_ref[...].astype(f32) + bias_ref[...]
     step = jnp.where(lane < HL, jax.nn.softplus(raw), 0.0)
     row = lax.broadcasted_iota(jnp.int32, (SPAN, SPAN), 0)
     col = lax.broadcasted_iota(jnp.int32, (SPAN, SPAN), 1)
-    run = dot((col <= row).astype(f32), rate_ref[...] * step, 1, 0, HI)
+    run = running_sums(col <= row, rate_ref[...] * step)
     step_ref[...] = step
     run_ref[...] = run
     run_t = run.T
     mask = span_masks(segc_ref, segr_ref)
-    xc = v_ref[:, :W]
-    b_low = v_ref[:, W : W + N].astype(bf)
-    c_low = v_ref[:, W + N :].astype(bf)
+    xc = v[:, :W]
+    b_low = v[:, W : W + N].astype(bf)
+    c_low = v[:, W + N :].astype(bf)
     gram = dot(c_low, b_low, 1, 1)
     xs = (by_lanes(step) * xc).astype(bf)
     half = lane < HP
@@ -361,16 +542,17 @@
 
 
 def gate_kernel(
-    last, seg_ref, back_ref, local_ref, before_ref, run_ref, v_ref, within_ref, z_ref, segc_ref,
+    last, order_ref, seg_ref, back_ref, local_ref, before_ref, run_ref, v_ref, within_ref, z_ref, segc_ref,
     skip_ref, wo_ref, *rest,
 ):
     if last:
-        grad_ref, y0_ref, part_ref, sums_ref, carry_ref = rest
+        dq_ref, y0_ref, other_ref, mine_ref, sums_ref, carry_ref = rest
     else:
-        y0_ref, part_ref, sums_ref, carry_ref = rest
-    k = pl.program_id(0)
-
-    @pl.when(k == 0)
+        y0_ref, other_ref, mine_ref, sums_ref, carry_ref = rest
+    i = pl.program_id(0)
+    k = order_ref[i]
+
+    @pl.when(i == 0)
     def _():
         carry_ref[...] = read_states(back_ref)
 
@@ -382,17 +564,16 @@
     y0_ref[...] = y0
     mixed = (y0 + skip_ref[...] * xc).astype(bf).astype(f32)
     gated = mixed * silu_both(z_ref[...])[0]
-    part_ref[...] = dot(gated.astype(bf), wo_ref[...], 1, 0).astype(bf)
+    write_half(other_ref, mine_ref, dot(gated.astype(bf), wo_ref[...], 1, 0).astype(bf))
     sums = token_sums(gated * gated)
     if last:
-        d_q = dot(grad_ref[...], wo_ref[...], 1, 1)
         row = lax.broadcasted_iota(jnp.int32, (8, SPAN), 0)
-        sums = jnp.where(row < 1, sums, token_sums(gated * d_q))
+        sums = jnp.where(row < 1, sums, token_sums(gated * dq_ref[...]))
     sums_ref[...] = sums
 
 
 def gate_back_kernel(
-    seg_ref, grad_ref, wo_ref, scale_ref, v_ref, y0_ref, z_ref, run_ref, segc_ref, skip_ref,
+    last, seg_ref, grad_ref, wo_ref, scale_ref, v_ref, y0_ref, z_ref, run_ref, segc_ref, skip_ref,
     decay_ref, dy_ref, dz_ref, gr_ref, local_ref, after_ref, sent_ref, acc_ref, dec_ref,
 ):
     i = pl.program_id(0)
@@ -403,9 +584,23 @@
         acc_ref[...] = jnp.zeros_like(acc_ref)
         dec_ref[...] = jnp.ones_like(dec_ref)
 
-    scales = scale_ref[...].T
-    r, kappa = scales[:, 0:1], scales[:, 1:2]
-    d_q = dot(grad_ref[...], wo_ref[...], 1, 1)
+    if last:
+        sums = scale_ref[...]
+        odd = lax.broadcasted_iota(jnp.int32, (2 * NG, SPAN), 0) % 2 == 1
+        square = jnp.sum(jnp.where(odd, 0.0, sums), axis=0, keepdims=True)
+        inner = jnp.sum(jnp.where(odd, sums, 0.0), axis=0, keepdims=True)
+        r_row = lax.rsqrt(square / DI + EPS)
+        k_row = r_row * r_row * r_row * inner / DI
+    else:
+        rows = scale_ref[...].astype(f32)
+        pieces = [rows[:, i * TOK : (i + 1) * TOK] for i in range(6)]
+        r_two = pieces[0] + pieces[1] + pieces[2]
+        k_two = pieces[3] + pieces[4] + pieces[5]
+        r_row = jnp.concatenate([r_two[0:1], r_two[16:17]], axis=1)
+        k_row = jnp.concatenate([k_two[0:1], k_two[16:17]], axis=1)
+    r = jnp.broadcast_to(r_row, (8, SPAN)).T[:, 0:1]
+    kappa = jnp.broadcast_to(k_row, (8, SPAN)).T[:, 0:1]
+    d_q = grad_ref[...] if last else dot(grad_ref[...], wo_ref[...], 1, 1)
     mixed = (y0_ref[...] + skip_ref[...] * v_ref[:, :W]).astype(bf).astype(f32)
     silu, d_silu = silu_both(z_ref[...])
     gated = mixed * silu
@@ -496,19 +691,18 @@
     d_step = head_sums(xc * dxs)
     d_w = head_sums(d_weighted * xc)
     product = d_end * carried
-    ones = jnp.ones((8, N), f32)
-    lane8 = lax.broadcasted_iota(jnp.int32, (8, 128), 1)
-    d_span = jnp.zeros((8, 128), f32)
+    lane1 = lax.broadcasted_iota(jnp.int32, (1, 128), 1)
+    d_span = jnp.zeros((1, 128), f32)
     for h in range(HL):
-        rows = dot(ones, product[h * HP : (h + 1) * HP], 1, 1, HI)
-        d_span = d_span + jnp.where(lane8 == h, jnp.sum(rows, axis=1, keepdims=True), 0.0)
+        rows = jnp.sum(product[h * HP : (h + 1) * HP], axis=0, keepdims=True)
+        d_span = d_span + jnp.where(lane1 == h, jnp.sum(rows, axis=1, keepdims=True), 0.0)
     d_step = d_step + d_w * w_end
     d_ww = d_w * w_end * step
     d_run = d_run - d_ww
-    d_last = jnp.sum(d_ww, axis=0, keepdims=True) + d_span[:1] * decay_ref[0]
+    d_last = jnp.sum(d_ww, axis=0, keepdims=True) + d_span * decay_ref[0]
     row = lax.broadcasted_iota(jnp.int32, (SPAN, SPAN), 0)
     col = lax.broadcasted_iota(jnp.int32, (SPAN, SPAN), 1)
-    d_a = dot((col >= row).astype(f32), d_run, 1, 0, HI) + d_last
+    d_a = running_sums(col >= row, d_run) + d_last
     d_step = d_step + rate * d_a
     raw = raw_ref[...].astype(f32) + bias_ref[...]
     lane = lax.broadcasted_iota(jnp.int32, (SPAN, 128), 1)
@@ -526,6 +720,38 @@
     sums_ref[...] = sums_ref[...] + sums
 
 
+def conv_back_kernel(
+    order_ref, dpre_ref, next_ref, after_ref, u_ref, past_ref, edge_ref, same_ref, conv_ref, draw_ref, dz_ref,
+    wa_ref, wz_ref, da_ref, other_ref, mine_ref, taps_ref,
+):
+    i = pl.program_id(0)
+    k = order_ref[i]
+
+    @pl.when(i == 0)
+    def _():
+        taps_ref[...] = jnp.zeros_like(taps_ref)
+
+    d_pre = dpre_ref[...]
+    later = jnp.where(k == LAST, after_ref[...], next_ref[...])
+    d_rows = jnp.concatenate([d_pre, later], axis=0)
+    rows = past_rows(k, u_ref, past_ref, edge_ref)
+    du = jnp.zeros((SPAN, CC), f32)
+    taps = []
+    for tap in range(CONV):
+        ahead = pltpu.roll(d_rows, SPAN + 8 - tap, 0) if tap else d_rows
+        same = same_ref[:, CONV + tap : CONV + tap + 1]
+        du = du + conv_ref[tap : tap + 1] * ahead[:SPAN] * same
+        product = d_pre * back_by(rows, tap) * same_ref[:, tap : tap + 1]
+        taps.append(jnp.sum(product, axis=0, keepdims=True))
+    taps.append(jnp.sum(d_pre, axis=0, keepdims=True))
+    taps.append(jnp.zeros((3, CC), f32))
+    taps_ref[...] = taps_ref[...] + jnp.concatenate(taps, axis=0)
+    da = jnp.concatenate([du.astype(bf), draw_ref[...]], axis=1)
+    da_ref[...] = da
+    part = dot(da, wa_ref[...], 1, 1) + dot(dz_ref[...], wz_ref[...], 1, 1)
+    write_half(other_ref, mine_ref, part.astype(bf))
+
+
 def tok_block(n, reverse=False):
     return pl.BlockSpec((SPAN, n), lambda k: (LAST - k if reverse else k, 0))
 
@@ -556,49 +782,115 @@
             dimension_semantics=("arbitrary",), vmem_limit_bytes=60 * 1024 * 1024
         ),
         cost_estimate=pl.CostEstimate(
-            flops=int(us * 8e8), bytes_accessed=int(us * 3e6), transcendentals=0
+            flops=int(us * 4e7), bytes_accessed=int(us * 2e5), transcendentals=0
         ),
         name=name,
     )(*args)
 
 
-def span_mix(seg, v, raw, bias, rate, segc, segr):
+def ordered_call(kernel, name, ins, outs, shapes, scratch, args, us):
+    return pl.pallas_call(
+        kernel,
+        grid_spec=pltpu.PrefetchScalarGridSpec(
+            num_scalar_prefetch=1, grid=(NS,), in_specs=ins, out_specs=outs, scratch_shapes=scratch
+        ),
+        out_shape=shapes,
+        compiler_params=pltpu.CompilerParams(
+            dimension_semantics=("arbitrary",), vmem_limit_bytes=60 * 1024 * 1024
+        ),
+        cost_estimate=pl.CostEstimate(
+            flops=int(us * 4e7), bytes_accessed=int(us * 2e5), transcendentals=0
+        ),
+        name=name,
+    )(span_order(), *args)
+
+
+def tok_at(n):
+    return pl.BlockSpec((SPAN, n), lambda i, order: (order[i], 0))
+
+
+def span_at(rows, n):
+    return pl.BlockSpec((1, rows, n), lambda i, order: (order[i], 0, 0))
+
+
+def whole_at(*shape):
+    return pl.BlockSpec(shape, lambda i, order: (0,) * len(shape))
+
+
+HALVES = [
+    pl.BlockSpec((SPAN, D), lambda i, order: (jnp.minimum(i, 1), 0)),
+    pl.BlockSpec((SPAN, D), lambda i, order: (jnp.maximum(i - 2, 0), 0)),
+]
+HALF_SHAPES = [struct((GT // 2, D), bf)] * 2
+
+
+def past_block(n):
+    return pl.BlockSpec((16, n), lambda k: (jnp.maximum(k * (SPAN // 16) - 1, 0), 0))
+
+
+def span_mix(seg, u, edge, same, conv, raw, bias, rate, segc, segr):
     return call(
         mix_kernel,
         "span_mix",
-        [SMEM, tok_block(CC), tok_block(128), whole(1, 128), whole(1, 128), tok_block(1),
-         span_block(1, SPAN)],
-        [tok_block(W), span_block(W, N), tok_block(128), tok_block(128), span_block(1, 128),
-         span_block(1, 128), whole(NQ, 32, N)],
-        [struct((GT, W)), STATE, struct((GT, 128)), struct((GT, 128)), ROW, ROW, SENT],
+        [SMEM, tok_block(CC), past_block(CC), whole(16, CC), tok_block(8), whole(8, CC),
+         tok_block(128), whole(1, 128), whole(1, 128), tok_block(1), span_block(1, SPAN)],
+        [tok_block(CC), tok_block(CC), tok_block(W), span_block(W, N), tok_block(128),
+         tok_block(128), span_block(1, 128), span_block(1, 128), whole(NQ, 32, N)],
+        [struct((GT, CC)), struct((GT, CC)), struct((GT, W)), STATE, struct((GT, 128)),
+         struct((GT, 128)), ROW, ROW, SENT],
         [STATE_SCRATCH, pltpu.VMEM((1, 128), f32)],
-        (seg, v, raw, bias, rate, segc, segr),
-        12,
-    )
-
-
-def span_gate(seg, back, local, before, run, v, within, z, segc, skip, wo, grad):
-    last = grad is not None
-    ins = [SMEM, whole(NQ, 32, N), span_block(W, N), span_block(1, 128), tok_block(128),
-           tok_block(CC), tok_block(W), tok_block(W), tok_block(1), whole(1, W), whole(W, D)]
+        (seg, u, u, edge, same, conv, raw, bias, rate, segc, segr),
+        10,
+    )
+
+
+def conv_back(d_pre, after, u, edge, same, conv, d_raw, dz, wa, wz, at):
+    following = pl.BlockSpec(
+        (8, CC), lambda i, order: (jnp.minimum((order[i] + 1) * (SPAN // 8), GT // 8 - 1), 0)
+    )
+    past = pl.BlockSpec(
+        (16, CC), lambda i, order: (jnp.maximum(order[i] * (SPAN // 16) - 1, 0), 0)
+    )
+    return ordered_call(
+        conv_back_kernel,
+        "conv_back",
+        [tok_at(CC), following, whole_at(8, CC), tok_at(CC), past, whole_at(16, CC), tok_at(8),
+         whole_at(8, CC), tok_at(128), tok_at(W), whole_at(D, CA),
+         pl.BlockSpec((D, W), lambda i, order: (0, at))],
+        [tok_at(CA)] + HALVES + [whole_at(8, CC)],
+        [struct((GT, CA), bf)] + HALF_SHAPES + [struct((8, CC))],
+        [],
+        (d_pre, d_pre, after, u, u, edge, same, conv, d_raw, dz, wa, wz),
+        10,
+    )
+
+
+def span_gate(seg, back, local, before, run, v, within, z, segc, skip, wo, d_q):
+    last = d_q is not None
+    ins = [SMEM, whole_at(NQ, 32, N), span_at(W, N), span_at(1, 128), tok_at(128), tok_at(CC),
+           tok_at(W), tok_at(W), tok_at(1), whole_at(1, W), whole_at(W, D)]
     args = (seg, back, local, before, run, v, within, z, segc, skip, wo)
-    return call(
+    return ordered_call(
         functools.partial(gate_kernel, last),
         "span_gate",
-        ins + [tok_block(D)] if last else ins,
-        [tok_block(W), tok_block(D), pl.BlockSpec((8, SPAN), lambda k: (0, k))],
-        [struct((GT, W)), struct((GT, D), bf), struct((8, GT))],
+        ins + [tok_at(W)] if last else ins,
+        [tok_at(W)] + HALVES + [pl.BlockSpec((8, SPAN), lambda i, order: (0, order[i]))],
+        [struct((GT, W))] + HALF_SHAPES + [struct((8, GT))],
         [STATE_SCRATCH],
-        args + (grad,) if last else args,
+        args + (d_q,) if last else args,
         10,
     )
 
 
-def span_gate_back(seg, grad, wo, scales, v, y0, z, run, segc, skip, decay):
+def span_gate_back(last, seg, grad, wo, scales, v, y0, z, run, segc, skip, decay):
+    if last:
+        scale_block = pl.BlockSpec((2 * NG, SPAN), lambda k: (0, LAST - k))
+    else:
+        scale_block = pl.BlockSpec((32, D), lambda k: (LAST - k, 0))
     return call(
-        gate_back_kernel,
+        functools.partial(gate_back_kernel, last),
         "span_gate_back",
-        [SMEM, tok_block(D, True), whole(W, D), pl.BlockSpec((8, SPAN), lambda k: (0, LAST - k)),
+        [SMEM, tok_block(W if last else D, True), whole(W, D), scale_block,
          tok_block(CC, True), tok_block(W, True), tok_block(W, True), tok_block(128, True),
          tok_block(1, True), whole(1, W), span_block(1, 128, True)],
         [tok_block(W, True), tok_block(W, True), tok_block(W, True), span_block(W, N, True),
@@ -640,6 +932,13 @@
          segc, skip, dy, dxs, dbc, y0),
         16,
     )
+
+
+def z_out_sums(normed, dz, out_part):
+    z_part = mm(normed, dz, 0, 0).astype(bf).reshape(NQ, 96, W)
+    out_part = out_part.reshape(NQ, 24, 4, W).transpose(0, 2, 1, 3).reshape(NQ, 96, W)
+    sent = jnp.concatenate([z_part, out_part], axis=1)
+    return jnp.sum(a2a(sent, ZX).astype(f32), axis=0), sent
 
 
 SMALL = CC + HL
@@ -681,22 +980,14 @@
     conv_own = jnp.concatenate([conv_weight, conv_bias[:, None]], axis=1).reshape(-1, own_ch)
     conv_own = jnp.pad(conv_own, ((0, 12 - conv_own.shape[0]), (0, 0)))
     sent = [in_blocks(in_weight[l], norm_gain[l], conv_own if l == 0 else conv_own[:, :0]) for l in range(LAYERS)]
-    got = a2a(jnp.stack(sent, axis=1), LINE)
-    got, tokens, out_weight = tie(got, tokens, out_weight)
+    sent = jnp.stack(sent, axis=1)
+    got = a2a(sent, LINE)
     in_0 = got[:, 0].reshape(NG * 12, CA + W)
     in_1 = got[:, 1].reshape(NG * 12, CA + W)
-    folded_out = (out_weight.astype(f32) * gate_gain.astype(f32)[:, :, None]).astype(bf)
-    out_blocks = lax.ppermute(folded_out, AX, TO_HEADS)
-    w_a0 = group_gather_now(in_0[:, :CA])
-    conv_all = w_a0[:, W + 2 * N + HL : W + 2 * N + HL + own_ch].reshape(NQ * NG, 12, own_ch)
-    conv_all = conv_all[:, : LAYERS * (CONV + 1)].transpose(1, 0, 2)
-    conv_all = conv_all.reshape(LAYERS, CONV + 1, CH).astype(f32)
-    conv_x = lax.dynamic_slice_in_dim(conv_all, group * W, W, 2)
-    conv_here = jnp.concatenate([conv_x, conv_all[:, :, DI:]], axis=2)
-    w_z0 = group_gather_now(in_0[:, CA:])
-    w_o = [group_gather(out_blocks[l]) for l in range(LAYERS)]
-    w_in1 = group_gather(in_1)
-
+    own_0 = jnp.broadcast_to(in_0[None, :, :CA], (NQ, NG * 12, CA))
+    w_a0 = a2a(own_0, ZX).reshape(D, CA)
+    h = tokens.astype(f32)
+    normed = (h * lax.rsqrt(jnp.mean(h * h, axis=-1, keepdims=True) + EPS)).astype(bf)
     pos = q * GT + jnp.arange(-(CONV - 1), GT + CONV - 1, dtype=jnp.int32)
     seg_ext = jnp.sum((doc_starts[None, :] <= pos[:, None]).astype(jnp.int32), axis=1) - 1
     seg = seg_ext[CONV - 1 : CONV - 1 + GT]
@@ -704,161 +995,186 @@
     seg_before = seg_ext[CONV - 2 : CONV - 2 + GT : SPAN]
     seg_ends = jnp.stack([seg_before, seg_spans[:, -1]])
     seg_col, seg_row = seg[:, None], seg_spans[:, None, :]
-    same_back = [
-        (seg_ext[CONV - 1 - k : CONV - 1 - k + GT] == seg).astype(f32)[:, None] for k in range(CONV)
-    ]
-    same_fwd = [
-        (seg_ext[CONV - 1 + k : CONV - 1 + k + GT] == seg).astype(f32)[:, None] for k in range(CONV)
-    ]
+    same = jnp.stack(
+        [seg_ext[CONV - 1 - k : CONV - 1 - k + GT] == seg for k in range(CONV)]
+        + [seg_ext[CONV - 1 + k : CONV - 1 + k + GT] == seg for k in range(CONV)],
+        axis=1,
+    ).astype(f32)
 
     def pick_heads(a):
         own = lax.dynamic_slice_in_dim(a, sub * HL, HL, 0)
         return jnp.pad(own, (0, 128 - HL))[None]
 
-    h = tokens.astype(f32)
-    saved = []
-    cot_late, w_a0 = tie(cotangent, w_a0)
-    grad_full = line_gather(cot_late)
-
+    onward = [(i, i + 1) for i in range(NQ - 1)]
+    consts = []
     for l in range(LAYERS):
-        bias_h = pick_heads(step_bias[l])
         rate = jnp.where(jnp.arange(128)[None] < HL, -jnp.exp(pick_heads(decay_log[l])), 0.0)
         skip_x = jnp.repeat(lax.dynamic_slice_in_dim(skip_gain[l], sub * HL, HL, 0), HP)[None]
-        r_in = lax.rsqrt(jnp.mean(h * h, axis=-1, keepdims=True) + EPS)
-        normed = line_gather((h * r_in).astype(bf))
-        proj = mm(normed, w_a0 if l == 0 else w_in1)
-        u = proj[:, :CC].astype(bf)
-        raw = proj[:, CC:CA].astype(bf)
-        edge = lax.ppermute(u[GT - (CONV - 1) :], ZX, [(i, i + 1) for i in range(NQ - 1)])
-        z = mm(normed, w_z0) if l == 0 else proj[:, CA:]
-        ext = jnp.concatenate([edge, u], axis=0).astype(f32)
-        cw = conv_here[l]
-        pre = jnp.broadcast_to(cw[CONV][None], (GT, W + 2 * N))
-        for k in range(CONV):
-            pre = pre + cw[k][None] * ext[CONV - 1 - k : CONV - 1 - k + GT] * same_back[k]
-        v = pre * jax.nn.sigmoid(pre)
-        within, local, step, run, before, decay, sent = span_mix(
-            seg_ends, v, raw, bias_h, rate, seg_col, seg_row
+        consts.append((pick_heads(step_bias[l]), rate, skip_x))
+    prepared = own_0, consts, same, seg_ends, seg_col, seg_row, span_order()
+    places, blocks = line_blocks(wait_for(normed, got), prepared)
+    cot_places, cot_blocks = line_blocks(wait_for(cotangent, blocks[6]))
+    grad_full = place_tokens(cot_places, cot_blocks)
+    folded_out = (out_weight.astype(f32) * gate_gain.astype(f32)[:, :, None]).astype(bf)
+    out_blocks = lax.ppermute(folded_out, AX, TO_HEADS)
+
+    w_a0 = wait_for(w_a0, cot_blocks)
+    normed, u, raw = place_project(places, blocks, w_a0)
+    tail = u[GT - 16 :]
+    conv_all = wait_for(w_a0, tail)[:, SMALL : SMALL + own_ch].reshape(NQ * NG, 12, own_ch)
+    conv_all = conv_all[:, : LAYERS * (CONV + 1)].transpose(1, 0, 2)
+    conv_all = conv_all.reshape(LAYERS, CONV + 1, CH).astype(f32)
+    conv_x = lax.dynamic_slice_in_dim(conv_all, group * W, W, 2)
+    conv_here = jnp.concatenate([conv_x, conv_all[:, :, DI:]], axis=2)
+    conv_here = jnp.pad(conv_here, ((0, 0), (0, 7 - CONV), (0, 0)))
+    zo = jnp.concatenate([in_0[:, CA:], out_blocks[0].reshape(96, W)], axis=0)
+    zo = group_gather(wait_for(zo, tail)).reshape(NQ, 192, W)
+    w_z0 = zo[:, :96].reshape(D, W)
+    w_o = [zo[:, 96:].reshape(W, D), None]
+    w_in1 = group_gather(wait_for(in_1, tail))
+    saved = []
+    for l in range(LAYERS):
+        bias_h, rate, skip_x = consts[l]
+        if l > 0:
+            normed, u, raw = line_project(normed, w_in1)
+        edge = lax.ppermute(u[GT - 16 :], ZX, onward)
+        v, pre, within, local, step, run, before, decay, sent = span_mix(
+            seg_ends, u, edge, same, conv_here[l], raw, bias_h, rate, seg_col, seg_row
         )
         if l == 0:
-            sent, w_z0 = tie(sent, w_z0)
-        back = exclusive_scan(sent, False)
-        if l == 0:
-            back, grad_full, w_o[0] = tie(back, grad_full, w_o[0])
-        y0, part, sums = span_gate(
+            w_o[1] = group_gather(wait_for(out_blocks[1], v))
+            z, d_q = mm(normed, w_z0), None
+            back = exclusive_scan(sent, False, grad_full, z)
+        else:
+            z, d_q = mm(normed, w_in1[:, CA:]), mm(grad_full, w_o[1], 1, 1)
+            back = exclusive_scan(sent, False, z, d_q)
+        y0, other, mine, sums = span_gate(
             seg_ends, back, local, before, run, v, within, z, seg_col, skip_x, w_o[l],
-            grad_full if l == LAYERS - 1 else None,
+            d_q,
         )
-        total = line_reduce(part)
-        if l == LAYERS - 1:
-            sums = small_sum(sums[:2])
-            r_all = lax.rsqrt(sums[0] / DI + EPS)
-            gate_scales = jnp.stack([r_all, r_all * r_all * r_all * sums[1] / DI])
-            r_gate = lax.dynamic_slice_in_dim(r_all, (line_index() // 2 * 4 + core * 2 + yl) * TOK, TOK, 0)
-        else:
-            gate_scales = None
-            total, square, w_in1, w_o[1] = tie(total, small_reduce(sums[:1])[0], w_in1, w_o[1])
-            r_gate = lax.rsqrt(square / DI + EPS)
-        branch = total * r_gate[:, None]
         saved.append(
             dict(
-                h=h, r_in=r_in, normed=normed, ext=ext, pre=pre, v=v, z=z, raw=raw, bias_h=bias_h,
+                h=h, normed=normed, u=u, edge=edge, pre=pre, v=v, z=z, raw=raw, bias_h=bias_h,
                 rate=rate, skip_x=skip_x, step=step, run=run, before=before, decay=decay,
-                local=local, back=back, y0=y0, r_gate=r_gate, branch=branch,
-                gate_scales=gate_scales,
+                local=local, back=back, y0=y0,
             )
         )
-        h = h + branch
-    output = h.astype(bf)
-
-    grad = cotangent.astype(f32)
-    in_grads, gain_grads, out_grads, gate_grads = ([None] * LAYERS for _ in range(4))
+        if l < LAYERS - 1:
+            parts = line_parts(other, mine)
+            square = wait_for(to_owners(sums[0]), *parts[1:])
+            h, branch, normed, r_gate = plain_call(
+                advance_kernel,
+                "advance",
+                [struct((TOK, D)), struct((TOK, D)), struct((TOK, D), bf), struct((8, TOK))],
+                (*parts, square, h),
+            )
+        else:
+            scales = to_line(sums[:2])
+            at = (line_index() // 2 * 4 + core * 2 + yl) * TOK
+            square = lax.dynamic_slice_in_dim(scales, at, TOK, 1)
+            square = jnp.sum(square.reshape(NG, 2, TOK)[:, 0], axis=0)
+            r_last = lax.rsqrt(square / DI + EPS)[:, None]
+            last_halves = other, mine
+
+    grad = cotangent
     conv_grads, head_grads = [None] * LAYERS, [None] * LAYERS
-    in_sums, out_sums = [None] * LAYERS, [None] * LAYERS
+    a_sums, z_sums, out_sums = ([None] * LAYERS for _ in range(3))
     for l in reversed(range(LAYERS)):
         s = saved[l]
-        if l == LAYERS - 1:
-            gate_scales = s["gate_scales"]
+        dy, dz, gr, dlocal, after, sent = span_gate_back(
+            l == LAYERS - 1, seg_ends, d_q if l else grad_full, w_o[l], scales, s["v"], s["y0"], s["z"], s["run"],
+            seg_col, s["skip_x"], s["decay"],
+        )
+        out_part = mm(gr, grad_full, 0, 0).astype(bf)
+        dxs, dbc = span_mix_back(s["v"], s["step"], s["run"], seg_col, seg_row, dy)
+        later = exclusive_scan(sent, True, out_part, dxs)
+        if l == 0:
+            both = z_out_sums(s["normed"], wait_for(dz, later), out_part)
+            d_pre_first = both[1]
         else:
-            grad_low = grad.astype(bf)
-            inner = jnp.sum(grad_low.astype(f32) * s["branch"], axis=1)
-            kappa = s["r_gate"] * s["r_gate"] * inner / DI
-            extra = jnp.concatenate(three_parts(s["r_gate"]) + three_parts(kappa))
-            extra = jnp.pad(extra[None], ((0, 15), (0, D - 6 * TOK)))
-            grad_full, extra = line_gather(jnp.concatenate([grad_low, extra], axis=0))
-            extra = extra.reshape(NG, 16, D)[:, 0, : 6 * TOK].reshape(NG, 2, 3, TOK).astype(f32)
-            gate_scales = jnp.sum(extra, axis=2).transpose(1, 0, 2).reshape(2, GT)
-            grad_full, in_sums[1] = tie(grad_full, in_sums[1])
-        scales = jnp.pad(gate_scales, ((0, 6), (0, 0)))
-        dy, dz, gr, dlocal, after, sent = span_gate_back(
-            seg_ends, grad_full, w_o[l], scales, s["v"], s["y0"], s["z"], s["run"], seg_col,
-            s["skip_x"], s["decay"],
-        )
-        later = exclusive_scan(sent, True)
-        later, dz, gr = tie(later, dz, gr)
-        if l == LAYERS - 1:
-            later, output = tie(later, output)
-        else:
-            z_sum = group_reduce(mm(s["normed"], dz, 0, 0).astype(bf))
-        out_sum = group_reduce(mm(gr, grad_full, 0, 0).astype(bf))
-        dxs, dbc = span_mix_back(s["v"], s["step"], s["run"], seg_col, seg_row, dy)
+            d_pre_first = later
         d_pre, d_raw, head_sum = span_end(
-            seg_ends, later, s["back"], s["local"], s["before"], dlocal, after, s["decay"], s["v"],
+            seg_ends, wait_for(later, d_pre_first), s["back"], s["local"], s["before"], dlocal, after, s["decay"], s["v"],
             s["pre"], s["raw"], s["bias_h"], s["rate"], s["step"], s["run"], seg_col, s["skip_x"],
             dy, dxs, dbc, s["y0"],
         )
+        following = lax.ppermute(d_pre[:8], ZX, [(b, a) for a, b in onward])
+        if l > 0:
+            both = z_out_sums(s["normed"], wait_for(dz, following), out_part)
+        both = both[0]
+        z_sums[l] = both[:96]
+        out_sums[l] = both[96:].reshape(4, 24, W).transpose(1, 0, 2).reshape(24, D)
         if l == LAYERS - 1:
-            d_pre, out_sum = tie(d_pre, out_sum)
-        edge = lax.ppermute(d_pre[: CONV - 1], ZX, [(i + 1, i) for i in range(NQ - 1)])
-        d_ext = jnp.concatenate([d_pre, edge], axis=0)
-        cw = conv_here[l]
-        du = jnp.zeros_like(d_pre)
-        taps = []
-        for k in range(CONV):
-            du = du + cw[k][None] * d_ext[k : k + GT] * same_fwd[k]
-            past = s["ext"][CONV - 1 - k : CONV - 1 - k + GT]
-            taps.append(jnp.sum(d_pre * past * same_back[k], axis=0))
-        taps.append(jnp.sum(d_pre, axis=0))
-        taps = jnp.stack(taps)
+            w_a, w_z, at = w_in1, w_in1, CA // W
+        else:
+            w_a, w_z, at = w_a0, w_z0, 0
+        da, other, mine, taps = conv_back(
+            d_pre, following, s["u"], s["edge"], same, conv_here[l], d_raw, dz, w_a, w_z, at
+        )
         conv_full = jnp.zeros((CONV + 1, CH), f32)
-        conv_full = lax.dynamic_update_slice_in_dim(conv_full, taps[:, :W], group * W, 1)
-        conv_grads[l] = conv_full.at[:, DI:].set(taps[:, W:])
+        conv_full = lax.dynamic_update_slice_in_dim(
+            conv_full, taps[: CONV + 1, :W], group * W, 1
+        )
+        conv_grads[l] = conv_full.at[:, DI:].set(taps[: CONV + 1, W:])
         head_full = lax.dynamic_update_slice_in_dim(
             jnp.zeros((3, H), f32), head_sum[:3, :HL], group * HL, 1
         )
         head_grads[l] = head_full.reshape(3, 2, H // 2).transpose(1, 0, 2).reshape(2, 3 * H // 2)
-        da = jnp.concatenate([du.astype(bf), d_raw], axis=1)
         if l == 0:
-            small = small_block(conv_grads, head_grads)
-            a_part = mm(s["normed"], da, 0, 0) + small.astype(f32)
-            in_sum = jnp.concatenate([group_reduce(a_part.astype(bf)), z_sum], axis=1)
-            d_norm = line_reduce(mm(da, w_a0, 1, 1) + mm(dz, w_z0, 1, 1))
+            out_sums = [lax.ppermute(a, AX, TO_OWNER) for a in out_sums]
+            da = wait_for(da, out_sums)
+        a_part = mm(s["normed"], da, 0, 0)
+        if l == 0:
+            a_part = a_part + small_block(conv_grads, head_grads).astype(f32)
+        a_part = a_part.astype(bf)
+        if l == 0:
+            parts = line_parts(other, mine, a_part)
+            a_sums[l] = group_reduce(a_part)
         else:
-            da = jnp.concatenate([da, dz], axis=1)
-            d_norm = line_reduce(mm(da, w_in1, 1, 1))
-            in_sum = group_reduce(mm(s["normed"], da, 0, 0).astype(bf))
-        hidden, r_in = s["h"], s["r_in"]
-        inner = jnp.mean(hidden * d_norm, axis=1, keepdims=True)
-        grad = grad + r_in * d_norm - hidden * (r_in * r_in * r_in) * inner
-        in_sums[l], out_sums[l] = in_sum, out_sum
-
-    for l in reversed(range(LAYERS)):
-        both = in_sums[l].reshape(NG, 12, CA + W)
-        both = a2a(both, LINE)
-        if l == 0:
-            small = jnp.sum(both[:, :, SMALL:CA], axis=0)
+            parts = line_parts(other, mine)
+            a_sums[l] = group_reduce(wait_for(a_part, parts[0]))
+        if l > 0:
+            grad, block = plain_call(
+                functools.partial(retreat_kernel, True),
+                "retreat",
+                [struct((TOK, D)), struct((TOK + 16, D), bf)],
+                (*parts, s["h"], grad, branch, r_gate),
+            )
+            early = jnp.concatenate([a_sums[1], z_sums[1]], axis=1).reshape(NG, 12, CA + W)
+            grad_full, scales = line_gather_more(block, early)
+            early = a2a(early, LINE)
+            scales = wait_for(scales, early)
+        else:
+            grad = plain_call(
+                functools.partial(retreat_kernel, False),
+                "retreat_last",
+                struct((TOK, D)),
+                (*parts, s["h"], grad),
+            )
+            early = wait_for(early, parts[1])
+            parts = line_parts(*last_halves, parts[1:])
+            total = parts[0] + parts[1].astype(f32) + parts[2].astype(f32) + parts[3].astype(f32)
+            output = (h + total * r_last).astype(bf)
+
+    late = jnp.concatenate([a_sums[0], z_sums[0]], axis=1)
+    late = a2a(late.reshape(NG, 12, CA + W), LINE)
+    small = jnp.sum(late[:, :, SMALL:CA], axis=0)
+    in_grads, gain_grads, out_grads, gate_grads = ([None] * LAYERS for _ in range(4))
+    for l in range(LAYERS):
+        got = (late, early)[l]
+        a_piece, z_piece = got[:, :, :CA], got[:, :, CA:]
         g_in = jnp.concatenate(
             [
-                heads_in(both[:, :, CA:]),
-                heads_in(both[:, :, :W]),
-                jnp.sum(both[:, :, W : W + 2 * N], axis=0),
-                heads_in(both[:, :, W + 2 * N : W + 2 * N + HL]),
+                heads_in(z_piece),
+                heads_in(a_piece[:, :, :W]),
+                jnp.sum(a_piece[:, :, W:CC], axis=0),
+                heads_in(a_piece[:, :, CC : CC + HL]),
             ],
             axis=1,
         )
         in_grads[l] = g_in * norm_gain[l].astype(f32)[:, None]
         gain_grads[l] = jnp.sum(g_in * in_weight[l].astype(f32), axis=1)
-        g_out = lax.ppermute(out_sums[l], AX, TO_OWNER)
+        g_out = out_sums[l]
         out_grads[l] = g_out * gate_gain[l].astype(f32)[:, None]
         gate_grads[l] = jnp.sum(g_out * out_weight[l].astype(f32), axis=1)
 

time: 750 us -> 679 us (0.905)
  other arithmetic: 71.9 us -> 25.8 us
  Pallas kernels: 132 us -> 176 us
  waiting for transfers between devices: 154 us -> 123 us
  local copies, waits for them, and re-layouts: 86 us -> 63.2 us
  blocking collectives: 24.2 us -> 12.4 us
  matrix products: 49.8 us -> 40.2 us
    pallas_call x4 -> x11, Pallas kernels: 23.8 us -> 67.3 us  [the longest x4 43.3 us: ordered_call(): pl.pallas_call(kernel, grid_spec=pltpu.PrefetchScalarGridSpec(num_scalar_...]
    all_to_all x18 -> x17, waiting for transfers between devices: 74.7 us -> 46.5 us  [a2a(): return lax.all_to_all(a, axes, 0, 0, tiled=True)]
    reduce_sum x12 -> x7, other arithmetic: 18.5 us -> 0.93 us  [the longest x2 0.64 us: z_out_sums(): return (jnp.sum(a2a(sent, ZX).astype(f32), axis=0), sent)]
    ppermute x24, waiting for transfers between devices: 69.1 us -> 54.4 us  [along_line(): return lax.ppermute(a, Y, [(i, (i + distance) % 4) for i in range(4)])]
    add x5 -> x0, other arithmetic: 12.3 us -> none  [the longest x4 10.1 us: line_reduce(): chip = (mine.astype(f32) + got.astype(f32)).reshape(4, TOK, n)]
    ppermute x20, starting transfers between devices: 34 us -> 46.1 us  [core_swap(): return lax.ppermute(a, 'c', [(0, 1), (1, 0)])]
    all_to_all x2 -> x1, blocking collectives: 24.2 us -> 12.4 us  [a2a(): return lax.all_to_all(a, axes, 0, 0, tiled=True)]
    unnamed x262 -> x160, local copies, waits for them, and re-layouts: 28.8 us -> 17.2 us
  transfers between devices with their start and end apart: 72 -> 71, of which waited for: 35 -> 31; matrix products, arithmetic and copies ran while one was open for 19% -> 13% of each run, Pallas kernels for 11% -> 19%
where the time goes in v3:
time: 679 us; the launch traced here: 667 us
  starting transfers between devices  211 us (31%)
  Pallas kernels  176 us (26%)
  waiting for transfers between devices  123 us (18%)
  local copies, waits for them, and re-layouts  63.2 us (9%)
  matrix products  40.2 us (6%)
  other arithmetic  25.8 us (4%)
  between operations  16 us (2%)
  blocking collectives  12.4 us (2%)
    all_to_all x17, starting transfers between devices, a2a(): return lax.all_to_all(a, axes, 0, 0, tiled=True)  104 us
    pallas_call x12, Pallas kernels, call(): pl.pallas_call(kernel, grid=(NS,), in_specs=ins, out_specs=outs, out_shap...  102 us
    ppermute x24, waiting for transfers between devices, along_line(): return lax.ppermute(a, Y, [(i, (i + distance) % 4) for i in range(4)])  54.4 us
    all_to_all x17, waiting for transfers between devices, a2a(): return lax.all_to_all(a, axes, 0, 0, tiled=True)  46.5 us
    ppermute x20, starting transfers between devices, core_swap(): return lax.ppermute(a, 'c', [(0, 1), (1, 0)])  46.1 us
    pallas_call x4, Pallas kernels, ordered_call(): pl.pallas_call(kernel, grid_spec=pltpu.PrefetchScalarGridSpec(num_scalar_...  43.3 us
    dot_general x9, matrix products, mm(): lax.dot_general(a, b, (((ca,), (cb,)), ((), ())), preferred_element_type=...  40.2 us
    ppermute x24, starting transfers between devices, along_line(): return lax.ppermute(a, Y, [(i, (i + distance) % 4) for i in range(4)])  31.6 us
  transfers between devices with their start and end apart: 71, of which 31 were waited for; matrix products, arithmetic and copies ran while one was open for 13% of the time, Pallas kernels for 19%

profile of v3, /device:TPU:1, one launch (start us, length us, event | category | flops | bytes accessed | tf_op | source)
XLA Modules:
  0.0 667.1 jit_solution(7859149022439143928)
XLA Ops:
  31.5 7.7 %all-to-all-start.1 = ((bf16[16,96,768]{2,1,0:T(8,128)(2,1)}), bf16[16,96,768]{2,1,0:T(8,128)(2,1)S(1)}, u32[]{:S(2)}, u32[]{:S(2)}) async-start(bf16[16,96,768]{2,1,0:T(8,128)(2,1)} %broadcast_in_dim.31), calls=%async_computation.1 | async-start | bytes 4718592 | tf_op jit(solution)/shard_map/all_to_all | solution.py:52
  43.8 7.6 %collective-permute-done.5.refs_6_ = bf16[128,1536]{1,0:T(8,128)(2,1)S(1)} collective-permute-done((bf16[128,1536]{1,0:T(8,128)(2,1)S(1)}, bf16[128,1536]{1,0:T(8,128)(2,1)S(1)}, u32[]{:S(2)}, u32[]{:S(2)}) %collective-permute-start.5) | collective-permute-done | bytes 393248 | tf_op jit(solution)/shard_map/ppermute | solution.py:64
  62.2 9.3 %collective-permute-done.8.refs_2_ = bf16[128,1536]{1,0:T(8,128)(2,1)} collective-permute-done((bf16[128,1536]{1,0:T(8,128)(2,1)S(1)}, bf16[128,1536]{1,0:T(8,128)(2,1)}, u32[]{:S(2)}, u32[]{:S(2)}) %collective-permute-start.8) | collective-permute-done | bytes 393248 | tf_op jit(solution)/shard_map/ppermute | solution.py:64
  74.5 11.0 %collective-permute-start.15 = (bf16[2,24,1536]{2,1,0:T(8,128)(2,1)}, bf16[2,24,1536]{2,1,0:T(8,128)(2,1)}, u32[]{:S(2)}, u32[]{:S(2)}) collective-permute-start(bf16[2,24,1536]{2,1,0:T(8,128)(2,1)} %multiply_convert_fusion.1), channel_id=1, source_target_pairs={{0,0},{1,8},{2,16},{3,24},{4,32},{5,40},{6,48},{7,56},{8,64},{9,72... | collective-permute-start | bytes 442376 | tf_op jit(solution)/shard_map/ppermute | solution.py:1019
  96.0 6.9 %place_project.2 = (bf16[1024,1536]{1,0:T(8,128)(2,1)}, bf16[1024,640]{1,0:T(8,128)(2,1)}, bf16[1024,128]{1,0:T(8,128)(2,1)}) custom-call(s32[8]{0:T(128)} %stack.195.pos_ref, bf16[128,1536]{1,0:T(8,128)(2,1)} %copy-done.15, bf16[128,1536]{1,0:T(8,128)(2,1)} %collective-permute-done.refs_1_, bf16[128,1536]{1,0:T(8,128)(2,1)} %copy-done.37, ...), custom_call_target="tpu_custom_call" | custom-call | flops 360000000 | bytes 1800000 | tf_op jit(solution)/shard_map/place_project/pallas_call | solution.py:774
  113.1 11.5 %span_mix.2 = (f32[1024,640]{1,0:T(8,128)}, f32[1024,640]{1,0:T(8,128)}, f32[1024,384]{1,0:T(8,128)}, f32[4,384,128]{2,1,0:T(8,128)}, f32[1024,128]{1,0:T(8,128)...) custom-call(s32[2,4]{1,0:T(2,128)} %pad_add_fusion.seg_ref, ...), custom_call_target="tpu_custom_call" | custom-call | flops 400000000 | bytes 2000000 | tf_op jit(solution)/shard_map/span_mix/pallas_call | solution.py:774
  124.7 12.8 %all-to-all-start.2 = ((bf16[16,32,128]{2,1,0:T(8,128)(2,1)}), bf16[16,32,128]{2,1,0:T(8,128)(2,1)S(1)}, u32[]{:S(2)}, u32[]{:S(2)}) async-start(bf16[16,32,128]{2,1,0:T(8,128)(2,1)} %get-tuple-element.161), calls=%async_computation.2 | async-start | bytes 262144 | tf_op jit(solution)/shard_map/all_to_all | solution.py:52
  161.9 9.6 %span_gate.2 = (f32[1024,384]{1,0:T(8,128)}, bf16[512,1536]{1,0:T(8,128)(2,1)}, bf16[512,1536]{1,0:T(8,128)(2,1)}, f32[8,1024]{1,0:T(8,128)}) custom-call(s32[4]{0:T(128)} %pad_add_fusion.1.order_ref, s32[2,4]{1,0:T(2,128)} %pad_add_fusion.seg_ref, bf16[16,32,128]{2,1,0:T(8,128)(2,1)} %copy-done.17, f32[4,384,128]{2,1,0:T(8,128)} %get-tuple-element.166.local_ref, ...), custom_call_target="tpu_custom_call" | custom-call | flops 400000000 | bytes 2000000 | tf_op jit(solution)/shard_map/span_gate/pallas_call | solution.py:792
  192.2 10.5 %all-to-all-done.4 = f32[8,1,128]{2,1,0:T(1,128)S(1)} async-done(((f32[8,1,128]{2,1,0:T(1,128)}), f32[8,1,128]{2,1,0:T(1,128)S(1)}, u32[]{:S(2)}, u32[]{:S(2)}) %all-to-all-start.4) | async-done | bytes 4128 | tf_op jit(solution)/shard_map/all_to_all | solution.py:52
  211.5 7.2 %collective-permute-done.21.refs_2_ = bf16[128,1536]{1,0:T(8,128)(2,1)S(1)} collective-permute-done((bf16[128,1536]{1,0:T(8,128)(2,1)}, bf16[128,1536]{1,0:T(8,128)(2,1)S(1)}, u32[]{:S(2)}, u32[]{:S(2)}) %collective-permute-start.21) | collective-permute-done | bytes 393248 | tf_op jit(solution)/shard_map/ppermute | solution.py:64
  220.1 7.8 %collective-permute-start.24 = (bf16[128,1536]{1,0:T(8,128)(2,1)S(1)}, bf16[128,1536]{1,0:T(8,128)(2,1)S(1)}, u32[]{:S(2)}, u32[]{:S(2)}) collective-permute-start(bf16[128,1536]{1,0:T(8,128)(2,1)S(1)} %collective-permute-done.23.refs_4_), channel_id=1, source_target_pairs={{0,2},{2,0},{1,3},{3,1},{4,6},{6,4},{5,7},{7,5},{8,10},{10,8},{9,1... | collective-permute-start | bytes 1179656 | tf_op jit(solution)/shard_map/ppermute | solution.py:56
  231.6 6.9 %place_project.3 = (bf16[1024,1536]{1,0:T(8,128)(2,1)}, bf16[1024,640]{1,0:T(8,128)(2,1)}, bf16[1024,128]{1,0:T(8,128)(2,1)}) custom-call(s32[8]{0:T(128)} %stack.195.pos_ref, bf16[128,1536]{1,0:T(8,128)(2,1)} %get-tuple-element.180.refs_0_, bf16[128,1536]{1,0:T(8,128)(2,1)} %copy-done.50, bf16[128,1536]{1,0:T(8,128)(2,1)} %copy-done.47, ...), custom_call_target="tpu_custom_call" | custom-call | flops 360000000 | bytes 1800000 | tf_op jit(solution)/shard_map/place_project/pallas_call | solution.py:774
  243.9 11.5 %span_mix.3 = (f32[1024,640]{1,0:T(8,128)}, f32[1024,640]{1,0:T(8,128)}, f32[1024,384]{1,0:T(8,128)}, f32[4,384,128]{2,1,0:T(8,128)}, f32[1024,128]{1,0:T(8,128)...) custom-call(s32[2,4]{1,0:T(2,128)} %pad_add_fusion.seg_ref, ...), custom_call_target="tpu_custom_call" | custom-call | flops 400000000 | bytes 2000000 | tf_op jit(solution)/shard_map/span_mix/pallas_call | solution.py:774
  283.0 10.1 %span_gate.3 = (f32[1024,384]{1,0:T(8,128)}, bf16[512,1536]{1,0:T(8,128)(2,1)}, bf16[512,1536]{1,0:T(8,128)(2,1)}, f32[8,1024]{1,0:T(8,128)}) custom-call(s32[4]{0:T(128)} %pad_add_fusion.1.order_ref, s32[2,4]{1,0:T(2,128)} %pad_add_fusion.seg_ref, bf16[16,32,128]{2,1,0:T(8,128)(2,1)} %copy-done.18, f32[4,384,128]{2,1,0:T(8,128)} %get-tuple-element.189.local_ref, ...), custom_call_target="tpu_custom_call" | custom-call | flops 400000000 | bytes 2000000 | tf_op jit(solution)/shard_map/span_gate/pallas_call | solution.py:792
  293.9 12.4 %all_to_all.97 = f32[8,2,1024]{2,1,0:T(2,128)S(1)} all-to-all(f32[8,2,1024]{2,1,0:T(2,128)S(1)} %broadcast_in_dim.38), channel_id=1, replica_groups=mesh['z'=4,'x'=4,'yh'=2,'c'=2,'yl'=2] {'yh','c','yl'}, dimensions={0} | all-to-all | bytes 131072 | tf_op jit(solution)/shard_map/all_to_all | solution.py:52
  306.9 8.1 %span_gate_back.2 = (bf16[1024,384]{1,0:T(8,128)(2,1)}, bf16[1024,384]{1,0:T(8,128)(2,1)}, bf16[1024,384]{1,0:T(8,128)(2,1)}, f32[4,384,128]{2,1,0:T(8,128)}, f3...) custom-call(s32[2,4]{1,0:T(2,128)} %pad_add_fusion.seg_ref, f32[1024,384]{1,0:T(8,128)} %fusion.41.rest_0_.grad_ref, ...), custom_call_target="tpu_custom_call" | custom-call | flops 480000000 | bytes 2400000 | tf_op jit(solution)/shard_map/span_gate_back/pallas_call | solution.py:774
  331.6 8.0 %span_mix_back.2 = (f32[1024,384]{1,0:T(8,128)}, f32[1024,256]{1,0:T(8,128)}) custom-call(f32[1024,640]{1,0:T(8,128)} %get-tuple-element.192.v_ref, f32[1024,128]{1,0:T(8,128)} %get-tuple-element.202.step_ref, f32[1024,128]{1,0:T(8,128)} %get-tuple-element.191.run_ref, s32[1024,1]{1,0:T(8,128)} %copy.276.segc_ref, s32[4,1,256]{2,1,0:T(1,128)} %bitcast.241, ...), custom_call_target="tpu_custom_call" | custom-call | flops 560000000 | bytes 2800000 | tf_op jit(solution)/shard_map/span_mix_back/pallas_call | solution.py:774
  340.3 11.8 %span_end.2 = (f32[1024,640]{1,0:T(8,128)}, bf16[1024,128]{1,0:T(8,128)(2,1)}, f32[8,128]{1,0:T(8,128)}) custom-call(s32[2,4]{1,0:T(2,128)} %pad_add_fusion.seg_ref, bf16[16,32,128]{2,1,0:T(8,128)(2,1)} %copy-done.27, bf16[16,32,128]{2,1,0:T(8,128)(2,1)} %copy-done.18, f32[4,384,128]{2,1,0:T(8,128)} %get-tuple-element.189.local_ref, ...), custom_call_target="tpu_custom_call" | custom-call | flops 640000000 | bytes 3200000 | tf_op jit(solution)/shard_map/span_end/pallas_call | solution.py:774
  363.1 8.5 %all-to-all-start.11 = ((bf16[16,192,384]{2,1,0:T(8,128)(2,1)}), bf16[16,192,384]{2,1,0:T(8,128)(2,1)S(1)}, u32[]{:S(2)}, u32[]{:S(2)}) async-start(bf16[16,192,384]{2,1,0:T(8,128)(2,1)} %pad_maximum_fusion), calls=%async_computation.11 | async-start | bytes 4718592 | tf_op jit(solution)/shard_map/all_to_all | solution.py:52
  371.6 11.8 %conv_back.2 = (bf16[1024,768]{1,0:T(8,128)(2,1)}, bf16[512,1536]{1,0:T(8,128)(2,1)}, bf16[512,1536]{1,0:T(8,128)(2,1)}, f32[8,640]{1,0:T(8,128)}) custom-call(s32[4]{0:T(128)} %pad_add_fusion.1.order_ref, f32[1024,640]{1,0:T(8,128)} %get-tuple-element.210.dpre_ref.next_ref, f32[1024,640]{1,0:T(8,128)} %get-tuple-element.210.dpre_ref.next_ref, ...), custom_call_target="tpu_custom_call" | custom-call | flops 400000000 | bytes 2000000 | tf_op jit(solution)/shard_map/conv_back/pallas_call | solution.py:792
  399.1 8.3 %all-to-all-start.10 = ((bf16[16,96,768]{2,1,0:T(8,128)(2,1)}), bf16[16,96,768]{2,1,0:T(8,128)(2,1)}, u32[]{:S(2)}, u32[]{:S(2)}) async-start(bf16[16,96,768]{2,1,0:T(8,128)(2,1)} %bitcast.215), calls=%async_computation.10 | async-start | bytes 4718592 | tf_op jit(solution)/shard_map/all_to_all | solution.py:52
  410.8 6.8 %collective-permute-done.31.p1 = bf16[128,1536]{1,0:T(8,128)(2,1)S(1)} collective-permute-done((bf16[128,1536]{1,0:T(8,128)(2,1)}, bf16[128,1536]{1,0:T(8,128)(2,1)S(1)}, u32[]{:S(2)}, u32[]{:S(2)}) %collective-permute-start.31) | collective-permute-done | bytes 393248 | tf_op jit(solution)/shard_map/ppermute | solution.py:64
  417.6 7.2 %collective-permute-done.33.p3 = bf16[128,1536]{1,0:T(8,128)(2,1)S(1)} collective-permute-done((bf16[128,1536]{1,0:T(8,128)(2,1)S(1)}, bf16[128,1536]{1,0:T(8,128)(2,1)S(1)}, u32[]{:S(2)}, u32[]{:S(2)}) %collective-permute-start.33) | collective-permute-done | bytes 393248 | tf_op jit(solution)/shard_map/ppermute | solution.py:64
  447.6 8.8 %collective-permute-start.38 = (bf16[144,1536]{1,0:T(8,128)(2,1)}, bf16[144,1536]{1,0:T(8,128)(2,1)S(1)}, u32[]{:S(2)}, u32[]{:S(2)}) collective-permute-start(bf16[144,1536]{1,0:T(8,128)(2,1)} %collective-permute-done.37.refs_4_), channel_id=1, source_target_pairs={{0,2},{2,0},{1,3},{3,1},{4,6},{6,4},{5,7},{7,5},{8,10},{10,8},{9,1... | collective-permute-start | bytes 1327112 | tf_op jit(solution)/shard_map/ppermute | solution.py:56
  472.8 8.8 %span_gate_back.3 = (bf16[1024,384]{1,0:T(8,128)(2,1)}, bf16[1024,384]{1,0:T(8,128)(2,1)}, bf16[1024,384]{1,0:T(8,128)(2,1)}, f32[4,384,128]{2,1,0:T(8,128)}, f3...) custom-call(s32[2,4]{1,0:T(2,128)} %pad_add_fusion.seg_ref, bf16[1024,1536]{1,0:T(8,128)(2,1)} %get-tuple-element.228.grad_ref, ...), custom_call_target="tpu_custom_call" | custom-call | flops 480000000 | bytes 2400000 | tf_op jit(solution)/shard_map/span_gate_back/pallas_call | solution.py:774
  481.6 6.6 all-to-all-start.13
  503.6 8.1 %span_mix_back.3 = (f32[1024,384]{1,0:T(8,128)}, f32[1024,256]{1,0:T(8,128)}) custom-call(f32[1024,640]{1,0:T(8,128)} %get-tuple-element.169.v_ref, f32[1024,128]{1,0:T(8,128)} %get-tuple-element.236.step_ref, f32[1024,128]{1,0:T(8,128)} %get-tuple-element.168.run_ref, s32[1024,1]{1,0:T(8,128)} %copy.276.segc_ref, s32[4,1,256]{2,1,0:T(1,128)} %bitcast.242, ...), custom_call_target="tpu_custom_call" | custom-call | flops 560000000 | bytes 2800000 | tf_op jit(solution)/shard_map/span_mix_back/pallas_call | solution.py:774
  517.4 6.7 %all-to-all-start.15 = ((bf16[16,192,384]{2,1,0:T(8,128)(2,1)}), bf16[16,192,384]{2,1,0:T(8,128)(2,1)S(1)}, u32[]{:S(2)}, u32[]{:S(2)}) async-start(bf16[16,192,384]{2,1,0:T(8,128)(2,1)} %pad_maximum_fusion.1), calls=%async_computation.15 | async-start | bytes 4718592 | tf_op jit(solution)/shard_map/all_to_all | solution.py:52
  534.2 11.8 %span_end.3 = (f32[1024,640]{1,0:T(8,128)}, bf16[1024,128]{1,0:T(8,128)(2,1)}, f32[8,128]{1,0:T(8,128)}) custom-call(s32[2,4]{1,0:T(2,128)} %pad_add_fusion.seg_ref, bf16[16,32,128]{2,1,0:T(8,128)(2,1)} %copy-done.26, bf16[16,32,128]{2,1,0:T(8,128)(2,1)} %copy-done.17, f32[4,384,128]{2,1,0:T(8,128)} %get-tuple-element.166.local_ref, ...), custom_call_target="tpu_custom_call" | custom-call | flops 640000000 | bytes 3200000 | tf_op jit(solution)/shard_map/span_end/pallas_call | solution.py:774
  553.4 11.9 %conv_back.3 = (bf16[1024,768]{1,0:T(8,128)(2,1)}, bf16[512,1536]{1,0:T(8,128)(2,1)}, bf16[512,1536]{1,0:T(8,128)(2,1)}, f32[8,640]{1,0:T(8,128)}) custom-call(s32[4]{0:T(128)} %pad_add_fusion.1.order_ref, f32[1024,640]{1,0:T(8,128)} %get-tuple-element.247.dpre_ref.next_ref, f32[1024,640]{1,0:T(8,128)} %get-tuple-element.247.dpre_ref.next_ref, ...), custom_call_target="tpu_custom_call" | custom-call | flops 400000000 | bytes 2000000 | tf_op jit(solution)/shard_map/conv_back/pallas_call | solution.py:792
  636.7 7.8 %all-to-all-start.17 = ((f32[8,12,1152]{2,1,0:T(8,128)}), f32[8,12,1152]{2,1,0:T(8,128)S(1)}, u32[]{:S(2)}, u32[]{:S(2)}) async-start(f32[8,12,1152]{2,1,0:T(8,128)} %reshape.528), calls=%async_computation.17 | async-start | bytes 1179648 | tf_op jit(solution)/shard_map/all_to_all | solution.py:52
  646.8 7.9 %all-to-all-done.17 = f32[8,12,1152]{2,1,0:T(8,128)S(1)} async-done(((f32[8,12,1152]{2,1,0:T(8,128)}), f32[8,12,1152]{2,1,0:T(8,128)S(1)}, u32[]{:S(2)}, u32[]{:S(2)}) %all-to-all-start.17) | async-done | bytes 442400 | tf_op jit(solution)/shard_map/all_to_all | solution.py:52
  (514 shorter events, 359.5 us)
Async XLA Ops:
  31.5 63.0 %all-to-all-start.1 = ((bf16[16,96,768]{2,1,0:T(8,128)(2,1)}), bf16[16,96,768]{2,1,0:T(8,128)(2,1)S(1)}, u32[]{:S(2)}, u32[]{:S(2)}) async-start(bf16[16,96,768]{2,1,0:T(8,128)(2,1)} %broadcast_in_dim.31), calls=%async_computation.1 | async-start | bytes 4718592 | tf_op jit(solution)/shard_map/all_to_all | solution.py:52
  39.3 115.5 %all-gather.4.cloned.1.call-start = ((), (), s32[]{:S(2)}) async-start(), calls=%async_computation.18 | async-start | bytes 2506752 | tf_op jit(solution)/shard_map/all_gather | solution.py:294
  43.0 18.5 %collective-permute-start.1 = (bf16[128,1536]{1,0:T(8,128)(2,1)S(1)}, bf16[128,1536]{1,0:T(8,128)(2,1)S(1)}, u32[]{:S(2)}, u32[]{:S(2)}) collective-permute-start(bf16[128,1536]{1,0:T(8,128)(2,1)S(1)} %multiply_convert_fusion.refs_0_), channel_id=1, source_target_pairs={{0,1},{1,4},{4,5},{5,0},{2,3},{3,6},{6,7},{7,2},{8,9},{9,12},{12,1... | collective-permute-start | bytes 1179656 | tf_op jit(solution)/shard_map/ppermute | solution.py:64
  51.5 20.0 %collective-permute-start.8 = (bf16[128,1536]{1,0:T(8,128)(2,1)S(1)}, bf16[128,1536]{1,0:T(8,128)(2,1)}, u32[]{:S(2)}, u32[]{:S(2)}) collective-permute-start(bf16[128,1536]{1,0:T(8,128)(2,1)S(1)} %copy-done.14), channel_id=1, source_target_pairs={{0,1},{1,4},{4,5},{5,0},{2,3},{3,6},{6,7},{7,2},{8,9},{9,12},{12,1... | collective-permute-start | bytes 1179656 | tf_op jit(solution)/shard_map/ppermute | solution.py:64
  51.7 20.4 %collective-permute-start.10 = (bf16[128,1536]{1,0:T(8,128)(2,1)S(1)}, bf16[128,1536]{1,0:T(8,128)(2,1)}, u32[]{:S(2)}, u32[]{:S(2)}) collective-permute-start(bf16[128,1536]{1,0:T(8,128)(2,1)S(1)} %copy-done.14), channel_id=1, source_target_pairs={{0,5},{1,0},{4,1},{5,4},{2,7},{3,2},{6,3},{7,6},{8,13},{9,8},{12,9... | collective-permute-start | bytes 1179656 | tf_op jit(solution)/shard_map/ppermute | solution.py:64
  54.2 19.6 %collective-permute-start.3 = (bf16[128,1536]{1,0:T(8,128)(2,1)S(1)}, bf16[128,1536]{1,0:T(8,128)(2,1)S(1)}, u32[]{:S(2)}, u32[]{:S(2)}) collective-permute-start(bf16[128,1536]{1,0:T(8,128)(2,1)S(1)} %multiply_convert_fusion.refs_0_), channel_id=1, source_target_pairs={{0,5},{1,0},{4,1},{5,4},{2,7},{3,2},{6,3},{7,6},{8,13},{9,8},{12,9... | collective-permute-start | bytes 1179656 | tf_op jit(solution)/shard_map/ppermute | solution.py:64
  54.2 34.5 %collective-permute-start.7 = (bf16[128,1536]{1,0:T(8,128)(2,1)S(1)}, bf16[128,1536]{1,0:T(8,128)(2,1)}, u32[]{:S(2)}, u32[]{:S(2)}) collective-permute-start(bf16[128,1536]{1,0:T(8,128)(2,1)S(1)} %copy-done.14), channel_id=1, source_target_pairs={{0,2},{2,0},{1,3},{3,1},{4,6},{6,4},{5,7},{7,5},{8,10},{10,8},{9,1... | collective-permute-start | bytes 1179656 | tf_op jit(solution)/shard_map/ppermute | solution.py:56
  61.4 27.8 %collective-permute-start.12 = (bf16[128,1536]{1,0:T(8,128)(2,1)S(1)}, bf16[128,1536]{1,0:T(8,128)(2,1)}, u32[]{:S(2)}, u32[]{:S(2)}) collective-permute-start(bf16[128,1536]{1,0:T(8,128)(2,1)S(1)} %copy-done.14), channel_id=1, source_target_pairs={{0,4},{1,5},{4,0},{5,1},{2,6},{3,7},{6,2},{7,3},{8,12},{9,13},{12,... | collective-permute-start | bytes 1179656 | tf_op jit(solution)/shard_map/ppermute | solution.py:64
  71.5 17.8 %collective-permute-start.9 = (bf16[128,1536]{1,0:T(8,128)(2,1)}, bf16[128,1536]{1,0:T(8,128)(2,1)}, u32[]{:S(2)}, u32[]{:S(2)}) collective-permute-start(bf16[128,1536]{1,0:T(8,128)(2,1)} %collective-permute-done.8.refs_2_), channel_id=1, source_target_pairs={{0,2},{2,0},{1,3},{3,1},{4,6},{6,4},{5,7},{7,5},{8,10},{10,8},{9,1... | collective-permute-start | bytes 1179656 | tf_op jit(solution)/shard_map/ppermute | solution.py:56
  103.7 125.7 %all-gather.6.cloned.1.call-start = ((), (), s32[]{:S(2)}) async-start(), calls=%async_computation.19 | async-start | bytes 3760128 | tf_op jit(solution)/shard_map/all_gather | solution.py:294
  124.7 19.6 %all-to-all-start.2 = ((bf16[16,32,128]{2,1,0:T(8,128)(2,1)}), bf16[16,32,128]{2,1,0:T(8,128)(2,1)S(1)}, u32[]{:S(2)}, u32[]{:S(2)}) async-start(bf16[16,32,128]{2,1,0:T(8,128)(2,1)} %get-tuple-element.161), calls=%async_computation.2 | async-start | bytes 262144 | tf_op jit(solution)/shard_map/all_to_all | solution.py:52
  150.7 124.8 %all-gather.8.cloned.1.call-start = ((), (), s32[]{:S(2)}) async-start(), calls=%async_computation.20 | async-start | bytes 1253376 | tf_op jit(solution)/shard_map/all_gather | solution.py:294
  181.2 21.5 %collective-permute-start.17 = (bf16[128,1536]{1,0:T(8,128)(2,1)}, bf16[128,1536]{1,0:T(8,128)(2,1)S(1)}, u32[]{:S(2)}, u32[]{:S(2)}) collective-permute-start(bf16[128,1536]{1,0:T(8,128)(2,1)} %get-tuple-element.174), channel_id=1, source_target_pairs={{0,1},{1,4},{4,5},{5,0},{2,3},{3,6},{6,7},{7,2},{8,9},{9,12},{12,1... | collective-permute-start | bytes 1179656 | tf_op jit(solution)/shard_map/ppermute | solution.py:64
  182.5 20.3 %collective-permute-start.18 = (bf16[128,1536]{1,0:T(8,128)(2,1)}, bf16[128,1536]{1,0:T(8,128)(2,1)S(1)}, u32[]{:S(2)}, u32[]{:S(2)}) collective-permute-start(bf16[128,1536]{1,0:T(8,128)(2,1)} %get-tuple-element.175), channel_id=1, source_target_pairs={{0,5},{1,0},{4,1},{5,4},{2,7},{3,2},{6,3},{7,6},{8,13},{9,8},{12,9... | collective-permute-start | bytes 1179656 | tf_op jit(solution)/shard_map/ppermute | solution.py:64
  183.9 18.9 %collective-permute-start.19 = (bf16[128,1536]{1,0:T(8,128)(2,1)}, bf16[128,1536]{1,0:T(8,128)(2,1)S(1)}, u32[]{:S(2)}, u32[]{:S(2)}) collective-permute-start(bf16[128,1536]{1,0:T(8,128)(2,1)} %get-tuple-element.176), channel_id=1, source_target_pairs={{0,4},{1,5},{4,0},{5,1},{2,6},{3,7},{6,2},{7,3},{8,12},{9,13},{12,... | collective-permute-start | bytes 1179656 | tf_op jit(solution)/shard_map/ppermute | solution.py:64
  209.8 18.2 %collective-permute-start.25 = (bf16[128,1536]{1,0:T(8,128)(2,1)}, bf16[128,1536]{1,0:T(8,128)(2,1)S(1)}, u32[]{:S(2)}, u32[]{:S(2)}) collective-permute-start(bf16[128,1536]{1,0:T(8,128)(2,1)} %get-tuple-element.180.refs_0_), channel_id=1, source_target_pairs={{0,4},{1,5},{4,0},{5,1},{2,6},{3,7},{6,2},{7,3},{8,12},{9,13},{12,... | collective-permute-start | bytes 1179656 | tf_op jit(solution)/shard_map/ppermute | solution.py:64
  210.5 18.9 %collective-permute-start.20 = (bf16[128,1536]{1,0:T(8,128)(2,1)}, bf16[128,1536]{1,0:T(8,128)(2,1)S(1)}, u32[]{:S(2)}, u32[]{:S(2)}) collective-permute-start(bf16[128,1536]{1,0:T(8,128)(2,1)} %get-tuple-element.180.refs_0_), channel_id=1, source_target_pairs={{0,2},{2,0},{1,3},{3,1},{4,6},{6,4},{5,7},{7,5},{8,10},{10,8},{9,1... | collective-permute-start | bytes 1179656 | tf_op jit(solution)/shard_map/ppermute | solution.py:56
  363.1 36.0 %all-to-all-start.11 = ((bf16[16,192,384]{2,1,0:T(8,128)(2,1)}), bf16[16,192,384]{2,1,0:T(8,128)(2,1)S(1)}, u32[]{:S(2)}, u32[]{:S(2)}) async-start(bf16[16,192,384]{2,1,0:T(8,128)(2,1)} %pad_maximum_fusion), calls=%async_computation.11 | async-start | bytes 4718592 | tf_op jit(solution)/shard_map/all_to_all | solution.py:52
  399.1 38.6 %all-to-all-start.10 = ((bf16[16,96,768]{2,1,0:T(8,128)(2,1)}), bf16[16,96,768]{2,1,0:T(8,128)(2,1)}, u32[]{:S(2)}, u32[]{:S(2)}) async-start(bf16[16,96,768]{2,1,0:T(8,128)(2,1)} %bitcast.215), calls=%async_computation.10 | async-start | bytes 4718592 | tf_op jit(solution)/shard_map/all_to_all | solution.py:52
  429.1 32.8 %collective-permute-start.34 = (bf16[144,1536]{1,0:T(8,128)(2,1)}, bf16[144,1536]{1,0:T(8,128)(2,1)S(1)}, u32[]{:S(2)}, u32[]{:S(2)}) collective-permute-start(bf16[144,1536]{1,0:T(8,128)(2,1)} %get-tuple-element.221.refs_0_), channel_id=1, source_target_pairs={{0,2},{2,0},{1,3},{3,1},{4,6},{6,4},{5,7},{7,5},{8,10},{10,8},{9,1... | collective-permute-start | bytes 1327112 | tf_op jit(solution)/shard_map/ppermute | solution.py:56
  436.2 21.3 %collective-permute-start.39 = (bf16[144,1536]{1,0:T(8,128)(2,1)}, bf16[144,1536]{1,0:T(8,128)(2,1)}, u32[]{:S(2)}, u32[]{:S(2)}) collective-permute-start(bf16[144,1536]{1,0:T(8,128)(2,1)} %get-tuple-element.221.refs_0_), channel_id=1, source_target_pairs={{0,4},{1,5},{4,0},{5,1},{2,6},{3,7},{6,2},{7,3},{8,12},{9,13},{12,... | collective-permute-start | bytes 1327112 | tf_op jit(solution)/shard_map/ppermute | solution.py:64
  517.4 54.7 %all-to-all-start.15 = ((bf16[16,192,384]{2,1,0:T(8,128)(2,1)}), bf16[16,192,384]{2,1,0:T(8,128)(2,1)S(1)}, u32[]{:S(2)}, u32[]{:S(2)}) async-start(bf16[16,192,384]{2,1,0:T(8,128)(2,1)} %pad_maximum_fusion.1), calls=%async_computation.15 | async-start | bytes 4718592 | tf_op jit(solution)/shard_map/all_to_all | solution.py:52
  524.6 85.6 %collective-permute-start.28 = (bf16[512,1536]{1,0:T(8,128)(2,1)}, bf16[512,1536]{1,0:T(8,128)(2,1)}, u32[]{:S(2)}, u32[]{:S(2)}) collective-permute-start(bf16[512,1536]{1,0:T(8,128)(2,1)} %get-tuple-element.195), channel_id=1, source_target_pairs={{0,2},{2,0},{1,3},{3,1},{4,6},{6,4},{5,7},{7,5},{8,10},{10,8},{9,1... | collective-permute-start | bytes 4718600 | tf_op jit(solution)/shard_map/ppermute | solution.py:56
  529.2 48.5 %collective-permute-start.44 = (f32[24,1536]{1,0:T(8,128)S(1)}, f32[24,1536]{1,0:T(8,128)S(1)}, u32[]{:S(2)}, u32[]{:S(2)}) collective-permute-start(f32[24,1536]{1,0:T(8,128)S(1)} %bitcast.245), channel_id=1, source_target_pairs={{0,0},{8,1},{16,2},{24,3},{32,4},{40,5},{48,6},{56,7},{64,8},{72,9... | collective-permute-start | bytes 442376 | tf_op jit(solution)/shard_map/ppermute | solution.py:1124
  565.3 22.4 %collective-permute-start.42 = (bf16[512,1536]{1,0:T(8,128)(2,1)}, bf16[512,1536]{1,0:T(8,128)(2,1)}, u32[]{:S(2)}, u32[]{:S(2)}) collective-permute-start(bf16[512,1536]{1,0:T(8,128)(2,1)} %get-tuple-element.250), channel_id=1, source_target_pairs={{0,2},{2,0},{1,3},{3,1},{4,6},{6,4},{5,7},{7,5},{8,10},{10,8},{9,1... | collective-permute-start | bytes 4718600 | tf_op jit(solution)/shard_map/ppermute | solution.py:56
  592.6 21.2 %collective-permute-start.46 = (bf16[128,1536]{1,0:T(8,128)(2,1)}, bf16[128,1536]{1,0:T(8,128)(2,1)}, u32[]{:S(2)}, u32[]{:S(2)}) collective-permute-start(bf16[128,1536]{1,0:T(8,128)(2,1)} %get-tuple-element.259), channel_id=1, source_target_pairs={{0,5},{1,0},{4,1},{5,4},{2,7},{3,2},{6,3},{7,6},{8,13},{9,8},{12,9... | collective-permute-start | bytes 1179656 | tf_op jit(solution)/shard_map/ppermute | solution.py:64
  596.4 19.5 %collective-permute-start.47 = (bf16[128,1536]{1,0:T(8,128)(2,1)}, bf16[128,1536]{1,0:T(8,128)(2,1)}, u32[]{:S(2)}, u32[]{:S(2)}) collective-permute-start(bf16[128,1536]{1,0:T(8,128)(2,1)} %get-tuple-element.260), channel_id=1, source_target_pairs={{0,4},{1,5},{4,0},{5,1},{2,6},{3,7},{6,2},{7,3},{8,12},{9,13},{12,... | collective-permute-start | bytes 1179656 | tf_op jit(solution)/shard_map/ppermute | solution.py:64
  597.6 36.9 %all-to-all-start.16 = ((bf16[16,96,768]{2,1,0:T(8,128)(2,1)}), bf16[16,96,768]{2,1,0:T(8,128)(2,1)S(1)}, u32[]{:S(2)}, u32[]{:S(2)}) async-start(bf16[16,96,768]{2,1,0:T(8,128)(2,1)} %bitcast.213), calls=%async_computation.16 | async-start | bytes 4718592 | tf_op jit(solution)/shard_map/all_to_all | solution.py:52
  619.3 25.2 %collective-permute-start.50 = (bf16[128,1536]{1,0:T(8,128)(2,1)}, bf16[128,1536]{1,0:T(8,128)(2,1)}, u32[]{:S(2)}, u32[]{:S(2)}) collective-permute-start(bf16[128,1536]{1,0:T(8,128)(2,1)} %get-tuple-element.265), channel_id=1, source_target_pairs={{0,4},{1,5},{4,0},{5,1},{2,6},{3,7},{6,2},{7,3},{8,12},{9,13},{12,... | collective-permute-start | bytes 1179656 | tf_op jit(solution)/shard_map/ppermute | solution.py:64
  623.1 21.4 %collective-permute-start.49 = (bf16[128,1536]{1,0:T(8,128)(2,1)}, bf16[128,1536]{1,0:T(8,128)(2,1)}, u32[]{:S(2)}, u32[]{:S(2)}) collective-permute-start(bf16[128,1536]{1,0:T(8,128)(2,1)} %get-tuple-element.264), channel_id=1, source_target_pairs={{0,5},{1,0},{4,1},{5,4},{2,7},{3,2},{6,3},{7,6},{8,13},{9,8},{12,9... | collective-permute-start | bytes 1179656 | tf_op jit(solution)/shard_map/ppermute | solution.py:64
  623.1 21.4 %collective-permute-start.48 = (bf16[128,1536]{1,0:T(8,128)(2,1)}, bf16[128,1536]{1,0:T(8,128)(2,1)}, u32[]{:S(2)}, u32[]{:S(2)}) collective-permute-start(bf16[128,1536]{1,0:T(8,128)(2,1)} %get-tuple-element.263), channel_id=1, source_target_pairs={{0,1},{1,4},{4,5},{5,0},{2,3},{3,6},{6,7},{7,2},{8,9},{9,12},{12,1... | collective-permute-start | bytes 1179656 | tf_op jit(solution)/shard_map/ppermute | solution.py:64
  636.7 18.0 %all-to-all-start.17 = ((f32[8,12,1152]{2,1,0:T(8,128)}), f32[8,12,1152]{2,1,0:T(8,128)S(1)}, u32[]{:S(2)}, u32[]{:S(2)}) async-start(f32[8,12,1152]{2,1,0:T(8,128)} %reshape.528), calls=%async_computation.17 | async-start | bytes 1179648 | tf_op jit(solution)/shard_map/all_to_all | solution.py:52
  (118 other events, 1029.5 us)
Sparse Core Ops, SparseCore 0:
  103.8 50.8 all-gather.3
  156.9 49.1 all-gather.5
  208.2 41.8 all-gather.7

commit v4 on v3

--- a/solution.py
+++ b/solution.py
@@ -38,6 +38,8 @@
 
 
 SMEM = pl.BlockSpec(memory_space=pltpu.SMEM)
+VMEM_BYTES = 60 * 1024 * 1024
+SMALL_VMEM = 16 * 1024 * 1024
 
 
 def struct(shape, dtype=f32):
@@ -79,17 +81,6 @@
         fill_places(pos_ref, blocks, x_ref)
         for i, block in enumerate(blocks):
             extra_ref[pl.ds(pl.multiple_of(pos_ref[i] * 16, 16), 16)] = block[TOK:]
-
-    out_ref[...] = x_ref[pl.ds(pl.multiple_of(k * SPAN, SPAN), SPAN)]
-
-
-def place_plain_kernel(pos_ref, *refs):
-    blocks, (out_ref, x_ref) = refs[:NG], refs[NG:]
-    k = pl.program_id(0)
-
-    @pl.when(k == 0)
-    def _():
-        fill_places(pos_ref, blocks, x_ref)
 
     out_ref[...] = x_ref[pl.ds(pl.multiple_of(k * SPAN, SPAN), SPAN)]
 
@@ -127,19 +118,6 @@
 
 
 X_SCRATCH = pltpu.VMEM((GT, D), bf)
-
-
-def place_tokens(places, blocks):
-    return call(
-        place_plain_kernel,
-        "place_tokens",
-        [SMEM] + [whole(TOK, D)] * NG,
-        tok_block(D),
-        struct((GT, D), bf),
-        [X_SCRATCH],
-        (places, *blocks),
-        4,
-    )
 
 
 def line_gather_more(own, first):
@@ -192,7 +170,7 @@
         out_shape=[struct((TOK, D))] + [struct((TOK, D), bf)] * 3,
         in_specs=[SMEM] + [pl.BlockSpec(memory_space=pltpu.VMEM)] * 2,
         out_specs=[pl.BlockSpec(memory_space=pltpu.VMEM)] * 4,
-        compiler_params=pltpu.CompilerParams(vmem_limit_bytes=60 * 1024 * 1024),
+        compiler_params=pltpu.CompilerParams(vmem_limit_bytes=SMALL_VMEM),
         name="chip_sum",
     )(line_index().reshape(1).astype(jnp.int32), mine, got)
     return [own] + [along_line(block, d) for block, d in zip(sent, (1, 3, 2))]
@@ -216,7 +194,7 @@
 
 
 def parts_sum(refs):
-    total = refs[0][...]
+    total = refs[0][...].astype(f32)
     for ref in refs[1:]:
         total = total + ref[...].astype(f32)
     return total
@@ -243,10 +221,12 @@
     return [hi, mid, row - hi - mid]
 
 
-def retreat_kernel(extra, p0, p1, p2, p3, h_ref, grad_ref, *refs):
+def retreat_kernel(extra, *refs):
+    n = 4 if extra else 1
+    parts, (h_ref, grad_ref, *refs) = refs[:n], refs[n:]
     h = h_ref[...]
     r_in = inverse_rms(h)
-    d_norm = parts_sum((p0, p1, p2, p3))
+    d_norm = parts_sum(parts)
     inner = jnp.mean(h * d_norm, axis=1, keepdims=True)
     grad = grad_ref[...].astype(f32) + r_in * d_norm - h * (r_in * r_in * r_in * inner)
     if not extra:
@@ -269,7 +249,7 @@
     return pl.pallas_call(
         kernel,
         out_shape=shapes,
-        compiler_params=pltpu.CompilerParams(vmem_limit_bytes=60 * 1024 * 1024),
+        compiler_params=pltpu.CompilerParams(vmem_limit_bytes=SMALL_VMEM),
         cost_estimate=pl.CostEstimate(
             flops=int(2e8), bytes_accessed=int(1e6), transcendentals=0
         ),
@@ -375,7 +355,8 @@
         out_specs=pl.BlockSpec(memory_space=pltpu.VMEM),
         name="group_scan",
     )(q.reshape(1).astype(jnp.int32), got)
-    return wait_for(a2a(outs, ZX), second)
+    extra = second(outs)
+    return wait_for(a2a(outs, ZX), extra), extra
 
 
 PAIRS = HL // 2
@@ -492,9 +473,9 @@
     pre = jnp.broadcast_to(conv_ref[CONV : CONV + 1], (SPAN, CC))
     for i in range(CONV):
         pre = pre + conv_ref[i : i + 1] * back_by(rows, i) * same_ref[:, i : i + 1]
-    pre_ref[...] = pre
-    v = silu_both(pre)[0]
-    v_ref[...] = v
+    pre_ref[...] = pre.astype(bf)
+    v_low = silu_both(pre)[0].astype(bf)
+    v_ref[...] = v_low
     lane = lax.broadcasted_iota(jnp.int32, (SPAN, 128), 1)
     raw = raw_ref[...].astype(f32) + bias_ref[...]
     step = jnp.where(lane < HL, jax.nn.softplus(raw), 0.0)
@@ -505,9 +486,9 @@
     run_ref[...] = run
     run_t = run.T
     mask = span_masks(segc_ref, segr_ref)
-    xc = v[:, :W]
-    b_low = v[:, W : W + N].astype(bf)
-    c_low = v[:, W + N :].astype(bf)
+    xc = v_low[:, :W].astype(f32)
+    b_low = v_low[:, W : W + N]
+    c_low = v_low[:, W + N :]
     gram = dot(c_low, b_low, 1, 1)
     xs = (by_lanes(step) * xc).astype(bf)
     half = lane < HP
@@ -546,7 +527,7 @@
     skip_ref, wo_ref, *rest,
 ):
     if last:
-        dq_ref, y0_ref, other_ref, mine_ref, sums_ref, carry_ref = rest
+        dq_ref, y0_ref, part_ref, sums_ref, carry_ref = rest
     else:
         y0_ref, other_ref, mine_ref, sums_ref, carry_ref = rest
     i = pl.program_id(0)
@@ -557,14 +538,18 @@
         carry_ref[...] = read_states(back_ref)
 
     carried = (by_rows(before_ref[0], carry_ref[...]) + local_ref[0]).astype(bf)
-    xc = v_ref[:, :W]
-    c_low = v_ref[:, W + N :].astype(bf)
+    xc = v_ref[:, :W].astype(f32)
+    c_low = v_ref[:, W + N :]
     reading = dot(c_low, carried, 1, 1)
     y0 = within_ref[...] + by_lanes(inflow_of(run_ref[...], segc_ref, seg_ref[0, k])) * reading
     y0_ref[...] = y0
     mixed = (y0 + skip_ref[...] * xc).astype(bf).astype(f32)
-    gated = mixed * silu_both(z_ref[...])[0]
-    write_half(other_ref, mine_ref, dot(gated.astype(bf), wo_ref[...], 1, 0).astype(bf))
+    gated = mixed * silu_both(z_ref[...].astype(f32))[0]
+    part = dot(gated.astype(bf), wo_ref[...], 1, 0).astype(bf)
+    if last:
+        part_ref[...] = part
+    else:
+        write_half(other_ref, mine_ref, part)
     sums = token_sums(gated * gated)
     if last:
         row = lax.broadcasted_iota(jnp.int32, (8, SPAN), 0)
@@ -601,8 +586,8 @@
     r = jnp.broadcast_to(r_row, (8, SPAN)).T[:, 0:1]
     kappa = jnp.broadcast_to(k_row, (8, SPAN)).T[:, 0:1]
     d_q = grad_ref[...] if last else dot(grad_ref[...], wo_ref[...], 1, 1)
-    mixed = (y0_ref[...] + skip_ref[...] * v_ref[:, :W]).astype(bf).astype(f32)
-    silu, d_silu = silu_both(z_ref[...])
+    mixed = (y0_ref[...] + skip_ref[...] * v_ref[:, :W].astype(f32)).astype(bf).astype(f32)
+    silu, d_silu = silu_both(z_ref[...].astype(f32))
     gated = mixed * silu
     gr_ref[...] = (r * gated).astype(bf)
     d_gated = r * d_q - kappa * gated
@@ -611,7 +596,7 @@
     dz_ref[...] = (d_gated * mixed * d_silu).astype(bf)
     inflow = by_lanes(inflow_of(run_ref[...], segc_ref, seg_ref[0, k]))
     scaled = (inflow * dy.astype(f32)).astype(bf)
-    d_carried = dot(scaled, v_ref[:, W + N :].astype(bf), 0, 0)
+    d_carried = dot(scaled, v_ref[:, W + N :], 0, 0)
     local_ref[0] = acc_ref[...]
     after_ref[0] = dec_ref[...]
     decay = decay_ref[0]
@@ -631,9 +616,9 @@
     run = run_ref[...]
     run_t = run.T
     mask = span_masks(segc_ref, segr_ref)
-    xs = (by_lanes(step_ref[...]) * v_ref[:, :W]).astype(bf)
-    b_low = v_ref[:, W : W + N].astype(bf)
-    c_low = v_ref[:, W + N :].astype(bf)
+    xs = (by_lanes(step_ref[...]) * v_ref[:, :W].astype(f32)).astype(bf)
+    b_low = v_ref[:, W : W + N]
+    c_low = v_ref[:, W + N :]
     gram = dot(c_low, b_low, 1, 1)
     d_gram = jnp.zeros((SPAN, SPAN), f32)
     zero = jnp.zeros((SPAN, 128), bf)
@@ -649,8 +634,8 @@
             out.append(dot(mixing, dy, 0, 0))
         dxs_ref[:, cols] = jnp.where(half, out[0], out[1])
     d_gram = d_gram.astype(bf)
-    dbc_ref[:, :N] = dot(d_gram, c_low, 0, 0)
-    dbc_ref[:, N:] = dot(d_gram, b_low, 1, 0)
+    dbc_ref[:, :N] = dot(d_gram, c_low, 0, 0).astype(bf)
+    dbc_ref[:, N:] = dot(d_gram, b_low, 1, 0).astype(bf)
 
 
 def end_kernel(
@@ -670,8 +655,8 @@
     carried = by_rows(before_ref[0], carry_s[...]) + local_ref[0]
     d_end_low = d_end.astype(bf)
     run, step, rate = run_ref[...], step_ref[...], rate_ref[...]
-    xc = v_ref[:, :W]
-    b_low = v_ref[:, W : W + N].astype(bf)
+    xc = v_ref[:, :W].astype(f32)
+    b_low = v_ref[:, W : W + N]
     dy = dy_ref[...].astype(f32)
     dxs = dxs_ref[...]
     step_x = by_lanes(step)
@@ -681,11 +666,11 @@
     weighted = (weights_x * xc).astype(bf)
     scaled = (by_lanes(inflow_of(run, segc_ref, seg_ref[0, k])) * dy).astype(bf)
     d_weighted = dot(b_low, d_end_low, 1, 1)
-    d_b = dbc_ref[:, :N] + dot(weighted, d_end_low, 1, 0)
-    d_c = dbc_ref[:, N:] + dot(scaled, carried.astype(bf), 1, 0)
+    d_b = dbc_ref[:, :N].astype(f32) + dot(weighted, d_end_low, 1, 0)
+    d_c = dbc_ref[:, N:].astype(f32) + dot(scaled, carried.astype(bf), 1, 0)
     d_xc = skip_ref[...] * dy + step_x * dxs + weights_x * d_weighted
     dv = jnp.concatenate([d_xc, d_b, d_c], axis=1)
-    dpre_ref[...] = dv * silu_both(pre_ref[...])[1]
+    dpre_ref[...] = (dv * silu_both(pre_ref[...].astype(f32))[1]).astype(bf)
     skip_sum = head_sums(dy * xc)
     d_run = head_sums(dy * y0_ref[...] - xs * dxs)
     d_step = head_sums(xc * dxs)
@@ -721,9 +706,10 @@
 
 
 def conv_back_kernel(
-    order_ref, dpre_ref, next_ref, after_ref, u_ref, past_ref, edge_ref, same_ref, conv_ref, draw_ref, dz_ref,
-    wa_ref, wz_ref, da_ref, other_ref, mine_ref, taps_ref,
+    first, order_ref, dpre_ref, next_ref, after_ref, u_ref, past_ref, edge_ref, same_ref, conv_ref, draw_ref, dz_ref,
+    wa_ref, wz_ref, da_ref, *outs,
 ):
+    taps_ref = outs[-1]
     i = pl.program_id(0)
     k = order_ref[i]
 
@@ -731,14 +717,14 @@
     def _():
         taps_ref[...] = jnp.zeros_like(taps_ref)
 
-    d_pre = dpre_ref[...]
-    later = jnp.where(k == LAST, after_ref[...], next_ref[...])
+    d_pre = dpre_ref[...].astype(f32)
+    later = jnp.where(k == LAST, after_ref[...].astype(f32), next_ref[...].astype(f32))
     d_rows = jnp.concatenate([d_pre, later], axis=0)
     rows = past_rows(k, u_ref, past_ref, edge_ref)
     du = jnp.zeros((SPAN, CC), f32)
     taps = []
     for tap in range(CONV):
-        ahead = pltpu.roll(d_rows, SPAN + 8 - tap, 0) if tap else d_rows
+        ahead = pltpu.roll(d_rows, SPAN + 16 - tap, 0) if tap else d_rows
         same = same_ref[:, CONV + tap : CONV + tap + 1]
         du = du + conv_ref[tap : tap + 1] * ahead[:SPAN] * same
         product = d_pre * back_by(rows, tap) * same_ref[:, tap : tap + 1]
@@ -749,7 +735,10 @@
     da = jnp.concatenate([du.astype(bf), draw_ref[...]], axis=1)
     da_ref[...] = da
     part = dot(da, wa_ref[...], 1, 1) + dot(dz_ref[...], wz_ref[...], 1, 1)
-    write_half(other_ref, mine_ref, part.astype(bf))
+    if first:
+        outs[0][...] = part.astype(bf)
+    else:
+        write_half(*outs[:2], part.astype(bf))
 
 
 def tok_block(n, reverse=False):
@@ -770,7 +759,7 @@
 STATE_SCRATCH = pltpu.VMEM((W, N), f32)
 
 
-def call(kernel, name, ins, outs, shapes, scratch, args, us):
+def call(kernel, name, ins, outs, shapes, scratch, args, us, vmem=VMEM_BYTES):
     return pl.pallas_call(
         kernel,
         grid=(NS,),
@@ -779,7 +768,7 @@
         out_shape=shapes,
         scratch_shapes=scratch,
         compiler_params=pltpu.CompilerParams(
-            dimension_semantics=("arbitrary",), vmem_limit_bytes=60 * 1024 * 1024
+            dimension_semantics=("arbitrary",), vmem_limit_bytes=vmem
         ),
         cost_estimate=pl.CostEstimate(
             flops=int(us * 4e7), bytes_accessed=int(us * 2e5), transcendentals=0
@@ -796,7 +785,7 @@
         ),
         out_shape=shapes,
         compiler_params=pltpu.CompilerParams(
-            dimension_semantics=("arbitrary",), vmem_limit_bytes=60 * 1024 * 1024
+            dimension_semantics=("arbitrary",), vmem_limit_bytes=VMEM_BYTES
         ),
         cost_estimate=pl.CostEstimate(
             flops=int(us * 4e7), bytes_accessed=int(us * 2e5), transcendentals=0
@@ -836,7 +825,7 @@
          tok_block(128), whole(1, 128), whole(1, 128), tok_block(1), span_block(1, SPAN)],
         [tok_block(CC), tok_block(CC), tok_block(W), span_block(W, N), tok_block(128),
          tok_block(128), span_block(1, 128), span_block(1, 128), whole(NQ, 32, N)],
-        [struct((GT, CC)), struct((GT, CC)), struct((GT, W)), STATE, struct((GT, 128)),
+        [struct((GT, CC), bf), struct((GT, CC), bf), struct((GT, W)), STATE, struct((GT, 128)),
          struct((GT, 128)), ROW, ROW, SENT],
         [STATE_SCRATCH, pltpu.VMEM((1, 128), f32)],
         (seg, u, u, edge, same, conv, raw, bias, rate, segc, segr),
@@ -844,21 +833,22 @@
     )
 
 
-def conv_back(d_pre, after, u, edge, same, conv, d_raw, dz, wa, wz, at):
+def conv_back(first, d_pre, after, u, edge, same, conv, d_raw, dz, wa, wz, at):
     following = pl.BlockSpec(
-        (8, CC), lambda i, order: (jnp.minimum((order[i] + 1) * (SPAN // 8), GT // 8 - 1), 0)
+        (16, CC), lambda i, order: (jnp.minimum((order[i] + 1) * (SPAN // 16), GT // 16 - 1), 0)
     )
     past = pl.BlockSpec(
         (16, CC), lambda i, order: (jnp.maximum(order[i] * (SPAN // 16) - 1, 0), 0)
     )
     return ordered_call(
-        conv_back_kernel,
+        functools.partial(conv_back_kernel, first),
         "conv_back",
-        [tok_at(CC), following, whole_at(8, CC), tok_at(CC), past, whole_at(16, CC), tok_at(8),
+        [tok_at(CC), following, whole_at(16, CC), tok_at(CC), past, whole_at(16, CC), tok_at(8),
          whole_at(8, CC), tok_at(128), tok_at(W), whole_at(D, CA),
          pl.BlockSpec((D, W), lambda i, order: (0, at))],
-        [tok_at(CA)] + HALVES + [whole_at(8, CC)],
-        [struct((GT, CA), bf)] + HALF_SHAPES + [struct((8, CC))],
+        [tok_at(CA)] + ([tok_at(D)] if first else HALVES) + [whole_at(8, CC)],
+        [struct((GT, CA), bf)] + ([struct((GT, D), bf)] if first else HALF_SHAPES)
+        + [struct((8, CC))],
         [],
         (d_pre, d_pre, after, u, u, edge, same, conv, d_raw, dz, wa, wz),
         10,
@@ -874,8 +864,10 @@
         functools.partial(gate_kernel, last),
         "span_gate",
         ins + [tok_at(W)] if last else ins,
-        [tok_at(W)] + HALVES + [pl.BlockSpec((8, SPAN), lambda i, order: (0, order[i]))],
-        [struct((GT, W))] + HALF_SHAPES + [struct((8, GT))],
+        [tok_at(W)] + ([tok_at(D)] if last else HALVES)
+        + [pl.BlockSpec((8, SPAN), lambda i, order: (0, order[i]))],
+        [struct((GT, W))] + ([struct((GT, D), bf)] if last else HALF_SHAPES)
+        + [struct((8, GT))],
         [STATE_SCRATCH],
         args + (d_q,) if last else args,
         10,
@@ -909,7 +901,7 @@
         [tok_block(CC), tok_block(128), tok_block(128), tok_block(1), span_block(1, SPAN),
          tok_block(W)],
         [tok_block(W), tok_block(2 * N)],
-        [struct((GT, W)), struct((GT, 2 * N))],
+        [struct((GT, W)), struct((GT, 2 * N), bf)],
         [],
         (v, step, run, segc, segr, dy),
         14,
@@ -926,7 +918,7 @@
          tok_block(128), whole(1, 128), whole(1, 128), tok_block(128), tok_block(128),
          tok_block(1), whole(1, W), tok_block(W), tok_block(W), tok_block(2 * N), tok_block(W)],
         [tok_block(CC), tok_block(128), whole(8, 128)],
-        [struct((GT, CC)), struct((GT, 128), bf), struct((8, 128))],
+        [struct((GT, CC), bf), struct((GT, 128), bf), struct((8, 128))],
         [STATE_SCRATCH, STATE_SCRATCH],
         (seg, later, back, local, before, dlocal, after, decay, v, pre, raw, bias, rate, step, run,
          segc, skip, dy, dxs, dbc, y0),
@@ -934,11 +926,8 @@
     )
 
 
-def z_out_sums(normed, dz, out_part):
-    z_part = mm(normed, dz, 0, 0).astype(bf).reshape(NQ, 96, W)
-    out_part = out_part.reshape(NQ, 24, 4, W).transpose(0, 2, 1, 3).reshape(NQ, 96, W)
-    sent = jnp.concatenate([z_part, out_part], axis=1)
-    return jnp.sum(a2a(sent, ZX).astype(f32), axis=0), sent
+def group_reduce_blocks(sent):
+    return jnp.sum(a2a(sent, ZX).astype(f32), axis=0)
 
 
 SMALL = CC + HL
@@ -1013,12 +1002,11 @@
         consts.append((pick_heads(step_bias[l]), rate, skip_x))
     prepared = own_0, consts, same, seg_ends, seg_col, seg_row, span_order()
     places, blocks = line_blocks(wait_for(normed, got), prepared)
-    cot_places, cot_blocks = line_blocks(wait_for(cotangent, blocks[6]))
-    grad_full = place_tokens(cot_places, cot_blocks)
     folded_out = (out_weight.astype(f32) * gate_gain.astype(f32)[:, :, None]).astype(bf)
     out_blocks = lax.ppermute(folded_out, AX, TO_HEADS)
-
-    w_a0 = wait_for(w_a0, cot_blocks)
+    zo = jnp.concatenate([in_0[:, CA:], out_blocks.reshape(192, W)], axis=0)
+    grad_full = lax.all_gather(cotangent, LINE, axis=0, tiled=True)
+    w_a0 = wait_for(w_a0, zo)
     normed, u, raw = place_project(places, blocks, w_a0)
     tail = u[GT - 16 :]
     conv_all = wait_for(w_a0, tail)[:, SMALL : SMALL + own_ch].reshape(NQ * NG, 12, own_ch)
@@ -1027,10 +1015,9 @@
     conv_x = lax.dynamic_slice_in_dim(conv_all, group * W, W, 2)
     conv_here = jnp.concatenate([conv_x, conv_all[:, :, DI:]], axis=2)
     conv_here = jnp.pad(conv_here, ((0, 0), (0, 7 - CONV), (0, 0)))
-    zo = jnp.concatenate([in_0[:, CA:], out_blocks[0].reshape(96, W)], axis=0)
-    zo = group_gather(wait_for(zo, tail)).reshape(NQ, 192, W)
+    zo = group_gather(wait_for(zo, tail)).reshape(NQ, 288, W)
     w_z0 = zo[:, :96].reshape(D, W)
-    w_o = [zo[:, 96:].reshape(W, D), None]
+    w_o = [zo[:, 96:192].reshape(W, D), None]
     w_in1 = group_gather(wait_for(in_1, tail))
     saved = []
     for l in range(LAYERS):
@@ -1042,13 +1029,17 @@
             seg_ends, u, edge, same, conv_here[l], raw, bias_h, rate, seg_col, seg_row
         )
         if l == 0:
-            w_o[1] = group_gather(wait_for(out_blocks[1], v))
-            z, d_q = mm(normed, w_z0), None
-            back = exclusive_scan(sent, False, grad_full, z)
+            w_o[1] = wait_for(zo, v)[:, 192:].reshape(W, D)
+            d_q = None
+            back, z = exclusive_scan(
+                sent, False, None, lambda outs: mm(wait_for(normed, outs), w_z0).astype(bf)
+            )
         else:
-            z, d_q = mm(normed, w_in1[:, CA:]), mm(grad_full, w_o[1], 1, 1)
-            back = exclusive_scan(sent, False, z, d_q)
-        y0, other, mine, sums = span_gate(
+            z = mm(normed, w_in1[:, CA:]).astype(bf)
+            back, d_q = exclusive_scan(
+                sent, False, z, lambda outs: mm(wait_for(grad_full, outs), w_o[1], 1, 1)
+            )
+        y0, *parts, sums = span_gate(
             seg_ends, back, local, before, run, v, within, z, seg_col, skip_x, w_o[l],
             d_q,
         )
@@ -1060,7 +1051,7 @@
             )
         )
         if l < LAYERS - 1:
-            parts = line_parts(other, mine)
+            parts = line_parts(*parts)
             square = wait_for(to_owners(sums[0]), *parts[1:])
             h, branch, normed, r_gate = plain_call(
                 advance_kernel,
@@ -1074,7 +1065,8 @@
             square = lax.dynamic_slice_in_dim(scales, at, TOK, 1)
             square = jnp.sum(square.reshape(NG, 2, TOK)[:, 0], axis=0)
             r_last = lax.rsqrt(square / DI + EPS)[:, None]
-            last_halves = other, mine
+            total = lax.psum_scatter(parts[0], LINE, scatter_dimension=0, tiled=True)
+            output = (h + total.astype(f32) * r_last).astype(bf)
 
     grad = cotangent
     conv_grads, head_grads = [None] * LAYERS, [None] * LAYERS
@@ -1085,31 +1077,33 @@
             l == LAYERS - 1, seg_ends, d_q if l else grad_full, w_o[l], scales, s["v"], s["y0"], s["z"], s["run"],
             seg_col, s["skip_x"], s["decay"],
         )
-        out_part = mm(gr, grad_full, 0, 0).astype(bf)
-        dxs, dbc = span_mix_back(s["v"], s["step"], s["run"], seg_col, seg_row, dy)
-        later = exclusive_scan(sent, True, out_part, dxs)
-        if l == 0:
-            both = z_out_sums(s["normed"], wait_for(dz, later), out_part)
-            d_pre_first = both[1]
-        else:
-            d_pre_first = later
+        z_part = mm(s["normed"], dz, 0, 0).astype(bf).reshape(NQ, 96, W)
+
+        def out_blocks_of(outs):
+            low = wait_for(gr, outs)
+            return [
+                mm(low, grad_full[:, i * W : (i + 1) * W], 0, 0).astype(bf).reshape(NQ, 24, W)
+                for i in range(D // W)
+            ]
+
+        later, out_part = exclusive_scan(sent, True, z_part, out_blocks_of)
+        sums = jnp.concatenate([z_part, *out_part], axis=1)
+        both = group_reduce_blocks(wait_for(sums, later))
+        dxs, dbc = span_mix_back(s["v"], s["step"], s["run"], seg_col, seg_row, wait_for(dy, sums))
         d_pre, d_raw, head_sum = span_end(
-            seg_ends, wait_for(later, d_pre_first), s["back"], s["local"], s["before"], dlocal, after, s["decay"], s["v"],
+            seg_ends, later, s["back"], s["local"], s["before"], dlocal, after, s["decay"], s["v"],
             s["pre"], s["raw"], s["bias_h"], s["rate"], s["step"], s["run"], seg_col, s["skip_x"],
             dy, dxs, dbc, s["y0"],
         )
-        following = lax.ppermute(d_pre[:8], ZX, [(b, a) for a, b in onward])
-        if l > 0:
-            both = z_out_sums(s["normed"], wait_for(dz, following), out_part)
-        both = both[0]
+        following = lax.ppermute(d_pre[:16], ZX, [(b, a) for a, b in onward])
         z_sums[l] = both[:96]
         out_sums[l] = both[96:].reshape(4, 24, W).transpose(1, 0, 2).reshape(24, D)
         if l == LAYERS - 1:
             w_a, w_z, at = w_in1, w_in1, CA // W
         else:
             w_a, w_z, at = w_a0, w_z0, 0
-        da, other, mine, taps = conv_back(
-            d_pre, following, s["u"], s["edge"], same, conv_here[l], d_raw, dz, w_a, w_z, at
+        da, *parts, taps = conv_back(
+            l == 0, d_pre, following, s["u"], s["edge"], same, conv_here[l], d_raw, dz, w_a, w_z, at
         )
         conv_full = jnp.zeros((CONV + 1, CH), f32)
         conv_full = lax.dynamic_update_slice_in_dim(
@@ -1120,18 +1114,15 @@
             jnp.zeros((3, H), f32), head_sum[:3, :HL], group * HL, 1
         )
         head_grads[l] = head_full.reshape(3, 2, H // 2).transpose(1, 0, 2).reshape(2, 3 * H // 2)
-        if l == 0:
-            out_sums = [lax.ppermute(a, AX, TO_OWNER) for a in out_sums]
-            da = wait_for(da, out_sums)
         a_part = mm(s["normed"], da, 0, 0)
         if l == 0:
             a_part = a_part + small_block(conv_grads, head_grads).astype(f32)
         a_part = a_part.astype(bf)
         if l == 0:
-            parts = line_parts(other, mine, a_part)
+            parts = [lax.psum_scatter(parts[0], LINE, scatter_dimension=0, tiled=True)]
             a_sums[l] = group_reduce(a_part)
         else:
-            parts = line_parts(other, mine)
+            parts = line_parts(*parts, output)
             a_sums[l] = group_reduce(wait_for(a_part, parts[0]))
         if l > 0:
             grad, block = plain_call(
@@ -1151,11 +1142,11 @@
                 struct((TOK, D)),
                 (*parts, s["h"], grad),
             )
-            early = wait_for(early, parts[1])
-            parts = line_parts(*last_halves, parts[1:])
-            total = parts[0] + parts[1].astype(f32) + parts[2].astype(f32) + parts[3].astype(f32)
-            output = (h + total * r_last).astype(bf)
-
+
+    out_sums = [
+        lax.ppermute(wait_for(out_sums[l], a_part if l else a_sums[0]), AX, TO_OWNER)
+        for l in range(LAYERS)
+    ]
     late = jnp.concatenate([a_sums[0], z_sums[0]], axis=1)
     late = a2a(late.reshape(NG, 12, CA + W), LINE)
     small = jnp.sum(late[:, :, SMALL:CA], axis=0)

time: 679 us -> 649 us (0.956)
  starting transfers between devices: 211 us -> 164 us
  Pallas kernels: 176 us -> 151 us
  blocking collectives: 12.4 us -> 28.9 us
  waiting for transfers between devices: 123 us -> 138 us
  local copies, waits for them, and re-layouts: 63.2 us -> 72.3 us
    all_to_all x17 -> x16, waiting for transfers between devices: 46.5 us -> 77.9 us  [a2a(): return lax.all_to_all(a, axes, 0, 0, tiled=True)]
    ppermute x24 -> x15, waiting for transfers between devices: 54.4 us -> 30.1 us  [along_line(): return lax.ppermute(a, Y, [(i, (i + distance) % 4) for i in range(4)])]
    ppermute x20 -> x14, starting transfers between devices: 46.1 us -> 29.4 us  [core_swap(): return lax.ppermute(a, 'c', [(0, 1), (1, 0)])]
    all_to_all x1 -> x2, blocking collectives: 12.4 us -> 28.9 us  [a2a(): return lax.all_to_all(a, axes, 0, 0, tiled=True)]
    ppermute x24 -> x15, starting transfers between devices: 31.6 us -> 17.3 us  [along_line(): return lax.ppermute(a, Y, [(i, (i + distance) % 4) for i in range(4)])]
    all_to_all x17 -> x16, starting transfers between devices: 104 us -> 91.7 us  [a2a(): return lax.all_to_all(a, axes, 0, 0, tiled=True)]
    pallas_call x4 -> x2, Pallas kernels: 13.7 us -> 2.82 us  [line_parts(): pl.pallas_call(chip_kernel, out_shape=[struct((TOK, D))] + [struct((TOK,...]
    unnamed x160 -> x148, local copies, waits for them, and re-layouts: 17.2 us -> 25.7 us
  transfers between devices with their start and end apart: 71 -> 57, of which waited for: 31 -> 21; matrix products, arithmetic and copies ran while one was open for 13% -> 18% of each run, Pallas kernels for 19% -> 17%
where the time goes in v4:
time: 649 us; the launch traced here: 637 us
  starting transfers between devices  164 us (25%)
  Pallas kernels  151 us (23%)
  waiting for transfers between devices  138 us (21%)
  local copies, waits for them, and re-layouts  72.3 us (11%)
  matrix products  43.6 us (7%)
  blocking collectives  28.9 us (4%)
  other arithmetic  23.4 us (4%)
  between operations  16.1 us (2%)
    pallas_call x11, Pallas kernels, call(): pl.pallas_call(kernel, grid=(NS,), in_specs=ins, out_specs=outs, out_shap...  96.9 us
    all_to_all x16, starting transfers between devices, a2a(): return lax.all_to_all(a, axes, 0, 0, tiled=True)  91.7 us
    all_to_all x16, waiting for transfers between devices, a2a(): return lax.all_to_all(a, axes, 0, 0, tiled=True)  77.9 us
    dot_general x15, matrix products, mm(): lax.dot_general(a, b, (((ca,), (cb,)), ((), ())), preferred_element_type=...  43.6 us
    pallas_call x4, Pallas kernels, ordered_call(): pl.pallas_call(kernel, grid_spec=pltpu.PrefetchScalarGridSpec(num_scalar_...  40.7 us
    ppermute x15, waiting for transfers between devices, along_line(): return lax.ppermute(a, Y, [(i, (i + distance) % 4) for i in range(4)])  30.1 us
    ppermute x14, starting transfers between devices, core_swap(): return lax.ppermute(a, 'c', [(0, 1), (1, 0)])  29.4 us
    all_to_all x2, blocking collectives, a2a(): return lax.all_to_all(a, axes, 0, 0, tiled=True)  28.9 us
  transfers between devices with their start and end apart: 57, of which 21 were waited for; matrix products, arithmetic and copies ran while one was open for 18% of the time, Pallas kernels for 17%

profile of v4, /device:TPU:1, one launch (start us, length us, event | category | flops | bytes accessed | tf_op | source)
XLA Modules:
  0.0 637.2 jit_solution(10928532722059747117)
XLA Ops:
  31.4 7.8 %all-to-all-start.1 = ((bf16[16,96,768]{2,1,0:T(8,128)(2,1)}), bf16[16,96,768]{2,1,0:T(8,128)(2,1)}, u32[]{:S(2)}, u32[]{:S(2)}) async-start(bf16[16,96,768]{2,1,0:T(8,128)(2,1)} %broadcast_in_dim.31), calls=%async_computation.1 | async-start | bytes 4718592 | tf_op jit(solution)/shard_map/all_to_all | solution.py:54
  51.1 9.8 %collective-permute-start.2 = (bf16[128,1536]{1,0:T(8,128)(2,1)S(1)}, bf16[128,1536]{1,0:T(8,128)(2,1)S(1)}, u32[]{:S(2)}, u32[]{:S(2)}) collective-permute-start(bf16[128,1536]{1,0:T(8,128)(2,1)S(1)} %collective-permute-done.1.refs_2_), channel_id=1, source_target_pairs={{0,2},{2,0},{1,3},{3,1},{4,6},{6,4},{5,7},{7,5},{8,10},{10,8},{9,1... | collective-permute-start | bytes 1179656 | tf_op jit(solution)/shard_map/ppermute | solution.py:58
  67.0 9.2 %collective-permute-done.7 = bf16[2,24,1536]{2,1,0:T(8,128)(2,1)S(1)} collective-permute-done((bf16[2,24,1536]{2,1,0:T(8,128)(2,1)S(1)}, bf16[2,24,1536]{2,1,0:T(8,128)(2,1)S(1)}, u32[]{:S(2)}, u32[]{:S(2)}) %collective-permute-start.7) | collective-permute-done | bytes 147488 | tf_op jit(solution)/shard_map/ppermute | solution.py:1006
  77.9 6.9 %place_project.2 = (bf16[1024,1536]{1,0:T(8,128)(2,1)}, bf16[1024,640]{1,0:T(8,128)(2,1)}, bf16[1024,128]{1,0:T(8,128)(2,1)}) custom-call(s32[8]{0:T(128)} %stack.186.pos_ref, bf16[128,1536]{1,0:T(8,128)(2,1)} %copy-done.21, bf16[128,1536]{1,0:T(8,128)(2,1)} %copy-done.37, bf16[128,1536]{1,0:T(8,128)(2,1)} %copy-done.34, bf16[128,1536]{1,0:T(8,128)(2,1)} %copy-done.38, ...), custom_call_target="tpu_custom_call" | custom-call | flops 360000000 | bytes 1800000 | tf_op jit(solution)/shard_map/place_project/pallas_call | solution.py:763
  92.9 11.4 %span_mix.2 = (bf16[1024,640]{1,0:T(8,128)(2,1)}, bf16[1024,640]{1,0:T(8,128)(2,1)}, f32[1024,384]{1,0:T(8,128)}, f32[4,384,128]{2,1,0:T(8,128)}, f32[1024,128]{...) custom-call(s32[2,4]{1,0:T(2,128)} %pad_add_fusion.seg_ref, ...), custom_call_target="tpu_custom_call" | custom-call | flops 400000000 | bytes 2000000 | tf_op jit(solution)/shard_map/span_mix/pallas_call | solution.py:763
  104.3 16.9 %all_to_all.97.got_ref = bf16[16,32,128]{2,1,0:T(8,128)(2,1)} all-to-all(bf16[16,32,128]{2,1,0:T(8,128)(2,1)} %get-tuple-element.152), channel_id=1, replica_groups=mesh['z'=4,'x'=4,'yh'=2,'c'=2,'yl'=2] {'z','x'}, dimensions={0} | all-to-all | bytes 262144 | tf_op jit(solution)/shard_map/all_to_all | solution.py:54
  126.4 9.6 %all-gather.4.cloned.1.call-done = bf16[4608,384]{1,0:T(8,128)(2,1)} async-done(((bf16[288,384]{1,0:T(8,128)(2,1)}), bf16[4608,384]{1,0:T(8,128)(2,1)}) %all-gather.4.cloned.1.call-update) | async-done | bytes 3538960 | tf_op jit(solution)/shard_map/all_gather | solution.py:274
  143.3 9.2 %span_gate.2 = (f32[1024,384]{1,0:T(8,128)}, bf16[512,1536]{1,0:T(8,128)(2,1)}, bf16[512,1536]{1,0:T(8,128)(2,1)}, f32[8,1024]{1,0:T(8,128)}) custom-call(s32[4]{0:T(128)} %pad_add_fusion.1.order_ref, s32[2,4]{1,0:T(2,128)} %pad_add_fusion.seg_ref, bf16[16,32,128]{2,1,0:T(8,128)(2,1)} %copy-done.23, f32[4,384,128]{2,1,0:T(8,128)} %get-tuple-element.157.local_ref, ...), custom_call_target="tpu_custom_call" | custom-call | flops 400000000 | bytes 2000000 | tf_op jit(solution)/shard_map/span_gate/pallas_call | solution.py:781
  169.7 10.9 %all-to-all-done.4 = f32[8,1,128]{2,1,0:T(1,128)S(1)} async-done(((f32[8,1,128]{2,1,0:T(1,128)}), f32[8,1,128]{2,1,0:T(1,128)S(1)}, u32[]{:S(2)}, u32[]{:S(2)}) %all-to-all-start.4) | async-done | bytes 4128 | tf_op jit(solution)/shard_map/all_to_all | solution.py:54
  186.7 7.7 %collective-permute-done.14.refs_2_ = bf16[128,1536]{1,0:T(8,128)(2,1)S(1)} collective-permute-done((bf16[128,1536]{1,0:T(8,128)(2,1)}, bf16[128,1536]{1,0:T(8,128)(2,1)S(1)}, u32[]{:S(2)}, u32[]{:S(2)}) %collective-permute-start.14) | collective-permute-done | bytes 393248 | tf_op jit(solution)/shard_map/ppermute | solution.py:66
  199.9 6.7 %collective-permute-done.18.refs_6_ = bf16[128,1536]{1,0:T(8,128)(2,1)S(1)} collective-permute-done((bf16[128,1536]{1,0:T(8,128)(2,1)}, bf16[128,1536]{1,0:T(8,128)(2,1)S(1)}, u32[]{:S(2)}, u32[]{:S(2)}) %collective-permute-start.18) | collective-permute-done | bytes 393248 | tf_op jit(solution)/shard_map/ppermute | solution.py:66
  210.9 7.0 %place_project.3 = (bf16[1024,1536]{1,0:T(8,128)(2,1)}, bf16[1024,640]{1,0:T(8,128)(2,1)}, bf16[1024,128]{1,0:T(8,128)(2,1)}) custom-call(s32[8]{0:T(128)} %stack.186.pos_ref, bf16[128,1536]{1,0:T(8,128)(2,1)} %get-tuple-element.171.refs_0_, bf16[128,1536]{1,0:T(8,128)(2,1)} %copy-done.42, bf16[128,1536]{1,0:T(8,128)(2,1)} %copy-done.39, ...), custom_call_target="tpu_custom_call" | custom-call | flops 360000000 | bytes 1800000 | tf_op jit(solution)/shard_map/place_project/pallas_call | solution.py:763
  226.7 11.4 %span_mix.3 = (bf16[1024,640]{1,0:T(8,128)(2,1)}, bf16[1024,640]{1,0:T(8,128)(2,1)}, f32[1024,384]{1,0:T(8,128)}, f32[4,384,128]{2,1,0:T(8,128)}, f32[1024,128]{...) custom-call(s32[2,4]{1,0:T(2,128)} %pad_add_fusion.seg_ref, ...), custom_call_target="tpu_custom_call" | custom-call | flops 400000000 | bytes 2000000 | tf_op jit(solution)/shard_map/span_mix/pallas_call | solution.py:763
  264.5 8.6 %span_gate.3 = (f32[1024,384]{1,0:T(8,128)}, bf16[1024,1536]{1,0:T(8,128)(2,1)}, f32[8,1024]{1,0:T(8,128)}) custom-call(s32[4]{0:T(128)} %pad_add_fusion.1.order_ref, s32[2,4]{1,0:T(2,128)} %pad_add_fusion.seg_ref, bf16[16,32,128]{2,1,0:T(8,128)(2,1)} %copy-done.22, f32[4,384,128]{2,1,0:T(8,128)} %get-tuple-element.181.local_ref, ...), custom_call_target="tpu_custom_call" | custom-call | flops 400000000 | bytes 2000000 | tf_op jit(solution)/shard_map/span_gate/pallas_call | solution.py:781
  274.0 12.1 %all_to_all.98 = f32[8,2,1024]{2,1,0:T(2,128)S(1)} all-to-all(f32[8,2,1024]{2,1,0:T(2,128)S(1)} %broadcast_in_dim.38), channel_id=1, replica_groups=mesh['z'=4,'x'=4,'yh'=2,'c'=2,'yl'=2] {'yh','c','yl'}, dimensions={0} | all-to-all | bytes 131072 | tf_op jit(solution)/shard_map/all_to_all | solution.py:54
  286.7 7.9 %span_gate_back.2 = (bf16[1024,384]{1,0:T(8,128)(2,1)}, bf16[1024,384]{1,0:T(8,128)(2,1)}, bf16[1024,384]{1,0:T(8,128)(2,1)}, f32[4,384,128]{2,1,0:T(8,128)}, f3...) custom-call(s32[2,4]{1,0:T(2,128)} %pad_add_fusion.seg_ref, f32[1024,384]{1,0:T(8,128)} %fusion.47.rest_0_.grad_ref, ...), custom_call_target="tpu_custom_call" | custom-call | flops 480000000 | bytes 2400000 | tf_op jit(solution)/shard_map/span_gate_back/pallas_call | solution.py:763
  321.4 6.9 %all-to-all-start.11 = ((bf16[16,192,384]{2,1,0:T(8,128)(2,1)}), bf16[16,192,384]{2,1,0:T(8,128)(2,1)}, u32[]{:S(2)}, u32[]{:S(2)}) async-start(bf16[16,192,384]{2,1,0:T(8,128)(2,1)} %constant_dynamic-update-slice_fusion), calls=%async_computation.12 | async-start | bytes 4718592 | tf_op jit(solution)/shard_map/all_to_all | solution.py:54
  328.3 7.9 %span_mix_back.2 = (f32[1024,384]{1,0:T(8,128)}, bf16[1024,256]{1,0:T(8,128)(2,1)}) custom-call(bf16[1024,640]{1,0:T(8,128)(2,1)} %get-tuple-element.184.v_ref, f32[1024,128]{1,0:T(8,128)} %get-tuple-element.199.step_ref, f32[1024,128]{1,0:T(8,128)} %get-tuple-element.183.run_ref, s32[1024,1]{1,0:T(8,128)} %copy.268.segc_ref, s32[4,1,256]{2,1,0:T(1,128)} %bitcast.250, ...), custom_call_target="tpu_custom_call" | custom-call | flops 560000000 | bytes 2800000 | tf_op jit(solution)/shard_map/span_mix_back/pallas_call | solution.py:763
  336.2 11.8 %span_end.2 = (bf16[1024,640]{1,0:T(8,128)(2,1)}, bf16[1024,128]{1,0:T(8,128)(2,1)}, f32[8,128]{1,0:T(8,128)}) custom-call(s32[2,4]{1,0:T(2,128)} %pad_add_fusion.seg_ref, bf16[16,32,128]{2,1,0:T(8,128)(2,1)} %copy-done.28, bf16[16,32,128]{2,1,0:T(8,128)(2,1)} %copy-done.22, f32[4,384,128]{2,1,0:T(8,128)} %get-tuple-element.181.local_ref, ...), custom_call_target="tpu_custom_call" | custom-call | flops 640000000 | bytes 3200000 | tf_op jit(solution)/shard_map/span_end/pallas_call | solution.py:763
  356.9 11.8 %conv_back.2 = (bf16[1024,768]{1,0:T(8,128)(2,1)}, bf16[512,1536]{1,0:T(8,128)(2,1)}, bf16[512,1536]{1,0:T(8,128)(2,1)}, f32[8,640]{1,0:T(8,128)}) custom-call(s32[4]{0:T(128)} %pad_add_fusion.1.order_ref, bf16[1024,640]{1,0:T(8,128)(2,1)} %get-tuple-element.204.dpre_ref.next_ref, bf16[1024,640]{1,0:T(8,128)(2,1)} %get-tuple-element.204.dpre_ref.next_ref, ...), custom_call_target="tpu_custom_call" | custom-call | flops 400000000 | bytes 2000000 | tf_op jit(solution)/shard_map/conv_back/pallas_call | solution.py:781
  406.2 7.7 %collective-permute-done.25.refs_3_ = bf16[128,1536]{1,0:T(8,128)(2,1)S(1)} collective-permute-done((bf16[128,1536]{1,0:T(8,128)(2,1)}, bf16[128,1536]{1,0:T(8,128)(2,1)S(1)}, u32[]{:S(2)}, u32[]{:S(2)}) %collective-permute-start.25) | collective-permute-done | bytes 393248 | tf_op jit(solution)/shard_map/ppermute | solution.py:66
  420.6 8.8 %all-to-all-done.10 = bf16[16,96,768]{2,1,0:T(8,128)(2,1)} async-done(((bf16[16,96,768]{2,1,0:T(8,128)(2,1)}), bf16[16,96,768]{2,1,0:T(8,128)(2,1)}, u32[]{:S(2)}, u32[]{:S(2)}) %all-to-all-start.10) | async-done | bytes 2359328 | tf_op jit(solution)/shard_map/all_to_all | solution.py:54
  451.9 8.2 %span_gate_back.3 = (bf16[1024,384]{1,0:T(8,128)(2,1)}, bf16[1024,384]{1,0:T(8,128)(2,1)}, bf16[1024,384]{1,0:T(8,128)(2,1)}, f32[4,384,128]{2,1,0:T(8,128)}, f3...) custom-call(s32[2,4]{1,0:T(2,128)} %pad_add_fusion.seg_ref, bf16[1024,1536]{1,0:T(8,128)(2,1)} %get-tuple-element.222.grad_ref, ...), custom_call_target="tpu_custom_call" | custom-call | flops 480000000 | bytes 2400000 | tf_op jit(solution)/shard_map/span_gate_back/pallas_call | solution.py:763
  487.0 7.9 %span_mix_back.3 = (f32[1024,384]{1,0:T(8,128)}, bf16[1024,256]{1,0:T(8,128)(2,1)}) custom-call(bf16[1024,640]{1,0:T(8,128)(2,1)} %get-tuple-element.160.v_ref, f32[1024,128]{1,0:T(8,128)} %get-tuple-element.236.step_ref, f32[1024,128]{1,0:T(8,128)} %get-tuple-element.159.run_ref, s32[1024,1]{1,0:T(8,128)} %copy.268.segc_ref, s32[4,1,256]{2,1,0:T(1,128)} %bitcast.251, ...), custom_call_target="tpu_custom_call" | custom-call | flops 560000000 | bytes 2800000 | tf_op jit(solution)/shard_map/span_mix_back/pallas_call | solution.py:763
  495.6 11.8 %span_end.3 = (bf16[1024,640]{1,0:T(8,128)(2,1)}, bf16[1024,128]{1,0:T(8,128)(2,1)}, f32[8,128]{1,0:T(8,128)}) custom-call(s32[2,4]{1,0:T(2,128)} %pad_add_fusion.seg_ref, bf16[16,32,128]{2,1,0:T(8,128)(2,1)} %copy-done.29, bf16[16,32,128]{2,1,0:T(8,128)(2,1)} %copy-done.23, f32[4,384,128]{2,1,0:T(8,128)} %get-tuple-element.157.local_ref, ...), custom_call_target="tpu_custom_call" | custom-call | flops 640000000 | bytes 3200000 | tf_op jit(solution)/shard_map/span_end/pallas_call | solution.py:763
  509.6 7.9 %all-to-all-start.16 = ((bf16[16,192,384]{2,1,0:T(8,128)(2,1)}), bf16[16,192,384]{2,1,0:T(8,128)(2,1)}, u32[]{:S(2)}, u32[]{:S(2)}) async-start(bf16[16,192,384]{2,1,0:T(8,128)(2,1)} %constant_dynamic-update-slice_fusion.5), calls=%async_computation.18 | async-start | bytes 4718592 | tf_op jit(solution)/shard_map/all_to_all | solution.py:54
  518.6 11.1 %conv_back.3 = (bf16[1024,768]{1,0:T(8,128)(2,1)}, bf16[1024,1536]{1,0:T(8,128)(2,1)}, f32[8,640]{1,0:T(8,128)}) custom-call(s32[4]{0:T(128)} %pad_add_fusion.1.order_ref, bf16[1024,640]{1,0:T(8,128)(2,1)} %get-tuple-element.241.dpre_ref.next_ref, bf16[1024,640]{1,0:T(8,128)(2,1)} %get-tuple-element.241.dpre_ref.next_ref, bf16[16,640]{1,0:T(8,128)(2,1)} %copy-done.49, ...), custom_call_target="tpu_custom_call" | custom-call | flops 400000000 | bytes 2000000 | tf_op jit(solution)/shard_map/conv_back/pallas_call | solution.py:781
  545.8 8.6 %all-to-all-start.15 = ((bf16[16,96,768]{2,1,0:T(8,128)(2,1)}), bf16[16,96,768]{2,1,0:T(8,128)(2,1)}, u32[]{:S(2)}, u32[]{:S(2)}) async-start(bf16[16,96,768]{2,1,0:T(8,128)(2,1)} %bitcast.216), calls=%async_computation.17 | async-start | bytes 4718592 | tf_op jit(solution)/shard_map/all_to_all | solution.py:54
  556.7 6.9 %collective-permute-start.35 = (f32[24,1536]{1,0:T(8,128)S(1)}, f32[24,1536]{1,0:T(8,128)S(1)}, u32[]{:S(2)}, u32[]{:S(2)}) collective-permute-start(f32[24,1536]{1,0:T(8,128)S(1)} %bitcast.254), channel_id=1, source_target_pairs={{0,0},{8,1},{16,2},{24,3},{32,4},{40,5},{48,6},{56,7},{64,8},{72,9... | collective-permute-start | bytes 442376 | tf_op jit(solution)/shard_map/ppermute | solution.py:1147
  565.7 20.1 %all-to-all-done.15 = bf16[16,96,768]{2,1,0:T(8,128)(2,1)} async-done(((bf16[16,96,768]{2,1,0:T(8,128)(2,1)}), bf16[16,96,768]{2,1,0:T(8,128)(2,1)}, u32[]{:S(2)}, u32[]{:S(2)}) %all-to-all-start.15) | async-done | bytes 2359328 | tf_op jit(solution)/shard_map/all_to_all | solution.py:54
  595.2 7.8 %all-to-all-start.17 = ((f32[8,12,1152]{2,1,0:T(8,128)}), f32[8,12,1152]{2,1,0:T(8,128)S(1)}, u32[]{:S(2)}, u32[]{:S(2)}) async-start(f32[8,12,1152]{2,1,0:T(8,128)} %reshape.546), calls=%async_computation.19 | async-start | bytes 1179648 | tf_op jit(solution)/shard_map/all_to_all | solution.py:54
  605.5 13.3 %all-to-all-done.17 = f32[8,12,1152]{2,1,0:T(8,128)S(1)} async-done(((f32[8,12,1152]{2,1,0:T(8,128)}), f32[8,12,1152]{2,1,0:T(8,128)S(1)}, u32[]{:S(2)}, u32[]{:S(2)}) %all-to-all-start.17) | async-done | bytes 442400 | tf_op jit(solution)/shard_map/all_to_all | solution.py:54
  (476 shorter events, 309.6 us)
Async XLA Ops:
  31.4 45.6 %all-to-all-start.1 = ((bf16[16,96,768]{2,1,0:T(8,128)(2,1)}), bf16[16,96,768]{2,1,0:T(8,128)(2,1)}, u32[]{:S(2)}, u32[]{:S(2)}) async-start(bf16[16,96,768]{2,1,0:T(8,128)(2,1)} %broadcast_in_dim.31), calls=%async_computation.1 | async-start | bytes 4718592 | tf_op jit(solution)/shard_map/all_to_all | solution.py:54
  39.2 96.8 %all-gather.4.cloned.1.call-start = ((), (), s32[]{:S(2)}) async-start(), calls=%async_computation.20 | async-start | bytes 3760128 | tf_op jit(solution)/shard_map/all_gather | solution.py:274
  40.0 20.9 %collective-permute-start.3 = (bf16[128,1536]{1,0:T(8,128)(2,1)S(1)}, bf16[128,1536]{1,0:T(8,128)(2,1)S(1)}, u32[]{:S(2)}, u32[]{:S(2)}) collective-permute-start(bf16[128,1536]{1,0:T(8,128)(2,1)S(1)} %multiply_convert_fusion.refs_0_), channel_id=1, source_target_pairs={{0,5},{1,0},{4,1},{5,4},{2,7},{3,2},{6,3},{7,6},{8,13},{9,8},{12,9... | collective-permute-start | bytes 1179656 | tf_op jit(solution)/shard_map/ppermute | solution.py:66
  42.4 18.6 %collective-permute-start.5 = (bf16[128,1536]{1,0:T(8,128)(2,1)S(1)}, bf16[128,1536]{1,0:T(8,128)(2,1)S(1)}, u32[]{:S(2)}, u32[]{:S(2)}) collective-permute-start(bf16[128,1536]{1,0:T(8,128)(2,1)S(1)} %multiply_convert_fusion.refs_0_), channel_id=1, source_target_pairs={{0,4},{1,5},{4,0},{5,1},{2,6},{3,7},{6,2},{7,3},{8,12},{9,13},{12,... | collective-permute-start | bytes 1179656 | tf_op jit(solution)/shard_map/ppermute | solution.py:66
  47.2 29.8 %collective-permute-start = (bf16[128,1536]{1,0:T(8,128)(2,1)S(1)}, bf16[128,1536]{1,0:T(8,128)(2,1)S(1)}, u32[]{:S(2)}, u32[]{:S(2)}) collective-permute-start(bf16[128,1536]{1,0:T(8,128)(2,1)S(1)} %multiply_convert_fusion.refs_0_), channel_id=1, source_target_pairs={{0,2},{2,0},{1,3},{3,1},{4,6},{6,4},{5,7},{7,5},{8,10},{10,8},{9,1... | collective-permute-start | bytes 1179656 | tf_op jit(solution)/shard_map/ppermute | solution.py:58
  51.1 26.0 %collective-permute-start.2 = (bf16[128,1536]{1,0:T(8,128)(2,1)S(1)}, bf16[128,1536]{1,0:T(8,128)(2,1)S(1)}, u32[]{:S(2)}, u32[]{:S(2)}) collective-permute-start(bf16[128,1536]{1,0:T(8,128)(2,1)S(1)} %collective-permute-done.1.refs_2_), channel_id=1, source_target_pairs={{0,2},{2,0},{1,3},{3,1},{4,6},{6,4},{5,7},{7,5},{8,10},{10,8},{9,1... | collective-permute-start | bytes 1179656 | tf_op jit(solution)/shard_map/ppermute | solution.py:58
  60.9 16.2 %collective-permute-start.4 = (bf16[128,1536]{1,0:T(8,128)(2,1)S(1)}, bf16[128,1536]{1,0:T(8,128)(2,1)}, u32[]{:S(2)}, u32[]{:S(2)}) collective-permute-start(bf16[128,1536]{1,0:T(8,128)(2,1)S(1)} %collective-permute-done.3.refs_4_), channel_id=1, source_target_pairs={{0,2},{2,0},{1,3},{3,1},{4,6},{6,4},{5,7},{7,5},{8,10},{10,8},{9,1... | collective-permute-start | bytes 1179656 | tf_op jit(solution)/shard_map/ppermute | solution.py:58
  61.0 16.1 %collective-permute-start.6 = (bf16[128,1536]{1,0:T(8,128)(2,1)S(1)}, bf16[128,1536]{1,0:T(8,128)(2,1)}, u32[]{:S(2)}, u32[]{:S(2)}) collective-permute-start(bf16[128,1536]{1,0:T(8,128)(2,1)S(1)} %collective-permute-done.5.refs_6_), channel_id=1, source_target_pairs={{0,2},{2,0},{1,3},{3,1},{4,6},{6,4},{5,7},{7,5},{8,10},{10,8},{9,1... | collective-permute-start | bytes 1179656 | tf_op jit(solution)/shard_map/ppermute | solution.py:58
  85.5 123.9 %all-gather.6.cloned.1.call-start = ((), (), s32[]{:S(2)}) async-start(), calls=%async_computation.21 | async-start | bytes 3760128 | tf_op jit(solution)/shard_map/all_gather | solution.py:274
  86.3 170.7 %all-gather.8.cloned.1.call-start = ((), (), s32[]{:S(2)}) async-start(), calls=%async_computation.22 | async-start | bytes 3538944 | tf_op jit(solution)/shard_map/all_gather | solution.py:1008
  122.9 18.9 %all-to-all-start.3 = ((bf16[16,32,128]{2,1,0:T(8,128)(2,1)}), bf16[16,32,128]{2,1,0:T(8,128)(2,1)S(1)}, u32[]{:S(2)}, u32[]{:S(2)}) async-start(bf16[16,32,128]{2,1,0:T(8,128)(2,1)} %group_scan.4), calls=%async_computation.3 | async-start | bytes 262144 | tf_op jit(solution)/shard_map/all_to_all | solution.py:54
  158.9 21.8 %collective-permute-start.10 = (bf16[128,1536]{1,0:T(8,128)(2,1)}, bf16[128,1536]{1,0:T(8,128)(2,1)S(1)}, u32[]{:S(2)}, u32[]{:S(2)}) collective-permute-start(bf16[128,1536]{1,0:T(8,128)(2,1)} %get-tuple-element.165), channel_id=1, source_target_pairs={{0,1},{1,4},{4,5},{5,0},{2,3},{3,6},{6,7},{7,2},{8,9},{9,12},{12,1... | collective-permute-start | bytes 1179656 | tf_op jit(solution)/shard_map/ppermute | solution.py:66
  159.9 20.8 %collective-permute-start.11 = (bf16[128,1536]{1,0:T(8,128)(2,1)S(1)}, bf16[128,1536]{1,0:T(8,128)(2,1)S(1)}, u32[]{:S(2)}, u32[]{:S(2)}) collective-permute-start(bf16[128,1536]{1,0:T(8,128)(2,1)S(1)} %get-tuple-element.166), channel_id=1, source_target_pairs={{0,5},{1,0},{4,1},{5,4},{2,7},{3,2},{6,3},{7,6},{8,13},{9,8},{12,9... | collective-permute-start | bytes 1179656 | tf_op jit(solution)/shard_map/ppermute | solution.py:66
  161.6 19.1 %collective-permute-start.12 = (bf16[128,1536]{1,0:T(8,128)(2,1)S(1)}, bf16[128,1536]{1,0:T(8,128)(2,1)S(1)}, u32[]{:S(2)}, u32[]{:S(2)}) collective-permute-start(bf16[128,1536]{1,0:T(8,128)(2,1)S(1)} %get-tuple-element.167), channel_id=1, source_target_pairs={{0,4},{1,5},{4,0},{5,1},{2,6},{3,7},{6,2},{7,3},{8,12},{9,13},{12,... | collective-permute-start | bytes 1179656 | tf_op jit(solution)/shard_map/ppermute | solution.py:66
  164.2 16.4 %all-to-all-start.4 = ((f32[8,1,128]{2,1,0:T(1,128)}), f32[8,1,128]{2,1,0:T(1,128)S(1)}, u32[]{:S(2)}, u32[]{:S(2)}) async-start(f32[8,1,128]{2,1,0:T(1,128)} %slice_bitcast_fusion.2), calls=%async_computation.4 | async-start | bytes 8192 | tf_op jit(solution)/shard_map/all_to_all | solution.py:54
  185.4 21.1 %collective-permute-start.18 = (bf16[128,1536]{1,0:T(8,128)(2,1)}, bf16[128,1536]{1,0:T(8,128)(2,1)S(1)}, u32[]{:S(2)}, u32[]{:S(2)}) collective-permute-start(bf16[128,1536]{1,0:T(8,128)(2,1)} %get-tuple-element.171.refs_0_), channel_id=1, source_target_pairs={{0,4},{1,5},{4,0},{5,1},{2,6},{3,7},{6,2},{7,3},{8,12},{9,13},{12,... | collective-permute-start | bytes 1179656 | tf_op jit(solution)/shard_map/ppermute | solution.py:66
  185.7 23.7 %collective-permute-start.13 = (bf16[128,1536]{1,0:T(8,128)(2,1)}, bf16[128,1536]{1,0:T(8,128)(2,1)S(1)}, u32[]{:S(2)}, u32[]{:S(2)}) collective-permute-start(bf16[128,1536]{1,0:T(8,128)(2,1)} %get-tuple-element.171.refs_0_), channel_id=1, source_target_pairs={{0,2},{2,0},{1,3},{3,1},{4,6},{6,4},{5,7},{7,5},{8,10},{10,8},{9,1... | collective-permute-start | bytes 1179656 | tf_op jit(solution)/shard_map/ppermute | solution.py:58
  194.4 15.0 %collective-permute-start.15 = (bf16[128,1536]{1,0:T(8,128)(2,1)S(1)}, bf16[128,1536]{1,0:T(8,128)(2,1)S(1)}, u32[]{:S(2)}, u32[]{:S(2)}) collective-permute-start(bf16[128,1536]{1,0:T(8,128)(2,1)S(1)} %collective-permute-done.14.refs_2_), channel_id=1, source_target_pairs={{0,2},{2,0},{1,3},{3,1},{4,6},{6,4},{5,7},{7,5},{8,10},{10,8},{9,1... | collective-permute-start | bytes 1179656 | tf_op jit(solution)/shard_map/ppermute | solution.py:58
  257.0 121.9 %reduce-scatter.3.cloned.1.call-start = ((), (), s32[]{:S(2)}) async-start(), calls=%async_computation.23 | async-start | bytes 3538944 | tf_op jit(solution)/shard_map/reduce_scatter | solution.py:1068
  321.4 63.7 %all-to-all-start.11 = ((bf16[16,192,384]{2,1,0:T(8,128)(2,1)}), bf16[16,192,384]{2,1,0:T(8,128)(2,1)}, u32[]{:S(2)}, u32[]{:S(2)}) async-start(bf16[16,192,384]{2,1,0:T(8,128)(2,1)} %constant_dynamic-update-slice_fusion), calls=%async_computation.12 | async-start | bytes 4718592 | tf_op jit(solution)/shard_map/all_to_all | solution.py:54
  385.9 43.5 %all-to-all-start.10 = ((bf16[16,96,768]{2,1,0:T(8,128)(2,1)}), bf16[16,96,768]{2,1,0:T(8,128)(2,1)}, u32[]{:S(2)}, u32[]{:S(2)}) async-start(bf16[16,96,768]{2,1,0:T(8,128)(2,1)} %bitcast.215), calls=%async_computation.11 | async-start | bytes 4718592 | tf_op jit(solution)/shard_map/all_to_all | solution.py:54
  396.6 17.2 %collective-permute-start.25 = (bf16[128,1536]{1,0:T(8,128)(2,1)}, bf16[128,1536]{1,0:T(8,128)(2,1)S(1)}, u32[]{:S(2)}, u32[]{:S(2)}) collective-permute-start(bf16[128,1536]{1,0:T(8,128)(2,1)} %copy-done.8), channel_id=1, source_target_pairs={{0,4},{1,5},{4,0},{5,1},{2,6},{3,7},{6,2},{7,3},{8,12},{9,13},{12,... | collective-permute-start | bytes 1179656 | tf_op jit(solution)/shard_map/ppermute | solution.py:66
  416.5 20.7 %collective-permute-start.27 = (bf16[144,1536]{1,0:T(8,128)(2,1)}, bf16[144,1536]{1,0:T(8,128)(2,1)S(1)}, u32[]{:S(2)}, u32[]{:S(2)}) collective-permute-start(bf16[144,1536]{1,0:T(8,128)(2,1)} %get-tuple-element.215.refs_0_), channel_id=1, source_target_pairs={{0,1},{1,4},{4,5},{5,0},{2,3},{3,6},{6,7},{7,2},{8,9},{9,12},{12,1... | collective-permute-start | bytes 1327112 | tf_op jit(solution)/shard_map/ppermute | solution.py:66
  417.2 20.5 %collective-permute-start.29 = (bf16[144,1536]{1,0:T(8,128)(2,1)}, bf16[144,1536]{1,0:T(8,128)(2,1)}, u32[]{:S(2)}, u32[]{:S(2)}) collective-permute-start(bf16[144,1536]{1,0:T(8,128)(2,1)} %get-tuple-element.215.refs_0_), channel_id=1, source_target_pairs={{0,5},{1,0},{4,1},{5,4},{2,7},{3,2},{6,3},{7,6},{8,13},{9,8},{12,9... | collective-permute-start | bytes 1327112 | tf_op jit(solution)/shard_map/ppermute | solution.py:66
  419.5 21.2 %collective-permute-start.31 = (bf16[144,1536]{1,0:T(8,128)(2,1)}, bf16[144,1536]{1,0:T(8,128)(2,1)}, u32[]{:S(2)}, u32[]{:S(2)}) collective-permute-start(bf16[144,1536]{1,0:T(8,128)(2,1)} %get-tuple-element.215.refs_0_), channel_id=1, source_target_pairs={{0,4},{1,5},{4,0},{5,1},{2,6},{3,7},{6,2},{7,3},{8,12},{9,13},{12,... | collective-permute-start | bytes 1327112 | tf_op jit(solution)/shard_map/ppermute | solution.py:66
  473.6 21.3 %all-to-all-start.14 = ((bf16[16,32,128]{2,1,0:T(8,128)(2,1)}), bf16[16,32,128]{2,1,0:T(8,128)(2,1)S(1)}, u32[]{:S(2)}, u32[]{:S(2)}) async-start(bf16[16,32,128]{2,1,0:T(8,128)(2,1)} %group_scan.7), calls=%async_computation.15 | async-start | bytes 262144 | tf_op jit(solution)/shard_map/all_to_all | solution.py:54
  509.6 36.2 %all-to-all-start.16 = ((bf16[16,192,384]{2,1,0:T(8,128)(2,1)}), bf16[16,192,384]{2,1,0:T(8,128)(2,1)}, u32[]{:S(2)}, u32[]{:S(2)}) async-start(bf16[16,192,384]{2,1,0:T(8,128)(2,1)} %constant_dynamic-update-slice_fusion.5), calls=%async_computation.18 | async-start | bytes 4718592 | tf_op jit(solution)/shard_map/all_to_all | solution.py:54
  545.8 40.0 %all-to-all-start.15 = ((bf16[16,96,768]{2,1,0:T(8,128)(2,1)}), bf16[16,96,768]{2,1,0:T(8,128)(2,1)}, u32[]{:S(2)}, u32[]{:S(2)}) async-start(bf16[16,96,768]{2,1,0:T(8,128)(2,1)} %bitcast.216), calls=%async_computation.17 | async-start | bytes 4718592 | tf_op jit(solution)/shard_map/all_to_all | solution.py:54
  554.4 73.7 %reduce-scatter.5.cloned.1.call-start = ((), (), s32[]{:S(2)}) async-start(), calls=%async_computation.24 | async-start | bytes 3538944 | tf_op jit(solution)/shard_map/reduce_scatter | solution.py:1122
  556.7 46.3 %collective-permute-start.35 = (f32[24,1536]{1,0:T(8,128)S(1)}, f32[24,1536]{1,0:T(8,128)S(1)}, u32[]{:S(2)}, u32[]{:S(2)}) collective-permute-start(f32[24,1536]{1,0:T(8,128)S(1)} %bitcast.254), channel_id=1, source_target_pairs={{0,0},{8,1},{16,2},{24,3},{32,4},{40,5},{48,6},{56,7},{64,8},{72,9... | collective-permute-start | bytes 442376 | tf_op jit(solution)/shard_map/ppermute | solution.py:1147
  587.8 15.2 %collective-permute-start.34 = (f32[24,1536]{1,0:T(8,128)S(1)}, f32[24,1536]{1,0:T(8,128)}, u32[]{:S(2)}, u32[]{:S(2)}) collective-permute-start(f32[24,1536]{1,0:T(8,128)S(1)} %bitcast.255), channel_id=1, source_target_pairs={{0,0},{8,1},{16,2},{24,3},{32,4},{40,5},{48,6},{56,7},{64,8},{72,9... | collective-permute-start | bytes 442376 | tf_op jit(solution)/shard_map/ppermute | solution.py:1147
  595.2 23.6 %all-to-all-start.17 = ((f32[8,12,1152]{2,1,0:T(8,128)}), f32[8,12,1152]{2,1,0:T(8,128)S(1)}, u32[]{:S(2)}, u32[]{:S(2)}) async-start(f32[8,12,1152]{2,1,0:T(8,128)} %reshape.546), calls=%async_computation.19 | async-start | bytes 1179648 | tf_op jit(solution)/shard_map/all_to_all | solution.py:54
  (93 other events, 876.1 us)
Sparse Core Ops, SparseCore 0:
  85.6 50.3 all-gather.3
  138.8 47.6 all-gather.5
  188.1 59.1 all-gather.7
  273.3 56.1 reduce-scatter.2
  557.3 69.4 reduce-scatter.4

commit v5 on v4

--- a/solution.py
+++ b/solution.py
@@ -319,44 +319,65 @@
     return jnp.concatenate([x, bc, step, z], axis=2)
 
 
-SCAN_ROWS = HL * HP // NQ
-
-
-def scan_kernel(reverse, q_ref, got_ref, out_ref):
-    row = q_ref[0] * SCAN_ROWS + lax.broadcasted_iota(jnp.int32, (SCAN_ROWS, N), 0)
-    lane = lax.broadcasted_iota(jnp.int32, (SCAN_ROWS, N), 1)
-    head = jnp.zeros((SCAN_ROWS, N), jnp.int32)
-    for k in range(1, HL):
-        head = head + (row >= k * HP).astype(jnp.int32)
-    chosen = (lane == head) | (lane == head + HL) | (lane == head + 2 * HL)
-    carry = jnp.zeros((SCAN_ROWS, N), f32)
-    pad = jnp.zeros((32 - SCAN_ROWS, N), f32)
-    for j in range(NQ - 1, -1, -1) if reverse else range(NQ):
-        out_ref[j] = jnp.concatenate([carry, pad], axis=0).astype(bf)
-        block = got_ref[j].astype(f32)
-        decay = jnp.sum(
-            jnp.where(chosen, block[SCAN_ROWS : SCAN_ROWS + 1], 0.0), axis=1, keepdims=True
-        )
-        carry = decay * carry + block[:SCAN_ROWS]
+STATE_ROWS = W + 16
+
+
+def line_scan_kernel(reverse, at_ref, own_ref, r1, r2, r3, sent_ref, before_ref, decay_ref):
+    rank = 3 - at_ref[0] if reverse else at_ref[0]
+    blocks = [read_states(ref) for ref in ((r3, r2, r1) if reverse else (r1, r2, r3))]
+    own, own_decay = read_states(own_ref)
+    state, decay = fold_before(rank, blocks)
+    before_ref[...] = state
+    decay_ref[...] = jnp.broadcast_to(decay, (8, 128))
+    total = by_rows(own_decay, state) + own
+    decay = decay * own_decay
+    for i in (1, 2, 3):
+        next_state, next_decay = blocks[3 - i]
+        there = rank + i <= 3
+        total = jnp.where(there, by_rows(next_decay, total) + next_state, total)
+        decay = jnp.where(there, decay * next_decay, decay)
+    write_states(sent_ref, total, decay)
+
+
+def fold_before(rank, blocks):
+    state = jnp.zeros((W, N), f32)
+    decay = jnp.ones((1, 128), f32)
+    for i in (3, 2, 1):
+        block, block_decay = blocks[i - 1]
+        there = rank >= i
+        state = jnp.where(there, by_rows(block_decay, state) + block, state)
+        decay = jnp.where(there, decay * block_decay, decay)
+    return state, decay
+
+
+def final_states(reverse, at_ref, r1, r2, r3, before_ref, decay_ref):
+    rank = 3 - at_ref[0] if reverse else at_ref[0]
+    blocks = [read_states(ref) for ref in ((r3, r2, r1) if reverse else (r1, r2, r3))]
+    entering = fold_before(rank, blocks)[0]
+    return by_rows(decay_ref[0:1], entering) + before_ref[...]
 
 
 def exclusive_scan(sent, reverse, first, second):
-    q = lax.axis_index(ZX)
-    got = a2a(sent, ZX)
+    def around(a, axis):
+        return [lax.ppermute(a, axis, [(i, (i + d) % 4) for i in range(4)]) for d in (1, 2, 3)]
+
+    def index(axis):
+        return lax.axis_index(axis).reshape(1).astype(jnp.int32)
+
+    got = around(sent, "x")
     if first is not None:
-        got = wait_for(got, first)
-    outs = pl.pallas_call(
-        functools.partial(scan_kernel, reverse),
-        out_shape=jax.ShapeDtypeStruct((NQ, 32, N), bf),
-        in_specs=[
-            pl.BlockSpec(memory_space=pltpu.SMEM),
-            pl.BlockSpec(memory_space=pltpu.VMEM),
-        ],
-        out_specs=pl.BlockSpec(memory_space=pltpu.VMEM),
-        name="group_scan",
-    )(q.reshape(1).astype(jnp.int32), got)
-    extra = second(outs)
-    return wait_for(a2a(outs, ZX), extra), extra
+        got[0] = wait_for(got[0], first)
+    line, before, decay = pl.pallas_call(
+        functools.partial(line_scan_kernel, reverse),
+        out_shape=[SENT, struct((W, N)), struct((8, 128))],
+        in_specs=[SMEM] + [pl.BlockSpec(memory_space=pltpu.VMEM)] * 4,
+        out_specs=[pl.BlockSpec(memory_space=pltpu.VMEM)] * 3,
+        name="line_scan",
+    )(index("x"), sent, *got)
+    got = around(line, "z")
+    extra = second(line)
+    got[0] = wait_for(got[0], extra)
+    return (index("z"), *got, before, decay), extra
 
 
 PAIRS = HL // 2
@@ -422,13 +443,14 @@
     mid = (decay - hi).astype(bf).astype(f32)
     low = decay - hi - mid
     tail = hi + pltpu.roll(mid, HL, 1) + pltpu.roll(low, 2 * HL, 1)
-    for j in range(NQ):
-        block = states[j * SCAN_ROWS : (j + 1) * SCAN_ROWS]
-        sent_ref[j] = jnp.concatenate([block, tail], axis=0).astype(bf)
-
-
-def read_states(back_ref):
-    return jnp.concatenate([back_ref[j].astype(f32)[:SCAN_ROWS] for j in range(NQ)], axis=0)
+    sent_ref[...] = jnp.concatenate([states, tail, tail], axis=0).astype(bf)
+
+
+def read_states(ref):
+    block = ref[...].astype(f32)
+    tail = block[W : W + 8]
+    decay = tail + pltpu.roll(tail, 128 - HL, 1) + pltpu.roll(tail, 128 - 2 * HL, 1)
+    return block[:W], decay[:1]
 
 
 def span_masks(segc_ref, segr_ref):
@@ -523,7 +545,7 @@
 
 
 def gate_kernel(
-    last, order_ref, seg_ref, back_ref, local_ref, before_ref, run_ref, v_ref, within_ref, z_ref, segc_ref,
+    last, order_ref, seg_ref, at_ref, r1, r2, r3, line_ref, line_decay_ref, local_ref, before_ref, run_ref, v_ref, within_ref, z_ref, segc_ref,
     skip_ref, wo_ref, *rest,
 ):
     if last:
@@ -535,7 +557,7 @@
 
     @pl.when(i == 0)
     def _():
-        carry_ref[...] = read_states(back_ref)
+        carry_ref[...] = final_states(False, at_ref, r1, r2, r3, line_ref, line_decay_ref)
 
     carried = (by_rows(before_ref[0], carry_ref[...]) + local_ref[0]).astype(bf)
     xc = v_ref[:, :W].astype(f32)
@@ -639,20 +661,19 @@
 
 
 def end_kernel(
-    seg_ref, later_ref, back_ref, local_ref, before_ref, dlocal_ref, after_ref, decay_ref, v_ref,
+    seg_ref, at_ref, r1, r2, r3, line_ref, line_decay_ref, carry_ref, local_ref, before_ref, dlocal_ref, after_ref, decay_ref, v_ref,
     pre_ref, raw_ref, bias_ref, rate_ref, step_ref, run_ref, segc_ref, skip_ref, dy_ref, dxs_ref,
-    dbc_ref, y0_ref, dpre_ref, draw_ref, sums_ref, later_s, carry_s,
+    dbc_ref, y0_ref, dpre_ref, draw_ref, sums_ref, later_s,
 ):
     k = pl.program_id(0)
 
     @pl.when(k == 0)
     def _():
-        later_s[...] = read_states(later_ref)
-        carry_s[...] = read_states(back_ref)
+        later_s[...] = final_states(True, at_ref, r1, r2, r3, line_ref, line_decay_ref)
         sums_ref[...] = jnp.zeros_like(sums_ref)
 
     d_end = by_rows(after_ref[0], later_s[...]) + dlocal_ref[0]
-    carried = by_rows(before_ref[0], carry_s[...]) + local_ref[0]
+    carried = by_rows(before_ref[0], carry_ref[...]) + local_ref[0]
     d_end_low = d_end.astype(bf)
     run, step, rate = run_ref[...], step_ref[...], rate_ref[...]
     xc = v_ref[:, :W].astype(f32)
@@ -755,7 +776,7 @@
 
 STATE = struct((NS, W, N))
 ROW = struct((NS, 1, 128))
-SENT = struct((NQ, 32, N), bf)
+SENT = struct((STATE_ROWS, N), bf)
 STATE_SCRATCH = pltpu.VMEM((W, N), f32)
 
 
@@ -824,7 +845,7 @@
         [SMEM, tok_block(CC), past_block(CC), whole(16, CC), tok_block(8), whole(8, CC),
          tok_block(128), whole(1, 128), whole(1, 128), tok_block(1), span_block(1, SPAN)],
         [tok_block(CC), tok_block(CC), tok_block(W), span_block(W, N), tok_block(128),
-         tok_block(128), span_block(1, 128), span_block(1, 128), whole(NQ, 32, N)],
+         tok_block(128), span_block(1, 128), span_block(1, 128), whole(STATE_ROWS, N)],
         [struct((GT, CC), bf), struct((GT, CC), bf), struct((GT, W)), STATE, struct((GT, 128)),
          struct((GT, 128)), ROW, ROW, SENT],
         [STATE_SCRATCH, pltpu.VMEM((1, 128), f32)],
@@ -857,18 +878,19 @@
 
 def span_gate(seg, back, local, before, run, v, within, z, segc, skip, wo, d_q):
     last = d_q is not None
-    ins = [SMEM, whole_at(NQ, 32, N), span_at(W, N), span_at(1, 128), tok_at(128), tok_at(CC),
+    ins = [SMEM, SMEM] + [whole_at(STATE_ROWS, N)] * 3 + [
+           whole_at(W, N), whole_at(8, 128), span_at(W, N), span_at(1, 128), tok_at(128), tok_at(CC),
            tok_at(W), tok_at(W), tok_at(1), whole_at(1, W), whole_at(W, D)]
-    args = (seg, back, local, before, run, v, within, z, segc, skip, wo)
+    args = (seg, *back, local, before, run, v, within, z, segc, skip, wo)
     return ordered_call(
         functools.partial(gate_kernel, last),
         "span_gate",
         ins + [tok_at(W)] if last else ins,
         [tok_at(W)] + ([tok_at(D)] if last else HALVES)
-        + [pl.BlockSpec((8, SPAN), lambda i, order: (0, order[i]))],
+        + [pl.BlockSpec((8, SPAN), lambda i, order: (0, order[i])), whole_at(W, N)],
         [struct((GT, W))] + ([struct((GT, D), bf)] if last else HALF_SHAPES)
-        + [struct((8, GT))],
-        [STATE_SCRATCH],
+        + [struct((8, GT)), struct((W, N))],
+        [],
         args + (d_q,) if last else args,
         10,
     )
@@ -886,7 +908,7 @@
          tok_block(CC, True), tok_block(W, True), tok_block(W, True), tok_block(128, True),
          tok_block(1, True), whole(1, W), span_block(1, 128, True)],
         [tok_block(W, True), tok_block(W, True), tok_block(W, True), span_block(W, N, True),
-         span_block(1, 128, True), whole(NQ, 32, N)],
+         span_block(1, 128, True), whole(STATE_ROWS, N)],
         [struct((GT, W), bf), struct((GT, W), bf), struct((GT, W), bf), STATE, ROW, SENT],
         [STATE_SCRATCH, pltpu.VMEM((1, 128), f32)],
         (seg, grad, wo, scales, v, y0, z, run, segc, skip, decay),
@@ -913,14 +935,15 @@
     return call(
         end_kernel,
         "span_end",
-        [SMEM, whole(NQ, 32, N), whole(NQ, 32, N), span_block(W, N), span_block(1, 128),
+        [SMEM, SMEM] + [whole(STATE_ROWS, N)] * 3 + [
+         whole(W, N), whole(8, 128), whole(W, N), span_block(W, N), span_block(1, 128),
          span_block(W, N), span_block(1, 128), span_block(1, 128), tok_block(CC), tok_block(CC),
          tok_block(128), whole(1, 128), whole(1, 128), tok_block(128), tok_block(128),
          tok_block(1), whole(1, W), tok_block(W), tok_block(W), tok_block(2 * N), tok_block(W)],
         [tok_block(CC), tok_block(128), whole(8, 128)],
         [struct((GT, CC), bf), struct((GT, 128), bf), struct((8, 128))],
-        [STATE_SCRATCH, STATE_SCRATCH],
-        (seg, later, back, local, before, dlocal, after, decay, v, pre, raw, bias, rate, step, run,
+        [STATE_SCRATCH],
+        (seg, *later, back, local, before, dlocal, after, decay, v, pre, raw, bias, rate, step, run,
          segc, skip, dy, dxs, dbc, y0),
         16,
     )
@@ -1039,7 +1062,7 @@
             back, d_q = exclusive_scan(
                 sent, False, z, lambda outs: mm(wait_for(grad_full, outs), w_o[1], 1, 1)
             )
-        y0, *parts, sums = span_gate(
+        y0, *parts, sums, carry = span_gate(
             seg_ends, back, local, before, run, v, within, z, seg_col, skip_x, w_o[l],
             d_q,
         )
@@ -1047,7 +1070,7 @@
             dict(
                 h=h, normed=normed, u=u, edge=edge, pre=pre, v=v, z=z, raw=raw, bias_h=bias_h,
                 rate=rate, skip_x=skip_x, step=step, run=run, before=before, decay=decay,
-                local=local, back=back, y0=y0,
+                local=local, carry=carry, y0=y0,
             )
         )
         if l < LAYERS - 1:
@@ -1091,7 +1114,7 @@
         both = group_reduce_blocks(wait_for(sums, later))
         dxs, dbc = span_mix_back(s["v"], s["step"], s["run"], seg_col, seg_row, wait_for(dy, sums))
         d_pre, d_raw, head_sum = span_end(
-            seg_ends, later, s["back"], s["local"], s["before"], dlocal, after, s["decay"], s["v"],
+            seg_ends, later, s["carry"], s["local"], s["before"], dlocal, after, s["decay"], s["v"],
             s["pre"], s["raw"], s["bias_h"], s["rate"], s["step"], s["run"], seg_col, s["skip_x"],
             dy, dxs, dbc, s["y0"],
         )

time: 649 us -> 637 us (0.982)
  blocking collectives: 28.9 us -> 11.4 us
    ppermute x0 -> x24, starting transfers between devices: none -> 36.4 us  [around(): lax.ppermute(a, axis, [(i, (i + d) % 4) for i in range(4)])]
    all_to_all x16 -> x9, starting transfers between devices: 91.7 us -> 55.5 us  [a2a(): return lax.all_to_all(a, axes, 0, 0, tiled=True)]
    all_to_all x2 -> x1, blocking collectives: 28.9 us -> 11.4 us  [a2a(): return lax.all_to_all(a, axes, 0, 0, tiled=True)]
    all_to_all x16 -> x9, waiting for transfers between devices: 77.9 us -> 70.3 us  [a2a(): return lax.all_to_all(a, axes, 0, 0, tiled=True)]
    unnamed x148 -> x184, local copies, waits for them, and re-layouts: 25.7 us -> 28.6 us
  transfers between devices with their start and end apart: 57 -> 74, of which waited for: 21 -> 19; matrix products, arithmetic and copies ran while one was open for 18% -> 18% of each run, Pallas kernels for 17% -> 18%
where the time goes in v5:
time: 637 us; the launch traced here: 626 us
  starting transfers between devices  164 us (26%)
  Pallas kernels  154 us (24%)
  waiting for transfers between devices  138 us (22%)
  local copies, waits for them, and re-layouts  75.3 us (12%)
  matrix products  43.4 us (7%)
  other arithmetic  23.3 us (4%)
  between operations  16.2 us (3%)
  blocking collectives  11.4 us (2%)
    pallas_call x11, Pallas kernels, call(): pl.pallas_call(kernel, grid=(NS,), in_specs=ins, out_specs=outs, out_shap...  97.6 us
    all_to_all x9, waiting for transfers between devices, a2a(): return lax.all_to_all(a, axes, 0, 0, tiled=True)  70.3 us
    all_to_all x9, starting transfers between devices, a2a(): return lax.all_to_all(a, axes, 0, 0, tiled=True)  55.5 us
    dot_general x15, matrix products, mm(): lax.dot_general(a, b, (((ca,), (cb,)), ((), ())), preferred_element_type=...  43.4 us
    pallas_call x4, Pallas kernels, ordered_call(): pl.pallas_call(kernel, grid_spec=pltpu.PrefetchScalarGridSpec(num_scalar_...  41.6 us
    ppermute x24, starting transfers between devices, around(): lax.ppermute(a, axis, [(i, (i + d) % 4) for i in range(4)])  36.4 us
    ppermute x14, starting transfers between devices, core_swap(): return lax.ppermute(a, 'c', [(0, 1), (1, 0)])  30.6 us
    ppermute x15, waiting for transfers between devices, along_line(): return lax.ppermute(a, Y, [(i, (i + distance) % 4) for i in range(4)])  30.3 us
  transfers between devices with their start and end apart: 74, of which 19 were waited for; matrix products, arithmetic and copies ran while one was open for 18% of the time, Pallas kernels for 18%

profile of v5, /device:TPU:1, one launch (start us, length us, event | category | flops | bytes accessed | tf_op | source)
XLA Modules:
  0.0 626.1 jit_solution(10138746265275162170)
XLA Ops:
  31.6 7.8 %all-to-all-start.1 = ((bf16[16,96,768]{2,1,0:T(8,128)(2,1)}), bf16[16,96,768]{2,1,0:T(8,128)(2,1)}, u32[]{:S(2)}, u32[]{:S(2)}) async-start(bf16[16,96,768]{2,1,0:T(8,128)(2,1)} %broadcast_in_dim.31), calls=%async_computation.1 | async-start | bytes 4718592 | tf_op jit(solution)/shard_map/all_to_all | solution.py:54
  51.2 9.8 %collective-permute-start.2 = (bf16[128,1536]{1,0:T(8,128)(2,1)S(1)}, bf16[128,1536]{1,0:T(8,128)(2,1)S(1)}, u32[]{:S(2)}, u32[]{:S(2)}) collective-permute-start(bf16[128,1536]{1,0:T(8,128)(2,1)S(1)} %collective-permute-done.1.refs_2_), channel_id=1, source_target_pairs={{0,2},{2,0},{1,3},{3,1},{4,6},{6,4},{5,7},{7,5},{8,10},{10,8},{9,1... | collective-permute-start | bytes 1179656 | tf_op jit(solution)/shard_map/ppermute | solution.py:58
  67.1 9.2 %collective-permute-done.7 = bf16[2,24,1536]{2,1,0:T(8,128)(2,1)S(1)} collective-permute-done((bf16[2,24,1536]{2,1,0:T(8,128)(2,1)S(1)}, bf16[2,24,1536]{2,1,0:T(8,128)(2,1)S(1)}, u32[]{:S(2)}, u32[]{:S(2)}) %collective-permute-start.7) | collective-permute-done | bytes 147488 | tf_op jit(solution)/shard_map/ppermute | solution.py:1029
  78.0 6.9 %place_project.2 = (bf16[1024,1536]{1,0:T(8,128)(2,1)}, bf16[1024,640]{1,0:T(8,128)(2,1)}, bf16[1024,128]{1,0:T(8,128)(2,1)}) custom-call(s32[8]{0:T(128)} %stack.186.pos_ref, bf16[128,1536]{1,0:T(8,128)(2,1)} %copy-done.21, bf16[128,1536]{1,0:T(8,128)(2,1)} %copy-done.30, bf16[128,1536]{1,0:T(8,128)(2,1)} %copy-done.27, bf16[128,1536]{1,0:T(8,128)(2,1)} %copy-done.31, ...), custom_call_target="tpu_custom_call" | custom-call | flops 360000000 | bytes 1800000 | tf_op jit(solution)/shard_map/place_project/pallas_call | solution.py:784
  93.0 11.4 %span_mix.2 = (bf16[1024,640]{1,0:T(8,128)(2,1)}, bf16[1024,640]{1,0:T(8,128)(2,1)}, f32[1024,384]{1,0:T(8,128)}, f32[4,384,128]{2,1,0:T(8,128)}, f32[1024,128]{...) custom-call(s32[2,4]{1,0:T(2,128)} %pad_add_fusion.seg_ref, ...), custom_call_target="tpu_custom_call" | custom-call | flops 400000000 | bytes 2000000 | tf_op jit(solution)/shard_map/span_mix/pallas_call | solution.py:784
  104.5 7.4 %collective-permute-start.10 = (bf16[400,128]{1,0:T(8,128)(2,1)}, bf16[400,128]{1,0:T(8,128)(2,1)S(1)}, u32[]{:S(2)}, u32[]{:S(2)}) collective-permute-start(bf16[400,128]{1,0:T(8,128)(2,1)} %get-tuple-element.166.own_ref), channel_id=1, source_target_pairs={{0,16},{8,24},{16,0},{24,8},{1,17},{9,25},{17,1},{25,9},{2,18},{10... | collective-permute-start | bytes 307208 | tf_op jit(solution)/shard_map/ppermute | solution.py:362
  125.5 12.8 %all-gather.4.cloned.1.call-done = bf16[4608,384]{1,0:T(8,128)(2,1)} async-done(((bf16[288,384]{1,0:T(8,128)(2,1)}), bf16[4608,384]{1,0:T(8,128)(2,1)}) %all-gather.4.cloned.1.call-update) | async-done | bytes 3538960 | tf_op jit(solution)/shard_map/all_gather | solution.py:274
  145.9 9.7 %span_gate.2 = (f32[1024,384]{1,0:T(8,128)}, bf16[512,1536]{1,0:T(8,128)(2,1)}, bf16[512,1536]{1,0:T(8,128)(2,1)}, f32[8,1024]{1,0:T(8,128)}, f32[384,128]{1,0:T(8,128)}) custom-call(s32[4]{0:T(128)} %pad_add_fusion.1.order_ref, s32[2,4]{1,0:T(2,128)} %pad_add_fusion.seg_ref, s32[1]{0:T(128)} %bitcast.6.at_ref, bf16[400,128]{1,0:T(8,128)(2,1)} %copy-done.39, ...), custom_call_target="tpu_custom_call" | custom-call | flops 400000000 | bytes 2000000 | tf_op jit(solution)/shard_map/span_gate/pallas_call | solution.py:802
  173.5 11.1 %all-to-all-done.2 = f32[8,1,128]{2,1,0:T(1,128)S(1)} async-done(((f32[8,1,128]{2,1,0:T(1,128)}), f32[8,1,128]{2,1,0:T(1,128)S(1)}, u32[]{:S(2)}, u32[]{:S(2)}) %all-to-all-start.2) | async-done | bytes 4128 | tf_op jit(solution)/shard_map/all_to_all | solution.py:54
  190.8 7.7 %collective-permute-done.20.refs_2_ = bf16[128,1536]{1,0:T(8,128)(2,1)S(1)} collective-permute-done((bf16[128,1536]{1,0:T(8,128)(2,1)}, bf16[128,1536]{1,0:T(8,128)(2,1)S(1)}, u32[]{:S(2)}, u32[]{:S(2)}) %collective-permute-start.20) | collective-permute-done | bytes 393248 | tf_op jit(solution)/shard_map/ppermute | solution.py:66
  214.8 7.0 %place_project.3 = (bf16[1024,1536]{1,0:T(8,128)(2,1)}, bf16[1024,640]{1,0:T(8,128)(2,1)}, bf16[1024,128]{1,0:T(8,128)(2,1)}) custom-call(s32[8]{0:T(128)} %stack.186.pos_ref, bf16[128,1536]{1,0:T(8,128)(2,1)} %get-tuple-element.188.refs_0_, bf16[128,1536]{1,0:T(8,128)(2,1)} %copy-done.35, bf16[128,1536]{1,0:T(8,128)(2,1)} %copy-done.32, ...), custom_call_target="tpu_custom_call" | custom-call | flops 360000000 | bytes 1800000 | tf_op jit(solution)/shard_map/place_project/pallas_call | solution.py:784
  230.4 11.4 %span_mix.3 = (bf16[1024,640]{1,0:T(8,128)(2,1)}, bf16[1024,640]{1,0:T(8,128)(2,1)}, f32[1024,384]{1,0:T(8,128)}, f32[4,384,128]{2,1,0:T(8,128)}, f32[1024,128]{...) custom-call(s32[2,4]{1,0:T(2,128)} %pad_add_fusion.seg_ref, ...), custom_call_target="tpu_custom_call" | custom-call | flops 400000000 | bytes 2000000 | tf_op jit(solution)/shard_map/span_mix/pallas_call | solution.py:784
  262.9 9.1 %span_gate.3 = (f32[1024,384]{1,0:T(8,128)}, bf16[1024,1536]{1,0:T(8,128)(2,1)}, f32[8,1024]{1,0:T(8,128)}, f32[384,128]{1,0:T(8,128)}) custom-call(s32[4]{0:T(128)} %pad_add_fusion.1.order_ref, s32[2,4]{1,0:T(2,128)} %pad_add_fusion.seg_ref, s32[1]{0:T(128)} %bitcast.6.at_ref, bf16[400,128]{1,0:T(8,128)(2,1)} %copy-done.60, bf16[400,128]{1,0:T(8,128)(2,1)} %copy-done.61, ...), custom_call_target="tpu_custom_call" | custom-call | flops 400000000 | bytes 2000000 | tf_op jit(solution)/shard_map/span_gate/pallas_call | solution.py:802
  272.8 11.4 %all_to_all.57 = f32[8,2,1024]{2,1,0:T(2,128)S(1)} all-to-all(f32[8,2,1024]{2,1,0:T(2,128)S(1)} %broadcast_in_dim.38), channel_id=1, replica_groups=mesh['z'=4,'x'=4,'yh'=2,'c'=2,'yl'=2] {'yh','c','yl'}, dimensions={0} | all-to-all | bytes 131072 | tf_op jit(solution)/shard_map/all_to_all | solution.py:54
  284.8 7.9 %span_gate_back.2 = (bf16[1024,384]{1,0:T(8,128)(2,1)}, bf16[1024,384]{1,0:T(8,128)(2,1)}, bf16[1024,384]{1,0:T(8,128)(2,1)}, f32[4,384,128]{2,1,0:T(8,128)}, f3...) custom-call(s32[2,4]{1,0:T(2,128)} %pad_add_fusion.seg_ref, f32[1024,384]{1,0:T(8,128)} %fusion.47.rest_0_.grad_ref, ...), custom_call_target="tpu_custom_call" | custom-call | flops 480000000 | bytes 2400000 | tf_op jit(solution)/shard_map/span_gate_back/pallas_call | solution.py:784
  322.3 7.9 %span_mix_back.2 = (f32[1024,384]{1,0:T(8,128)}, bf16[1024,256]{1,0:T(8,128)(2,1)}) custom-call(bf16[1024,640]{1,0:T(8,128)(2,1)} %get-tuple-element.204.v_ref, f32[1024,128]{1,0:T(8,128)} %get-tuple-element.223.step_ref, f32[1024,128]{1,0:T(8,128)} %get-tuple-element.203.run_ref, s32[1024,1]{1,0:T(8,128)} %copy.268.segc_ref, s32[4,1,256]{2,1,0:T(1,128)} %bitcast.251, ...), custom_call_target="tpu_custom_call" | custom-call | flops 560000000 | bytes 2800000 | tf_op jit(solution)/shard_map/span_mix_back/pallas_call | solution.py:784
  330.3 12.2 %span_end.2 = (bf16[1024,640]{1,0:T(8,128)(2,1)}, bf16[1024,128]{1,0:T(8,128)(2,1)}, f32[8,128]{1,0:T(8,128)}) custom-call(s32[2,4]{1,0:T(2,128)} %pad_add_fusion.seg_ref, s32[1]{0:T(128)} %bitcast.6.at_ref, bf16[400,128]{1,0:T(8,128)(2,1)} %copy-done.54, bf16[400,128]{1,0:T(8,128)(2,1)} %copy-done.56, bf16[400,128]{1,0:T(8,128)(2,1)} %copy-done.57, ...), custom_call_target="tpu_custom_call" | custom-call | flops 640000000 | bytes 3200000 | tf_op jit(solution)/shard_map/span_end/pallas_call | solution.py:784
  350.8 11.8 %conv_back.2 = (bf16[1024,768]{1,0:T(8,128)(2,1)}, bf16[512,1536]{1,0:T(8,128)(2,1)}, bf16[512,1536]{1,0:T(8,128)(2,1)}, f32[8,640]{1,0:T(8,128)}) custom-call(s32[4]{0:T(128)} %pad_add_fusion.1.order_ref, bf16[1024,640]{1,0:T(8,128)(2,1)} %get-tuple-element.228.dpre_ref.next_ref, bf16[1024,640]{1,0:T(8,128)(2,1)} %get-tuple-element.228.dpre_ref.next_ref, ...), custom_call_target="tpu_custom_call" | custom-call | flops 400000000 | bytes 2000000 | tf_op jit(solution)/shard_map/conv_back/pallas_call | solution.py:802
  380.1 6.6 %all-to-all-start.4 = ((bf16[16,96,768]{2,1,0:T(8,128)(2,1)}), bf16[16,96,768]{2,1,0:T(8,128)(2,1)}, u32[]{:S(2)}, u32[]{:S(2)}) async-start(bf16[16,96,768]{2,1,0:T(8,128)(2,1)} %bitcast.216), calls=%async_computation.5 | async-start | bytes 4718592 | tf_op jit(solution)/shard_map/all_to_all | solution.py:54
  393.7 6.9 %collective-permute-done.41.refs_1_ = bf16[128,1536]{1,0:T(8,128)(2,1)S(1)} collective-permute-done((bf16[128,1536]{1,0:T(8,128)(2,1)S(1)}, bf16[128,1536]{1,0:T(8,128)(2,1)S(1)}, u32[]{:S(2)}, u32[]{:S(2)}) %collective-permute-start.41) | collective-permute-done | bytes 393248 | tf_op jit(solution)/shard_map/ppermute | solution.py:66
  400.7 7.4 %collective-permute-done.43.refs_3_ = bf16[128,1536]{1,0:T(8,128)(2,1)S(1)} collective-permute-done((bf16[128,1536]{1,0:T(8,128)(2,1)}, bf16[128,1536]{1,0:T(8,128)(2,1)S(1)}, u32[]{:S(2)}, u32[]{:S(2)}) %collective-permute-start.43) | collective-permute-done | bytes 393248 | tf_op jit(solution)/shard_map/ppermute | solution.py:66
  414.7 9.0 %all-to-all-done.4 = bf16[16,96,768]{2,1,0:T(8,128)(2,1)} async-done(((bf16[16,96,768]{2,1,0:T(8,128)(2,1)}), bf16[16,96,768]{2,1,0:T(8,128)(2,1)}, u32[]{:S(2)}, u32[]{:S(2)}) %all-to-all-start.4) | async-done | bytes 2359328 | tf_op jit(solution)/shard_map/all_to_all | solution.py:54
  446.0 8.2 %span_gate_back.3 = (bf16[1024,384]{1,0:T(8,128)(2,1)}, bf16[1024,384]{1,0:T(8,128)(2,1)}, bf16[1024,384]{1,0:T(8,128)(2,1)}, f32[4,384,128]{2,1,0:T(8,128)}, f3...) custom-call(s32[2,4]{1,0:T(2,128)} %pad_add_fusion.seg_ref, bf16[1024,1536]{1,0:T(8,128)(2,1)} %get-tuple-element.246.grad_ref, ...), custom_call_target="tpu_custom_call" | custom-call | flops 480000000 | bytes 2400000 | tf_op jit(solution)/shard_map/span_gate_back/pallas_call | solution.py:784
  478.4 7.9 %span_mix_back.3 = (f32[1024,384]{1,0:T(8,128)}, bf16[1024,256]{1,0:T(8,128)(2,1)}) custom-call(bf16[1024,640]{1,0:T(8,128)(2,1)} %get-tuple-element.177.v_ref, f32[1024,128]{1,0:T(8,128)} %get-tuple-element.264.step_ref, f32[1024,128]{1,0:T(8,128)} %get-tuple-element.176.run_ref, s32[1024,1]{1,0:T(8,128)} %copy.268.segc_ref, s32[4,1,256]{2,1,0:T(1,128)} %bitcast.252, ...), custom_call_target="tpu_custom_call" | custom-call | flops 560000000 | bytes 2800000 | tf_op jit(solution)/shard_map/span_mix_back/pallas_call | solution.py:784
  487.1 12.2 %span_end.3 = (bf16[1024,640]{1,0:T(8,128)(2,1)}, bf16[1024,128]{1,0:T(8,128)(2,1)}, f32[8,128]{1,0:T(8,128)}) custom-call(s32[2,4]{1,0:T(2,128)} %pad_add_fusion.seg_ref, s32[1]{0:T(128)} %bitcast.6.at_ref, bf16[400,128]{1,0:T(8,128)(2,1)} %copy-done.55, bf16[400,128]{1,0:T(8,128)(2,1)} %copy-done.58, bf16[400,128]{1,0:T(8,128)(2,1)} %copy-done.59, ...), custom_call_target="tpu_custom_call" | custom-call | flops 640000000 | bytes 3200000 | tf_op jit(solution)/shard_map/span_end/pallas_call | solution.py:784
  507.9 11.1 %conv_back.3 = (bf16[1024,768]{1,0:T(8,128)(2,1)}, bf16[1024,1536]{1,0:T(8,128)(2,1)}, f32[8,640]{1,0:T(8,128)}) custom-call(s32[4]{0:T(128)} %pad_add_fusion.1.order_ref, bf16[1024,640]{1,0:T(8,128)(2,1)} %get-tuple-element.269.dpre_ref.next_ref, bf16[1024,640]{1,0:T(8,128)(2,1)} %get-tuple-element.269.dpre_ref.next_ref, bf16[16,640]{1,0:T(8,128)(2,1)} %copy-done.66, ...), custom_call_target="tpu_custom_call" | custom-call | flops 400000000 | bytes 2000000 | tf_op jit(solution)/shard_map/conv_back/pallas_call | solution.py:802
  534.8 8.6 %all-to-all-start.7 = ((bf16[16,96,768]{2,1,0:T(8,128)(2,1)}), bf16[16,96,768]{2,1,0:T(8,128)(2,1)}, u32[]{:S(2)}, u32[]{:S(2)}) async-start(bf16[16,96,768]{2,1,0:T(8,128)(2,1)} %bitcast.217), calls=%async_computation.9 | async-start | bytes 4718592 | tf_op jit(solution)/shard_map/all_to_all | solution.py:54
  545.7 7.0 %collective-permute-start.59 = (f32[24,1536]{1,0:T(8,128)S(1)}, f32[24,1536]{1,0:T(8,128)S(1)}, u32[]{:S(2)}, u32[]{:S(2)}) collective-permute-start(f32[24,1536]{1,0:T(8,128)S(1)} %bitcast.255), channel_id=1, source_target_pairs={{0,0},{8,1},{16,2},{24,3},{32,4},{40,5},{48,6},{56,7},{64,8},{72,9... | collective-permute-start | bytes 442376 | tf_op jit(solution)/shard_map/ppermute | solution.py:1170
  554.9 19.8 %all-to-all-done.7 = bf16[16,96,768]{2,1,0:T(8,128)(2,1)} async-done(((bf16[16,96,768]{2,1,0:T(8,128)(2,1)}), bf16[16,96,768]{2,1,0:T(8,128)(2,1)}, u32[]{:S(2)}, u32[]{:S(2)}) %all-to-all-start.7) | async-done | bytes 2359328 | tf_op jit(solution)/shard_map/all_to_all | solution.py:54
  576.7 6.6 %collective-permute-start.58 = (f32[24,1536]{1,0:T(8,128)S(1)}, f32[24,1536]{1,0:T(8,128)}, u32[]{:S(2)}, u32[]{:S(2)}) collective-permute-start(f32[24,1536]{1,0:T(8,128)S(1)} %bitcast.256), channel_id=1, source_target_pairs={{0,0},{8,1},{16,2},{24,3},{32,4},{40,5},{48,6},{56,7},{64,8},{72,9... | collective-permute-start | bytes 442376 | tf_op jit(solution)/shard_map/ppermute | solution.py:1170
  584.2 7.8 %all-to-all-start.9 = ((f32[8,12,1152]{2,1,0:T(8,128)}), f32[8,12,1152]{2,1,0:T(8,128)S(1)}, u32[]{:S(2)}, u32[]{:S(2)}) async-start(f32[8,12,1152]{2,1,0:T(8,128)} %reshape.553), calls=%async_computation.11 | async-start | bytes 1179648 | tf_op jit(solution)/shard_map/all_to_all | solution.py:54
  594.4 13.2 %all-to-all-done.9 = f32[8,12,1152]{2,1,0:T(8,128)S(1)} async-done(((f32[8,12,1152]{2,1,0:T(8,128)}), f32[8,12,1152]{2,1,0:T(8,128)S(1)}, u32[]{:S(2)}, u32[]{:S(2)}) %all-to-all-start.9) | async-done | bytes 442400 | tf_op jit(solution)/shard_map/all_to_all | solution.py:54
  (545 shorter events, 305.1 us)
Async XLA Ops:
  31.6 45.6 %all-to-all-start.1 = ((bf16[16,96,768]{2,1,0:T(8,128)(2,1)}), bf16[16,96,768]{2,1,0:T(8,128)(2,1)}, u32[]{:S(2)}, u32[]{:S(2)}) async-start(bf16[16,96,768]{2,1,0:T(8,128)(2,1)} %broadcast_in_dim.31), calls=%async_computation.1 | async-start | bytes 4718592 | tf_op jit(solution)/shard_map/all_to_all | solution.py:54
  39.4 99.0 %all-gather.4.cloned.1.call-start = ((), (), s32[]{:S(2)}) async-start(), calls=%async_computation.12 | async-start | bytes 3760128 | tf_op jit(solution)/shard_map/all_gather | solution.py:274
  40.1 20.9 %collective-permute-start.3 = (bf16[128,1536]{1,0:T(8,128)(2,1)S(1)}, bf16[128,1536]{1,0:T(8,128)(2,1)S(1)}, u32[]{:S(2)}, u32[]{:S(2)}) collective-permute-start(bf16[128,1536]{1,0:T(8,128)(2,1)S(1)} %multiply_convert_fusion.refs_0_), channel_id=1, source_target_pairs={{0,5},{1,0},{4,1},{5,4},{2,7},{3,2},{6,3},{7,6},{8,13},{9,8},{12,9... | collective-permute-start | bytes 1179656 | tf_op jit(solution)/shard_map/ppermute | solution.py:66
  42.5 18.6 %collective-permute-start.5 = (bf16[128,1536]{1,0:T(8,128)(2,1)S(1)}, bf16[128,1536]{1,0:T(8,128)(2,1)S(1)}, u32[]{:S(2)}, u32[]{:S(2)}) collective-permute-start(bf16[128,1536]{1,0:T(8,128)(2,1)S(1)} %multiply_convert_fusion.refs_0_), channel_id=1, source_target_pairs={{0,4},{1,5},{4,0},{5,1},{2,6},{3,7},{6,2},{7,3},{8,12},{9,13},{12,... | collective-permute-start | bytes 1179656 | tf_op jit(solution)/shard_map/ppermute | solution.py:66
  47.2 29.9 %collective-permute-start = (bf16[128,1536]{1,0:T(8,128)(2,1)S(1)}, bf16[128,1536]{1,0:T(8,128)(2,1)S(1)}, u32[]{:S(2)}, u32[]{:S(2)}) collective-permute-start(bf16[128,1536]{1,0:T(8,128)(2,1)S(1)} %multiply_convert_fusion.refs_0_), channel_id=1, source_target_pairs={{0,2},{2,0},{1,3},{3,1},{4,6},{6,4},{5,7},{7,5},{8,10},{10,8},{9,1... | collective-permute-start | bytes 1179656 | tf_op jit(solution)/shard_map/ppermute | solution.py:58
  51.2 26.0 %collective-permute-start.2 = (bf16[128,1536]{1,0:T(8,128)(2,1)S(1)}, bf16[128,1536]{1,0:T(8,128)(2,1)S(1)}, u32[]{:S(2)}, u32[]{:S(2)}) collective-permute-start(bf16[128,1536]{1,0:T(8,128)(2,1)S(1)} %collective-permute-done.1.refs_2_), channel_id=1, source_target_pairs={{0,2},{2,0},{1,3},{3,1},{4,6},{6,4},{5,7},{7,5},{8,10},{10,8},{9,1... | collective-permute-start | bytes 1179656 | tf_op jit(solution)/shard_map/ppermute | solution.py:58
  61.0 16.2 %collective-permute-start.4 = (bf16[128,1536]{1,0:T(8,128)(2,1)S(1)}, bf16[128,1536]{1,0:T(8,128)(2,1)}, u32[]{:S(2)}, u32[]{:S(2)}) collective-permute-start(bf16[128,1536]{1,0:T(8,128)(2,1)S(1)} %collective-permute-done.3.refs_4_), channel_id=1, source_target_pairs={{0,2},{2,0},{1,3},{3,1},{4,6},{6,4},{5,7},{7,5},{8,10},{10,8},{9,1... | collective-permute-start | bytes 1179656 | tf_op jit(solution)/shard_map/ppermute | solution.py:58
  85.7 127.6 %all-gather.6.cloned.1.call-start = ((), (), s32[]{:S(2)}) async-start(), calls=%async_computation.13 | async-start | bytes 3760128 | tf_op jit(solution)/shard_map/all_gather | solution.py:274
  86.5 170.8 %all-gather.8.cloned.1.call-start = ((), (), s32[]{:S(2)}) async-start(), calls=%async_computation.14 | async-start | bytes 3538944 | tf_op jit(solution)/shard_map/all_gather | solution.py:1031
  119.0 24.7 %collective-permute-start.12 = (bf16[400,128]{1,0:T(8,128)(2,1)}, bf16[400,128]{1,0:T(8,128)(2,1)S(1)}, u32[]{:S(2)}, u32[]{:S(2)}) collective-permute-start(bf16[400,128]{1,0:T(8,128)(2,1)} %get-tuple-element.167), channel_id=1, source_target_pairs={{0,32},{32,64},{64,96},{96,0},{1,33},{33,65},{65,97},{97,1},{2,34}... | collective-permute-start | bytes 307208 | tf_op jit(solution)/shard_map/ppermute | solution.py:362
  122.0 23.2 %collective-permute-start.13 = (bf16[400,128]{1,0:T(8,128)(2,1)}, bf16[400,128]{1,0:T(8,128)(2,1)S(1)}, u32[]{:S(2)}, u32[]{:S(2)}) collective-permute-start(bf16[400,128]{1,0:T(8,128)(2,1)} %get-tuple-element.167), channel_id=1, source_target_pairs={{0,64},{32,96},{64,0},{96,32},{1,65},{33,97},{65,1},{97,33},{2,66}... | collective-permute-start | bytes 307208 | tf_op jit(solution)/shard_map/ppermute | solution.py:362
  124.1 21.1 %collective-permute-start.14 = (bf16[400,128]{1,0:T(8,128)(2,1)}, bf16[400,128]{1,0:T(8,128)(2,1)S(1)}, u32[]{:S(2)}, u32[]{:S(2)}) collective-permute-start(bf16[400,128]{1,0:T(8,128)(2,1)} %get-tuple-element.167), channel_id=1, source_target_pairs={{0,96},{32,0},{64,32},{96,64},{1,97},{33,1},{65,33},{97,65},{2,98}... | collective-permute-start | bytes 307208 | tf_op jit(solution)/shard_map/ppermute | solution.py:362
  162.1 22.6 %collective-permute-start.16 = (bf16[128,1536]{1,0:T(8,128)(2,1)}, bf16[128,1536]{1,0:T(8,128)(2,1)S(1)}, u32[]{:S(2)}, u32[]{:S(2)}) collective-permute-start(bf16[128,1536]{1,0:T(8,128)(2,1)} %get-tuple-element.182), channel_id=1, source_target_pairs={{0,1},{1,4},{4,5},{5,0},{2,3},{3,6},{6,7},{7,2},{8,9},{9,12},{12,1... | collective-permute-start | bytes 1179656 | tf_op jit(solution)/shard_map/ppermute | solution.py:66
  163.9 20.8 %collective-permute-start.17 = (bf16[128,1536]{1,0:T(8,128)(2,1)S(1)}, bf16[128,1536]{1,0:T(8,128)(2,1)S(1)}, u32[]{:S(2)}, u32[]{:S(2)}) collective-permute-start(bf16[128,1536]{1,0:T(8,128)(2,1)S(1)} %get-tuple-element.183), channel_id=1, source_target_pairs={{0,5},{1,0},{4,1},{5,4},{2,7},{3,2},{6,3},{7,6},{8,13},{9,8},{12,9... | collective-permute-start | bytes 1179656 | tf_op jit(solution)/shard_map/ppermute | solution.py:66
  165.1 19.5 %collective-permute-start.18 = (bf16[128,1536]{1,0:T(8,128)(2,1)S(1)}, bf16[128,1536]{1,0:T(8,128)(2,1)S(1)}, u32[]{:S(2)}, u32[]{:S(2)}) collective-permute-start(bf16[128,1536]{1,0:T(8,128)(2,1)S(1)} %get-tuple-element.184), channel_id=1, source_target_pairs={{0,4},{1,5},{4,0},{5,1},{2,6},{3,7},{6,2},{7,3},{8,12},{9,13},{12,... | collective-permute-start | bytes 1179656 | tf_op jit(solution)/shard_map/ppermute | solution.py:66
  168.1 16.6 %all-to-all-start.2 = ((f32[8,1,128]{2,1,0:T(1,128)}), f32[8,1,128]{2,1,0:T(1,128)S(1)}, u32[]{:S(2)}, u32[]{:S(2)}) async-start(f32[8,1,128]{2,1,0:T(1,128)} %slice_bitcast_fusion.2), calls=%async_computation.2 | async-start | bytes 8192 | tf_op jit(solution)/shard_map/all_to_all | solution.py:54
  172.4 200.7 %reduce-scatter.3.cloned.1.call-start = ((), (), s32[]{:S(2)}) async-start(), calls=%async_computation.15 | async-start | bytes 3538944 | tf_op jit(solution)/shard_map/reduce_scatter | solution.py:1091
  187.5 16.5 %collective-permute-start.22 = (bf16[128,1536]{1,0:T(8,128)(2,1)}, bf16[128,1536]{1,0:T(8,128)(2,1)S(1)}, u32[]{:S(2)}, u32[]{:S(2)}) collective-permute-start(bf16[128,1536]{1,0:T(8,128)(2,1)} %get-tuple-element.188.refs_0_), channel_id=1, source_target_pairs={{0,5},{1,0},{4,1},{5,4},{2,7},{3,2},{6,3},{7,6},{8,13},{9,8},{12,9... | collective-permute-start | bytes 1179656 | tf_op jit(solution)/shard_map/ppermute | solution.py:66
  189.4 20.6 %collective-permute-start.24 = (bf16[128,1536]{1,0:T(8,128)(2,1)}, bf16[128,1536]{1,0:T(8,128)(2,1)S(1)}, u32[]{:S(2)}, u32[]{:S(2)}) collective-permute-start(bf16[128,1536]{1,0:T(8,128)(2,1)} %get-tuple-element.188.refs_0_), channel_id=1, source_target_pairs={{0,4},{1,5},{4,0},{5,1},{2,6},{3,7},{6,2},{7,3},{8,12},{9,13},{12,... | collective-permute-start | bytes 1179656 | tf_op jit(solution)/shard_map/ppermute | solution.py:66
  189.5 23.8 %collective-permute-start.19 = (bf16[128,1536]{1,0:T(8,128)(2,1)}, bf16[128,1536]{1,0:T(8,128)(2,1)S(1)}, u32[]{:S(2)}, u32[]{:S(2)}) collective-permute-start(bf16[128,1536]{1,0:T(8,128)(2,1)} %get-tuple-element.188.refs_0_), channel_id=1, source_target_pairs={{0,2},{2,0},{1,3},{3,1},{4,6},{6,4},{5,7},{7,5},{8,10},{10,8},{9,1... | collective-permute-start | bytes 1179656 | tf_op jit(solution)/shard_map/ppermute | solution.py:58
  317.9 61.4 %all-to-all-start.5 = ((bf16[16,192,384]{2,1,0:T(8,128)(2,1)}), bf16[16,192,384]{2,1,0:T(8,128)(2,1)}, u32[]{:S(2)}, u32[]{:S(2)}) async-start(bf16[16,192,384]{2,1,0:T(8,128)(2,1)} %constant_dynamic-update-slice_fusion), calls=%async_computation.6 | async-start | bytes 4718592 | tf_op jit(solution)/shard_map/all_to_all | solution.py:54
  380.1 43.6 %all-to-all-start.4 = ((bf16[16,96,768]{2,1,0:T(8,128)(2,1)}), bf16[16,96,768]{2,1,0:T(8,128)(2,1)}, u32[]{:S(2)}, u32[]{:S(2)}) async-start(bf16[16,96,768]{2,1,0:T(8,128)(2,1)} %bitcast.216), calls=%async_computation.5 | async-start | bytes 4718592 | tf_op jit(solution)/shard_map/all_to_all | solution.py:54
  391.0 17.1 %collective-permute-start.43 = (bf16[128,1536]{1,0:T(8,128)(2,1)}, bf16[128,1536]{1,0:T(8,128)(2,1)S(1)}, u32[]{:S(2)}, u32[]{:S(2)}) collective-permute-start(bf16[128,1536]{1,0:T(8,128)(2,1)} %copy-done.8), channel_id=1, source_target_pairs={{0,4},{1,5},{4,0},{5,1},{2,6},{3,7},{6,2},{7,3},{8,12},{9,13},{12,... | collective-permute-start | bytes 1179656 | tf_op jit(solution)/shard_map/ppermute | solution.py:66
  410.7 20.7 %collective-permute-start.45 = (bf16[144,1536]{1,0:T(8,128)(2,1)}, bf16[144,1536]{1,0:T(8,128)(2,1)S(1)}, u32[]{:S(2)}, u32[]{:S(2)}) collective-permute-start(bf16[144,1536]{1,0:T(8,128)(2,1)} %get-tuple-element.239.refs_0_), channel_id=1, source_target_pairs={{0,1},{1,4},{4,5},{5,0},{2,3},{3,6},{6,7},{7,2},{8,9},{9,12},{12,1... | collective-permute-start | bytes 1327112 | tf_op jit(solution)/shard_map/ppermute | solution.py:66
  411.4 20.4 %collective-permute-start.47 = (bf16[144,1536]{1,0:T(8,128)(2,1)}, bf16[144,1536]{1,0:T(8,128)(2,1)}, u32[]{:S(2)}, u32[]{:S(2)}) collective-permute-start(bf16[144,1536]{1,0:T(8,128)(2,1)} %get-tuple-element.239.refs_0_), channel_id=1, source_target_pairs={{0,5},{1,0},{4,1},{5,4},{2,7},{3,2},{6,3},{7,6},{8,13},{9,8},{12,9... | collective-permute-start | bytes 1327112 | tf_op jit(solution)/shard_map/ppermute | solution.py:66
  413.6 21.0 %collective-permute-start.49 = (bf16[144,1536]{1,0:T(8,128)(2,1)}, bf16[144,1536]{1,0:T(8,128)(2,1)}, u32[]{:S(2)}, u32[]{:S(2)}) collective-permute-start(bf16[144,1536]{1,0:T(8,128)(2,1)} %get-tuple-element.239.refs_0_), channel_id=1, source_target_pairs={{0,4},{1,5},{4,0},{5,1},{2,6},{3,7},{6,2},{7,3},{8,12},{9,13},{12,... | collective-permute-start | bytes 1327112 | tf_op jit(solution)/shard_map/ppermute | solution.py:66
  465.7 20.6 %collective-permute-start.54 = (bf16[400,128]{1,0:T(8,128)(2,1)}, bf16[400,128]{1,0:T(8,128)(2,1)S(1)}, u32[]{:S(2)}, u32[]{:S(2)}) collective-permute-start(bf16[400,128]{1,0:T(8,128)(2,1)} %get-tuple-element.254), channel_id=1, source_target_pairs={{0,32},{32,64},{64,96},{96,0},{1,33},{33,65},{65,97},{97,1},{2,34}... | collective-permute-start | bytes 307208 | tf_op jit(solution)/shard_map/ppermute | solution.py:362
  501.4 33.4 %all-to-all-start.8 = ((bf16[16,192,384]{2,1,0:T(8,128)(2,1)}), bf16[16,192,384]{2,1,0:T(8,128)(2,1)}, u32[]{:S(2)}, u32[]{:S(2)}) async-start(bf16[16,192,384]{2,1,0:T(8,128)(2,1)} %constant_dynamic-update-slice_fusion.5), calls=%async_computation.10 | async-start | bytes 4718592 | tf_op jit(solution)/shard_map/all_to_all | solution.py:54
  534.8 39.9 %all-to-all-start.7 = ((bf16[16,96,768]{2,1,0:T(8,128)(2,1)}), bf16[16,96,768]{2,1,0:T(8,128)(2,1)}, u32[]{:S(2)}, u32[]{:S(2)}) async-start(bf16[16,96,768]{2,1,0:T(8,128)(2,1)} %bitcast.217), calls=%async_computation.9 | async-start | bytes 4718592 | tf_op jit(solution)/shard_map/all_to_all | solution.py:54
  543.5 73.6 %reduce-scatter.5.cloned.1.call-start = ((), (), s32[]{:S(2)}) async-start(), calls=%async_computation.16 | async-start | bytes 3538944 | tf_op jit(solution)/shard_map/reduce_scatter | solution.py:1145
  545.7 46.2 %collective-permute-start.59 = (f32[24,1536]{1,0:T(8,128)S(1)}, f32[24,1536]{1,0:T(8,128)S(1)}, u32[]{:S(2)}, u32[]{:S(2)}) collective-permute-start(f32[24,1536]{1,0:T(8,128)S(1)} %bitcast.255), channel_id=1, source_target_pairs={{0,0},{8,1},{16,2},{24,3},{32,4},{40,5},{48,6},{56,7},{64,8},{72,9... | collective-permute-start | bytes 442376 | tf_op jit(solution)/shard_map/ppermute | solution.py:1170
  584.2 23.4 %all-to-all-start.9 = ((f32[8,12,1152]{2,1,0:T(8,128)}), f32[8,12,1152]{2,1,0:T(8,128)S(1)}, u32[]{:S(2)}, u32[]{:S(2)}) async-start(f32[8,12,1152]{2,1,0:T(8,128)} %reshape.553), calls=%async_computation.11 | async-start | bytes 1179648 | tf_op jit(solution)/shard_map/all_to_all | solution.py:54
  (128 other events, 1033.7 us)
Sparse Core Ops, SparseCore 0:
  85.8 52.4 all-gather.3
  141.0 48.5 all-gather.5
  191.3 59.9 all-gather.7
  272.2 55.8 reduce-scatter.2
  546.4 69.3 reduce-scatter.4

commit v6 on v5

--- a/solution.py
+++ b/solution.py
@@ -471,18 +471,18 @@
     return jnp.exp(run) * (segc_ref[...] == seg_before).astype(f32)
 
 
-def past_rows(k, u_ref, past_ref, edge_ref):
-    past = jnp.where(k == 0, edge_ref[...].astype(f32), past_ref[...].astype(f32))
-    return jnp.concatenate([past, u_ref[...].astype(f32)], axis=0)
-
-
-def back_by(rows, distance):
-    return (pltpu.roll(rows, distance, 0) if distance else rows)[16:]
+def past_rows(k, u_ref, past_ref, edge_ref, rows_ref):
+    rows_ref[:16] = jnp.where(k == 0, edge_ref[...].astype(f32), past_ref[...].astype(f32))
+    rows_ref[16:] = u_ref[...].astype(f32)
+
+
+def back_by(rows_ref, distance):
+    return rows_ref[16 - distance : 16 - distance + SPAN]
 
 
 def mix_kernel(
     seg_ref, u_ref, past_ref, edge_ref, same_ref, conv_ref, raw_ref, bias_ref, rate_ref, segc_ref,
-    segr_ref, v_ref, pre_ref, within_ref, local_ref, step_ref, run_ref, before_ref, decay_ref, sent_ref, acc_ref, dec_ref,
+    segr_ref, v_ref, pre_ref, within_ref, local_ref, step_ref, run_ref, before_ref, decay_ref, sent_ref, acc_ref, dec_ref, rows,
 ):
     k = pl.program_id(0)
 
@@ -491,7 +491,7 @@
         acc_ref[...] = jnp.zeros_like(acc_ref)
         dec_ref[...] = jnp.ones_like(dec_ref)
 
-    rows = past_rows(k, u_ref, past_ref, edge_ref)
+    past_rows(k, u_ref, past_ref, edge_ref, rows)
     pre = jnp.broadcast_to(conv_ref[CONV : CONV + 1], (SPAN, CC))
     for i in range(CONV):
         pre = pre + conv_ref[i : i + 1] * back_by(rows, i) * same_ref[:, i : i + 1]
@@ -730,7 +730,7 @@
     first, order_ref, dpre_ref, next_ref, after_ref, u_ref, past_ref, edge_ref, same_ref, conv_ref, draw_ref, dz_ref,
     wa_ref, wz_ref, da_ref, *outs,
 ):
-    taps_ref = outs[-1]
+    *outs, taps_ref, rows, d_rows = outs
     i = pl.program_id(0)
     k = order_ref[i]
 
@@ -739,15 +739,17 @@
         taps_ref[...] = jnp.zeros_like(taps_ref)
 
     d_pre = dpre_ref[...].astype(f32)
-    later = jnp.where(k == LAST, after_ref[...].astype(f32), next_ref[...].astype(f32))
-    d_rows = jnp.concatenate([d_pre, later], axis=0)
-    rows = past_rows(k, u_ref, past_ref, edge_ref)
+    d_rows[:SPAN] = d_pre
+    d_rows[SPAN:] = jnp.where(
+        k == LAST, after_ref[...].astype(f32), next_ref[...].astype(f32)
+    )
+    past_rows(k, u_ref, past_ref, edge_ref, rows)
     du = jnp.zeros((SPAN, CC), f32)
     taps = []
     for tap in range(CONV):
-        ahead = pltpu.roll(d_rows, SPAN + 16 - tap, 0) if tap else d_rows
+        ahead = d_rows[tap : tap + SPAN]
         same = same_ref[:, CONV + tap : CONV + tap + 1]
-        du = du + conv_ref[tap : tap + 1] * ahead[:SPAN] * same
+        du = du + conv_ref[tap : tap + 1] * ahead * same
         product = d_pre * back_by(rows, tap) * same_ref[:, tap : tap + 1]
         taps.append(jnp.sum(product, axis=0, keepdims=True))
     taps.append(jnp.sum(d_pre, axis=0, keepdims=True))
@@ -848,7 +850,7 @@
          tok_block(128), span_block(1, 128), span_block(1, 128), whole(STATE_ROWS, N)],
         [struct((GT, CC), bf), struct((GT, CC), bf), struct((GT, W)), STATE, struct((GT, 128)),
          struct((GT, 128)), ROW, ROW, SENT],
-        [STATE_SCRATCH, pltpu.VMEM((1, 128), f32)],
+        [STATE_SCRATCH, pltpu.VMEM((1, 128), f32), pltpu.VMEM((SPAN + 16, CC), f32)],
         (seg, u, u, edge, same, conv, raw, bias, rate, segc, segr),
         10,
     )
@@ -870,7 +872,7 @@
         [tok_at(CA)] + ([tok_at(D)] if first else HALVES) + [whole_at(8, CC)],
         [struct((GT, CA), bf)] + ([struct((GT, D), bf)] if first else HALF_SHAPES)
         + [struct((8, CC))],
-        [],
+        [pltpu.VMEM((SPAN + 16, CC), f32)] * 2,
         (d_pre, d_pre, after, u, u, edge, same, conv, d_raw, dz, wa, wz),
         10,
     )
@@ -1038,7 +1040,7 @@
     conv_x = lax.dynamic_slice_in_dim(conv_all, group * W, W, 2)
     conv_here = jnp.concatenate([conv_x, conv_all[:, :, DI:]], axis=2)
     conv_here = jnp.pad(conv_here, ((0, 0), (0, 7 - CONV), (0, 0)))
-    zo = group_gather(wait_for(zo, tail)).reshape(NQ, 288, W)
+    zo = group_gather(wait_for(zo, w_a0, blocks)).reshape(NQ, 288, W)
     w_z0 = zo[:, :96].reshape(D, W)
     w_o = [zo[:, 96:192].reshape(W, D), None]
     w_in1 = group_gather(wait_for(in_1, tail))
@@ -1171,7 +1173,7 @@
         for l in range(LAYERS)
     ]
     late = jnp.concatenate([a_sums[0], z_sums[0]], axis=1)
-    late = a2a(late.reshape(NG, 12, CA + W), LINE)
+    late = a2a(late.reshape(NG, 12, CA + W).astype(bf), LINE).astype(f32)
     small = jnp.sum(late[:, :, SMALL:CA], axis=0)
     in_grads, gain_grads, out_grads, gate_grads = ([None] * LAYERS for _ in range(4))
     for l in range(LAYERS):

time: 637 us -> 629 us (0.987)
  waiting for transfers between devices: 138 us -> 127 us
    all_gather x2, waiting for transfers between devices: 12.8 us -> 0.01 us  [group_gather(): return lax.all_gather(block, ZX, axis=0, tiled=True)]
    all_to_all x9, waiting for transfers between devices: 70.3 us -> 63.9 us  [a2a(): return lax.all_to_all(a, axes, 0, 0, tiled=True)]
    unnamed x184 -> x186, local copies, waits for them, and re-layouts: 28.6 us -> 29.5 us
  transfers between devices with their start and end apart: 74 -> 74, of which waited for: 19 -> 20; matrix products, arithmetic and copies ran while one was open for 18% -> 18% of each run, Pallas kernels for 18% -> 19%
where the time goes in v6:
time: 629 us; the launch traced here: 618 us
  starting transfers between devices  170 us (27%)
  Pallas kernels  155 us (25%)
  waiting for transfers between devices  127 us (20%)
  local copies, waits for them, and re-layouts  74.7 us (12%)
  matrix products  43.4 us (7%)
  other arithmetic  22.2 us (4%)
  between operations  16.2 us (3%)
  blocking collectives  9.72 us (2%)
    pallas_call x11, Pallas kernels, call(): pl.pallas_call(kernel, grid=(NS,), in_specs=ins, out_specs=outs, out_shap...  97.7 us
    all_to_all x9, waiting for transfers between devices, a2a(): return lax.all_to_all(a, axes, 0, 0, tiled=True)  63.9 us
    all_to_all x9, starting transfers between devices, a2a(): return lax.all_to_all(a, axes, 0, 0, tiled=True)  55.7 us
    dot_general x15, matrix products, mm(): lax.dot_general(a, b, (((ca,), (cb,)), ((), ())), preferred_element_type=...  43.4 us
    pallas_call x4, Pallas kernels, ordered_call(): pl.pallas_call(kernel, grid_spec=pltpu.PrefetchScalarGridSpec(num_scalar_...  42.1 us
    ppermute x24, starting transfers between devices, around(): lax.ppermute(a, axis, [(i, (i + d) % 4) for i in range(4)])  40.4 us
    ppermute x14, starting transfers between devices, core_swap(): return lax.ppermute(a, 'c', [(0, 1), (1, 0)])  34.2 us
    ppermute x15, waiting for transfers between devices, along_line(): return lax.ppermute(a, Y, [(i, (i + distance) % 4) for i in range(4)])  31.6 us
  transfers between devices with their start and end apart: 74, of which 20 were waited for; matrix products, arithmetic and copies ran while one was open for 18% of the time, Pallas kernels for 19%

profile of v6, /device:TPU:1, one launch (start us, length us, event | category | flops | bytes accessed | tf_op | source)
XLA Modules:
  0.0 617.6 jit_solution(7471722589208331198)
XLA Ops:
  31.5 7.8 %all-to-all-start.1 = ((bf16[16,96,768]{2,1,0:T(8,128)(2,1)}), bf16[16,96,768]{2,1,0:T(8,128)(2,1)}, u32[]{:S(2)}, u32[]{:S(2)}) async-start(bf16[16,96,768]{2,1,0:T(8,128)(2,1)} %broadcast_in_dim.31), calls=%async_computation.1 | async-start | bytes 4718592 | tf_op jit(solution)/shard_map/all_to_all | solution.py:54
  51.1 9.8 %collective-permute-start.2 = (bf16[128,1536]{1,0:T(8,128)(2,1)S(1)}, bf16[128,1536]{1,0:T(8,128)(2,1)S(1)}, u32[]{:S(2)}, u32[]{:S(2)}) collective-permute-start(bf16[128,1536]{1,0:T(8,128)(2,1)S(1)} %collective-permute-done.1.refs_2_), channel_id=1, source_target_pairs={{0,2},{2,0},{1,3},{3,1},{4,6},{6,4},{5,7},{7,5},{8,10},{10,8},{9,1... | collective-permute-start | bytes 1179656 | tf_op jit(solution)/shard_map/ppermute | solution.py:58
  66.3 10.0 %collective-permute-done.7 = bf16[2,24,1536]{2,1,0:T(8,128)(2,1)S(1)} collective-permute-done((bf16[2,24,1536]{2,1,0:T(8,128)(2,1)S(1)}, bf16[2,24,1536]{2,1,0:T(8,128)(2,1)S(1)}, u32[]{:S(2)}, u32[]{:S(2)}) %collective-permute-start.7) | collective-permute-done | bytes 147488 | tf_op jit(solution)/shard_map/ppermute | solution.py:1031
  78.8 7.0 %place_project.2 = (bf16[1024,1536]{1,0:T(8,128)(2,1)}, bf16[1024,640]{1,0:T(8,128)(2,1)}, bf16[1024,128]{1,0:T(8,128)(2,1)}) custom-call(s32[8]{0:T(128)} %stack.186.pos_ref, bf16[128,1536]{1,0:T(8,128)(2,1)} %copy-done.21, bf16[128,1536]{1,0:T(8,128)(2,1)} %copy-done.32, bf16[128,1536]{1,0:T(8,128)(2,1)} %copy-done.29, bf16[128,1536]{1,0:T(8,128)(2,1)} %copy-done.33, ...), custom_call_target="tpu_custom_call" | custom-call | flops 360000000 | bytes 1800000 | tf_op jit(solution)/shard_map/place_project/pallas_call | solution.py:786
  93.0 11.5 %span_mix.2 = (bf16[1024,640]{1,0:T(8,128)(2,1)}, bf16[1024,640]{1,0:T(8,128)(2,1)}, f32[1024,384]{1,0:T(8,128)}, f32[4,384,128]{2,1,0:T(8,128)}, f32[1024,128]{...) custom-call(s32[2,4]{1,0:T(2,128)} %pad_add_fusion.seg_ref, ...), custom_call_target="tpu_custom_call" | custom-call | flops 400000000 | bytes 2000000 | tf_op jit(solution)/shard_map/span_mix/pallas_call | solution.py:786
  104.7 7.3 %collective-permute-start.10 = (bf16[400,128]{1,0:T(8,128)(2,1)}, bf16[400,128]{1,0:T(8,128)(2,1)S(1)}, u32[]{:S(2)}, u32[]{:S(2)}) collective-permute-start(bf16[400,128]{1,0:T(8,128)(2,1)} %get-tuple-element.166.own_ref), channel_id=1, source_target_pairs={{0,16},{8,24},{16,0},{24,8},{1,17},{9,25},{17,1},{25,9},{2,18},{10... | collective-permute-start | bytes 307208 | tf_op jit(solution)/shard_map/ppermute | solution.py:362
  137.6 9.6 %span_gate.2 = (f32[1024,384]{1,0:T(8,128)}, bf16[512,1536]{1,0:T(8,128)(2,1)}, bf16[512,1536]{1,0:T(8,128)(2,1)}, f32[8,1024]{1,0:T(8,128)}, f32[384,128]{1,0:T(8,128)}) custom-call(s32[4]{0:T(128)} %pad_add_fusion.1.order_ref, s32[2,4]{1,0:T(2,128)} %pad_add_fusion.seg_ref, s32[1]{0:T(128)} %bitcast.6.at_ref, bf16[400,128]{1,0:T(8,128)(2,1)} %copy-done.40, ...), custom_call_target="tpu_custom_call" | custom-call | flops 400000000 | bytes 2000000 | tf_op jit(solution)/shard_map/span_gate/pallas_call | solution.py:804
  165.5 10.2 %all-to-all-done.2 = f32[8,1,128]{2,1,0:T(1,128)S(1)} async-done(((f32[8,1,128]{2,1,0:T(1,128)}), f32[8,1,128]{2,1,0:T(1,128)S(1)}, u32[]{:S(2)}, u32[]{:S(2)}) %all-to-all-start.2) | async-done | bytes 4128 | tf_op jit(solution)/shard_map/all_to_all | solution.py:54
  182.6 7.0 %collective-permute-done.20.refs_2_ = bf16[128,1536]{1,0:T(8,128)(2,1)S(1)} collective-permute-done((bf16[128,1536]{1,0:T(8,128)(2,1)}, bf16[128,1536]{1,0:T(8,128)(2,1)S(1)}, u32[]{:S(2)}, u32[]{:S(2)}) %collective-permute-start.20) | collective-permute-done | bytes 393248 | tf_op jit(solution)/shard_map/ppermute | solution.py:66
  195.8 8.0 %collective-permute-done.24.refs_6_ = bf16[128,1536]{1,0:T(8,128)(2,1)S(1)} collective-permute-done((bf16[128,1536]{1,0:T(8,128)(2,1)}, bf16[128,1536]{1,0:T(8,128)(2,1)S(1)}, u32[]{:S(2)}, u32[]{:S(2)}) %collective-permute-start.24) | collective-permute-done | bytes 393248 | tf_op jit(solution)/shard_map/ppermute | solution.py:66
  208.1 7.0 %place_project.3 = (bf16[1024,1536]{1,0:T(8,128)(2,1)}, bf16[1024,640]{1,0:T(8,128)(2,1)}, bf16[1024,128]{1,0:T(8,128)(2,1)}) custom-call(s32[8]{0:T(128)} %stack.186.pos_ref, bf16[128,1536]{1,0:T(8,128)(2,1)} %get-tuple-element.188.refs_0_, bf16[128,1536]{1,0:T(8,128)(2,1)} %copy-done.37, bf16[128,1536]{1,0:T(8,128)(2,1)} %copy-done.34, ...), custom_call_target="tpu_custom_call" | custom-call | flops 360000000 | bytes 1800000 | tf_op jit(solution)/shard_map/place_project/pallas_call | solution.py:786
  222.6 11.4 %span_mix.3 = (bf16[1024,640]{1,0:T(8,128)(2,1)}, bf16[1024,640]{1,0:T(8,128)(2,1)}, f32[1024,384]{1,0:T(8,128)}, f32[4,384,128]{2,1,0:T(8,128)}, f32[1024,128]{...) custom-call(s32[2,4]{1,0:T(2,128)} %pad_add_fusion.seg_ref, ...), custom_call_target="tpu_custom_call" | custom-call | flops 400000000 | bytes 2000000 | tf_op jit(solution)/shard_map/span_mix/pallas_call | solution.py:786
  257.0 9.1 %span_gate.3 = (f32[1024,384]{1,0:T(8,128)}, bf16[1024,1536]{1,0:T(8,128)(2,1)}, f32[8,1024]{1,0:T(8,128)}, f32[384,128]{1,0:T(8,128)}) custom-call(s32[4]{0:T(128)} %pad_add_fusion.1.order_ref, s32[2,4]{1,0:T(2,128)} %pad_add_fusion.seg_ref, s32[1]{0:T(128)} %bitcast.6.at_ref, bf16[400,128]{1,0:T(8,128)(2,1)} %copy-done.61, bf16[400,128]{1,0:T(8,128)(2,1)} %copy-done.62, ...), custom_call_target="tpu_custom_call" | custom-call | flops 400000000 | bytes 2000000 | tf_op jit(solution)/shard_map/span_gate/pallas_call | solution.py:804
  266.9 9.7 %all_to_all.57 = f32[8,2,1024]{2,1,0:T(2,128)S(1)} all-to-all(f32[8,2,1024]{2,1,0:T(2,128)S(1)} %broadcast_in_dim.38), channel_id=1, replica_groups=mesh['z'=4,'x'=4,'yh'=2,'c'=2,'yl'=2] {'yh','c','yl'}, dimensions={0} | all-to-all | bytes 131072 | tf_op jit(solution)/shard_map/all_to_all | solution.py:54
  277.3 7.9 %span_gate_back.2 = (bf16[1024,384]{1,0:T(8,128)(2,1)}, bf16[1024,384]{1,0:T(8,128)(2,1)}, bf16[1024,384]{1,0:T(8,128)(2,1)}, f32[4,384,128]{2,1,0:T(8,128)}, f3...) custom-call(s32[2,4]{1,0:T(2,128)} %pad_add_fusion.seg_ref, f32[1024,384]{1,0:T(8,128)} %fusion.46.rest_0_.grad_ref, ...), custom_call_target="tpu_custom_call" | custom-call | flops 480000000 | bytes 2400000 | tf_op jit(solution)/shard_map/span_gate_back/pallas_call | solution.py:786
  314.9 7.9 %span_mix_back.2 = (f32[1024,384]{1,0:T(8,128)}, bf16[1024,256]{1,0:T(8,128)(2,1)}) custom-call(bf16[1024,640]{1,0:T(8,128)(2,1)} %get-tuple-element.204.v_ref, f32[1024,128]{1,0:T(8,128)} %get-tuple-element.223.step_ref, f32[1024,128]{1,0:T(8,128)} %get-tuple-element.203.run_ref, s32[1024,1]{1,0:T(8,128)} %copy.268.segc_ref, s32[4,1,256]{2,1,0:T(1,128)} %bitcast.251, ...), custom_call_target="tpu_custom_call" | custom-call | flops 560000000 | bytes 2800000 | tf_op jit(solution)/shard_map/span_mix_back/pallas_call | solution.py:786
  322.9 12.2 %span_end.2 = (bf16[1024,640]{1,0:T(8,128)(2,1)}, bf16[1024,128]{1,0:T(8,128)(2,1)}, f32[8,128]{1,0:T(8,128)}) custom-call(s32[2,4]{1,0:T(2,128)} %pad_add_fusion.seg_ref, s32[1]{0:T(128)} %bitcast.6.at_ref, bf16[400,128]{1,0:T(8,128)(2,1)} %copy-done.55, bf16[400,128]{1,0:T(8,128)(2,1)} %copy-done.57, bf16[400,128]{1,0:T(8,128)(2,1)} %copy-done.58, ...), custom_call_target="tpu_custom_call" | custom-call | flops 640000000 | bytes 3200000 | tf_op jit(solution)/shard_map/span_end/pallas_call | solution.py:786
  343.5 12.1 %conv_back.2 = (bf16[1024,768]{1,0:T(8,128)(2,1)}, bf16[512,1536]{1,0:T(8,128)(2,1)}, bf16[512,1536]{1,0:T(8,128)(2,1)}, f32[8,640]{1,0:T(8,128)}) custom-call(s32[4]{0:T(128)} %pad_add_fusion.1.order_ref, bf16[1024,640]{1,0:T(8,128)(2,1)} %get-tuple-element.228.dpre_ref.next_ref, bf16[1024,640]{1,0:T(8,128)(2,1)} %get-tuple-element.228.dpre_ref.next_ref, ...), custom_call_target="tpu_custom_call" | custom-call | flops 400000000 | bytes 2000000 | tf_op jit(solution)/shard_map/conv_back/pallas_call | solution.py:804
  372.8 6.7 %all-to-all-start.4 = ((bf16[16,96,768]{2,1,0:T(8,128)(2,1)}), bf16[16,96,768]{2,1,0:T(8,128)(2,1)}, u32[]{:S(2)}, u32[]{:S(2)}) async-start(bf16[16,96,768]{2,1,0:T(8,128)(2,1)} %bitcast.216), calls=%async_computation.5 | async-start | bytes 4718592 | tf_op jit(solution)/shard_map/all_to_all | solution.py:54
  386.6 7.0 %collective-permute-done.41.refs_1_ = bf16[128,1536]{1,0:T(8,128)(2,1)S(1)} collective-permute-done((bf16[128,1536]{1,0:T(8,128)(2,1)S(1)}, bf16[128,1536]{1,0:T(8,128)(2,1)S(1)}, u32[]{:S(2)}, u32[]{:S(2)}) %collective-permute-start.41) | collective-permute-done | bytes 393248 | tf_op jit(solution)/shard_map/ppermute | solution.py:66
  393.6 7.1 %collective-permute-done.43.refs_3_ = bf16[128,1536]{1,0:T(8,128)(2,1)S(1)} collective-permute-done((bf16[128,1536]{1,0:T(8,128)(2,1)}, bf16[128,1536]{1,0:T(8,128)(2,1)S(1)}, u32[]{:S(2)}, u32[]{:S(2)}) %collective-permute-start.43) | collective-permute-done | bytes 393248 | tf_op jit(solution)/shard_map/ppermute | solution.py:66
  408.8 7.8 %all-to-all-done.4 = bf16[16,96,768]{2,1,0:T(8,128)(2,1)} async-done(((bf16[16,96,768]{2,1,0:T(8,128)(2,1)}), bf16[16,96,768]{2,1,0:T(8,128)(2,1)}, u32[]{:S(2)}, u32[]{:S(2)}) %all-to-all-start.4) | async-done | bytes 2359328 | tf_op jit(solution)/shard_map/all_to_all | solution.py:54
  440.9 8.2 %span_gate_back.3 = (bf16[1024,384]{1,0:T(8,128)(2,1)}, bf16[1024,384]{1,0:T(8,128)(2,1)}, bf16[1024,384]{1,0:T(8,128)(2,1)}, f32[4,384,128]{2,1,0:T(8,128)}, f3...) custom-call(s32[2,4]{1,0:T(2,128)} %pad_add_fusion.seg_ref, bf16[1024,1536]{1,0:T(8,128)(2,1)} %get-tuple-element.246.grad_ref, ...), custom_call_target="tpu_custom_call" | custom-call | flops 480000000 | bytes 2400000 | tf_op jit(solution)/shard_map/span_gate_back/pallas_call | solution.py:786
  476.0 7.9 %span_mix_back.3 = (f32[1024,384]{1,0:T(8,128)}, bf16[1024,256]{1,0:T(8,128)(2,1)}) custom-call(bf16[1024,640]{1,0:T(8,128)(2,1)} %get-tuple-element.177.v_ref, f32[1024,128]{1,0:T(8,128)} %get-tuple-element.264.step_ref, f32[1024,128]{1,0:T(8,128)} %get-tuple-element.176.run_ref, s32[1024,1]{1,0:T(8,128)} %copy.268.segc_ref, s32[4,1,256]{2,1,0:T(1,128)} %bitcast.252, ...), custom_call_target="tpu_custom_call" | custom-call | flops 560000000 | bytes 2800000 | tf_op jit(solution)/shard_map/span_mix_back/pallas_call | solution.py:786
  484.6 12.2 %span_end.3 = (bf16[1024,640]{1,0:T(8,128)(2,1)}, bf16[1024,128]{1,0:T(8,128)(2,1)}, f32[8,128]{1,0:T(8,128)}) custom-call(s32[2,4]{1,0:T(2,128)} %pad_add_fusion.seg_ref, s32[1]{0:T(128)} %bitcast.6.at_ref, bf16[400,128]{1,0:T(8,128)(2,1)} %copy-done.56, bf16[400,128]{1,0:T(8,128)(2,1)} %copy-done.59, bf16[400,128]{1,0:T(8,128)(2,1)} %copy-done.60, ...), custom_call_target="tpu_custom_call" | custom-call | flops 640000000 | bytes 3200000 | tf_op jit(solution)/shard_map/span_end/pallas_call | solution.py:786
  504.9 11.3 %conv_back.3 = (bf16[1024,768]{1,0:T(8,128)(2,1)}, bf16[1024,1536]{1,0:T(8,128)(2,1)}, f32[8,640]{1,0:T(8,128)}) custom-call(s32[4]{0:T(128)} %pad_add_fusion.1.order_ref, bf16[1024,640]{1,0:T(8,128)(2,1)} %get-tuple-element.269.dpre_ref.next_ref, bf16[1024,640]{1,0:T(8,128)(2,1)} %get-tuple-element.269.dpre_ref.next_ref, bf16[16,640]{1,0:T(8,128)(2,1)} %copy-done.67, ...), custom_call_target="tpu_custom_call" | custom-call | flops 400000000 | bytes 2000000 | tf_op jit(solution)/shard_map/conv_back/pallas_call | solution.py:804
  520.0 6.5 %add_convert_fusion = bf16[1536,768]{1,0:T(8,128)(2,1)} fusion(bf16[1024,1536]{1,0:T(8,128)(2,1)} %get-tuple-element.169, bf16[1024,768]{1,0:T(8,128)(2,1)} %get-tuple-element.273, bf16[1536,98]{1,0:T(8,128)(2,1)} %convert_element_type.234), kind=kOutput, calls=%fused_computation.2 | convolution fusion | flops 2419458048 | bytes 7378944 | tf_op jit(solution)/shard_map/dot_general | solution.py:50
  532.4 8.3 %all-to-all-start.7 = ((bf16[16,96,768]{2,1,0:T(8,128)(2,1)}), bf16[16,96,768]{2,1,0:T(8,128)(2,1)}, u32[]{:S(2)}, u32[]{:S(2)}) async-start(bf16[16,96,768]{2,1,0:T(8,128)(2,1)} %bitcast.217), calls=%async_computation.9 | async-start | bytes 4718592 | tf_op jit(solution)/shard_map/all_to_all | solution.py:54
  543.2 6.9 %collective-permute-start.59 = (f32[24,1536]{1,0:T(8,128)S(1)}, f32[24,1536]{1,0:T(8,128)S(1)}, u32[]{:S(2)}, u32[]{:S(2)}) collective-permute-start(f32[24,1536]{1,0:T(8,128)S(1)} %bitcast.255), channel_id=1, source_target_pairs={{0,0},{8,1},{16,2},{24,3},{32,4},{40,5},{48,6},{56,7},{64,8},{72,9... | collective-permute-start | bytes 442376 | tf_op jit(solution)/shard_map/ppermute | solution.py:1172
  552.2 20.0 %all-to-all-done.7 = bf16[16,96,768]{2,1,0:T(8,128)(2,1)} async-done(((bf16[16,96,768]{2,1,0:T(8,128)(2,1)}), bf16[16,96,768]{2,1,0:T(8,128)(2,1)}, u32[]{:S(2)}, u32[]{:S(2)}) %all-to-all-start.7) | async-done | bytes 2359328 | tf_op jit(solution)/shard_map/all_to_all | solution.py:54
  581.3 7.5 %all-to-all-start.9 = ((bf16[8,12,1152]{2,1,0:T(8,128)(2,1)}), bf16[8,12,1152]{2,1,0:T(8,128)(2,1)S(1)}, u32[]{:S(2)}, u32[]{:S(2)}) async-start(bf16[8,12,1152]{2,1,0:T(8,128)(2,1)} %convert_element_type.239), calls=%async_computation.11 | async-start | bytes 589824 | tf_op jit(solution)/shard_map/all_to_all | solution.py:54
  590.4 8.7 %all-to-all-done.9 = bf16[8,12,1152]{2,1,0:T(8,128)(2,1)S(1)} async-done(((bf16[8,12,1152]{2,1,0:T(8,128)(2,1)}), bf16[8,12,1152]{2,1,0:T(8,128)(2,1)S(1)}, u32[]{:S(2)}, u32[]{:S(2)}) %all-to-all-start.9) | async-done | bytes 221216 | tf_op jit(solution)/shard_map/all_to_all | solution.py:54
  (549 shorter events, 310.0 us)
Async XLA Ops:
  31.5 45.6 %all-to-all-start.1 = ((bf16[16,96,768]{2,1,0:T(8,128)(2,1)}), bf16[16,96,768]{2,1,0:T(8,128)(2,1)}, u32[]{:S(2)}, u32[]{:S(2)}) async-start(bf16[16,96,768]{2,1,0:T(8,128)(2,1)} %broadcast_in_dim.31), calls=%async_computation.1 | async-start | bytes 4718592 | tf_op jit(solution)/shard_map/all_to_all | solution.py:54
  39.3 90.8 %all-gather.4.cloned.1.call-start = ((), (), s32[]{:S(2)}) async-start(), calls=%async_computation.12 | async-start | bytes 3760128 | tf_op jit(solution)/shard_map/all_gather | solution.py:274
  40.0 20.9 %collective-permute-start.3 = (bf16[128,1536]{1,0:T(8,128)(2,1)S(1)}, bf16[128,1536]{1,0:T(8,128)(2,1)S(1)}, u32[]{:S(2)}, u32[]{:S(2)}) collective-permute-start(bf16[128,1536]{1,0:T(8,128)(2,1)S(1)} %multiply_convert_fusion.refs_0_), channel_id=1, source_target_pairs={{0,5},{1,0},{4,1},{5,4},{2,7},{3,2},{6,3},{7,6},{8,13},{9,8},{12,9... | collective-permute-start | bytes 1179656 | tf_op jit(solution)/shard_map/ppermute | solution.py:66
  42.4 18.6 %collective-permute-start.5 = (bf16[128,1536]{1,0:T(8,128)(2,1)S(1)}, bf16[128,1536]{1,0:T(8,128)(2,1)S(1)}, u32[]{:S(2)}, u32[]{:S(2)}) collective-permute-start(bf16[128,1536]{1,0:T(8,128)(2,1)S(1)} %multiply_convert_fusion.refs_0_), channel_id=1, source_target_pairs={{0,4},{1,5},{4,0},{5,1},{2,6},{3,7},{6,2},{7,3},{8,12},{9,13},{12,... | collective-permute-start | bytes 1179656 | tf_op jit(solution)/shard_map/ppermute | solution.py:66
  47.1 29.9 %collective-permute-start = (bf16[128,1536]{1,0:T(8,128)(2,1)S(1)}, bf16[128,1536]{1,0:T(8,128)(2,1)S(1)}, u32[]{:S(2)}, u32[]{:S(2)}) collective-permute-start(bf16[128,1536]{1,0:T(8,128)(2,1)S(1)} %multiply_convert_fusion.refs_0_), channel_id=1, source_target_pairs={{0,2},{2,0},{1,3},{3,1},{4,6},{6,4},{5,7},{7,5},{8,10},{10,8},{9,1... | collective-permute-start | bytes 1179656 | tf_op jit(solution)/shard_map/ppermute | solution.py:58
  51.1 26.0 %collective-permute-start.2 = (bf16[128,1536]{1,0:T(8,128)(2,1)S(1)}, bf16[128,1536]{1,0:T(8,128)(2,1)S(1)}, u32[]{:S(2)}, u32[]{:S(2)}) collective-permute-start(bf16[128,1536]{1,0:T(8,128)(2,1)S(1)} %collective-permute-done.1.refs_2_), channel_id=1, source_target_pairs={{0,2},{2,0},{1,3},{3,1},{4,6},{6,4},{5,7},{7,5},{8,10},{10,8},{9,1... | collective-permute-start | bytes 1179656 | tf_op jit(solution)/shard_map/ppermute | solution.py:58
  60.9 16.2 %collective-permute-start.4 = (bf16[128,1536]{1,0:T(8,128)(2,1)S(1)}, bf16[128,1536]{1,0:T(8,128)(2,1)}, u32[]{:S(2)}, u32[]{:S(2)}) collective-permute-start(bf16[128,1536]{1,0:T(8,128)(2,1)S(1)} %collective-permute-done.3.refs_4_), channel_id=1, source_target_pairs={{0,2},{2,0},{1,3},{3,1},{4,6},{6,4},{5,7},{7,5},{8,10},{10,8},{9,1... | collective-permute-start | bytes 1179656 | tf_op jit(solution)/shard_map/ppermute | solution.py:58
  61.0 16.1 %collective-permute-start.6 = (bf16[128,1536]{1,0:T(8,128)(2,1)S(1)}, bf16[128,1536]{1,0:T(8,128)(2,1)}, u32[]{:S(2)}, u32[]{:S(2)}) collective-permute-start(bf16[128,1536]{1,0:T(8,128)(2,1)S(1)} %collective-permute-done.5.refs_6_), channel_id=1, source_target_pairs={{0,2},{2,0},{1,3},{3,1},{4,6},{6,4},{5,7},{7,5},{8,10},{10,8},{9,1... | collective-permute-start | bytes 1179656 | tf_op jit(solution)/shard_map/ppermute | solution.py:58
  77.1 129.4 %all-gather.6.cloned.1.call-start = ((), (), s32[]{:S(2)}) async-start(), calls=%async_computation.13 | async-start | bytes 3760128 | tf_op jit(solution)/shard_map/all_gather | solution.py:274
  86.5 164.9 %all-gather.8.cloned.1.call-start = ((), (), s32[]{:S(2)}) async-start(), calls=%async_computation.14 | async-start | bytes 3538944 | tf_op jit(solution)/shard_map/all_gather | solution.py:1033
  104.7 16.7 %collective-permute-start.10 = (bf16[400,128]{1,0:T(8,128)(2,1)}, bf16[400,128]{1,0:T(8,128)(2,1)S(1)}, u32[]{:S(2)}, u32[]{:S(2)}) collective-permute-start(bf16[400,128]{1,0:T(8,128)(2,1)} %get-tuple-element.166.own_ref), channel_id=1, source_target_pairs={{0,16},{8,24},{16,0},{24,8},{1,17},{9,25},{17,1},{25,9},{2,18},{10... | collective-permute-start | bytes 307208 | tf_op jit(solution)/shard_map/ppermute | solution.py:362
  154.7 21.1 %collective-permute-start.16 = (bf16[128,1536]{1,0:T(8,128)(2,1)}, bf16[128,1536]{1,0:T(8,128)(2,1)S(1)}, u32[]{:S(2)}, u32[]{:S(2)}) collective-permute-start(bf16[128,1536]{1,0:T(8,128)(2,1)} %get-tuple-element.182), channel_id=1, source_target_pairs={{0,1},{1,4},{4,5},{5,0},{2,3},{3,6},{6,7},{7,2},{8,9},{9,12},{12,1... | collective-permute-start | bytes 1179656 | tf_op jit(solution)/shard_map/ppermute | solution.py:66
  154.7 21.1 %collective-permute-start.17 = (bf16[128,1536]{1,0:T(8,128)(2,1)S(1)}, bf16[128,1536]{1,0:T(8,128)(2,1)S(1)}, u32[]{:S(2)}, u32[]{:S(2)}) collective-permute-start(bf16[128,1536]{1,0:T(8,128)(2,1)S(1)} %get-tuple-element.183), channel_id=1, source_target_pairs={{0,5},{1,0},{4,1},{5,4},{2,7},{3,2},{6,3},{7,6},{8,13},{9,8},{12,9... | collective-permute-start | bytes 1179656 | tf_op jit(solution)/shard_map/ppermute | solution.py:66
  157.3 18.4 %collective-permute-start.18 = (bf16[128,1536]{1,0:T(8,128)(2,1)S(1)}, bf16[128,1536]{1,0:T(8,128)(2,1)S(1)}, u32[]{:S(2)}, u32[]{:S(2)}) collective-permute-start(bf16[128,1536]{1,0:T(8,128)(2,1)S(1)} %get-tuple-element.184), channel_id=1, source_target_pairs={{0,4},{1,5},{4,0},{5,1},{2,6},{3,7},{6,2},{7,3},{8,12},{9,13},{12,... | collective-permute-start | bytes 1179656 | tf_op jit(solution)/shard_map/ppermute | solution.py:66
  158.7 17.1 %all-to-all-start.2 = ((f32[8,1,128]{2,1,0:T(1,128)}), f32[8,1,128]{2,1,0:T(1,128)S(1)}, u32[]{:S(2)}, u32[]{:S(2)}) async-start(f32[8,1,128]{2,1,0:T(1,128)} %slice_bitcast_fusion.2), calls=%async_computation.2 | async-start | bytes 8192 | tf_op jit(solution)/shard_map/all_to_all | solution.py:54
  164.5 201.4 %reduce-scatter.3.cloned.1.call-start = ((), (), s32[]{:S(2)}) async-start(), calls=%async_computation.15 | async-start | bytes 3538944 | tf_op jit(solution)/shard_map/reduce_scatter | solution.py:1093
  180.5 23.2 %collective-permute-start.24 = (bf16[128,1536]{1,0:T(8,128)(2,1)}, bf16[128,1536]{1,0:T(8,128)(2,1)S(1)}, u32[]{:S(2)}, u32[]{:S(2)}) collective-permute-start(bf16[128,1536]{1,0:T(8,128)(2,1)} %get-tuple-element.188.refs_0_), channel_id=1, source_target_pairs={{0,4},{1,5},{4,0},{5,1},{2,6},{3,7},{6,2},{7,3},{8,12},{9,13},{12,... | collective-permute-start | bytes 1179656 | tf_op jit(solution)/shard_map/ppermute | solution.py:66
  181.7 24.9 %collective-permute-start.19 = (bf16[128,1536]{1,0:T(8,128)(2,1)}, bf16[128,1536]{1,0:T(8,128)(2,1)S(1)}, u32[]{:S(2)}, u32[]{:S(2)}) collective-permute-start(bf16[128,1536]{1,0:T(8,128)(2,1)} %get-tuple-element.188.refs_0_), channel_id=1, source_target_pairs={{0,2},{2,0},{1,3},{3,1},{4,6},{6,4},{5,7},{7,5},{8,10},{10,8},{9,1... | collective-permute-start | bytes 1179656 | tf_op jit(solution)/shard_map/ppermute | solution.py:58
  189.6 17.0 %collective-permute-start.21 = (bf16[128,1536]{1,0:T(8,128)(2,1)S(1)}, bf16[128,1536]{1,0:T(8,128)(2,1)S(1)}, u32[]{:S(2)}, u32[]{:S(2)}) collective-permute-start(bf16[128,1536]{1,0:T(8,128)(2,1)S(1)} %collective-permute-done.20.refs_2_), channel_id=1, source_target_pairs={{0,2},{2,0},{1,3},{3,1},{4,6},{6,4},{5,7},{7,5},{8,10},{10,8},{9,1... | collective-permute-start | bytes 1179656 | tf_op jit(solution)/shard_map/ppermute | solution.py:58
  310.5 61.6 %all-to-all-start.5 = ((bf16[16,192,384]{2,1,0:T(8,128)(2,1)}), bf16[16,192,384]{2,1,0:T(8,128)(2,1)}, u32[]{:S(2)}, u32[]{:S(2)}) async-start(bf16[16,192,384]{2,1,0:T(8,128)(2,1)} %constant_dynamic-update-slice_fusion), calls=%async_computation.6 | async-start | bytes 4718592 | tf_op jit(solution)/shard_map/all_to_all | solution.py:54
  372.8 43.7 %all-to-all-start.4 = ((bf16[16,96,768]{2,1,0:T(8,128)(2,1)}), bf16[16,96,768]{2,1,0:T(8,128)(2,1)}, u32[]{:S(2)}, u32[]{:S(2)}) async-start(bf16[16,96,768]{2,1,0:T(8,128)(2,1)} %bitcast.216), calls=%async_computation.5 | async-start | bytes 4718592 | tf_op jit(solution)/shard_map/all_to_all | solution.py:54
  383.8 17.0 %collective-permute-start.43 = (bf16[128,1536]{1,0:T(8,128)(2,1)}, bf16[128,1536]{1,0:T(8,128)(2,1)S(1)}, u32[]{:S(2)}, u32[]{:S(2)}) collective-permute-start(bf16[128,1536]{1,0:T(8,128)(2,1)} %copy-done.8), channel_id=1, source_target_pairs={{0,4},{1,5},{4,0},{5,1},{2,6},{3,7},{6,2},{7,3},{8,12},{9,13},{12,... | collective-permute-start | bytes 1179656 | tf_op jit(solution)/shard_map/ppermute | solution.py:66
  403.3 32.2 %collective-permute-start.44 = (bf16[144,1536]{1,0:T(8,128)(2,1)}, bf16[144,1536]{1,0:T(8,128)(2,1)S(1)}, u32[]{:S(2)}, u32[]{:S(2)}) collective-permute-start(bf16[144,1536]{1,0:T(8,128)(2,1)} %get-tuple-element.239.refs_0_), channel_id=1, source_target_pairs={{0,2},{2,0},{1,3},{3,1},{4,6},{6,4},{5,7},{7,5},{8,10},{10,8},{9,1... | collective-permute-start | bytes 1327112 | tf_op jit(solution)/shard_map/ppermute | solution.py:58
  404.9 19.1 %collective-permute-start.45 = (bf16[144,1536]{1,0:T(8,128)(2,1)}, bf16[144,1536]{1,0:T(8,128)(2,1)}, u32[]{:S(2)}, u32[]{:S(2)}) collective-permute-start(bf16[144,1536]{1,0:T(8,128)(2,1)} %get-tuple-element.239.refs_0_), channel_id=1, source_target_pairs={{0,1},{1,4},{4,5},{5,0},{2,3},{3,6},{6,7},{7,2},{8,9},{9,12},{12,1... | collective-permute-start | bytes 1327112 | tf_op jit(solution)/shard_map/ppermute | solution.py:66
  405.5 18.7 %collective-permute-start.47 = (bf16[144,1536]{1,0:T(8,128)(2,1)}, bf16[144,1536]{1,0:T(8,128)(2,1)}, u32[]{:S(2)}, u32[]{:S(2)}) collective-permute-start(bf16[144,1536]{1,0:T(8,128)(2,1)} %get-tuple-element.239.refs_0_), channel_id=1, source_target_pairs={{0,5},{1,0},{4,1},{5,4},{2,7},{3,2},{6,3},{7,6},{8,13},{9,8},{12,9... | collective-permute-start | bytes 1327112 | tf_op jit(solution)/shard_map/ppermute | solution.py:66
  407.6 21.2 %collective-permute-start.49 = (bf16[144,1536]{1,0:T(8,128)(2,1)}, bf16[144,1536]{1,0:T(8,128)(2,1)}, u32[]{:S(2)}, u32[]{:S(2)}) collective-permute-start(bf16[144,1536]{1,0:T(8,128)(2,1)} %get-tuple-element.239.refs_0_), channel_id=1, source_target_pairs={{0,4},{1,5},{4,0},{5,1},{2,6},{3,7},{6,2},{7,3},{8,12},{9,13},{12,... | collective-permute-start | bytes 1327112 | tf_op jit(solution)/shard_map/ppermute | solution.py:66
  462.8 21.1 %collective-permute-start.54 = (bf16[400,128]{1,0:T(8,128)(2,1)}, bf16[400,128]{1,0:T(8,128)(2,1)S(1)}, u32[]{:S(2)}, u32[]{:S(2)}) collective-permute-start(bf16[400,128]{1,0:T(8,128)(2,1)} %get-tuple-element.254), channel_id=1, source_target_pairs={{0,32},{32,64},{64,96},{96,0},{1,33},{33,65},{65,97},{97,1},{2,34}... | collective-permute-start | bytes 307208 | tf_op jit(solution)/shard_map/ppermute | solution.py:362
  499.0 33.4 %all-to-all-start.8 = ((bf16[16,192,384]{2,1,0:T(8,128)(2,1)}), bf16[16,192,384]{2,1,0:T(8,128)(2,1)}, u32[]{:S(2)}, u32[]{:S(2)}) async-start(bf16[16,192,384]{2,1,0:T(8,128)(2,1)} %constant_dynamic-update-slice_fusion.5), calls=%async_computation.10 | async-start | bytes 4718592 | tf_op jit(solution)/shard_map/all_to_all | solution.py:54
  532.4 39.8 %all-to-all-start.7 = ((bf16[16,96,768]{2,1,0:T(8,128)(2,1)}), bf16[16,96,768]{2,1,0:T(8,128)(2,1)}, u32[]{:S(2)}, u32[]{:S(2)}) async-start(bf16[16,96,768]{2,1,0:T(8,128)(2,1)} %bitcast.217), calls=%async_computation.9 | async-start | bytes 4718592 | tf_op jit(solution)/shard_map/all_to_all | solution.py:54
  540.7 67.8 %reduce-scatter.5.cloned.1.call-start = ((), (), s32[]{:S(2)}) async-start(), calls=%async_computation.16 | async-start | bytes 3538944 | tf_op jit(solution)/shard_map/reduce_scatter | solution.py:1147
  543.2 45.6 %collective-permute-start.59 = (f32[24,1536]{1,0:T(8,128)S(1)}, f32[24,1536]{1,0:T(8,128)S(1)}, u32[]{:S(2)}, u32[]{:S(2)}) collective-permute-start(f32[24,1536]{1,0:T(8,128)S(1)} %bitcast.255), channel_id=1, source_target_pairs={{0,0},{8,1},{16,2},{24,3},{32,4},{40,5},{48,6},{56,7},{64,8},{72,9... | collective-permute-start | bytes 442376 | tf_op jit(solution)/shard_map/ppermute | solution.py:1172
  581.3 17.7 %all-to-all-start.9 = ((bf16[8,12,1152]{2,1,0:T(8,128)(2,1)}), bf16[8,12,1152]{2,1,0:T(8,128)(2,1)S(1)}, u32[]{:S(2)}, u32[]{:S(2)}) async-start(bf16[8,12,1152]{2,1,0:T(8,128)(2,1)} %convert_element_type.239), calls=%async_computation.11 | async-start | bytes 589824 | tf_op jit(solution)/shard_map/all_to_all | solution.py:54
  (129 other events, 1067.4 us)
Sparse Core Ops, SparseCore 0:
  77.3 52.4 all-gather.3
  131.9 48.8 all-gather.5
  182.5 59.5 all-gather.7
  266.2 54.3 reduce-scatter.2
  543.6 64.7 reduce-scatter.4

commit v7 on v6

--- a/solution.py
+++ b/solution.py
@@ -222,8 +222,7 @@
 
 
 def retreat_kernel(extra, *refs):
-    n = 4 if extra else 1
-    parts, (h_ref, grad_ref, *refs) = refs[:n], refs[n:]
+    parts, (h_ref, grad_ref, *refs) = refs[:4], refs[4:]
     h = h_ref[...]
     r_in = inverse_rms(h)
     d_norm = parts_sum(parts)
@@ -1128,7 +1127,7 @@
         else:
             w_a, w_z, at = w_a0, w_z0, 0
         da, *parts, taps = conv_back(
-            l == 0, d_pre, following, s["u"], s["edge"], same, conv_here[l], d_raw, dz, w_a, w_z, at
+            False, d_pre, following, s["u"], s["edge"], same, conv_here[l], d_raw, dz, w_a, w_z, at
         )
         conv_full = jnp.zeros((CONV + 1, CH), f32)
         conv_full = lax.dynamic_update_slice_in_dim(
@@ -1144,7 +1143,7 @@
             a_part = a_part + small_block(conv_grads, head_grads).astype(f32)
         a_part = a_part.astype(bf)
         if l == 0:
-            parts = [lax.psum_scatter(parts[0], LINE, scatter_dimension=0, tiled=True)]
+            parts = line_parts(*parts, a_part)
             a_sums[l] = group_reduce(a_part)
         else:
             parts = line_parts(*parts, output)

time: 629 us -> 619 us (0.984)
  waiting for transfers between devices: 127 us -> 96.3 us
  local copies, waits for them, and re-layouts: 74.7 us -> 81.5 us
    all_to_all x9, waiting for transfers between devices: 63.9 us -> 36.2 us  [a2a(): return lax.all_to_all(a, axes, 0, 0, tiled=True)]
    ppermute x15 -> x18, starting transfers between devices: 15.9 us -> 20.2 us  [along_line(): return lax.ppermute(a, Y, [(i, (i + distance) % 4) for i in range(4)])]
    unnamed x186 -> x210, local copies, waits for them, and re-layouts: 29.5 us -> 26.7 us
    ppermute x14 -> x15, starting transfers between devices: 34.2 us -> 35.6 us  [core_swap(): return lax.ppermute(a, 'c', [(0, 1), (1, 0)])]
    ppermute x15 -> x18, waiting for transfers between devices: 31.6 us -> 32.1 us  [along_line(): return lax.ppermute(a, Y, [(i, (i + distance) % 4) for i in range(4)])]
  transfers between devices with their start and end apart: 74 -> 77, of which waited for: 20 -> 20; matrix products, arithmetic and copies ran while one was open for 18% -> 19% of each run, Pallas kernels for 19% -> 20%
where the time goes in v7:
time: 619 us; the launch traced here: 609 us
  starting transfers between devices  174 us (28%)
  Pallas kernels  159 us (26%)
  waiting for transfers between devices  96.3 us (16%)
  local copies, waits for them, and re-layouts  81.5 us (13%)
  matrix products  41.8 us (7%)
  other arithmetic  28.1 us (5%)
  between operations  16.3 us (3%)
  blocking collectives  11.2 us (2%)
    pallas_call x11, Pallas kernels, call(): pl.pallas_call(kernel, grid=(NS,), in_specs=ins, out_specs=outs, out_shap...  98.5 us
    all_to_all x9, starting transfers between devices, a2a(): return lax.all_to_all(a, axes, 0, 0, tiled=True)  55.4 us
    pallas_call x4, Pallas kernels, ordered_call(): pl.pallas_call(kernel, grid_spec=pltpu.PrefetchScalarGridSpec(num_scalar_...  43.1 us
    dot_general x15, matrix products, mm(): lax.dot_general(a, b, (((ca,), (cb,)), ((), ())), preferred_element_type=...  41.8 us
    ppermute x24, starting transfers between devices, around(): lax.ppermute(a, axis, [(i, (i + d) % 4) for i in range(4)])  39.2 us
    all_to_all x9, waiting for transfers between devices, a2a(): return lax.all_to_all(a, axes, 0, 0, tiled=True)  36.2 us
    ppermute x15, starting transfers between devices, core_swap(): return lax.ppermute(a, 'c', [(0, 1), (1, 0)])  35.6 us
    ppermute x18, waiting for transfers between devices, along_line(): return lax.ppermute(a, Y, [(i, (i + distance) % 4) for i in range(4)])  32.1 us
  transfers between devices with their start and end apart: 77, of which 20 were waited for; matrix products, arithmetic and copies ran while one was open for 19% of the time, Pallas kernels for 20%

profile of v7, /device:TPU:1, one launch (start us, length us, event | category | flops | bytes accessed | tf_op | source)
XLA Modules:
  0.0 608.9 jit_solution(11959011548739879323)
XLA Ops:
  13.2 6.0 all-to-all-start
  31.6 7.7 %all-to-all-start.1 = ((bf16[16,96,768]{2,1,0:T(8,128)(2,1)}), bf16[16,96,768]{2,1,0:T(8,128)(2,1)S(1)}, u32[]{:S(2)}, u32[]{:S(2)}) async-start(bf16[16,96,768]{2,1,0:T(8,128)(2,1)} %broadcast_in_dim.31), calls=%async_computation.1 | async-start | bytes 4718592 | tf_op jit(solution)/shard_map/all_to_all | solution.py:54
  51.8 9.9 %collective-permute-start.2 = (bf16[128,1536]{1,0:T(8,128)(2,1)}, bf16[128,1536]{1,0:T(8,128)(2,1)}, u32[]{:S(2)}, u32[]{:S(2)}) collective-permute-start(bf16[128,1536]{1,0:T(8,128)(2,1)} %collective-permute-done.1.refs_2_), channel_id=1, source_target_pairs={{0,2},{2,0},{1,3},{3,1},{4,6},{6,4},{5,7},{7,5},{8,10},{10,8},{9,1... | collective-permute-start | bytes 1179656 | tf_op jit(solution)/shard_map/ppermute | solution.py:58
  68.0 7.5 %collective-permute-done.7 = bf16[2,24,1536]{2,1,0:T(8,128)(2,1)S(1)} collective-permute-done((bf16[2,24,1536]{2,1,0:T(8,128)(2,1)S(1)}, bf16[2,24,1536]{2,1,0:T(8,128)(2,1)S(1)}, u32[]{:S(2)}, u32[]{:S(2)}) %collective-permute-start.7) | collective-permute-done | bytes 147488 | tf_op jit(solution)/shard_map/ppermute | solution.py:1030
  78.3 6.9 %place_project.2 = (bf16[1024,1536]{1,0:T(8,128)(2,1)}, bf16[1024,640]{1,0:T(8,128)(2,1)}, bf16[1024,128]{1,0:T(8,128)(2,1)}) custom-call(s32[8]{0:T(128)} %stack.186.pos_ref, bf16[128,1536]{1,0:T(8,128)(2,1)} %copy-done.28, bf16[128,1536]{1,0:T(8,128)(2,1)} %collective-permute-done.refs_1_, bf16[128,1536]{1,0:T(8,128)(2,1)} %collective-permute-done.1.refs_2_, ...), custom_call_target="tpu_custom_call" | custom-call | flops 360000000 | bytes 1800000 | tf_op jit(solution)/shard_map/place_project/pallas_call | solution.py:785
  93.0 11.5 %span_mix.2 = (bf16[1024,640]{1,0:T(8,128)(2,1)}, bf16[1024,640]{1,0:T(8,128)(2,1)}, f32[1024,384]{1,0:T(8,128)}, f32[4,384,128]{2,1,0:T(8,128)}, f32[1024,128]{...) custom-call(s32[2,4]{1,0:T(2,128)} %pad_add_fusion.seg_ref, ...), custom_call_target="tpu_custom_call" | custom-call | flops 400000000 | bytes 2000000 | tf_op jit(solution)/shard_map/span_mix/pallas_call | solution.py:785
  104.9 8.0 %collective-permute-start.10 = (bf16[400,128]{1,0:T(8,128)(2,1)}, bf16[400,128]{1,0:T(8,128)(2,1)S(1)}, u32[]{:S(2)}, u32[]{:S(2)}) collective-permute-start(bf16[400,128]{1,0:T(8,128)(2,1)} %get-tuple-element.172.own_ref), channel_id=1, source_target_pairs={{0,16},{8,24},{16,0},{24,8},{1,17},{9,25},{17,1},{25,9},{2,18},{10... | collective-permute-start | bytes 307208 | tf_op jit(solution)/shard_map/ppermute | solution.py:361
  138.7 9.6 %span_gate.2 = (f32[1024,384]{1,0:T(8,128)}, bf16[512,1536]{1,0:T(8,128)(2,1)}, bf16[512,1536]{1,0:T(8,128)(2,1)}, f32[8,1024]{1,0:T(8,128)}, f32[384,128]{1,0:T(8,128)}) custom-call(s32[4]{0:T(128)} %pad_add_fusion.1.order_ref, s32[2,4]{1,0:T(2,128)} %pad_add_fusion.seg_ref, s32[1]{0:T(128)} %bitcast.6.at_ref, bf16[400,128]{1,0:T(8,128)(2,1)} %copy-done.50, ...), custom_call_target="tpu_custom_call" | custom-call | flops 400000000 | bytes 2000000 | tf_op jit(solution)/shard_map/span_gate/pallas_call | solution.py:803
  166.6 10.6 %all-to-all-done.2 = f32[8,1,128]{2,1,0:T(1,128)S(1)} async-done(((f32[8,1,128]{2,1,0:T(1,128)}), f32[8,1,128]{2,1,0:T(1,128)S(1)}, u32[]{:S(2)}, u32[]{:S(2)}) %all-to-all-start.2) | async-done | bytes 4128 | tf_op jit(solution)/shard_map/all_to_all | solution.py:54
  184.0 7.1 %collective-permute-done.20.refs_2_ = bf16[128,1536]{1,0:T(8,128)(2,1)S(1)} collective-permute-done((bf16[128,1536]{1,0:T(8,128)(2,1)}, bf16[128,1536]{1,0:T(8,128)(2,1)S(1)}, u32[]{:S(2)}, u32[]{:S(2)}) %collective-permute-start.20) | collective-permute-done | bytes 393248 | tf_op jit(solution)/shard_map/ppermute | solution.py:66
  196.4 9.5 %collective-permute-done.24.refs_6_ = bf16[128,1536]{1,0:T(8,128)(2,1)S(1)} collective-permute-done((bf16[128,1536]{1,0:T(8,128)(2,1)}, bf16[128,1536]{1,0:T(8,128)(2,1)S(1)}, u32[]{:S(2)}, u32[]{:S(2)}) %collective-permute-start.24) | collective-permute-done | bytes 393248 | tf_op jit(solution)/shard_map/ppermute | solution.py:66
  210.5 7.0 %place_project.3 = (bf16[1024,1536]{1,0:T(8,128)(2,1)}, bf16[1024,640]{1,0:T(8,128)(2,1)}, bf16[1024,128]{1,0:T(8,128)(2,1)}) custom-call(s32[8]{0:T(128)} %stack.186.pos_ref, bf16[128,1536]{1,0:T(8,128)(2,1)} %get-tuple-element.194.refs_0_, bf16[128,1536]{1,0:T(8,128)(2,1)} %copy-done.45, bf16[128,1536]{1,0:T(8,128)(2,1)} %copy-done.42, ...), custom_call_target="tpu_custom_call" | custom-call | flops 360000000 | bytes 1800000 | tf_op jit(solution)/shard_map/place_project/pallas_call | solution.py:785
  225.0 11.4 %span_mix.3 = (bf16[1024,640]{1,0:T(8,128)(2,1)}, bf16[1024,640]{1,0:T(8,128)(2,1)}, f32[1024,384]{1,0:T(8,128)}, f32[4,384,128]{2,1,0:T(8,128)}, f32[1024,128]{...) custom-call(s32[2,4]{1,0:T(2,128)} %pad_add_fusion.seg_ref, ...), custom_call_target="tpu_custom_call" | custom-call | flops 400000000 | bytes 2000000 | tf_op jit(solution)/shard_map/span_mix/pallas_call | solution.py:785
  256.5 9.1 %span_gate.3 = (f32[1024,384]{1,0:T(8,128)}, bf16[1024,1536]{1,0:T(8,128)(2,1)}, f32[8,1024]{1,0:T(8,128)}, f32[384,128]{1,0:T(8,128)}) custom-call(s32[4]{0:T(128)} %pad_add_fusion.1.order_ref, s32[2,4]{1,0:T(2,128)} %pad_add_fusion.seg_ref, s32[1]{0:T(128)} %bitcast.6.at_ref, bf16[400,128]{1,0:T(8,128)(2,1)} %copy-done.71, bf16[400,128]{1,0:T(8,128)(2,1)} %copy-done.72, ...), custom_call_target="tpu_custom_call" | custom-call | flops 400000000 | bytes 2000000 | tf_op jit(solution)/shard_map/span_gate/pallas_call | solution.py:803
  266.4 11.2 %all_to_all.57 = f32[8,2,1024]{2,1,0:T(2,128)S(1)} all-to-all(f32[8,2,1024]{2,1,0:T(2,128)S(1)} %broadcast_in_dim.38), channel_id=1, replica_groups=mesh['z'=4,'x'=4,'yh'=2,'c'=2,'yl'=2] {'yh','c','yl'}, dimensions={0} | all-to-all | bytes 131072 | tf_op jit(solution)/shard_map/all_to_all | solution.py:54
  278.3 7.8 %span_gate_back.2 = (bf16[1024,384]{1,0:T(8,128)(2,1)}, bf16[1024,384]{1,0:T(8,128)(2,1)}, bf16[1024,384]{1,0:T(8,128)(2,1)}, f32[4,384,128]{2,1,0:T(8,128)}, f3...) custom-call(s32[2,4]{1,0:T(2,128)} %pad_add_fusion.seg_ref, f32[1024,384]{1,0:T(8,128)} %fusion.46.rest_0_.grad_ref, ...), custom_call_target="tpu_custom_call" | custom-call | flops 480000000 | bytes 2400000 | tf_op jit(solution)/shard_map/span_gate_back/pallas_call | solution.py:785
  315.3 7.9 %span_mix_back.2 = (f32[1024,384]{1,0:T(8,128)}, bf16[1024,256]{1,0:T(8,128)(2,1)}) custom-call(bf16[1024,640]{1,0:T(8,128)(2,1)} %get-tuple-element.210.v_ref, f32[1024,128]{1,0:T(8,128)} %get-tuple-element.229.step_ref, f32[1024,128]{1,0:T(8,128)} %get-tuple-element.209.run_ref, s32[1024,1]{1,0:T(8,128)} %copy.268.segc_ref, s32[4,1,256]{2,1,0:T(1,128)} %bitcast.254, ...), custom_call_target="tpu_custom_call" | custom-call | flops 560000000 | bytes 2800000 | tf_op jit(solution)/shard_map/span_mix_back/pallas_call | solution.py:785
  323.2 12.2 %span_end.2 = (bf16[1024,640]{1,0:T(8,128)(2,1)}, bf16[1024,128]{1,0:T(8,128)(2,1)}, f32[8,128]{1,0:T(8,128)}) custom-call(s32[2,4]{1,0:T(2,128)} %pad_add_fusion.seg_ref, s32[1]{0:T(128)} %bitcast.6.at_ref, bf16[400,128]{1,0:T(8,128)(2,1)} %copy-done.65, bf16[400,128]{1,0:T(8,128)(2,1)} %copy-done.67, bf16[400,128]{1,0:T(8,128)(2,1)} %copy-done.68, ...), custom_call_target="tpu_custom_call" | custom-call | flops 640000000 | bytes 3200000 | tf_op jit(solution)/shard_map/span_end/pallas_call | solution.py:785
  343.5 12.1 %conv_back.2 = (bf16[1024,768]{1,0:T(8,128)(2,1)}, bf16[512,1536]{1,0:T(8,128)(2,1)}, bf16[512,1536]{1,0:T(8,128)(2,1)}, f32[8,640]{1,0:T(8,128)}) custom-call(s32[4]{0:T(128)} %pad_add_fusion.1.order_ref, bf16[1024,640]{1,0:T(8,128)(2,1)} %get-tuple-element.234.dpre_ref.next_ref, bf16[1024,640]{1,0:T(8,128)(2,1)} %get-tuple-element.234.dpre_ref.next_ref, ...), custom_call_target="tpu_custom_call" | custom-call | flops 400000000 | bytes 2000000 | tf_op jit(solution)/shard_map/conv_back/pallas_call | solution.py:803
  359.8 6.5 %convolution_convert_fusion = bf16[1536,768]{1,0:T(8,128)(2,1)} fusion(bf16[1024,1536]{1,0:T(8,128)(2,1)} %get-tuple-element.199, bf16[1024,768]{1,0:T(8,128)(2,1)} %get-tuple-element.246), kind=kOutput, calls=%fused_computation.5 | convolution fusion | flops 2417098752 | bytes 7077888 | tf_op jit(solution)/shard_map/dot_general | solution.py:50
  373.2 7.0 %all-to-all-start.4 = ((bf16[16,96,768]{2,1,0:T(8,128)(2,1)}), bf16[16,96,768]{2,1,0:T(8,128)(2,1)}, u32[]{:S(2)}, u32[]{:S(2)}) async-start(bf16[16,96,768]{2,1,0:T(8,128)(2,1)} %bitcast.219), calls=%async_computation.5 | async-start | bytes 4718592 | tf_op jit(solution)/shard_map/all_to_all | solution.py:54
  386.8 7.1 %collective-permute-done.41.refs_1_ = bf16[128,1536]{1,0:T(8,128)(2,1)S(1)} collective-permute-done((bf16[128,1536]{1,0:T(8,128)(2,1)}, bf16[128,1536]{1,0:T(8,128)(2,1)S(1)}, u32[]{:S(2)}, u32[]{:S(2)}) %collective-permute-start.41) | collective-permute-done | bytes 393248 | tf_op jit(solution)/shard_map/ppermute | solution.py:66
  393.8 7.4 %collective-permute-done.43.refs_3_ = bf16[128,1536]{1,0:T(8,128)(2,1)S(1)} collective-permute-done((bf16[128,1536]{1,0:T(8,128)(2,1)}, bf16[128,1536]{1,0:T(8,128)(2,1)S(1)}, u32[]{:S(2)}, u32[]{:S(2)}) %collective-permute-start.43) | collective-permute-done | bytes 393248 | tf_op jit(solution)/shard_map/ppermute | solution.py:66
  408.9 8.4 %all-to-all-done.4 = bf16[16,96,768]{2,1,0:T(8,128)(2,1)} async-done(((bf16[16,96,768]{2,1,0:T(8,128)(2,1)}), bf16[16,96,768]{2,1,0:T(8,128)(2,1)}, u32[]{:S(2)}, u32[]{:S(2)}) %all-to-all-start.4) | async-done | bytes 2359328 | tf_op jit(solution)/shard_map/all_to_all | solution.py:54
  440.9 8.2 %span_gate_back.3 = (bf16[1024,384]{1,0:T(8,128)(2,1)}, bf16[1024,384]{1,0:T(8,128)(2,1)}, bf16[1024,384]{1,0:T(8,128)(2,1)}, f32[4,384,128]{2,1,0:T(8,128)}, f3...) custom-call(s32[2,4]{1,0:T(2,128)} %pad_add_fusion.seg_ref, bf16[1024,1536]{1,0:T(8,128)(2,1)} %get-tuple-element.252.grad_ref, ...), custom_call_target="tpu_custom_call" | custom-call | flops 480000000 | bytes 2400000 | tf_op jit(solution)/shard_map/span_gate_back/pallas_call | solution.py:785
  471.9 8.8 %span_mix_back.3 = (f32[1024,384]{1,0:T(8,128)}, bf16[1024,256]{1,0:T(8,128)(2,1)}) custom-call(bf16[1024,640]{1,0:T(8,128)(2,1)} %get-tuple-element.183.v_ref, f32[1024,128]{1,0:T(8,128)} %get-tuple-element.270.step_ref, f32[1024,128]{1,0:T(8,128)} %get-tuple-element.182.run_ref, s32[1024,1]{1,0:T(8,128)} %copy.268.segc_ref, s32[4,1,256]{2,1,0:T(1,128)} %bitcast.255, ...), custom_call_target="tpu_custom_call" | custom-call | flops 560000000 | bytes 2800000 | tf_op jit(solution)/shard_map/span_mix_back/pallas_call | solution.py:785
  481.4 12.2 %span_end.3 = (bf16[1024,640]{1,0:T(8,128)(2,1)}, bf16[1024,128]{1,0:T(8,128)(2,1)}, f32[8,128]{1,0:T(8,128)}) custom-call(s32[2,4]{1,0:T(2,128)} %pad_add_fusion.seg_ref, s32[1]{0:T(128)} %bitcast.6.at_ref, bf16[400,128]{1,0:T(8,128)(2,1)} %copy-done.66, bf16[400,128]{1,0:T(8,128)(2,1)} %copy-done.69, bf16[400,128]{1,0:T(8,128)(2,1)} %copy-done.70, ...), custom_call_target="tpu_custom_call" | custom-call | flops 640000000 | bytes 3200000 | tf_op jit(solution)/shard_map/span_end/pallas_call | solution.py:785
  502.0 12.2 %conv_back.3 = (bf16[1024,768]{1,0:T(8,128)(2,1)}, bf16[512,1536]{1,0:T(8,128)(2,1)}, bf16[512,1536]{1,0:T(8,128)(2,1)}, f32[8,640]{1,0:T(8,128)}) custom-call(s32[4]{0:T(128)} %pad_add_fusion.1.order_ref, bf16[1024,640]{1,0:T(8,128)(2,1)} %get-tuple-element.275.dpre_ref.next_ref, bf16[1024,640]{1,0:T(8,128)(2,1)} %get-tuple-element.275.dpre_ref.next_ref, ...), custom_call_target="tpu_custom_call" | custom-call | flops 400000000 | bytes 2000000 | tf_op jit(solution)/shard_map/conv_back/pallas_call | solution.py:803
  524.8 6.5 %add_convert_fusion = bf16[1536,768]{1,0:T(8,128)(2,1)} fusion(bf16[1024,1536]{1,0:T(8,128)(2,1)} %get-tuple-element.175, bf16[1024,768]{1,0:T(8,128)(2,1)} %get-tuple-element.279, bf16[1536,98]{1,0:T(8,128)(2,1)} %convert_element_type.234), kind=kOutput, calls=%fused_computation.2 | convolution fusion | flops 2419458048 | bytes 7378944 | tf_op jit(solution)/shard_map/dot_general | solution.py:50
  532.8 7.0 %all-to-all-start.7 = ((bf16[16,96,768]{2,1,0:T(8,128)(2,1)}), bf16[16,96,768]{2,1,0:T(8,128)(2,1)}, u32[]{:S(2)}, u32[]{:S(2)}) async-start(bf16[16,96,768]{2,1,0:T(8,128)(2,1)} %bitcast.220), calls=%async_computation.8 | async-start | bytes 4718592 | tf_op jit(solution)/shard_map/all_to_all | solution.py:54
  559.5 7.7 %collective-permute-start.63 = (f32[24,1536]{1,0:T(8,128)}, f32[24,1536]{1,0:T(8,128)}, u32[]{:S(2)}, u32[]{:S(2)}) collective-permute-start(f32[24,1536]{1,0:T(8,128)} %bitcast.258), channel_id=1, source_target_pairs={{0,0},{8,1},{16,2},{24,3},{32,4},{40,5},{48,6},{56,7},{64,8},{72,9... | collective-permute-start | bytes 442376 | tf_op jit(solution)/shard_map/ppermute | solution.py:1171
  580.5 9.2 %all-to-all-start.9 = ((bf16[8,12,1152]{2,1,0:T(8,128)(2,1)}), bf16[8,12,1152]{2,1,0:T(8,128)(2,1)S(1)}, u32[]{:S(2)}, u32[]{:S(2)}) async-start(bf16[8,12,1152]{2,1,0:T(8,128)(2,1)} %convert_element_type.239), calls=%async_computation.10 | async-start | bytes 589824 | tf_op jit(solution)/shard_map/all_to_all | solution.py:54
  (580 shorter events, 311.3 us)
Async XLA Ops:
  31.6 44.7 %all-to-all-start.1 = ((bf16[16,96,768]{2,1,0:T(8,128)(2,1)}), bf16[16,96,768]{2,1,0:T(8,128)(2,1)S(1)}, u32[]{:S(2)}, u32[]{:S(2)}) async-start(bf16[16,96,768]{2,1,0:T(8,128)(2,1)} %broadcast_in_dim.31), calls=%async_computation.1 | async-start | bytes 4718592 | tf_op jit(solution)/shard_map/all_to_all | solution.py:54
  39.3 91.9 %all-gather.4.cloned.1.call-start = ((), (), s32[]{:S(2)}) async-start(), calls=%async_computation.11 | async-start | bytes 3760128 | tf_op jit(solution)/shard_map/all_gather | solution.py:273
  40.7 21.0 %collective-permute-start.3 = (bf16[128,1536]{1,0:T(8,128)(2,1)S(1)}, bf16[128,1536]{1,0:T(8,128)(2,1)}, u32[]{:S(2)}, u32[]{:S(2)}) collective-permute-start(bf16[128,1536]{1,0:T(8,128)(2,1)S(1)} %multiply_convert_fusion.refs_0_), channel_id=1, source_target_pairs={{0,5},{1,0},{4,1},{5,4},{2,7},{3,2},{6,3},{7,6},{8,13},{9,8},{12,9... | collective-permute-start | bytes 1179656 | tf_op jit(solution)/shard_map/ppermute | solution.py:66
  43.1 18.6 %collective-permute-start.5 = (bf16[128,1536]{1,0:T(8,128)(2,1)S(1)}, bf16[128,1536]{1,0:T(8,128)(2,1)}, u32[]{:S(2)}, u32[]{:S(2)}) collective-permute-start(bf16[128,1536]{1,0:T(8,128)(2,1)S(1)} %multiply_convert_fusion.refs_0_), channel_id=1, source_target_pairs={{0,4},{1,5},{4,0},{5,1},{2,6},{3,7},{6,2},{7,3},{8,12},{9,13},{12,... | collective-permute-start | bytes 1179656 | tf_op jit(solution)/shard_map/ppermute | solution.py:66
  49.3 27.0 %collective-permute-start = (bf16[128,1536]{1,0:T(8,128)(2,1)S(1)}, bf16[128,1536]{1,0:T(8,128)(2,1)}, u32[]{:S(2)}, u32[]{:S(2)}) collective-permute-start(bf16[128,1536]{1,0:T(8,128)(2,1)S(1)} %multiply_convert_fusion.refs_0_), channel_id=1, source_target_pairs={{0,2},{2,0},{1,3},{3,1},{4,6},{6,4},{5,7},{7,5},{8,10},{10,8},{9,1... | collective-permute-start | bytes 1179656 | tf_op jit(solution)/shard_map/ppermute | solution.py:58
  51.8 24.5 %collective-permute-start.2 = (bf16[128,1536]{1,0:T(8,128)(2,1)}, bf16[128,1536]{1,0:T(8,128)(2,1)}, u32[]{:S(2)}, u32[]{:S(2)}) collective-permute-start(bf16[128,1536]{1,0:T(8,128)(2,1)} %collective-permute-done.1.refs_2_), channel_id=1, source_target_pairs={{0,2},{2,0},{1,3},{3,1},{4,6},{6,4},{5,7},{7,5},{8,10},{10,8},{9,1... | collective-permute-start | bytes 1179656 | tf_op jit(solution)/shard_map/ppermute | solution.py:58
  76.4 132.7 %all-gather.6.cloned.1.call-start = ((), (), s32[]{:S(2)}) async-start(), calls=%async_computation.12 | async-start | bytes 3760128 | tf_op jit(solution)/shard_map/all_gather | solution.py:273
  85.9 164.9 %all-gather.8.cloned.1.call-start = ((), (), s32[]{:S(2)}) async-start(), calls=%async_computation.13 | async-start | bytes 3538944 | tf_op jit(solution)/shard_map/all_gather | solution.py:1032
  104.9 17.1 %collective-permute-start.10 = (bf16[400,128]{1,0:T(8,128)(2,1)}, bf16[400,128]{1,0:T(8,128)(2,1)S(1)}, u32[]{:S(2)}, u32[]{:S(2)}) collective-permute-start(bf16[400,128]{1,0:T(8,128)(2,1)} %get-tuple-element.172.own_ref), channel_id=1, source_target_pairs={{0,16},{8,24},{16,0},{24,8},{1,17},{9,25},{17,1},{25,9},{2,18},{10... | collective-permute-start | bytes 307208 | tf_op jit(solution)/shard_map/ppermute | solution.py:361
  154.9 22.3 %collective-permute-start.16 = (bf16[128,1536]{1,0:T(8,128)(2,1)}, bf16[128,1536]{1,0:T(8,128)(2,1)S(1)}, u32[]{:S(2)}, u32[]{:S(2)}) collective-permute-start(bf16[128,1536]{1,0:T(8,128)(2,1)} %get-tuple-element.188), channel_id=1, source_target_pairs={{0,1},{1,4},{4,5},{5,0},{2,3},{3,6},{6,7},{7,2},{8,9},{9,12},{12,1... | collective-permute-start | bytes 1179656 | tf_op jit(solution)/shard_map/ppermute | solution.py:66
  157.5 19.7 %collective-permute-start.17 = (bf16[128,1536]{1,0:T(8,128)(2,1)S(1)}, bf16[128,1536]{1,0:T(8,128)(2,1)S(1)}, u32[]{:S(2)}, u32[]{:S(2)}) collective-permute-start(bf16[128,1536]{1,0:T(8,128)(2,1)S(1)} %get-tuple-element.189), channel_id=1, source_target_pairs={{0,5},{1,0},{4,1},{5,4},{2,7},{3,2},{6,3},{7,6},{8,13},{9,8},{12,9... | collective-permute-start | bytes 1179656 | tf_op jit(solution)/shard_map/ppermute | solution.py:66
  157.6 19.6 %collective-permute-start.18 = (bf16[128,1536]{1,0:T(8,128)(2,1)S(1)}, bf16[128,1536]{1,0:T(8,128)(2,1)S(1)}, u32[]{:S(2)}, u32[]{:S(2)}) collective-permute-start(bf16[128,1536]{1,0:T(8,128)(2,1)S(1)} %get-tuple-element.190), channel_id=1, source_target_pairs={{0,4},{1,5},{4,0},{5,1},{2,6},{3,7},{6,2},{7,3},{8,12},{9,13},{12,... | collective-permute-start | bytes 1179656 | tf_op jit(solution)/shard_map/ppermute | solution.py:66
  160.7 16.5 %all-to-all-start.2 = ((f32[8,1,128]{2,1,0:T(1,128)}), f32[8,1,128]{2,1,0:T(1,128)S(1)}, u32[]{:S(2)}, u32[]{:S(2)}) async-start(f32[8,1,128]{2,1,0:T(1,128)} %slice_bitcast_fusion.2), calls=%async_computation.2 | async-start | bytes 8192 | tf_op jit(solution)/shard_map/all_to_all | solution.py:54
  165.5 200.7 %reduce-scatter.2.cloned.1.call-start = ((), (), s32[]{:S(2)}) async-start(), calls=%async_computation.14 | async-start | bytes 3538944 | tf_op jit(solution)/shard_map/reduce_scatter | solution.py:1092
  182.0 23.9 %collective-permute-start.24 = (bf16[128,1536]{1,0:T(8,128)(2,1)}, bf16[128,1536]{1,0:T(8,128)(2,1)S(1)}, u32[]{:S(2)}, u32[]{:S(2)}) collective-permute-start(bf16[128,1536]{1,0:T(8,128)(2,1)} %get-tuple-element.194.refs_0_), channel_id=1, source_target_pairs={{0,4},{1,5},{4,0},{5,1},{2,6},{3,7},{6,2},{7,3},{8,12},{9,13},{12,... | collective-permute-start | bytes 1179656 | tf_op jit(solution)/shard_map/ppermute | solution.py:66
  183.0 26.0 %collective-permute-start.19 = (bf16[128,1536]{1,0:T(8,128)(2,1)}, bf16[128,1536]{1,0:T(8,128)(2,1)S(1)}, u32[]{:S(2)}, u32[]{:S(2)}) collective-permute-start(bf16[128,1536]{1,0:T(8,128)(2,1)} %get-tuple-element.194.refs_0_), channel_id=1, source_target_pairs={{0,2},{2,0},{1,3},{3,1},{4,6},{6,4},{5,7},{7,5},{8,10},{10,8},{9,1... | collective-permute-start | bytes 1179656 | tf_op jit(solution)/shard_map/ppermute | solution.py:58
  191.2 17.8 %collective-permute-start.21 = (bf16[128,1536]{1,0:T(8,128)(2,1)S(1)}, bf16[128,1536]{1,0:T(8,128)(2,1)S(1)}, u32[]{:S(2)}, u32[]{:S(2)}) collective-permute-start(bf16[128,1536]{1,0:T(8,128)(2,1)S(1)} %collective-permute-done.20.refs_2_), channel_id=1, source_target_pairs={{0,2},{2,0},{1,3},{3,1},{4,6},{6,4},{5,7},{7,5},{8,10},{10,8},{9,1... | collective-permute-start | bytes 1179656 | tf_op jit(solution)/shard_map/ppermute | solution.py:58
  192.4 16.6 %collective-permute-start.23 = (bf16[128,1536]{1,0:T(8,128)(2,1)S(1)}, bf16[128,1536]{1,0:T(8,128)(2,1)}, u32[]{:S(2)}, u32[]{:S(2)}) collective-permute-start(bf16[128,1536]{1,0:T(8,128)(2,1)S(1)} %collective-permute-done.22.refs_4_), channel_id=1, source_target_pairs={{0,2},{2,0},{1,3},{3,1},{4,6},{6,4},{5,7},{7,5},{8,10},{10,8},{9,1... | collective-permute-start | bytes 1179656 | tf_op jit(solution)/shard_map/ppermute | solution.py:58
  310.9 62.3 %all-to-all-start.5 = ((bf16[16,192,384]{2,1,0:T(8,128)(2,1)}), bf16[16,192,384]{2,1,0:T(8,128)(2,1)}, u32[]{:S(2)}, u32[]{:S(2)}) async-start(bf16[16,192,384]{2,1,0:T(8,128)(2,1)} %constant_dynamic-update-slice_fusion), calls=%async_computation.6 | async-start | bytes 4718592 | tf_op jit(solution)/shard_map/all_to_all | solution.py:54
  373.2 44.0 %all-to-all-start.4 = ((bf16[16,96,768]{2,1,0:T(8,128)(2,1)}), bf16[16,96,768]{2,1,0:T(8,128)(2,1)}, u32[]{:S(2)}, u32[]{:S(2)}) async-start(bf16[16,96,768]{2,1,0:T(8,128)(2,1)} %bitcast.219), calls=%async_computation.5 | async-start | bytes 4718592 | tf_op jit(solution)/shard_map/all_to_all | solution.py:54
  383.9 17.3 %collective-permute-start.43 = (bf16[128,1536]{1,0:T(8,128)(2,1)}, bf16[128,1536]{1,0:T(8,128)(2,1)S(1)}, u32[]{:S(2)}, u32[]{:S(2)}) collective-permute-start(bf16[128,1536]{1,0:T(8,128)(2,1)} %copy-done.12), channel_id=1, source_target_pairs={{0,4},{1,5},{4,0},{5,1},{2,6},{3,7},{6,2},{7,3},{8,12},{9,13},{12,... | collective-permute-start | bytes 1179656 | tf_op jit(solution)/shard_map/ppermute | solution.py:66
  403.6 32.1 %collective-permute-start.44 = (bf16[144,1536]{1,0:T(8,128)(2,1)}, bf16[144,1536]{1,0:T(8,128)(2,1)S(1)}, u32[]{:S(2)}, u32[]{:S(2)}) collective-permute-start(bf16[144,1536]{1,0:T(8,128)(2,1)} %get-tuple-element.245.refs_0_), channel_id=1, source_target_pairs={{0,2},{2,0},{1,3},{3,1},{4,6},{6,4},{5,7},{7,5},{8,10},{10,8},{9,1... | collective-permute-start | bytes 1327112 | tf_op jit(solution)/shard_map/ppermute | solution.py:58
  405.0 19.7 %collective-permute-start.45 = (bf16[144,1536]{1,0:T(8,128)(2,1)}, bf16[144,1536]{1,0:T(8,128)(2,1)S(1)}, u32[]{:S(2)}, u32[]{:S(2)}) collective-permute-start(bf16[144,1536]{1,0:T(8,128)(2,1)} %get-tuple-element.245.refs_0_), channel_id=1, source_target_pairs={{0,1},{1,4},{4,5},{5,0},{2,3},{3,6},{6,7},{7,2},{8,9},{9,12},{12,1... | collective-permute-start | bytes 1327112 | tf_op jit(solution)/shard_map/ppermute | solution.py:66
  405.6 19.4 %collective-permute-start.47 = (bf16[144,1536]{1,0:T(8,128)(2,1)}, bf16[144,1536]{1,0:T(8,128)(2,1)S(1)}, u32[]{:S(2)}, u32[]{:S(2)}) collective-permute-start(bf16[144,1536]{1,0:T(8,128)(2,1)} %get-tuple-element.245.refs_0_), channel_id=1, source_target_pairs={{0,5},{1,0},{4,1},{5,4},{2,7},{3,2},{6,3},{7,6},{8,13},{9,8},{12,9... | collective-permute-start | bytes 1327112 | tf_op jit(solution)/shard_map/ppermute | solution.py:66
  407.7 21.1 %collective-permute-start.49 = (bf16[144,1536]{1,0:T(8,128)(2,1)}, bf16[144,1536]{1,0:T(8,128)(2,1)S(1)}, u32[]{:S(2)}, u32[]{:S(2)}) collective-permute-start(bf16[144,1536]{1,0:T(8,128)(2,1)} %get-tuple-element.245.refs_0_), channel_id=1, source_target_pairs={{0,4},{1,5},{4,0},{5,1},{2,6},{3,7},{6,2},{7,3},{8,12},{9,13},{12,... | collective-permute-start | bytes 1327112 | tf_op jit(solution)/shard_map/ppermute | solution.py:66
  461.7 18.9 %collective-permute-start.54 = (bf16[400,128]{1,0:T(8,128)(2,1)}, bf16[400,128]{1,0:T(8,128)(2,1)S(1)}, u32[]{:S(2)}, u32[]{:S(2)}) collective-permute-start(bf16[400,128]{1,0:T(8,128)(2,1)} %get-tuple-element.260), channel_id=1, source_target_pairs={{0,32},{32,64},{64,96},{96,0},{1,33},{33,65},{65,97},{97,1},{2,34}... | collective-permute-start | bytes 307208 | tf_op jit(solution)/shard_map/ppermute | solution.py:361
  496.7 34.6 %all-to-all-start.8 = ((bf16[16,192,384]{2,1,0:T(8,128)(2,1)}), bf16[16,192,384]{2,1,0:T(8,128)(2,1)S(1)}, u32[]{:S(2)}, u32[]{:S(2)}) async-start(bf16[16,192,384]{2,1,0:T(8,128)(2,1)} %copy-done.19), calls=%async_computation.9 | async-start | bytes 4718592 | tf_op jit(solution)/shard_map/all_to_all | solution.py:54
  514.2 30.3 %collective-permute-start.58 = (bf16[512,1536]{1,0:T(8,128)(2,1)}, bf16[512,1536]{1,0:T(8,128)(2,1)}, u32[]{:S(2)}, u32[]{:S(2)}) collective-permute-start(bf16[512,1536]{1,0:T(8,128)(2,1)} %get-tuple-element.278), channel_id=1, source_target_pairs={{0,2},{2,0},{1,3},{3,1},{4,6},{6,4},{5,7},{7,5},{8,10},{10,8},{9,1... | collective-permute-start | bytes 4718600 | tf_op jit(solution)/shard_map/ppermute | solution.py:58
  532.8 39.3 %all-to-all-start.7 = ((bf16[16,96,768]{2,1,0:T(8,128)(2,1)}), bf16[16,96,768]{2,1,0:T(8,128)(2,1)}, u32[]{:S(2)}, u32[]{:S(2)}) async-start(bf16[16,96,768]{2,1,0:T(8,128)(2,1)} %bitcast.220), calls=%async_computation.8 | async-start | bytes 4718592 | tf_op jit(solution)/shard_map/all_to_all | solution.py:54
  548.2 18.9 %collective-permute-start.59 = (bf16[128,1536]{1,0:T(8,128)(2,1)}, bf16[128,1536]{1,0:T(8,128)(2,1)S(1)}, u32[]{:S(2)}, u32[]{:S(2)}) collective-permute-start(bf16[128,1536]{1,0:T(8,128)(2,1)} %get-tuple-element.286), channel_id=1, source_target_pairs={{0,1},{1,4},{4,5},{5,0},{2,3},{3,6},{6,7},{7,2},{8,9},{9,12},{12,1... | collective-permute-start | bytes 1179656 | tf_op jit(solution)/shard_map/ppermute | solution.py:66
  549.2 18.0 %collective-permute-start.60 = (bf16[128,1536]{1,0:T(8,128)(2,1)}, bf16[128,1536]{1,0:T(8,128)(2,1)S(1)}, u32[]{:S(2)}, u32[]{:S(2)}) collective-permute-start(bf16[128,1536]{1,0:T(8,128)(2,1)} %get-tuple-element.287), channel_id=1, source_target_pairs={{0,5},{1,0},{4,1},{5,4},{2,7},{3,2},{6,3},{7,6},{8,13},{9,8},{12,9... | collective-permute-start | bytes 1179656 | tf_op jit(solution)/shard_map/ppermute | solution.py:66
  559.5 30.3 %collective-permute-start.63 = (f32[24,1536]{1,0:T(8,128)}, f32[24,1536]{1,0:T(8,128)}, u32[]{:S(2)}, u32[]{:S(2)}) collective-permute-start(f32[24,1536]{1,0:T(8,128)} %bitcast.258), channel_id=1, source_target_pairs={{0,0},{8,1},{16,2},{24,3},{32,4},{40,5},{48,6},{56,7},{64,8},{72,9... | collective-permute-start | bytes 442376 | tf_op jit(solution)/shard_map/ppermute | solution.py:1171
  (145 other events, 1266.9 us)
Sparse Core Ops, SparseCore 0:
  76.5 53.1 all-gather.3
  131.8 49.0 all-gather.5
  182.6 60.8 all-gather.7
  265.8 56.6 reduce-scatter.1
